TPU v7x, 32 devices: a whole 2x2x4 slice. The times are simulated.
32 devices in a mesh: dp: 8 (over y, x, core), seq: 4 (over z).
Axes of the slice: x: 2, y: 2, z: 4, core: 2. Of those that a mesh axis runs over, the one named last changes fastest.
Arguments:
- block_in: bfloat16 [8, 2048, 1536], P('dp', 'seq'), may hold values from -6 to 6
- cotangent: bfloat16 [8, 2048, 1536], P('dp', 'seq'), may hold values from -6 to 6
- segment_ids: int32 [8, 2048], P('dp'), may hold values from 0 to 4, as said below
- input_proj: float32 [1536, 1792], P('seq'), may hold values from -0.21875 to 0.21875
- output_proj: float32 [1536, 1536], P('seq'), may hold values from -0.4375 to 0.4375
- gate_up: float32 [1536, 9216], P('seq'), may hold values from -0.15625 to 0.15625
- down_weight: float32 [4608, 1536], P('seq'), may hold values from -0.1875 to 0.1875
- norm_gains: float32 [2, 1536], P(None, 'seq'), may hold values from 0.5 to 1.5
- input_moments: float32 [2, 1536, 1792], P(None, 'seq'), may hold values from -1 to 1, as said below
- output_moments: float32 [2, 1536, 1536], P(None, 'seq'), may hold values from -1 to 1, as said below
- gate_moments: float32 [2, 1536, 9216], P(None, 'seq'), may hold values from -1 to 1, as said below
- down_moments: float32 [2, 4608, 1536], P(None, 'seq'), may hold values from -1 to 1, as said below
- gain_moments: float32 [2, 2, 1536], P(None, None, 'seq'), may hold values from -1 to 1, as said below
- update_count: int32 [1], replicated, may hold values from 1 to 4
- optimizer_rates: float32 [2], replicated, may hold values from 0.01 to 0.1
Outputs:
- block_out: bfloat16 [8, 2048, 1536], P('dp', 'seq')
- block_in_grad: bfloat16 [8, 2048, 1536], P('dp', 'seq')
- input_grad: float32 [1536, 1792], P('seq')
- output_grad: float32 [1536, 1536], P('seq')
- gate_grad: float32 [1536, 9216], P('seq')
- down_grad: float32 [4608, 1536], P('seq')
- gain_grad: float32 [2, 1536], P(None, 'seq')
- input_new: float32 [1536, 1792], P('seq')
- output_new: float32 [1536, 1536], P('seq')
- gate_new: float32 [1536, 9216], P('seq')
- down_new: float32 [4608, 1536], P('seq')
- gains_step: float32 [2, 1536], P(None, 'seq')
- input_moments_new: float32 [2, 1536, 1792], P(None, 'seq')
- output_moments_new: float32 [2, 1536, 1536], P(None, 'seq')
- gate_moments_new: float32 [2, 1536, 9216], P(None, 'seq')
- down_moments_new: float32 [2, 4608, 1536], P(None, 'seq')
- gain_moments_new: float32 [2, 2, 1536], P(None, None, 'seq')
Inputs may be any that keep to these rules, and one draw needn't show every extreme that they name: `segment_ids`: within a sequence the ids are 1, 2, 3, 4 in order of the documents, never falling, followed by 0 over the last 1 to 63 tokens; document 2 starts within the first 256 tokens and ends within the last 256. `input_moments`: the first slice holds first moments, the second positive second moments. `output_moments`: Likewise. `gate_moments`: Likewise. `down_moments`: Likewise. `gain_moments`: Likewise.
All inputs are finite; a program needn't handle non-finite values.
Results may differ from a plain program's by a relative error of at most 0.022.
Values may be sent and summed in bfloat16 or wider, within the bound.
A program may use at most 448 MiB of HBM per device.

v0:
```python
import jax
import jax.numpy as jnp
from jax import lax
from jax.sharding import PartitionSpec as P

HEADS = 12
HEAD = 128
FF = 4608
WINDOW = 1024


norm_eps = 1e-06
adam_eps = 1e-08
beta_first = 0.9
beta_second = 0.95
head_group = 4


def passed_along(block, axis, distance):
    devices = range(lax.axis_size(axis))
    route = [(i - distance, i) for i in devices if i - distance in devices]
    return lax.ppermute(block, axis, route)


def rotate(values, positions, sign_value):
    half_width = values.shape[-1] // 2
    frequency = 10000.0 ** (-2.0 * jnp.arange(half_width).astype(jnp.float32) / values.shape[-1])
    angles = positions.astype(jnp.float32)[:, None] * frequency[None, :]
    cosine = jnp.cos(angles)
    sine_part = sign_value * jnp.sin(angles)
    if values.ndim == 3:
        cosine = cosine[:, None, :]
        sine_part = sine_part[:, None, :]
    lower_half = values[..., :half_width]
    upper_half = values[..., half_width:]
    return jnp.concatenate(
        [
            lower_half * cosine - upper_half * sine_part,
            upper_half * cosine + lower_half * sine_part,
        ],
        axis=-1,
    )


def root_norm(values, gain):
    return values * lax.rsqrt(jnp.mean(values * values, axis=-1, keepdims=True) + norm_eps) * gain


def gated_unit(gate_part, up_part):
    return jax.nn.gelu(gate_part, approximate=True) * up_part


def adamw_step(weight, moments, grad, step_value, optimizer_rates):
    fix_first = 1.0 - beta_first**step_value
    fix_second = 1.0 - beta_second**step_value
    first_moment = beta_first * moments[0] + (1.0 - beta_first) * grad
    second = beta_second * moments[1] + (1.0 - beta_second) * grad * grad
    update = (
        first_moment / fix_first / (jnp.sqrt(second / fix_second) + adam_eps)
        + optimizer_rates[1] * weight
    )
    return (optimizer_rates[0] * update, jnp.stack([first_moment, second]))


def adamw_update(weight, moments, grad, step_value, optimizer_rates):
    change, new_moments = adamw_step(weight, moments, grad, step_value, optimizer_rates)
    return (weight - change, new_moments)


def on_device(
    block_in,
    cotangent,
    segment_ids,
    input_proj,
    output_proj,
    gate_up,
    down_weight,
    norm_gains,
    input_moments,
    output_moments,
    gate_moments,
    down_moments,
    gain_moments,
    update_count,
    optimizer_rates,
):
    seq_place = lax.axis_index("seq")
    proj_in_full, proj_out_full, gate_full, down_full, gains_full = (
        lax.all_gather(input_proj.astype(jnp.bfloat16), "seq", axis=0, tiled=True),
        lax.all_gather(output_proj.astype(jnp.bfloat16), "seq", axis=0, tiled=True),
        lax.all_gather(gate_up.astype(jnp.bfloat16), "seq", axis=0, tiled=True),
        lax.all_gather(down_weight.astype(jnp.bfloat16), "seq", axis=0, tiled=True),
        lax.all_gather(norm_gains.astype(jnp.bfloat16), "seq", axis=1, tiled=True),
    )
    gains_wide = gains_full.astype(jnp.float32)
    tokens = block_in[0].astype(jnp.float32)
    piece_len = tokens.shape[0]
    width_q = HEADS * HEAD
    positions = seq_place * piece_len + jnp.arange(piece_len, dtype=jnp.int32)
    normed = root_norm(tokens, gains_wide[0]).astype(jnp.bfloat16)
    mixed_proj = jnp.dot(normed, proj_in_full, preferred_element_type=jnp.float32)
    queries = rotate(
        mixed_proj[:, :width_q].reshape(piece_len, HEADS, HEAD), positions, 1.0
    ).astype(jnp.bfloat16)
    own_keys = rotate(mixed_proj[:, width_q : width_q + HEAD], positions, 1.0)
    own_pair = jnp.concatenate([own_keys, mixed_proj[:, width_q + HEAD :]], axis=1).astype(
        jnp.bfloat16
    )
    reach_count = (WINDOW + piece_len - 2) // piece_len
    earlier = []
    for back_step in range(reach_count, 0, -1):
        earlier.append(passed_along(own_pair, "seq", back_step))
    key_pairs = jnp.concatenate(earlier + [own_pair], axis=0)
    key_rows = key_pairs[:, :HEAD]
    values = key_pairs[:, HEAD:]
    segments = segment_ids[0]
    key_span = reach_count * piece_len
    padded_ids = jnp.concatenate([jnp.full((key_span,), -1, jnp.int32), segments])
    query_ids = lax.dynamic_slice_in_dim(segments, seq_place * piece_len, piece_len)
    key_ids = lax.dynamic_slice_in_dim(padded_ids, seq_place * piece_len, key_span + piece_len)
    distance = jnp.arange(piece_len)[:, None] + key_span - jnp.arange(key_span + piece_len)[None, :]
    allowed = (distance >= 0) & (distance < WINDOW) & (query_ids[:, None] == key_ids[None, :])
    live_rows = query_ids != 0
    score_scale = HEAD ** (-0.5)

    def masked_scores(query_part):
        scores = (
            jnp.einsum("thd,kd->htk", query_part, key_rows, preferred_element_type=jnp.float32)
            * score_scale
        )
        return jnp.where(allowed[None], scores, -1e30)

    group_outputs = []
    group_totals = []
    for first_head in range(0, HEADS, head_group):
        scores = masked_scores(queries[:, first_head : first_head + head_group])
        log_totals = jax.nn.logsumexp(scores, axis=-1)
        weights = jnp.exp(scores - log_totals[..., None]).astype(jnp.bfloat16)
        group_outputs.append(
            jnp.einsum("htk,kd->thd", weights, values, preferred_element_type=jnp.float32)
        )
        group_totals.append(log_totals)
    attended = jnp.concatenate(group_outputs, axis=1)
    attended = jnp.where(live_rows[:, None, None], attended, 0.0)
    flat_heads = attended.reshape(piece_len, width_q).astype(jnp.bfloat16)
    middle = tokens + jnp.dot(flat_heads, proj_out_full, preferred_element_type=jnp.float32)
    normed_two = root_norm(middle, gains_wide[1]).astype(jnp.bfloat16)
    gated_proj = jnp.dot(normed_two, gate_full, preferred_element_type=jnp.float32)
    hidden = gated_unit(gated_proj[:, :FF], gated_proj[:, FF:]).astype(jnp.bfloat16)
    output = middle + jnp.dot(hidden, down_full, preferred_element_type=jnp.float32)
    block_out = output.astype(jnp.bfloat16)[None]
    upstream = cotangent[0].astype(jnp.float32)
    upstream_low = upstream.astype(jnp.bfloat16)
    grad_down_local = jnp.einsum(
        "tf,td->fd", hidden, upstream_low, preferred_element_type=jnp.float32
    )
    grad_hidden = jnp.einsum(
        "td,fd->tf", upstream_low, down_full, preferred_element_type=jnp.float32
    )
    ignored, unit_pull = jax.vjp(gated_unit, gated_proj[:, :FF], gated_proj[:, FF:])
    grad_gate, grad_up = unit_pull(grad_hidden)
    grad_gated = jnp.concatenate([grad_gate, grad_up], axis=1).astype(jnp.bfloat16)
    grad_gate_local = jnp.einsum(
        "td,tf->df", normed_two, grad_gated, preferred_element_type=jnp.float32
    )
    grad_normed_two = jnp.einsum(
        "tf,df->td", grad_gated, gate_full, preferred_element_type=jnp.float32
    )
    ignored, norm_pull_two = jax.vjp(root_norm, middle, gains_wide[1])
    grad_middle_norm, grad_gain_two = norm_pull_two(grad_normed_two)
    grad_middle = upstream + grad_middle_norm
    grad_branch = grad_middle.astype(jnp.bfloat16)
    grad_out_local = jnp.einsum(
        "tq,td->qd", flat_heads, grad_branch, preferred_element_type=jnp.float32
    )
    grad_flat = jnp.einsum(
        "td,qd->tq", grad_branch, proj_out_full, preferred_element_type=jnp.float32
    )
    grad_attended = (
        jnp.where(live_rows[:, None], grad_flat, 0.0)
        .astype(jnp.bfloat16)
        .reshape(piece_len, HEADS, HEAD)
    )
    grad_queries = []
    grad_key_sum = jnp.zeros((key_span + piece_len, HEAD), jnp.float32)
    grad_value_sum = jnp.zeros((key_span + piece_len, HEAD), jnp.float32)
    for group_index, first_head in enumerate(range(0, HEADS, head_group)):
        query_part = queries[:, first_head : first_head + head_group]
        scores = masked_scores(query_part)
        probabilities = jnp.exp(scores - group_totals[group_index][..., None])
        weights = probabilities.astype(jnp.bfloat16)
        grad_part = grad_attended[:, first_head : first_head + head_group]
        grad_probs = jnp.einsum(
            "thd,kd->htk", grad_part, values, preferred_element_type=jnp.float32
        )
        grad_scores = probabilities * (
            grad_probs - jnp.sum(probabilities * grad_probs, axis=-1, keepdims=True)
        )
        grad_raw = (grad_scores * score_scale).astype(jnp.bfloat16)
        grad_queries.append(
            jnp.einsum("htk,kd->thd", grad_raw, key_rows, preferred_element_type=jnp.float32)
        )
        grad_key_sum = grad_key_sum + jnp.einsum(
            "htk,thd->kd", grad_raw, query_part, preferred_element_type=jnp.float32
        )
        grad_value_sum = grad_value_sum + jnp.einsum(
            "htk,thd->kd", weights, grad_part, preferred_element_type=jnp.float32
        )
    grad_pairs = jnp.concatenate([grad_key_sum, grad_value_sum], axis=1)
    own_grad = grad_pairs[key_span:]
    for back_step in range(1, reach_count + 1):
        sent_rows = grad_pairs[
            key_span - back_step * piece_len : key_span - (back_step - 1) * piece_len
        ]
        own_grad = own_grad + passed_along(sent_rows, "seq", -back_step)
    grad_query_all = jnp.concatenate(grad_queries, axis=1)
    grad_query_raw = rotate(grad_query_all, positions, -1.0).reshape(piece_len, width_q)
    grad_key_raw = rotate(own_grad[:, :HEAD], positions, -1.0)
    grad_mixed = jnp.concatenate([grad_query_raw, grad_key_raw, own_grad[:, HEAD:]], axis=1).astype(
        jnp.bfloat16
    )
    grad_in_local = jnp.einsum("td,tq->dq", normed, grad_mixed, preferred_element_type=jnp.float32)
    grad_normed = jnp.einsum(
        "tq,dq->td", grad_mixed, proj_in_full, preferred_element_type=jnp.float32
    )
    ignored, norm_pull_one = jax.vjp(root_norm, tokens, gains_wide[0])
    grad_tokens_norm, grad_gain_one = norm_pull_one(grad_normed)
    block_in_grad = (grad_middle + grad_tokens_norm).astype(jnp.bfloat16)[None]
    grad_gains_local = jnp.stack([grad_gain_one, grad_gain_two])
    token_total = piece_len * lax.axis_size("seq") * lax.axis_size("dp") * block_in.shape[0]
    step_value = update_count[0].astype(jnp.float32)
    masters = (input_proj, output_proj, gate_up, down_weight)
    prior = (input_moments, output_moments, gate_moments, down_moments)
    summed = (
        lax.psum_scatter(
            grad_in_local.astype(jnp.bfloat16), "seq", scatter_dimension=0, tiled=True
        ).astype(jnp.float32),
        lax.psum_scatter(
            grad_out_local.astype(jnp.bfloat16), "seq", scatter_dimension=0, tiled=True
        ).astype(jnp.float32),
        lax.psum_scatter(
            grad_gate_local.astype(jnp.bfloat16), "seq", scatter_dimension=0, tiled=True
        ).astype(jnp.float32),
        lax.psum_scatter(
            grad_down_local.astype(jnp.bfloat16), "seq", scatter_dimension=0, tiled=True
        ).astype(jnp.float32),
        lax.psum_scatter(
            grad_gains_local.astype(jnp.bfloat16), "seq", scatter_dimension=1, tiled=True
        ).astype(jnp.float32),
    )
    summed = (
        lax.psum(summed[0].astype(jnp.bfloat16), "dp").astype(jnp.float32),
        lax.psum(summed[1].astype(jnp.bfloat16), "dp").astype(jnp.float32),
        lax.psum(summed[2].astype(jnp.bfloat16), "dp").astype(jnp.float32),
        lax.psum(summed[3].astype(jnp.bfloat16), "dp").astype(jnp.float32),
        lax.psum(summed[4].astype(jnp.bfloat16), "dp").astype(jnp.float32),
    )
    grad_list = [part_sum / token_total for part_sum in summed]
    updates = [
        adamw_update(masters[which], prior[which], grad_list[which], step_value, optimizer_rates)
        for which in range(4)
    ]
    new_list = [pair[0] for pair in updates]
    moment_list = [pair[1] for pair in updates]
    gain_grad = grad_list[4]
    gains_step, gain_moments_new = adamw_step(
        norm_gains, gain_moments, gain_grad, step_value, optimizer_rates
    )
    return (
        block_out,
        block_in_grad,
        grad_list[0],
        grad_list[1],
        grad_list[2],
        grad_list[3],
        gain_grad,
        new_list[0],
        new_list[1],
        new_list[2],
        new_list[3],
        gains_step,
        moment_list[0],
        moment_list[1],
        moment_list[2],
        moment_list[3],
        gain_moments_new,
    )


def solution(mesh):
    in_specs = (
        P("dp", "seq", None),
        P("dp", "seq", None),
        P("dp", None),
        P("seq", None),
        P("seq", None),
        P("seq", None),
        P("seq", None),
        P(None, "seq"),
        P(None, "seq", None),
        P(None, "seq", None),
        P(None, "seq", None),
        P(None, "seq", None),
        P(None, None, "seq"),
        P(),
        P(),
    )
    out_specs = (
        P("dp", "seq", None),
        P("dp", "seq", None),
        P("seq", None),
        P("seq", None),
        P("seq", None),
        P("seq", None),
        P(None, "seq"),
        P("seq", None),
        P("seq", None),
        P("seq", None),
        P("seq", None),
        P(None, "seq"),
        P(None, "seq", None),
        P(None, "seq", None),
        P(None, "seq", None),
        P(None, "seq", None),
        P(None, None, "seq"),
    )
    return jax.shard_map(
        on_device, mesh=mesh, in_specs=in_specs, out_specs=out_specs, check_vma=False
    )
```

profile of v0, /device:TPU:0, one launch (start us, length us, event | category | flops | bytes accessed | tf_op | source)
XLA Modules:
  0.0 2343.2 jit_solution(13577630462365970249)
XLA Ops:
  7.2 3.1 convert_element_type.144
  11.7 9.0 convert_element_type.153
  20.8 6.0 convert_element_type.155
  26.8 15.6 all_gather.15
  44.4 71.3 %all-gather.5.cloned.1.call-done = bf16[1536,1792]{1,0:T(8,128)(2,1)} async-done(((bf16[384,1792]{1,0:T(8,128)(2,1)}), bf16[1536,1792]{1,0:T(8,128)(2,1)}) %all-gather.5.cloned.1.call-update) | async-done | bytes 5505040 | tf_op jit(solution)/shard_map/all_gather | solution.py:89
  115.8 5.6 fusion.118
  128.2 3.7 collective-permute-start
  132.0 3.6 copy.165
  135.8 4.0 fusion.165
  139.9 3.3 copy.242
  143.1 3.3 copy.241
  146.4 3.7 subtract_convert_fusion.1
  152.6 6.0 fusion.167
  158.7 2.8 fusion.169
  161.5 6.7 fusion.168
  168.2 7.7 exponential_reduce_fusion
  177.6 6.3 exponential_reduce_fusion.1
  183.9 7.0 fusion.91
  196.9 3.0 copy.176
  199.9 12.9 all-gather.7.cloned.1.call-done
  212.8 7.1 multiply_reduce_fusion.2
  220.0 479.0 %all-gather.9.cloned.1.call-done = bf16[1536,9216]{1,0:T(8,128)(2,1)} async-done(((bf16[384,9216]{1,0:T(8,128)(2,1)}), bf16[1536,9216]{1,0:T(8,128)(2,1)}) %all-gather.9.cloned.1.call-update) | async-done | bytes 28311568 | tf_op jit(solution)/shard_map/all_gather | solution.py:91
  699.0 25.4 %fusion.163 = f32[512,9216]{1,0:T(8,128)} fusion(bf16[1536,9216]{1,0:T(8,128)(2,1)} %all-gather.9.cloned.1.call-done, f32[512,1536]{1,0:T(8,128)} %get-tuple-element.78, f32[1536]{0:T(1024)S(1)} %get-tuple-element.21, f32[512]{0:T(512)S(1)} %fusion.140), kind=kOutput, calls=%fused_computation.258 | convolution fusion | flops 14497873920 | bytes 50339840 | tf_op jit(solution)/shard_map/dot_general | solution.py:148
  724.4 218.8 %all-gather.11.cloned.1.call-done = bf16[4608,1536]{1,0:T(8,128)(2,1)} async-done(((bf16[1152,1536]{1,0:T(8,128)(2,1)}), bf16[4608,1536]{1,0:T(8,128)(2,1)}) %all-gather.11.cloned.1.call-update) | async-done | bytes 14155792 | tf_op jit(solution)/shard_map/all_gather | solution.py:92
  943.1 23.4 fusion.24
  966.5 23.1 multiply_reduce_fusion
  989.6 4.2 fusion.44
  993.8 4.6 convolution_convert_fusion.2
  999.4 6.3 fusion.53
  1005.8 2.6 copy.177
  1008.3 7.9 fusion.111
  1016.2 19.3 fusion.61
  1035.5 7.7 fusion.108
  1043.3 19.4 fusion.60
  1062.7 7.6 fusion.114
  1070.3 20.3 fusion.66
  1090.6 7.0 convolution_bitcast_fusion.1
  1097.6 7.0 convolution_bitcast_fusion
  1110.6 18.8 fusion.96
  1129.3 19.4 fusion.95
  1148.7 19.4 fusion.94
  1173.2 3.0 copy.191
  1178.2 7.1 convolution_convert_fusion.3
  1186.7 12.5 convolution_convert_fusion.1
  1199.8 22.5 convolution_convert_fusion
  1223.8 7.7 fusion.43
  1232.6 54.9 %reduce-scatter.8.cloned.1.call-done = bf16[384,1792]{1,0:T(8,128)(2,1)} async-done(((bf16[1536,1792]{1,0:T(8,128)(2,1)}), bf16[384,1792]{1,0:T(8,128)(2,1)}) %reduce-scatter.8.cloned.1.call-update) | async-done | bytes 1376272 | tf_op jit(solution)/shard_map/reduce_scatter | solution.py:235
  1287.5 240.7 %reduce-scatter.14.cloned.1.call-done = bf16[1152,1536]{1,0:T(8,128)(2,1)} async-done(((bf16[4608,1536]{1,0:T(8,128)(2,1)}), bf16[1152,1536]{1,0:T(8,128)(2,1)}) %reduce-scatter.14.cloned.1.call-update) | async-done | bytes 3538960 | tf_op jit(solution)/shard_map/reduce_scatter | solution.py:244
  1528.2 468.8 %reduce-scatter.12.cloned.1.call-done = bf16[384,9216]{1,0:T(8,128)(2,1)} async-done(((bf16[1536,9216]{1,0:T(8,128)(2,1)}), bf16[384,9216]{1,0:T(8,128)(2,1)}) %reduce-scatter.12.cloned.1.call-update) | async-done | bytes 7077904 | tf_op jit(solution)/shard_map/reduce_scatter | solution.py:241
  1998.3 13.5 fusion.59
  2013.9 8.7 reduce-scatter.16.cloned.1.call-done
  2023.6 12.7 psum.39
  2038.8 166.2 %all-reduce.4.cloned.1.call-done = (bf16[384,1792]{1,0:T(8,128)(2,1)}, bf16[384,1536]{1,0:T(8,128)(2,1)}, bf16[384,9216]{1,0:T(8,128)(2,1)}, bf16[1152,1536]{1,0:T(8,128)(2,1)}) async-done(((bf16[384,1792]{1,0:T(8,128)(2,1)}, bf16[384,1536]{1,0:T(8,128)(2,1)}, bf16[384,9216]{1,0:T(8,128)(2,1)}, bf16[1152,1536]{1,0:T(8,128)(2,1)}), (bf16[384,1792]{1,0:T(8,128)(2,1)}, bf16[384,1536]{1,0:T(8,128)(2,1)}, ...) | async-done | bytes 13172752 | tf_op jit(solution)/shard_map/psum | solution.py:252
  2205.1 4.0 fusion.107
  2209.1 8.9 fusion.97
  2220.2 7.6 fusion.84
  2227.8 6.2 fusion.83
  2234.1 16.9 fusion.41
  2251.0 15.1 fusion.55
  2266.1 30.1 %fusion.25 = (f32[1,384,9216]{2,1,0:T(8,128)}, f32[384,9216]{1,0:T(8,128)}) fusion(bf16[384,9216]{1,0:T(8,128)(2,1)S(1)} %bitcast.291, f32[2,384,9216]{2,1,0:T(8,128)} %param.25, f32[384,9216]{1,0:T(8,128)} %param.20, f32[]{:T(128)} %bitcast.42, f32[]{:T(128)} %bitcast.41, f32[384,9216]{1,0:T(8,128)} %get-tuple-element.32, f32[]{:T(128)} %bitcast.39, f32[]{:T(128)} %bitcast.37), kind=kLoop, calls=%fused_computation.59 | loop fusion | flops 56623104 | bytes 92012560 | tf_op jit(solution)/shard_map/stack | solution.py:62
  2296.3 4.5 pad_maximum_fusion.6
  2300.8 2.8 pad_maximum_fusion.5
  2303.6 11.8 pad_maximum_fusion.1
  2315.3 20.8 pad_maximum_fusion
  (236 shorter events, 47.0 us)
Async XLA Ops:
  7.2 108.6 %all-gather.5.cloned.1.call-start = ((), (), s32[]{:S(2)}) async-start(), calls=%async_computation.5 | async-start | bytes 6881280 | tf_op jit(solution)/shard_map/all_gather | solution.py:89
  10.4 202.4 %all-gather.7.cloned.1.call-start = ((), (), s32[]{:S(2)}) async-start(), calls=%async_computation.6 | async-start | bytes 5898240 | tf_op jit(solution)/shard_map/all_gather | solution.py:90
  11.6 687.4 %all-gather.9.cloned.1.call-start = ((), (), s32[]{:S(2)}) async-start(), calls=%async_computation.7 | async-start | bytes 35389440 | tf_op jit(solution)/shard_map/all_gather | solution.py:91
  20.7 21.8 copy-start.45
  20.7 22.0 copy-start.19
  20.7 922.4 %all-gather.11.cloned.1.call-start = ((), (), s32[]{:S(2)}) async-start(), calls=%async_computation.8 | async-start | bytes 17694720 | tf_op jit(solution)/shard_map/all_gather | solution.py:92
  26.8 1205.8 %reduce-scatter.10.cloned.1.call-start = ((), (), s32[]{:S(2)}) async-start(), calls=%async_computation.10 | async-start | bytes 5898240 | tf_op jit(solution)/shard_map/reduce_scatter | solution.py:238
  42.5 81.4 %copy-start.55 = (f32[64]{0:T(128)}, f32[64]{0:T(128)S(1)}, u32[]{:S(2)}) copy-start(f32[64]{0:T(128)S(1)} %multiply_power_fusion) | copy-start | bytes 772
  42.5 81.4 %copy-start.40 = (f32[512]{0:T(512)}, f32[512]{0:T(512)S(1)}, u32[]{:S(2)}) copy-start(f32[512]{0:T(512)S(1)} %add_convert_fusion.2) | copy-start | bytes 6148
  42.7 78.7 %copy-start.38 = (f32[1536]{0:T(1024)}, f32[1536]{0:T(1024)S(1)}, u32[]{:S(2)}) copy-start(f32[1536]{0:T(1024)S(1)} %get-tuple-element.22) | copy-start | bytes 18436
  43.1 78.3 %copy-start.42 = (f32[512]{0:T(512)}, f32[512]{0:T(512)S(1)}, u32[]{:S(2)}) copy-start(f32[512]{0:T(512)S(1)} %fusion.47) | copy-start | bytes 6148
  43.1 950.7 %copy-start.57 = (pred[512]{0:T(512)(128)(4,1)}, pred[512]{0:T(512)(128)(4,1)S(1)}, u32[]{:S(2)}) copy-start(pred[512]{0:T(512)(128)(4,1)S(1)} %broadcast_compare_fusion) | copy-start | bytes 1540
  43.1 78.3 %copy-start.49 = (f32[512]{0:T(512)}, f32[512]{0:T(512)S(1)}, u32[]{:S(2)}) copy-start(f32[512]{0:T(512)S(1)} %fusion.139) | copy-start | bytes 6148
  126.2 24.2 %collective-permute-start.1 = (bf16[512,256]{1,0:T(8,128)(2,1)}, bf16[512,256]{1,0:T(8,128)(2,1)}, u32[]{:S(2)}, u32[]{:S(2)}) collective-permute-start(bf16[512,256]{1,0:T(8,128)(2,1)} %pad_maximum_fusion.15), channel_id=1, source_target_pairs={{0,1},{1,2},{2,3},{4,5},{5,6},{6,7},{8,9},{9,10},{10,11},{12,13},{... | collective-permute-start | bytes 786440 | tf_op jit(solution)/shard_map/ppermute | solution.py:22
  128.2 22.9 collective-permute-start
  135.7 10.7 copy-start.27
  150.1 11.3 copy-start.1
  150.1 11.3 copy-start.3
  150.5 8.2 copy-start.32
  152.6 40.6 %copy-start.5 = (bf16[1536,256]{1,0:T(8,128)(2,1)}, bf16[1536,256]{1,0:T(8,128)(2,1)S(1)}, u32[]{:S(2)}) copy-start(bf16[1536,256]{1,0:T(8,128)(2,1)S(1)} %maximum_maximum_fusion) | copy-start | bytes 2359300
  161.4 29.5 %copy-start = (f32[4,512,1536]{1,2,0:T(8,128)}, f32[4,512,1536]{1,2,0:T(8,128)S(1)}, u32[]{:S(2)}) copy-start(f32[4,512,1536]{1,2,0:T(8,128)S(1)} %get-tuple-element.76) | copy-start | bytes 37748740
  175.9 8.0 copy-start.34
  177.6 13.3 copy-start.36
  183.9 9.4 slice-start.3
  183.9 9.4 slice-start.4
  220.0 769.6 %copy-start.51 = (f32[512]{0:T(512)}, f32[512]{0:T(512)S(1)}, u32[]{:S(2)}) copy-start(f32[512]{0:T(512)S(1)} %fusion.140) | copy-start | bytes 6148
  724.4 242.1 %copy-start.24 = (f32[512,1536]{1,0:T(8,128)S(1)}, f32[512,1536]{1,0:T(8,128)}, u32[]{:S(2)}) copy-start(f32[512,1536]{1,0:T(8,128)} %get-tuple-element.78) | copy-start | bytes 9437188
  998.4 289.0 %reduce-scatter.8.cloned.1.call-start = ((), (), s32[]{:S(2)}) async-start(), calls=%async_computation.9 | async-start | bytes 6881280 | tf_op jit(solution)/shard_map/reduce_scatter | solution.py:235
  1008.3 7.9 copy-start.2
  1008.3 7.9 copy-start.4
  1035.5 7.7 copy-start.35
  1062.7 7.6 copy-start.37
  1090.6 7.0 copy-start.7
  1090.6 14.0 slice-start
  1090.6 14.0 slice-start.1
  1097.6 7.0 slice-start.2
  1108.0 68.2 %collective-permute-start.2 = (f32[512,256]{0,1:T(8,128)}, f32[512,256]{0,1:T(8,128)}, u32[]{:S(2)}, u32[]{:S(2)}) collective-permute-start(f32[512,256]{0,1:T(8,128)} %get-tuple-element.56), channel_id=1, source_target_pairs={{1,0},{2,1},{3,2},{5,4},{6,5},{7,6},{9,8},{10,9},{11,10},{13,12},{... | collective-permute-start | bytes 1572872 | tf_op jit(solution)/shard_map/ppermute | solution.py:22
  1109.3 66.9 %collective-permute-start.3 = (f32[512,256]{0,1:T(8,128)}, f32[512,256]{0,1:T(8,128)}, u32[]{:S(2)}, u32[]{:S(2)}) collective-permute-start(f32[512,256]{0,1:T(8,128)} %get-tuple-element.57), channel_id=1, source_target_pairs={{2,0},{3,1},{6,4},{7,5},{10,8},{11,9},{14,12},{15,13},{18,16},{19,... | collective-permute-start | bytes 1572872 | tf_op jit(solution)/shard_map/ppermute | solution.py:22
  1171.1 7.0 copy-start.20
  1185.3 342.9 %reduce-scatter.14.cloned.1.call-start = ((), (), s32[]{:S(2)}) async-start(), calls=%async_computation.12 | async-start | bytes 17694720 | tf_op jit(solution)/shard_map/reduce_scatter | solution.py:244
  1199.2 797.7 %reduce-scatter.12.cloned.1.call-start = ((), (), s32[]{:S(2)}) async-start(), calls=%async_computation.11 | async-start | bytes 35389440 | tf_op jit(solution)/shard_map/reduce_scatter | solution.py:241
  1222.4 800.2 %reduce-scatter.16.cloned.1.call-start = ((), (), s32[]{:S(2)}) async-start(), calls=%async_computation.13 | async-start | bytes 491520
  1232.5 972.5 %all-reduce.4.cloned.1.call-start = ((), (), s32[]{:S(2)}) async-start(), calls=%async_computation.14 | async-start | bytes 26345472 | tf_op jit(solution)/shard_map/psum | solution.py:252
  1998.3 13.5 copy-start.43
  1998.3 13.5 copy-start.10
  1998.3 13.5 copy-start.23
  2011.9 24.5 %copy-start.44 = (f32[2,2,384]{2,1,0:T(2,128)S(1)}, f32[2,2,384]{2,1,0:T(2,128)}, u32[]{:S(2)}) copy-start(f32[2,2,384]{2,1,0:T(2,128)} %param.27) | copy-start | bytes 18436
  2011.9 24.5 %copy-start.47 = (f32[2,384]{1,0:T(2,128)S(1)}, f32[2,384]{1,0:T(2,128)}, u32[]{:S(2)}) copy-start(f32[2,384]{1,0:T(2,128)} %param.22) | copy-start | bytes 9220
  2013.9 195.2 %copy-start.16 = (f32[384,1536]{1,0:T(8,128)S(1)}, f32[384,1536]{1,0:T(8,128)}, u32[]{:S(2)}) copy-start(f32[384,1536]{1,0:T(8,128)} %param.19) | copy-start | bytes 7077892
  2036.3 181.7 %copy-start.48 = (f32[2,384]{1,0:T(2,128)}, f32[2,384]{1,0:T(2,128)S(1)}, u32[]{:S(2)}) copy-start(f32[2,384]{1,0:T(2,128)S(1)} %get-tuple-element.28) | copy-start | bytes 9220
  2205.1 13.0 slice-start.12
  2209.1 8.9 copy-start.17
  2209.1 8.9 slice-start.13
  2209.1 8.9 copy-start.21
  2209.1 11.0 copy-start.11
  2218.1 9.7 slice-start.6
  2218.1 9.7 slice-start.7
  2220.2 7.6 copy-start.12
  2220.2 7.6 slice-start.8
  2220.2 7.6 slice-start.9
  2220.2 7.6 copy-start.8
  2227.8 23.2 slice-start.10
  2234.1 17.0 slice-start.11
  2266.1 30.1 %copy-start.18 = (f32[1,384,1536]{2,1,0:T(8,128)S(1)}, f32[1,384,1536]{2,1,0:T(8,128)}, u32[]{:S(2)}) copy-start(f32[1,384,1536]{2,1,0:T(8,128)} %get-tuple-element.33) | copy-start | bytes 7077892
  (22 other events, 82.3 us)
Sparse Core Ops, SparseCore 0:
  10.5 105.1 all-gather.4
  117.9 94.8 all-gather.6
  215.0 483.9 all-gather.8
  701.0 242.0 all-gather.10
  998.5 83.4 reduce-scatter.9
  1185.4 102.0 reduce-scatter.7
  1290.4 237.7 reduce-scatter.13
  1531.1 465.7 reduce-scatter.11
  1999.9 22.6 reduce-scatter.15
  2026.5 178.4 all-reduce.3
where the time goes:
time: 2350 us; the launch traced here: 2340 us
  waiting for transfers between devices  1720 us (73%)
  matrix products  342 us (15%)
  other arithmetic  193 us (8%)
  local copies, waits for them, and re-layouts  32.9 us (1%)
  blocking collectives  28.4 us (1%)
    all_gather x1, waiting for transfers between devices, on_device(): lax.all_gather(gate_up.astype(jnp.bfloat16), 'seq', axis=0, tiled=True)  479 us
    reduce_scatter x1, waiting for transfers between devices, on_device(): lax.psum_scatter(grad_gate_local.astype(jnp.bfloat16), 'seq', scatter_dim...  469 us
    reduce_scatter x1, waiting for transfers between devices, on_device(): lax.psum_scatter(grad_down_local.astype(jnp.bfloat16), 'seq', scatter_dim...  241 us
    all_gather x1, waiting for transfers between devices, on_device(): lax.all_gather(down_weight.astype(jnp.bfloat16), 'seq', axis=0, tiled=True)  219 us
    psum x1, waiting for transfers between devices, on_device(): lax.psum(summed[0].astype(jnp.bfloat16), 'dp').astype(jnp.float32)  166 us
    another operation x15, other arithmetic, adamw_step(): return (optimizer_rates[0] * update, jnp.stack([first_moment, second]))  133 us
    all_gather x1, waiting for transfers between devices, on_device(): lax.all_gather(input_proj.astype(jnp.bfloat16), 'seq', axis=0, tiled=True)  71.3 us
    dot_general x3, matrix products, on_device(): jnp.einsum('htk,thd->kd', grad_raw, query_part, preferred_element_type=jn...  59 us
  transfers between devices with their start and end apart: 14, of which 10 were waited for; matrix products, arithmetic and copies ran while one was open for 16% of the time, Pallas kernels for 0%

commit v1 on v0

v1 whole, which is shorter than its diff:
```python
import jax
import jax.numpy as jnp
from jax import lax
from jax.experimental import pallas as pl
from jax.experimental.pallas import tpu as pltpu
from jax.sharding import Mesh
from jax.sharding import PartitionSpec as P

HEADS = 12
HEAD = 128
FF = 4608
WINDOW = 1024


norm_eps = 1e-06
adam_eps = 1e-08
beta_first = 0.9
beta_second = 0.95
head_group = 4
BF = jnp.bfloat16
F32 = jnp.float32
MESH_ID = pl.DeviceIdType.MESH
VMEM_BYTES = 56 * 1024 * 1024
ANY = pl.BlockSpec(memory_space=pl.ANY)


def passed_along(block, axis, distance):
    devices = range(lax.axis_size(axis))
    route = [(i - distance, i) for i in devices if i - distance in devices]
    return lax.ppermute(block, axis, route)


def swapped(block, axis):
    return lax.ppermute(block, axis, [(0, 1), (1, 0)])


def rotate(values, positions, sign_value):
    half_width = values.shape[-1] // 2
    frequency = 10000.0 ** (-2.0 * jnp.arange(half_width).astype(jnp.float32) / values.shape[-1])
    angles = positions.astype(jnp.float32)[:, None] * frequency[None, :]
    cosine = jnp.cos(angles)
    sine_part = sign_value * jnp.sin(angles)
    if values.ndim == 3:
        cosine = cosine[:, None, :]
        sine_part = sine_part[:, None, :]
    lower_half = values[..., :half_width]
    upper_half = values[..., half_width:]
    return jnp.concatenate(
        [
            lower_half * cosine - upper_half * sine_part,
            upper_half * cosine + lower_half * sine_part,
        ],
        axis=-1,
    )


def root_norm(values, gain):
    return values * lax.rsqrt(jnp.mean(values * values, axis=-1, keepdims=True) + norm_eps) * gain


def gated_unit(gate_part, up_part):
    return jax.nn.gelu(gate_part, approximate=True) * up_part


def adamw_step(weight, moments, grad, step_value, optimizer_rates):
    fix_first = 1.0 - beta_first**step_value
    fix_second = 1.0 - beta_second**step_value
    first_moment = beta_first * moments[0] + (1.0 - beta_first) * grad
    second = beta_second * moments[1] + (1.0 - beta_second) * grad * grad
    update = (
        first_moment / fix_first / (jnp.sqrt(second / fix_second) + adam_eps)
        + optimizer_rates[1] * weight
    )
    return (optimizer_rates[0] * update, jnp.stack([first_moment, second]))


def gather_kernel(shared, chunks, S, refs):
    n = len(shared)
    nc = len(chunks)
    F = S - 1
    own = refs[:n]
    full = refs[n : 2 * n]
    loc, zs, zr, xs, xr, ys, yr, cs, cr = refs[2 * n :]
    y, x, c, z = (lax.axis_index(a) for a in ("y", "x", "c", "z"))
    k = y * 2 + x
    kx = y * 2 + 1 - x
    ky = (1 - y) * 2 + x
    kxy = 3 - k
    to_x = {"x": 1 - x}
    to_y = {"y": 1 - y}
    to_c = {"c": 1 - c}
    low = z
    high = S - 1 - z
    near_count = jnp.minimum(low, high)
    above = jnp.minimum(z + 1, S - 1)
    below = jnp.maximum(z - 1, 0)
    blocks = []
    for j in range(F):
        near = j < 2 * near_count
        dist = jnp.where(near, j // 2 + 1, j - near_count + 1)
        sign = jnp.where(near, (j % 2) * 2 - 1, jnp.where(high > low, 1, -1))
        blocks.append((z + sign * dist, sign))
    barrier = pltpu.get_barrier_semaphore()
    for target in (to_x, to_y, to_c):
        pl.semaphore_signal(barrier, inc=1, device_id=target, device_id_type=MESH_ID)

    @pl.when(z + 1 < S)
    def _():
        pl.semaphore_signal(barrier, inc=1, device_id={"z": above}, device_id_type=MESH_ID)

    @pl.when(z > 0)
    def _():
        pl.semaphore_signal(barrier, inc=1, device_id={"z": below}, device_id_type=MESH_ID)

    pl.semaphore_wait(barrier, 3 + jnp.minimum(low, 1) + jnp.minimum(high, 1))

    def own_half(i):
        return own[i].at[c] if shared[i] else own[i]

    def full_half(i):
        return full[i].at[c] if shared[i] else full[i]

    def part(ref, q, zz, kk, h=None):
        _, r0, rn = chunks[q]
        if h is None:
            return ref.at[zz, kk, :, pl.ds(r0, rn)]
        return ref.at[zz, kk, h, pl.ds(r0, rn)]

    def remote(src, dst, s, r, target):
        return pltpu.make_async_remote_copy(
            src_ref=src,
            dst_ref=dst,
            send_sem=s,
            recv_sem=r,
            device_id=target,
            device_id_type=MESH_ID,
        )

    tail = []
    local = []
    for i in range(n):
        if shared[i]:
            for half in range(2):
                local.append(
                    pltpu.make_async_copy(
                        own[i].at[half], full[i].at[half, z], loc.at[len(local)]
                    )
                )
        else:
            local.append(pltpu.make_async_copy(own[i], full[i].at[z], loc.at[len(local)]))

    def z_first(q):
        i, r0, rn = chunks[q]
        src = own_half(i).at[k, :, pl.ds(r0, rn)]
        dst = part(full_half(i), q, z, k)
        for ok, target, slot in ((z + 1 < S, above, F), (z > 0, below, F + 1)):

            def make(target=target, slot=slot):
                return remote(src, dst, zs.at[q, slot], zr.at[q, z], {"z": target})

            @pl.when(ok)
            def _(make=make):
                make().start()

            def finish(ok=ok, make=make):
                @pl.when(ok)
                def _():
                    make().wait_send()

            tail.append(finish)

    def z_next(q, j):
        zz, sign = blocks[j]
        held = full_half(chunks[q][0])
        piece = part(held, q, zz, k)
        remote(piece, piece, zs.at[q, j], zr.at[q, zz], {"z": above}).wait_recv()
        onward = z - sign
        ok = (onward >= 0) & (onward < S)
        target = jnp.clip(onward, 0, S - 1)

        def make():
            return remote(piece, piece, zs.at[q, j], zr.at[q, zz], {"z": target})

        @pl.when(ok)
        def _():
            make().start()

        def finish():
            @pl.when(ok)
            def _():
                make().wait_send()

        tail.append(finish)
        for h, s, r, target in ((0, xs, xr, to_x), (1, ys, yr, to_y)):
            p = part(held, q, zz, k, h)
            copy = remote(p, p, s.at[q, j, 0], r.at[q, j, 0], target)
            copy.start()
            tail.append(copy.wait_send)
        for h, s, r, target in ((0, ys, yr, to_y), (1, xs, xr, to_x)):
            p = part(held, q, zz, k, h)
            copy = remote(p, p, s.at[q, j, 1], r.at[q, j, 1], target)
            copy.start()
            tail.append(copy.wait_send)

    def xy_next(q, j):
        zz, _ = blocks[j]
        held = full_half(chunks[q][0])
        p = part(held, q, zz, kx, 0)
        remote(p, p, xs.at[q, j, 0], xr.at[q, j, 0], to_x).wait_recv()
        copy = remote(p, p, ys.at[q, j, 2], yr.at[q, j, 2], to_y)
        copy.start()
        tail.append(copy.wait_send)
        p = part(held, q, zz, ky, 1)
        remote(p, p, ys.at[q, j, 0], yr.at[q, j, 0], to_y).wait_recv()
        copy = remote(p, p, xs.at[q, j, 2], xr.at[q, j, 2], to_x)
        copy.start()
        tail.append(copy.wait_send)

    def last(q, j):
        i, r0, rn = chunks[q]
        zz, _ = blocks[j]
        held = full_half(i)
        for kk, h, s, r, slot, target in (
            (kx, 1, xs, xr, 1, to_x),
            (ky, 0, ys, yr, 1, to_y),
            (kxy, 1, xs, xr, 2, to_x),
            (kxy, 0, ys, yr, 2, to_y),
        ):
            p = part(held, q, zz, kk, h)
            remote(p, p, s.at[q, j, slot], r.at[q, j, slot], target).wait_recv()
        if shared[i]:
            p = held.at[zz, :, :, pl.ds(r0, rn)]
            copy = remote(p, p, cs.at[q, j], cr.at[q, j], to_c)
            copy.start()
            tail.append(copy.wait_send)
            other = full[i].at[1 - c].at[zz, :, :, pl.ds(r0, rn)]

            def finish():
                remote(other, other, cs.at[q, j], cr.at[q, j], to_c).wait_recv()

            tail.append(finish)

    z_first(0)
    for copy in local:
        copy.start()
    for t in range(1, nc + F + 3):
        if t < nc:
            z_first(t)
        for j in range(F):
            if 0 <= t - 1 - j < nc:
                z_next(t - 1 - j, j)
        for j in range(F):
            if 0 <= t - 2 - j < nc:
                xy_next(t - 2 - j, j)
        for j in range(F):
            if 0 <= t - 3 - j < nc:
                last(t - 3 - j, j)
    for copy in local:
        copy.wait()
    for wait in tail:
        wait()


def gathered(own, shared, chunks, S, cid):
    n = len(own)
    nc = len(chunks)
    F = S - 1
    outs = []
    for o, s in zip(own, shared):
        outs.append(jax.ShapeDtypeStruct((2, S) + o.shape[1:] if s else (S,) + o.shape, o.dtype))
    dma = pltpu.SemaphoreType.DMA

    def body(*refs):
        gather_kernel(shared, chunks, S, refs)

    return pl.pallas_call(
        body,
        out_shape=tuple(outs),
        in_specs=[pl.BlockSpec(memory_space=pltpu.VMEM)] * n,
        out_specs=tuple([ANY] * n),
        scratch_shapes=[
            dma((2 * n,)),
            dma((nc, F + 2)),
            dma((nc, S)),
            dma((nc, F, 3)),
            dma((nc, F, 3)),
            dma((nc, F, 3)),
            dma((nc, F, 3)),
            dma((nc, F)),
            dma((nc, F)),
        ],
        compiler_params=pltpu.CompilerParams(
            collective_id=cid, has_side_effects=True, vmem_limit_bytes=VMEM_BYTES
        ),
    )(*own)


def adam_kernel(total, parts, scal_ref, rates_ref, *refs):
    grads = refs[:parts]
    w_ref, m_ref, g_out, w_out, m_out = refs[parts:]
    step_value = scal_ref[0].astype(F32)
    log_first = jnp.log(jnp.full((8, 128), beta_first, F32))
    log_second = jnp.log(jnp.full((8, 128), beta_second, F32))
    fix_first = (1.0 - jnp.exp(step_value * log_first))[:1, :1]
    fix_second = (1.0 - jnp.exp(step_value * log_second))[:1, :1]

    def update(g_ref):
        grad = g_ref[0, 0].astype(F32) / total
        w = w_ref[...]
        first = beta_first * m_ref[0] + (1.0 - beta_first) * grad
        second = beta_second * m_ref[1] + (1.0 - beta_second) * grad * grad
        step = first / fix_first / (jnp.sqrt(second / fix_second) + adam_eps) + rates_ref[1] * w
        g_out[...] = grad
        w_out[...] = w - rates_ref[0] * step
        m_out[0] = first
        m_out[1] = second

    if parts == 1:
        update(grads[0])
    else:
        for j in range(parts):

            @pl.when(pl.program_id(0) == j)
            def _(j=j):
                update(grads[j])


def adam_call(weight, moments, grads, count, rates, total, tile_rows, tile_cols, sides):
    parts = len(grads)
    K, _, rows, _ = grads[0].shape
    tiles = rows // tile_rows

    def g_spec(j):
        def index(jj, kk, cc, ss, tt, *_):
            on = jj == j
            return (
                jnp.where(on, kk, 0),
                jnp.where(on, cc, 0),
                jnp.where(on, tt, 0),
                jnp.where(on, ss, 0),
            )

        return pl.BlockSpec((1, 1, tile_rows, tile_cols), index)

    def place(jj, kk, cc, ss, tt, *_):
        return (kk * tiles + tt, (ss * 2 + cc) * parts + jj)

    def place3(jj, kk, cc, ss, tt, *_):
        return (0,) + place(jj, kk, cc, ss, tt)

    w_spec = pl.BlockSpec((tile_rows, tile_cols), place)
    m_spec = pl.BlockSpec((2, tile_rows, tile_cols), place3)
    smem = pl.BlockSpec(memory_space=pltpu.SMEM)

    def body(*refs):
        adam_kernel(total, parts, *refs)

    return pl.pallas_call(
        body,
        grid=(parts, K, 2, sides, tiles),
        in_specs=[smem, smem] + [g_spec(j) for j in range(parts)] + [w_spec, m_spec],
        out_specs=[w_spec, w_spec, m_spec],
        out_shape=[
            jax.ShapeDtypeStruct(weight.shape, F32),
            jax.ShapeDtypeStruct(weight.shape, F32),
            jax.ShapeDtypeStruct(moments.shape, F32),
        ],
        compiler_params=pltpu.CompilerParams(
            dimension_semantics=("arbitrary",) * 5, vmem_limit_bytes=VMEM_BYTES
        ),
        cost_estimate=pl.CostEstimate(
            flops=20 * weight.size, bytes_accessed=30 * weight.size, transcendentals=weight.size
        ),
    )(count, rates, *grads, weight, moments)


def dot(a, b):
    return jnp.dot(a, b, preferred_element_type=F32)


def dot_rows(a, b):
    return lax.dot_general(a, b, (((1,), (0,)), ((), ())), preferred_element_type=F32)


def dot_t(a, b):
    return lax.dot_general(a, b, (((1,), (1,)), ((), ())), preferred_element_type=F32)


def plane_sum(left, right, zb):
    y = lax.axis_index("y")
    x = lax.axis_index("x")
    T, M = left.shape
    N = right.shape[1]
    r = M // (zb * 8)
    rows = left.T.reshape(zb, 2, 2, 2, r, T).transpose(3, 1, 2, 0, 4, 5)

    def pick(h, yy, xx):
        block = lax.dynamic_index_in_dim(rows[h], yy, 0, keepdims=False)
        return lax.dynamic_index_in_dim(block, xx, 0, keepdims=False).reshape(zb * r, T)

    sent0 = jnp.concatenate([pick(0, 0, 1 - x), pick(0, 1, 1 - x)], axis=0)
    sent1 = jnp.concatenate([pick(1, 1 - y, 0), pick(1, 1 - y, 1)], axis=0)
    got0 = swapped(dot_rows(sent0, right).astype(BF), "x").reshape(2, zb * r, N)
    got1 = swapped(dot_rows(sent1, right).astype(BF), "y").reshape(2, zb * r, N)

    def at(got, i):
        return lax.dynamic_index_in_dim(got, i, 0, keepdims=False).astype(F32)

    next0 = swapped((dot_rows(pick(0, 1 - y, x), right) + at(got0, 1 - y)).astype(BF), "y")
    next1 = swapped((dot_rows(pick(1, y, 1 - x), right) + at(got1, 1 - x)).astype(BF), "x")
    last0 = dot_rows(pick(0, y, x), right) + at(got0, y) + next0.astype(F32)
    last1 = dot_rows(pick(1, y, x), right) + at(got1, x) + next1.astype(F32)
    both = [v.astype(BF).reshape(zb, 1, r, N) for v in (last0, last1)]
    return jnp.concatenate(both, axis=1)


def handed_out(share):
    S, _, r, N = share.shape
    mine = lax.psum_scatter(share.reshape(S, 2 * r, N), "z", scatter_dimension=0, tiled=False)
    return lax.all_gather(mine, ("y", "x", "c"), axis=0).reshape(4, 2, 2 * r, N)


def on_device(
    Y,
    S,
    block_in,
    cotangent,
    segment_ids,
    input_proj,
    output_proj,
    gate_up,
    down_weight,
    norm_gains,
    input_moments,
    output_moments,
    gate_moments,
    down_moments,
    gain_moments,
    update_count,
    optimizer_rates,
):
    seq_place = lax.axis_index("z")
    core = lax.axis_index("c")
    D = block_in.shape[-1]
    half_ff = FF // 2
    quarter_ff = FF // 4
    rows_d = input_proj.shape[0]
    rows_f = down_weight.shape[0]
    fast = Y == 2 and rows_d % 128 == 0
    in_half = input_proj.shape[1] // 2
    d_half = D // 2

    in_low = input_proj.astype(BF)
    out_low = output_proj.astype(BF)
    down_low = down_weight.astype(BF)

    def halves(w):
        n = w.shape[1] // 2
        return jnp.stack([w[:, :n], w[:, n:]])

    def gate_part(j):
        cols = []
        for side in range(2):
            first = side * FF + core * half_ff + j * quarter_ff
            cols.append(lax.dynamic_slice_in_dim(gate_up, first, quarter_ff, 1))
        return jnp.concatenate(cols, axis=1).astype(BF)

    if fast:
        r = rows_d // 8
        rf = rows_f // 8
        own_in = halves(in_low).reshape(2, 4, 2, r, in_half)
        own_out = halves(out_low).reshape(2, 4, 2, r, d_half)
        own_down = halves(down_low).reshape(2, 4, 2, rf, d_half)
        in_full, out_full = gathered(
            [own_in, own_out], [True, True], [(0, 0, r), (1, 0, r)], S, 0
        )
        in_full = in_full.reshape(2, D, in_half)
        out_full = out_full.reshape(2, D, d_half)
    else:
        in_full = halves(lax.all_gather(in_low, "z", axis=0, tiled=True))
        out_full = halves(lax.all_gather(out_low, "z", axis=0, tiled=True))
        down_full = halves(lax.all_gather(down_low, "z", axis=0, tiled=True))
        gate_full = [lax.all_gather(gate_part(j), "z", axis=0, tiled=True) for j in range(2)]
    gains_full = lax.all_gather(norm_gains.astype(BF), "z", axis=1, tiled=True)

    gains_wide = gains_full.astype(F32)
    tokens = block_in[0].astype(F32)
    piece_len = tokens.shape[0]
    width_q = HEADS * HEAD
    positions = seq_place * piece_len + jnp.arange(piece_len, dtype=jnp.int32)
    normed = root_norm(tokens, gains_wide[0]).astype(BF)
    mixed_proj = jnp.concatenate([dot(normed, in_full[0]), dot(normed, in_full[1])], axis=1)
    queries = rotate(
        mixed_proj[:, :width_q].reshape(piece_len, HEADS, HEAD), positions, 1.0
    ).astype(BF)
    own_keys = rotate(mixed_proj[:, width_q : width_q + HEAD], positions, 1.0)
    own_pair = jnp.concatenate([own_keys, mixed_proj[:, width_q + HEAD :]], axis=1).astype(BF)
    reach_count = (WINDOW + piece_len - 2) // piece_len
    earlier = []
    for back_step in range(reach_count, 0, -1):
        earlier.append(passed_along(own_pair, "z", back_step))
    key_pairs = jnp.concatenate(earlier + [own_pair], axis=0)
    key_rows = key_pairs[:, :HEAD]
    values = key_pairs[:, HEAD:]
    segments = segment_ids[0]
    key_span = reach_count * piece_len
    padded_ids = jnp.concatenate([jnp.full((key_span,), -1, jnp.int32), segments])
    query_ids = lax.dynamic_slice_in_dim(segments, seq_place * piece_len, piece_len)
    key_ids = lax.dynamic_slice_in_dim(padded_ids, seq_place * piece_len, key_span + piece_len)
    distance = jnp.arange(piece_len)[:, None] + key_span - jnp.arange(key_span + piece_len)[None, :]
    allowed = (distance >= 0) & (distance < WINDOW) & (query_ids[:, None] == key_ids[None, :])
    live_rows = query_ids != 0
    score_scale = HEAD ** (-0.5)

    def masked_scores(query_part):
        scores = (
            jnp.einsum("thd,kd->htk", query_part, key_rows, preferred_element_type=F32)
            * score_scale
        )
        return jnp.where(allowed[None], scores, -1e30)

    group_outputs = []
    group_totals = []
    for first_head in range(0, HEADS, head_group):
        scores = masked_scores(queries[:, first_head : first_head + head_group])
        log_totals = jax.nn.logsumexp(scores, axis=-1)
        weights = jnp.exp(scores - log_totals[..., None]).astype(BF)
        group_outputs.append(
            jnp.einsum("htk,kd->thd", weights, values, preferred_element_type=F32)
        )
        group_totals.append(log_totals)
    attended = jnp.concatenate(group_outputs, axis=1)
    attended = jnp.where(live_rows[:, None, None], attended, 0.0)
    flat_heads = attended.reshape(piece_len, width_q).astype(BF)
    middle = tokens + jnp.concatenate(
        [dot(flat_heads, out_full[0]), dot(flat_heads, out_full[1])], axis=1
    )
    normed_two = root_norm(middle, gains_wide[1]).astype(BF)

    if fast:
        gate_own = [gate_part(j).reshape(4, 2, r, 2 * quarter_ff) for j in range(2)]
        down_full, gate_a, gate_b = gathered(
            [own_down] + gate_own,
            [True, False, False],
            [(0, i * 48, 48) for i in range(rf // 48)]
            + [(1 + j, i * 16, 16) for j in range(2) for i in range(r // 16)],
            S,
            1,
        )
        down_full = down_full.reshape(2, FF, d_half)
        gate_full = [g.reshape(D, 2 * quarter_ff) for g in (gate_a, gate_b)]
    down_mine = lax.dynamic_slice_in_dim(down_full, core * half_ff, half_ff, 1)

    upstream = cotangent[0].astype(F32)

    def pair(v):
        return jnp.concatenate([v, swapped(v, "c")], axis=0)

    low_both = pair(cotangent[0])
    normed_both = pair(normed)
    two_both = pair(normed_two)
    flat_both = pair(flat_heads)

    hidden = []
    grad_gated = []
    grad_two = 0.0
    out_sum = 0.0
    for j in range(2):
        gated = dot(two_both, gate_full[j])
        down_j = lax.slice_in_dim(down_mine, j * quarter_ff, (j + 1) * quarter_ff, axis=1)
        grad_hidden = dot_t(low_both[:, :d_half], down_j[0]) + dot_t(
            low_both[:, d_half:], down_j[1]
        )
        gate, up = gated[:, :quarter_ff], gated[:, quarter_ff:]
        unit, unit_pull = jax.vjp(gated_unit, gate, up)
        grad_gate, grad_up = unit_pull(grad_hidden)
        hidden.append(unit.astype(BF))
        grad_gated.append(jnp.concatenate([grad_gate, grad_up], axis=1).astype(BF))
        grad_two = grad_two + dot_t(grad_gated[j], gate_full[j])
        out_sum = out_sum + jnp.concatenate([dot(hidden[j], down_j[i]) for i in range(2)], axis=1)

    def core_sum(v):
        return v[:piece_len] + swapped(v[piece_len:].astype(BF), "c").astype(F32)

    hidden = jnp.concatenate(hidden, axis=1)

    def summed(left, right, zb):
        if fast:
            return handed_out(plane_sum(left, right, zb))
        whole = dot_rows(left.T, right).astype(BF)
        whole = whole.reshape(S, left.shape[1] // S, right.shape[1])
        mine = lax.psum_scatter(whole, "z", scatter_dimension=0, tiled=False)
        mine = lax.psum(mine, ("y", "x"))
        return lax.all_gather(mine, "c", axis=0)[None]

    def summed_down():
        if fast:
            share = plane_sum(hidden, low_both, S // 2)
            keep = lax.dynamic_slice_in_dim(share, core * d_half, d_half, 3)
            give = lax.dynamic_slice_in_dim(share, (1 - core) * d_half, d_half, 3)
            got = swapped(give, "c")
            first = jnp.where(core == 0, keep, got)
            second = jnp.where(core == 0, got, keep)
            return handed_out(jnp.concatenate([first, second], axis=0))
        whole = dot_rows(hidden.T, low_both).astype(BF)
        mine = lax.psum(whole, ("y", "x"))
        mine = lax.all_gather(mine, "c", axis=0, tiled=True)
        mine = lax.dynamic_slice_in_dim(mine, core * d_half, d_half, 1)
        mine = lax.psum_scatter(mine, "z", scatter_dimension=0, tiled=True)
        return lax.all_gather(mine, "c", axis=0)[None]

    gate_sums = [summed(two_both, grad_gated[j], S) for j in range(2)]
    down_sum = summed_down()

    output = middle + core_sum(out_sum)
    block_out = output.astype(BF)[None]
    grad_normed_two = core_sum(grad_two)
    _, norm_pull_two = jax.vjp(root_norm, middle, gains_wide[1])
    grad_middle_norm, grad_gain_two = norm_pull_two(grad_normed_two)
    grad_middle = upstream + grad_middle_norm
    grad_branch = grad_middle.astype(BF)

    def half_pair(v):
        n = v.shape[1] // 2
        keep = lax.dynamic_slice_in_dim(v, core * n, n, 1)
        give = lax.dynamic_slice_in_dim(v, (1 - core) * n, n, 1)
        return jnp.concatenate([keep, swapped(give, "c")], axis=0)

    out_total = summed(flat_both, half_pair(grad_branch), S)
    grad_flat = dot_t(grad_branch[:, :d_half], out_full[0]) + dot_t(
        grad_branch[:, d_half:], out_full[1]
    )
    grad_attended = (
        jnp.where(live_rows[:, None], grad_flat, 0.0).astype(BF).reshape(piece_len, HEADS, HEAD)
    )
    grad_queries = []
    grad_key_sum = jnp.zeros((key_span + piece_len, HEAD), F32)
    grad_value_sum = jnp.zeros((key_span + piece_len, HEAD), F32)
    for group_index, first_head in enumerate(range(0, HEADS, head_group)):
        query_part = queries[:, first_head : first_head + head_group]
        scores = masked_scores(query_part)
        probabilities = jnp.exp(scores - group_totals[group_index][..., None])
        weights = probabilities.astype(BF)
        grad_part = grad_attended[:, first_head : first_head + head_group]
        grad_probs = jnp.einsum("thd,kd->htk", grad_part, values, preferred_element_type=F32)
        grad_scores = probabilities * (
            grad_probs - jnp.sum(probabilities * grad_probs, axis=-1, keepdims=True)
        )
        grad_raw = (grad_scores * score_scale).astype(BF)
        grad_queries.append(
            jnp.einsum("htk,kd->thd", grad_raw, key_rows, preferred_element_type=F32)
        )
        grad_key_sum = grad_key_sum + jnp.einsum(
            "htk,thd->kd", grad_raw, query_part, preferred_element_type=F32
        )
        grad_value_sum = grad_value_sum + jnp.einsum(
            "htk,thd->kd", weights, grad_part, preferred_element_type=F32
        )
    grad_pairs = jnp.concatenate([grad_key_sum, grad_value_sum], axis=1)
    own_grad = grad_pairs[key_span:]
    for back_step in range(1, reach_count + 1):
        sent_rows = grad_pairs[
            key_span - back_step * piece_len : key_span - (back_step - 1) * piece_len
        ]
        own_grad = own_grad + passed_along(sent_rows, "z", -back_step)
    grad_query_all = jnp.concatenate(grad_queries, axis=1)
    grad_query_raw = rotate(grad_query_all, positions, -1.0).reshape(piece_len, width_q)
    grad_key_raw = rotate(own_grad[:, :HEAD], positions, -1.0)
    grad_mixed = jnp.concatenate([grad_query_raw, grad_key_raw, own_grad[:, HEAD:]], axis=1).astype(
        BF
    )
    in_total = summed(normed_both, half_pair(grad_mixed), S)
    grad_normed = dot_t(grad_mixed[:, :in_half], in_full[0]) + dot_t(
        grad_mixed[:, in_half:], in_full[1]
    )
    _, norm_pull_one = jax.vjp(root_norm, tokens, gains_wide[0])
    grad_tokens_norm, grad_gain_one = norm_pull_one(grad_normed)
    block_in_grad = (grad_middle + grad_tokens_norm).astype(BF)[None]
    gains_sum = lax.psum(jnp.stack([grad_gain_one, grad_gain_two]), ("y", "x", "c", "z"))
    gains_mine = lax.dynamic_slice_in_dim(gains_sum, seq_place * rows_d, rows_d, 1)

    token_total = piece_len * S * Y * 4 * block_in.shape[0]
    step_value = update_count[0].astype(F32)
    count = update_count
    rates = optimizer_rates

    def adam(weight, moments, grads, sides):
        rows, cols = grads[0].shape[2:]
        return adam_call(
            weight, moments, grads, count, rates, float(token_total), rows, cols // sides, sides
        )

    in_grad, in_new, in_mom = adam(input_proj, input_moments, [in_total], 1)
    out_grad, out_new, out_mom = adam(output_proj, output_moments, [out_total], 1)
    gate_grad, gate_new, gate_mom = adam(gate_up, gate_moments, gate_sums, 2)
    down_grad, down_new, down_mom = adam(down_weight, down_moments, [down_sum], 1)
    gain_grad = gains_mine / token_total
    gains_step, gain_moments_new = adamw_step(norm_gains, gain_moments, gain_grad, step_value, rates)
    return (
        block_out,
        block_in_grad,
        in_grad,
        out_grad,
        gate_grad,
        down_grad,
        gain_grad,
        in_new,
        out_new,
        gate_new,
        down_new,
        gains_step,
        in_mom,
        out_mom,
        gate_mom,
        down_mom,
        gain_moments_new,
    )


def solution(mesh):
    dp, S = mesh.shape["dp"], mesh.shape["seq"]
    Y = dp // 4
    grid = Mesh(mesh.devices.reshape(Y, 2, 2, S), ("y", "x", "c", "z"))
    data = ("y", "x", "c")
    tokens = P(data, "z", None)
    rows = P("z", None)
    moments = P(None, "z", None)
    in_specs = (
        (tokens, tokens, P(data, None))
        + (rows,) * 4
        + (P(None, "z"),)
        + (moments,) * 4
        + (P(None, None, "z"), P(), P())
    )
    out_specs = (
        (tokens, tokens)
        + (rows,) * 4
        + (P(None, "z"),)
        + (rows,) * 4
        + (P(None, "z"),)
        + (moments,) * 4
        + (P(None, None, "z"),)
    )

    def device_step(*arrays):
        return on_device(Y, S, *arrays)

    return jax.shard_map(
        device_step, mesh=grid, in_specs=in_specs, out_specs=out_specs, check_vma=False
    )
```

time: 2350 us -> 1210 us (0.51)
  waiting for transfers between devices: 1720 us -> 231 us
  Pallas kernels: 0 us -> 284 us
  other arithmetic: 193 us -> 90.7 us
  local copies, waits for them, and re-layouts: 32.9 us -> 111 us
  matrix products: 342 us -> 385 us
    all_gather x4 -> x5, waiting for transfers between devices: 782 us -> 55.3 us  [handed_out(): return lax.all_gather(mine, ('y', 'x', 'c'), axis=0).reshape(4, 2, 2 * r, N)]
    reduce_scatter x4 -> x5, waiting for transfers between devices: 764 us -> 42.2 us  [handed_out(): lax.psum_scatter(share.reshape(S, 2 * r, N), 'z', scatter_dimension=0, ti...]
    pallas_call x0 -> x6, Pallas kernels: none -> 284 us  [the longest x2 195 us: gathered(): pl.pallas_call(body, out_shape=tuple(outs), in_specs=[pl.BlockSpec(memory...]
    psum x1 -> x0, waiting for transfers between devices: 166 us -> none  [on_device(): lax.psum(summed[0].astype(jnp.bfloat16), 'dp').astype(jnp.float32)]
    another operation x15 -> x1, other arithmetic: 133 us -> 0.6 us  [adamw_step(): return (optimizer_rates[0] * update, jnp.stack([first_moment, second]))]
    ppermute x0 -> x29, waiting for transfers between devices: none -> 129 us  [swapped(): return lax.ppermute(block, axis, [(0, 1), (1, 0)])]
    dot_general x30 -> x68, matrix products: 342 us -> 385 us  [the longest x30 82.4 us: dot_rows(): lax.dot_general(a, b, (((1,), (0,)), ((), ())), preferred_element_type=F32)]
    psum x1, blocking collectives: 12.7 us -> 39.5 us  [on_device(): lax.psum(jnp.stack([grad_gain_one, grad_gain_two]), ('y', 'x', 'c', 'z'))]
  transfers between devices with their start and end apart: 14 -> 43, of which waited for: 10 -> 16; matrix products, arithmetic and copies ran while one was open for 16% -> 45% of each run, Pallas kernels for 0% -> 18%
where the time goes in v1:
time: 1210 us; the launch traced here: 1200 us
  matrix products  385 us (32%)
  Pallas kernels  284 us (23%)
  waiting for transfers between devices  231 us (19%)
  local copies, waits for them, and re-layouts  111 us (9%)
  other arithmetic  90.7 us (7%)
  blocking collectives  51.4 us (4%)
  starting transfers between devices  30.2 us (2%)
  between operations  17.3 us (1%)
    pallas_call x2, Pallas kernels, gathered(): pl.pallas_call(body, out_shape=tuple(outs), in_specs=[pl.BlockSpec(memory...  195 us
    ppermute x29, waiting for transfers between devices, swapped(): return lax.ppermute(block, axis, [(0, 1), (1, 0)])  129 us
    pallas_call x4, Pallas kernels, adam_call(): pl.pallas_call(body, grid=(parts, K, 2, sides, tiles), in_specs=[smem, sm...  89.5 us
    dot_general x30, matrix products, dot_rows(): lax.dot_general(a, b, (((1,), (0,)), ((), ())), preferred_element_type=F32)  82.4 us
    dot_general x10, matrix products, dot_t(): lax.dot_general(a, b, (((1,), (1,)), ((), ())), preferred_element_type=F32)  68.5 us
    dot_general x3, matrix products, on_device(): jnp.einsum('htk,kd->thd', grad_raw, key_rows, preferred_element_type=F32)  58.7 us
    dot_general x3, matrix products, on_device(): jnp.einsum('htk,thd->kd', grad_raw, query_part, preferred_element_type=F32)  58.3 us
    all_gather x5, waiting for transfers between devices, handed_out(): return lax.all_gather(mine, ('y', 'x', 'c'), axis=0).reshape(4, 2, 2 * r, N)  55.3 us
  transfers between devices with their start and end apart: 43, of which 16 were waited for; matrix products, arithmetic and copies ran while one was open for 45% of the time, Pallas kernels for 18%

profile of v1, /device:TPU:0, one launch (start us, length us, event | category | flops | bytes accessed | tf_op | source)
XLA Modules:
  0.0 1200.6 jit_solution(15645856535792333161)
XLA Ops:
  12.8 47.4 %shard_map.278 = (bf16[2,4,4,2,48,896]{5,4,3,2,1,0:T(8,128)(2,1)}, bf16[2,4,4,2,48,768]{5,4,3,2,1,0:T(8,128)(2,1)}) custom-call(bf16[2,4,2,48,896]{4,3,2,1,0:T(8,128)(2,1)} %pad_maximum_fusion.17.refs_0_, bf16[2,4,2,48,768]{4,3,2,1,0:T(8,128)(2,1)} %pad_maximum_fusion.18.refs_1_), custom_call_target="tpu_custom_call" | custom-call | tf_op jit(solution)/shard_map/pallas_call | solution.py:276
  60.2 4.7 fusion.249
  64.9 11.9 all_gather.18
  98.5 3.6 fusion.175
  112.1 3.4 copy.291
  117.2 5.0 fusion.252
  129.8 3.8 subtract_convert_fusion.1
  133.5 6.1 dynamic-slice_convert_fusion.1
  142.0 7.3 fusion.266
  152.1 6.8 fusion.265
  158.9 7.5 exponential_reduce_fusion
  166.4 6.8 fusion.113
  173.3 6.2 exponential_reduce_fusion.1
  179.6 6.9 fusion.110
  201.4 147.4 %shard_map.279 = (bf16[2,4,4,2,144,768]{5,4,3,2,1,0:T(8,128)(2,1)}, bf16[4,4,2,48,2304]{4,3,2,1,0:T(8,128)(2,1)}, bf16[4,4,2,48,2304]{4,3,2,1,0:T(8,128)(2,1)}) custom-call(bf16[2,4,2,144,768]{4,3,2,1,0:T(8,128)(2,1)} %pad_maximum_fusion.3.refs_0_, bf16[4,2,48,2304]{3,2,1,0:T(8,128)(2,1)} %get-tuple-element.161.refs_1_, ...), custom_call_target="tpu_custom_call" | custom-call | tf_op jit(solution)/shard_map/pallas_call | solution.py:276
  351.2 6.7 fusion.103
  358.0 4.1 fusion.105
  362.1 12.1 %fusion.142 = f32[1024,2304]{1,0:T(8,128)} fusion(bf16[1536,2304]{1,0:T(8,128)(2,1)S(1)} %bitcast.586, bf16[512,1536]{1,0:T(8,128)(2,1)} %collective-permute-done.2, bf16[512,1536]{1,0:T(8,128)(2,1)} %multiply_convert_fusion.4), kind=kOutput, calls=%fused_computation.259 | convolution fusion | flops 7254048768 | bytes 19660800 | tf_op jit(solution)/shard_map/dot_general | solution.py:378
  374.2 11.3 fusion.24
  385.6 3.9 fusion.104
  389.4 3.9 fusion.101
  393.3 11.9 fusion.141
  405.2 10.0 fusion.31
  415.2 3.9 fusion.106
  419.1 3.9 fusion.102
  423.0 3.7 fusion.140
  433.9 11.5 fusion.245
  445.4 12.2 %convolution_add_fusion.2 = f32[1024,1536]{1,0:T(8,128)S(1)} fusion(f32[1024,1536]{1,0:T(8,128)} %fusion.245, bf16[1536,2304]{1,0:T(8,128)(2,1)} %bitcast.579, bf16[1024,1152]{1,0:T(8,128)(2,1)} %get-tuple-element.65, bf16[1024,1152]{1,0:T(8,128)(2,1)} %get-tuple-element.64), kind=kOutput, calls=%fused_computation.75 | convolution fusion | flops 7258767360 | bytes 24379392 | tf_op jit(solution)/shard_map/dot_general | solution.py:386
  483.6 3.7 maximum_bitcast_fusion.2
  499.2 6.8 copy.250
  508.1 4.8 convolution_convert_fusion.5
  529.5 5.0 fusion.246
  541.5 6.6 fusion.166
  548.1 6.6 fusion.169
  554.6 6.3 fusion.172
  561.0 19.4 %fusion.116 = f32[512,4,128]{2,0,1:T(8,128)} fusion(f32[1536,512,4]{1,0,2:T(8,128)} %fusion.166, f32[4,512,1536]{1,2,0:T(8,128)} %get-tuple-element.155, f32[4,512]{1,0:T(4,128)S(1)} %copy-done.91, bf16[1536,256]{1,0:T(8,128)(2,1)S(1)} %copy-done.8), kind=kOutput, calls=%fused_computation.220 | convolution fusion | flops 827330048 | bytes 51789824 | tf_op jit(solution)/shard_map/htk,kd->thd/dot_general | solution.py:651
  580.4 19.3 %fusion.68 = f32[1536,128]{0,1:T(8,128)} fusion(bf16[512,4,128]{2,0,1:T(8,128)(2,1)S(1)} %copy-done.68, f32[1536,512,4]{1,0,2:T(8,128)} %fusion.166, f32[4,512,1536]{1,2,0:T(8,128)} %get-tuple-element.155, f32[4,512]{1,0:T(4,128)S(1)} %copy-done.91), kind=kOutput, calls=%fused_computation.143 | convolution fusion | flops 827330048 | bytes 26484736 | tf_op jit(solution)/shard_map/htk,thd->kd/dot_general | solution.py:653
  599.7 19.8 %fusion.117 = f32[512,4,128]{2,0,1:T(8,128)} fusion(f32[1536,512,4]{1,0,2:T(8,128)} %fusion.169, f32[4,512,1536]{1,2,0:T(8,128)} %get-tuple-element.157, f32[4,512]{1,0:T(4,128)S(1)} %copy-done.93, bf16[1536,256]{1,0:T(8,128)(2,1)} %copy-done.7), kind=kOutput, calls=%fused_computation.221 | convolution fusion | flops 827330048 | bytes 51789824 | tf_op jit(solution)/shard_map/htk,kd->thd/dot_general | solution.py:651
  619.5 19.1 %fusion.69 = f32[1536,128]{0,1:T(8,128)} fusion(f32[1536,512,4]{1,0,2:T(8,128)} %fusion.169, f32[4,512,1536]{1,2,0:T(8,128)} %get-tuple-element.157, f32[4,512]{1,0:T(4,128)S(1)} %copy-done.93, bf16[512,12,64]{2,0,1:T(8,128)(2,1)S(1)} %copy-done.4, bf16[512,12,64]{2,0,1:T(8,128)(2,1)S(1)} %copy-done.6), kind=kOutput, calls=%fused_computation.144 | convolution fusion | flops 828378624 | bytes 54280192 | tf_op jit(solution)/shard_map/htk,thd->kd/dot_general | solution.py:653
  638.7 7.0 convolution_bitcast_fusion
  645.7 7.0 convolution_bitcast_fusion.1
  655.9 19.9 %fusion.74 = f32[1536,128]{0,1:T(8,128)} fusion(f32[1536,128]{0,1:T(8,128)} %fusion.68, f32[1536,128]{0,1:T(8,128)} %fusion.69, f32[1536,512,4]{1,0,2:T(8,128)} %fusion.172, f32[4,512,1536]{1,2,0:T(8,128)} %copy-done, f32[4,512]{1,0:T(4,128)S(1)} %copy-done.95, bf16[512,12,64]{2,0,1:T(8,128)(2,1)S(1)} %copy-done.4, bf16[512,12,64]{2,0,1:T(8,128)(2,1)S(1)} %copy-done.6), kind=kOutput, calls=%fused_computation.152 | convolution fusion | flops 828771840 | bytes 55853056 | tf_op jit(solution)/shard_map/htk,thd->kd/dot_general | solution.py:653
  682.1 19.4 %fusion.118 = f32[512,4,128]{2,0,1:T(8,128)} fusion(f32[1536,512,4]{1,0,2:T(8,128)} %fusion.172, f32[4,512,1536]{1,2,0:T(8,128)} %copy-done, f32[4,512]{1,0:T(4,128)S(1)} %copy-done.95, bf16[1536,256]{1,0:T(8,128)(2,1)S(1)} %copy-done.9), kind=kOutput, calls=%fused_computation.222 | convolution fusion | flops 827330048 | bytes 51789824 | tf_op jit(solution)/shard_map/htk,kd->thd/dot_general | solution.py:651
  714.1 3.8 fusion.138
  719.3 4.8 fusion.47
  734.0 7.9 collective-permute-done.18
  749.4 4.2 collective-permute-done.19
  777.2 9.3 collective-permute-done.12
  789.0 17.4 %collective-permute-done.10 = bf16[384,896]{1,0:T(8,128)(2,1)} collective-permute-done((bf16[384,896]{1,0:T(8,128)(2,1)}, bf16[384,896]{1,0:T(8,128)(2,1)}, u32[]{:S(2)}, u32[]{:S(2)}) %collective-permute-start.10) | collective-permute-done | bytes 688160 | tf_op jit(solution)/shard_map/ppermute | solution.py:34
  813.7 17.6 %collective-permute-done.13 = bf16[192,896]{1,0:T(8,128)(2,1)S(1)} collective-permute-done((bf16[192,896]{1,0:T(8,128)(2,1)S(1)}, bf16[192,896]{1,0:T(8,128)(2,1)S(1)}, u32[]{:S(2)}, u32[]{:S(2)}) %collective-permute-start.13) | collective-permute-done | bytes 344096 | tf_op jit(solution)/shard_map/ppermute | solution.py:34
  840.5 15.1 %collective-permute-done.21 = bf16[192,2304]{1,0:T(8,128)(2,1)} collective-permute-done((bf16[192,2304]{1,0:T(8,128)(2,1)}, bf16[192,2304]{1,0:T(8,128)(2,1)}, u32[]{:S(2)}, u32[]{:S(2)}) %collective-permute-start.21) | collective-permute-done | bytes 884768 | tf_op jit(solution)/shard_map/ppermute | solution.py:34
  870.4 4.7 convolution_convert_fusion.4
  875.8 14.1 %collective-permute-done.27 = bf16[192,2304]{1,0:T(8,128)(2,1)S(1)} collective-permute-done((bf16[192,2304]{1,0:T(8,128)(2,1)S(1)}, bf16[192,2304]{1,0:T(8,128)(2,1)S(1)}, u32[]{:S(2)}, u32[]{:S(2)}) %collective-permute-start.27) | collective-permute-done | bytes 884768 | tf_op jit(solution)/shard_map/ppermute | solution.py:34
  900.5 29.1 %collective-permute-done.30 = bf16[576,1536]{1,0:T(8,128)(2,1)} collective-permute-done((bf16[576,1536]{1,0:T(8,128)(2,1)}, bf16[576,1536]{1,0:T(8,128)(2,1)}, u32[]{:S(2)}, u32[]{:S(2)}) %collective-permute-start.30) | collective-permute-done | bytes 1769504 | tf_op jit(solution)/shard_map/ppermute | solution.py:34
  933.9 11.2 collective-permute-done.29
  958.1 42.1 %reduce-scatter.14.cloned.1.call-done = bf16[1,288,768]{2,1,0:T(8,128)(2,1)} async-done(((bf16[4,288,768]{2,1,0:T(8,128)(2,1)}), bf16[1,288,768]{2,1,0:T(8,128)(2,1)}) %reduce-scatter.14.cloned.1.call-update) | async-done | bytes 442384 | tf_op jit(solution)/shard_map/reduce_scatter | solution.py:419
  1001.6 39.5 %psum.7 = f32[2,1536]{1,0:T(2,128)S(1)} all-reduce(f32[2,1536]{1,0:T(2,128)S(1)} %pad_maximum_fusion.32), channel_id=1, replica_groups=mesh['y'=2,'x'=2,'c'=2,'z'=4] {'y','x','c','z'}, use_global_device_ids=true, to_apply=%region_20.21 | all-reduce | flops 3072 | bytes 24576 | tf_op jit(solution)/shard_map/psum | solution.py:679
  1043.7 5.0 fusion.97
  1048.8 9.6 shard_map.281
  1058.3 10.5 shard_map.280
  1068.8 19.4 %all-gather.10.cloned.1.call-done = bf16[8,96,2304]{2,1,0:T(8,128)(2,1)} async-done(((bf16[1,96,2304]{2,1,0:T(8,128)(2,1)}), bf16[8,96,2304]{2,1,0:T(8,128)(2,1)}) %all-gather.10.cloned.1.call-update) | async-done | bytes 3538960 | tf_op jit(solution)/shard_map/all_gather | solution.py:420
  1088.2 35.9 %all-gather.12.cloned.1.call-done = bf16[8,96,2304]{2,1,0:T(8,128)(2,1)} async-done(((bf16[1,96,2304]{2,1,0:T(8,128)(2,1)}), bf16[8,96,2304]{2,1,0:T(8,128)(2,1)}) %all-gather.12.cloned.1.call-update) | async-done | bytes 3538960 | tf_op jit(solution)/shard_map/all_gather | solution.py:420
  1124.1 49.2 %shard_map.282 = (f32[384,9216]{1,0:T(8,128)}, f32[384,9216]{1,0:T(8,128)}, f32[2,384,9216]{2,1,0:T(8,128)}) custom-call(s32[1]{0:T(128)S(6)} %copy.296.refs_0_, f32[2]{0:T(128)} %refs_1_.7, bf16[4,2,96,2304]{3,2,1,0:T(8,128)(2,1)} %bitcast.496, bf16[4,2,96,2304]{3,2,1,0:T(8,128)(2,1)} %bitcast.497, f32[384,9216]{1,0:T(8,128)} %refs_4_.6, ...), custom_call_target="tpu_custom_call" | custom-call | flops 70778880 | bytes 106168320 | tf_op jit(solution)/shard_map/pallas_call | solution.py:358
  1173.4 20.2 %shard_map.283 = (f32[1152,1536]{1,0:T(8,128)}, f32[1152,1536]{1,0:T(8,128)}, f32[2,1152,1536]{2,1,0:T(8,128)}) custom-call(s32[1]{0:T(128)S(6)} %copy.296.refs_0_, f32[2]{0:T(128)} %refs_1_.7, bf16[4,2,288,768]{3,2,1,0:T(8,128)(2,1)} %bitcast.487, f32[1152,1536]{1,0:T(8,128)} %refs_3_.5, f32[2,1152,1536]{2,1,0:T(8,128)} %refs_4_.7), custom_call_target="tpu_custom_call" | custom-call | flops 35389440 | bytes 53084160 | tf_op jit(solution)/shard_map/pallas_call | solution.py:358
  (563 shorter events, 268.1 us)
Async XLA Ops:
  7.2 948.1 %reduce-scatter.8.cloned.1.call-start = ((), (), s32[]{:S(2)}) async-start(), calls=%async_computation.7 | async-start | bytes 737280 | tf_op jit(solution)/shard_map/reduce_scatter | solution.py:419
  76.8 21.7 %copy-start.96 = (f32[1536]{0:T(1024)}, f32[1536]{0:T(1024)S(1)}, u32[]{:S(2)}) copy-start(f32[1536]{0:T(1024)S(1)} %get-tuple-element.56) | copy-start | bytes 18436
  76.8 118.9 %copy-start.88 = (f32[1536]{0:T(1024)}, f32[1536]{0:T(1024)S(1)}, u32[]{:S(2)}) copy-start(f32[1536]{0:T(1024)S(1)} %get-tuple-element.55) | copy-start | bytes 18436
  80.6 21.6 %copy-start.59 = (bf16[512,128]{1,0:T(8,128)(2,1)}, bf16[512,128]{1,0:T(8,128)(2,1)S(1)}, u32[]{:S(2)}) copy-start(bf16[512,128]{1,0:T(8,128)(2,1)S(1)} %slice.556) | copy-start | bytes 393220
  91.9 48.8 %collective-permute-start.1 = (bf16[512,256]{1,0:T(8,128)(2,1)}, bf16[512,256]{1,0:T(8,128)(2,1)}, u32[]{:S(2)}, u32[]{:S(2)}) collective-permute-start(bf16[512,256]{1,0:T(8,128)(2,1)} %pad_maximum_fusion.31), channel_id=1, source_target_pairs={{0,1},{1,2},{2,3},{4,5},{5,6},{6,7},{8,9},{9,10},{10,11},{12,13},{... | collective-permute-start | bytes 786440 | tf_op jit(solution)/shard_map/ppermute | solution.py:30
  94.9 45.8 %collective-permute-start = (bf16[512,256]{1,0:T(8,128)(2,1)}, bf16[512,256]{1,0:T(8,128)(2,1)}, u32[]{:S(2)}, u32[]{:S(2)}) collective-permute-start(bf16[512,256]{1,0:T(8,128)(2,1)} %pad_maximum_fusion.31), channel_id=1, source_target_pairs={{0,2},{1,3},{4,6},{5,7},{8,10},{9,11},{12,14},{13,15},{16,18},{17,... | collective-permute-start | bytes 786440 | tf_op jit(solution)/shard_map/ppermute | solution.py:30
  97.9 253.2 %collective-permute-start.4 = (bf16[512,1536]{1,0:T(8,128)(2,1)}, bf16[512,1536]{1,0:T(8,128)(2,1)}, u32[]{:S(2)}, u32[]{:S(2)}) collective-permute-start(bf16[512,1536]{1,0:T(8,128)(2,1)} %bitcast.508), channel_id=1, source_target_pairs={{0,4},{4,0},{1,5},{5,1},{2,6},{6,2},{3,7},{7,3},{8,12},{12,8},{9,1... | collective-permute-start | bytes 4718600 | tf_op jit(solution)/shard_map/ppermute | solution.py:34
  140.7 208.8 %copy-start.115 = (pred[512]{0:T(512)(128)(4,1)}, pred[512]{0:T(512)(128)(4,1)S(1)}, u32[]{:S(2)}) copy-start(pred[512]{0:T(512)(128)(4,1)S(1)} %broadcast_compare_fusion) | copy-start | bytes 1540
  142.0 46.2 %copy-start.7 = (bf16[1536,256]{1,0:T(8,128)(2,1)}, bf16[1536,256]{1,0:T(8,128)(2,1)S(1)}, u32[]{:S(2)}) copy-start(bf16[1536,256]{1,0:T(8,128)(2,1)S(1)} %maximum_maximum_fusion) | copy-start | bytes 2359300
  152.1 36.0 %copy-start = (f32[4,512,1536]{1,2,0:T(8,128)}, f32[4,512,1536]{1,2,0:T(8,128)S(1)}, u32[]{:S(2)}) copy-start(f32[4,512,1536]{1,2,0:T(8,128)S(1)} %get-tuple-element.159) | copy-start | bytes 37748740
  198.8 163.2 %collective-permute-start.2 = (bf16[512,1536]{1,0:T(8,128)(2,1)}, bf16[512,1536]{1,0:T(8,128)(2,1)}, u32[]{:S(2)}, u32[]{:S(2)}) collective-permute-start(bf16[512,1536]{1,0:T(8,128)(2,1)} %multiply_convert_fusion.4), channel_id=1, source_target_pairs={{0,4},{4,0},{1,5},{5,1},{2,6},{6,2},{3,7},{7,3},{8,12},{12,8},{9,1... | collective-permute-start | bytes 4718600 | tf_op jit(solution)/shard_map/ppermute | solution.py:34
  351.1 132.5 %collective-permute-start.14 = (bf16[512,1536]{1,0:T(8,128)(2,1)}, bf16[512,1536]{1,0:T(8,128)(2,1)}, u32[]{:S(2)}, u32[]{:S(2)}) collective-permute-start(bf16[512,1536]{1,0:T(8,128)(2,1)} %select_convert_fusion), channel_id=1, source_target_pairs={{0,4},{4,0},{1,5},{5,1},{2,6},{6,2},{3,7},{7,3},{8,12},{12,8},{9,1... | collective-permute-start | bytes 4718600 | tf_op jit(solution)/shard_map/ppermute | solution.py:34
  459.0 66.3 %collective-permute-start.5 = (bf16[512,1536]{1,0:T(8,128)(2,1)}, bf16[512,1536]{1,0:T(8,128)(2,1)}, u32[]{:S(2)}, u32[]{:S(2)}) collective-permute-start(bf16[512,1536]{1,0:T(8,128)(2,1)} %slice.553), channel_id=1, source_target_pairs={{0,4},{4,0},{1,5},{5,1},{2,6},{6,2},{3,7},{7,3},{8,12},{12,8},{9,1... | collective-permute-start | bytes 4718600 | tf_op jit(solution)/shard_map/ppermute | solution.py:34
  464.1 65.4 %collective-permute-start.3 = (bf16[512,1536]{1,0:T(8,128)(2,1)}, bf16[512,1536]{1,0:T(8,128)(2,1)}, u32[]{:S(2)}, u32[]{:S(2)}) collective-permute-start(bf16[512,1536]{1,0:T(8,128)(2,1)} %slice.554), channel_id=1, source_target_pairs={{0,4},{4,0},{1,5},{5,1},{2,6},{6,2},{3,7},{7,3},{8,12},{12,8},{9,1... | collective-permute-start | bytes 4718600 | tf_op jit(solution)/shard_map/ppermute | solution.py:34
  496.9 233.2 %collective-permute-start.22 = (bf16[384,2304]{1,0:T(8,128)(2,1)}, bf16[384,2304]{1,0:T(8,128)(2,1)}, u32[]{:S(2)}, u32[]{:S(2)}) collective-permute-start(bf16[384,2304]{1,0:T(8,128)(2,1)} %convolution_convert_fusion.2), channel_id=1, source_target_pairs={{0,16},{16,0},{1,17},{17,1},{2,18},{18,2},{3,19},{19,3},{4,20},{20... | collective-permute-start | bytes 5308424 | tf_op jit(solution)/shard_map/ppermute | solution.py:34
  497.1 313.0 %collective-permute-start.20 = (bf16[384,2304]{1,0:T(8,128)(2,1)}, bf16[384,2304]{1,0:T(8,128)(2,1)}, u32[]{:S(2)}, u32[]{:S(2)}) collective-permute-start(bf16[384,2304]{1,0:T(8,128)(2,1)} %convolution_convert_fusion.3), channel_id=1, source_target_pairs={{0,8},{8,0},{1,9},{9,1},{2,10},{10,2},{3,11},{11,3},{4,12},{12,4},... | collective-permute-start | bytes 5308424 | tf_op jit(solution)/shard_map/ppermute | solution.py:34
  498.9 364.0 %collective-permute-start.26 = (bf16[384,2304]{1,0:T(8,128)(2,1)}, bf16[384,2304]{1,0:T(8,128)(2,1)}, u32[]{:S(2)}, u32[]{:S(2)}) collective-permute-start(bf16[384,2304]{1,0:T(8,128)(2,1)} %convolution_convert_fusion), channel_id=1, source_target_pairs={{0,16},{16,0},{1,17},{17,1},{2,18},{18,2},{3,19},{19,3},{4,20},{20... | collective-permute-start | bytes 5308424 | tf_op jit(solution)/shard_map/ppermute | solution.py:34
  561.0 19.5 %copy-start.68 = (bf16[512,4,128]{2,0,1:T(8,128)(2,1)S(1)}, bf16[512,4,128]{2,0,1:T(8,128)(2,1)}, u32[]{:S(2)}) copy-start(bf16[512,4,128]{2,0,1:T(8,128)(2,1)} %pad_maximum_fusion.26) | copy-start | bytes 1572868
  599.7 19.8 %copy-start.4 = (bf16[512,12,64]{2,0,1:T(8,128)(2,1)S(1)}, bf16[512,12,64]{2,0,1:T(8,128)(2,1)}, u32[]{:S(2)}) copy-start(bf16[512,12,64]{2,0,1:T(8,128)(2,1)} %copy-done.3) | copy-start | bytes 2359300
  599.7 19.8 %copy-start.6 = (bf16[512,12,64]{2,0,1:T(8,128)(2,1)S(1)}, bf16[512,12,64]{2,0,1:T(8,128)(2,1)}, u32[]{:S(2)}) copy-start(bf16[512,12,64]{2,0,1:T(8,128)(2,1)} %copy-done.5) | copy-start | bytes 2359300
  678.2 26.5 %collective-permute-start.7 = (f32[512,256]{0,1:T(8,128)}, f32[512,256]{0,1:T(8,128)}, u32[]{:S(2)}, u32[]{:S(2)}) collective-permute-start(f32[512,256]{0,1:T(8,128)} %get-tuple-element.139), channel_id=1, source_target_pairs={{2,0},{3,1},{6,4},{7,5},{10,8},{11,9},{14,12},{15,13},{18,16},{19,... | collective-permute-start | bytes 1572872 | tf_op jit(solution)/shard_map/ppermute | solution.py:30
  679.5 26.3 %collective-permute-start.6 = (f32[512,256]{0,1:T(8,128)}, f32[512,256]{0,1:T(8,128)}, u32[]{:S(2)}, u32[]{:S(2)}) collective-permute-start(f32[512,256]{0,1:T(8,128)} %get-tuple-element.138), channel_id=1, source_target_pairs={{1,0},{2,1},{3,2},{5,4},{6,5},{7,6},{9,8},{10,9},{11,10},{13,12},{... | collective-permute-start | bytes 1572872 | tf_op jit(solution)/shard_map/ppermute | solution.py:30
  704.7 19.3 %collective-permute-start.15 = (bf16[512,768]{1,0:T(8,128)(2,1)}, bf16[512,768]{1,0:T(8,128)(2,1)}, u32[]{:S(2)}, u32[]{:S(2)}) collective-permute-start(bf16[512,768]{1,0:T(8,128)(2,1)} %get-tuple-element.125), channel_id=1, source_target_pairs={{0,4},{4,0},{1,5},{5,1},{2,6},{6,2},{3,7},{7,3},{8,12},{12,8},{9,1... | collective-permute-start | bytes 2359304 | tf_op jit(solution)/shard_map/ppermute | solution.py:34
  724.0 31.9 %collective-permute-start.8 = (bf16[512,1536]{1,0:T(8,128)(2,1)S(1)}, bf16[512,1536]{1,0:T(8,128)(2,1)S(1)}, u32[]{:S(2)}, u32[]{:S(2)}) collective-permute-start(bf16[512,1536]{1,0:T(8,128)(2,1)S(1)} %get-tuple-element.115), channel_id=1, source_target_pairs={{0,4},{4,0},{1,5},{5,1},{2,6},{6,2},{3,7},{7,3},{8,12},{12,8},{9,1... | collective-permute-start | bytes 4718600 | tf_op jit(solution)/shard_map/ppermute | solution.py:34
  726.1 15.8 %collective-permute-start.18 = (bf16[384,768]{1,0:T(8,128)(2,1)S(1)}, bf16[384,768]{1,0:T(8,128)(2,1)S(1)}, u32[]{:S(2)}, u32[]{:S(2)}) collective-permute-start(bf16[384,768]{1,0:T(8,128)(2,1)S(1)} %convolution_convert_fusion.8), channel_id=1, source_target_pairs={{0,16},{16,0},{1,17},{17,1},{2,18},{18,2},{3,19},{19,3},{4,20},{20... | collective-permute-start | bytes 1769480 | tf_op jit(solution)/shard_map/ppermute | solution.py:34
  730.1 16.7 %collective-permute-start.16 = (bf16[384,768]{1,0:T(8,128)(2,1)S(1)}, bf16[384,768]{1,0:T(8,128)(2,1)S(1)}, u32[]{:S(2)}, u32[]{:S(2)}) collective-permute-start(bf16[384,768]{1,0:T(8,128)(2,1)S(1)} %convolution_convert_fusion.9), channel_id=1, source_target_pairs={{0,8},{8,0},{1,9},{9,1},{2,10},{10,2},{3,11},{11,3},{4,12},{12,4},... | collective-permute-start | bytes 1769480 | tf_op jit(solution)/shard_map/ppermute | solution.py:34
  743.6 10.0 collective-permute-start.19
  746.8 119.4 %collective-permute-start.24 = (bf16[384,2304]{1,0:T(8,128)(2,1)}, bf16[384,2304]{1,0:T(8,128)(2,1)}, u32[]{:S(2)}, u32[]{:S(2)}) collective-permute-start(bf16[384,2304]{1,0:T(8,128)(2,1)} %convolution_convert_fusion.1), channel_id=1, source_target_pairs={{0,8},{8,0},{1,9},{9,1},{2,10},{10,2},{3,11},{11,3},{4,12},{12,4},... | collective-permute-start | bytes 5308424 | tf_op jit(solution)/shard_map/ppermute | solution.py:34
  753.6 11.6 collective-permute-start.9
  756.0 16.4 %collective-permute-start.17 = (bf16[192,768]{1,0:T(8,128)(2,1)}, bf16[192,768]{1,0:T(8,128)(2,1)}, u32[]{:S(2)}, u32[]{:S(2)}) collective-permute-start(bf16[192,768]{1,0:T(8,128)(2,1)} %fusion.127), channel_id=1, source_target_pairs={{0,16},{16,0},{1,17},{17,1},{2,18},{18,2},{3,19},{19,3},{4,20},{20... | collective-permute-start | bytes 884744 | tf_op jit(solution)/shard_map/ppermute | solution.py:34
  768.6 17.9 %collective-permute-start.12 = (bf16[384,896]{1,0:T(8,128)(2,1)}, bf16[384,896]{1,0:T(8,128)(2,1)}, u32[]{:S(2)}, u32[]{:S(2)}) collective-permute-start(bf16[384,896]{1,0:T(8,128)(2,1)} %convolution_convert_fusion.6), channel_id=1, source_target_pairs={{0,16},{16,0},{1,17},{17,1},{2,18},{18,2},{3,19},{19,3},{4,20},{20... | collective-permute-start | bytes 2064392 | tf_op jit(solution)/shard_map/ppermute | solution.py:34
  772.4 34.0 %collective-permute-start.10 = (bf16[384,896]{1,0:T(8,128)(2,1)}, bf16[384,896]{1,0:T(8,128)(2,1)}, u32[]{:S(2)}, u32[]{:S(2)}) collective-permute-start(bf16[384,896]{1,0:T(8,128)(2,1)} %convolution_convert_fusion.7), channel_id=1, source_target_pairs={{0,8},{8,0},{1,9},{9,1},{2,10},{10,2},{3,11},{11,3},{4,12},{12,4},... | collective-permute-start | bytes 2064392 | tf_op jit(solution)/shard_map/ppermute | solution.py:34
  776.9 178.9 %reduce-scatter.6.cloned.1.call-start = ((), (), s32[]{:S(2)}) async-start(), calls=%async_computation.5 | async-start | bytes 860160 | tf_op jit(solution)/shard_map/reduce_scatter | solution.py:419
  786.5 52.3 %collective-permute-start.23 = (bf16[192,2304]{1,0:T(8,128)(2,1)}, bf16[192,2304]{1,0:T(8,128)(2,1)}, u32[]{:S(2)}, u32[]{:S(2)}) collective-permute-start(bf16[192,2304]{1,0:T(8,128)(2,1)} %fusion.81), channel_id=1, source_target_pairs={{0,8},{8,0},{1,9},{9,1},{2,10},{10,2},{3,11},{11,3},{4,12},{12,4},... | collective-permute-start | bytes 2654216 | tf_op jit(solution)/shard_map/ppermute | solution.py:34
  786.8 23.7 %copy-start.138 = (bf16[1024,1152]{1,0:T(8,128)(2,1)S(1)}, bf16[1024,1152]{1,0:T(8,128)(2,1)}, u32[]{:S(2)}) copy-start(bf16[1024,1152]{1,0:T(8,128)(2,1)} %get-tuple-element.67) | copy-start | bytes 7077892
  789.0 21.5 %copy-start.79 = (bf16[1,1,1,4,48,1024]{5,4,0,2,1,3:T(8,128)(2,1)S(1)}, bf16[1,1,1,4,48,1024]{5,4,0,2,1,3:T(8,128)(2,1)}, u32[]{:S(2)}) copy-start(bf16[1,1,1,4,48,1024]{5,4,0,2,1,3:T(8,128)(2,1)} %get-tuple-element.116) | copy-start | bytes 1179652
  789.0 21.5 %copy-start.132 = (bf16[1024,1152]{1,0:T(8,128)(2,1)S(1)}, bf16[1024,1152]{1,0:T(8,128)(2,1)}, u32[]{:S(2)}) copy-start(bf16[1024,1152]{1,0:T(8,128)(2,1)} %get-tuple-element.66) | copy-start | bytes 7077892
  806.4 25.0 %collective-permute-start.13 = (bf16[192,896]{1,0:T(8,128)(2,1)S(1)}, bf16[192,896]{1,0:T(8,128)(2,1)S(1)}, u32[]{:S(2)}, u32[]{:S(2)}) collective-permute-start(bf16[192,896]{1,0:T(8,128)(2,1)S(1)} %fusion.126), channel_id=1, source_target_pairs={{0,8},{8,0},{1,9},{9,1},{2,10},{10,2},{3,11},{11,3},{4,12},{12,4},... | collective-permute-start | bytes 1032200 | tf_op jit(solution)/shard_map/ppermute | solution.py:34
  810.2 25.0 %collective-permute-start.11 = (bf16[192,896]{1,0:T(8,128)(2,1)S(1)}, bf16[192,896]{1,0:T(8,128)(2,1)S(1)}, u32[]{:S(2)}, u32[]{:S(2)}) collective-permute-start(bf16[192,896]{1,0:T(8,128)(2,1)S(1)} %fusion.124), channel_id=1, source_target_pairs={{0,16},{16,0},{1,17},{17,1},{2,18},{18,2},{3,19},{19,3},{4,20},{20... | collective-permute-start | bytes 1032200 | tf_op jit(solution)/shard_map/ppermute | solution.py:34
  831.3 64.3 %collective-permute-start.28 = (bf16[576,1536]{1,0:T(8,128)(2,1)}, bf16[576,1536]{1,0:T(8,128)(2,1)}, u32[]{:S(2)}, u32[]{:S(2)}) collective-permute-start(bf16[576,1536]{1,0:T(8,128)(2,1)} %convolution_convert_fusion.5), channel_id=1, source_target_pairs={{0,8},{8,0},{1,9},{9,1},{2,10},{10,2},{3,11},{11,3},{4,12},{12,4},... | collective-permute-start | bytes 5308424 | tf_op jit(solution)/shard_map/ppermute | solution.py:34
  835.1 20.5 %collective-permute-start.21 = (bf16[192,2304]{1,0:T(8,128)(2,1)}, bf16[192,2304]{1,0:T(8,128)(2,1)}, u32[]{:S(2)}, u32[]{:S(2)}) collective-permute-start(bf16[192,2304]{1,0:T(8,128)(2,1)} %fusion.84), channel_id=1, source_target_pairs={{0,16},{16,0},{1,17},{17,1},{2,18},{18,2},{3,19},{19,3},{4,20},{20... | collective-permute-start | bytes 2654216 | tf_op jit(solution)/shard_map/ppermute | solution.py:34
  838.7 117.9 %reduce-scatter.10.cloned.1.call-start = ((), (), s32[]{:S(2)}) async-start(), calls=%async_computation.9 | async-start | bytes 2211840 | tf_op jit(solution)/shard_map/reduce_scatter | solution.py:419
  858.9 98.5 %reduce-scatter.12.cloned.1.call-start = ((), (), s32[]{:S(2)}) async-start(), calls=%async_computation.11 | async-start | bytes 2211840 | tf_op jit(solution)/shard_map/reduce_scatter | solution.py:419
  865.6 24.3 %collective-permute-start.27 = (bf16[192,2304]{1,0:T(8,128)(2,1)S(1)}, bf16[192,2304]{1,0:T(8,128)(2,1)S(1)}, u32[]{:S(2)}, u32[]{:S(2)}) collective-permute-start(bf16[192,2304]{1,0:T(8,128)(2,1)S(1)} %fusion.75), channel_id=1, source_target_pairs={{0,8},{8,0},{1,9},{9,1},{2,10},{10,2},{3,11},{11,3},{4,12},{12,4},... | collective-permute-start | bytes 2654216 | tf_op jit(solution)/shard_map/ppermute | solution.py:34
  868.9 22.7 %collective-permute-start.25 = (bf16[192,2304]{1,0:T(8,128)(2,1)S(1)}, bf16[192,2304]{1,0:T(8,128)(2,1)S(1)}, u32[]{:S(2)}, u32[]{:S(2)}) collective-permute-start(bf16[192,2304]{1,0:T(8,128)(2,1)S(1)} %fusion.78), channel_id=1, source_target_pairs={{0,16},{16,0},{1,17},{17,1},{2,18},{18,2},{3,19},{19,3},{4,20},{20... | collective-permute-start | bytes 2654216 | tf_op jit(solution)/shard_map/ppermute | solution.py:34
  870.4 19.4 %copy-start.48 = (f32[192,2304]{1,0:T(8,128)S(1)}, f32[192,2304]{1,0:T(8,128)}, u32[]{:S(2)}) copy-start(f32[192,2304]{1,0:T(8,128)} %fusion.238) | copy-start | bytes 5308420
  875.2 54.5 %collective-permute-start.30 = (bf16[576,1536]{1,0:T(8,128)(2,1)}, bf16[576,1536]{1,0:T(8,128)(2,1)}, u32[]{:S(2)}, u32[]{:S(2)}) collective-permute-start(bf16[576,1536]{1,0:T(8,128)(2,1)} %convolution_convert_fusion.4), channel_id=1, source_target_pairs={{0,16},{16,0},{1,17},{17,1},{2,18},{18,2},{3,19},{19,3},{4,20},{20... | collective-permute-start | bytes 5308424 | tf_op jit(solution)/shard_map/ppermute | solution.py:34
  894.6 105.6 %reduce-scatter.14.cloned.1.call-start = ((), (), s32[]{:S(2)}) async-start(), calls=%async_computation.13 | async-start | bytes 2211840 | tf_op jit(solution)/shard_map/reduce_scatter | solution.py:419
  895.6 34.0 %copy-start.58 = (bf16[1,512,1536]{2,1,0:T(8,128)(2,1)S(1)}, bf16[1,512,1536]{2,1,0:T(8,128)(2,1)}, u32[]{:S(2)}) copy-start(bf16[1,512,1536]{2,1,0:T(8,128)(2,1)} %param.16) | copy-start | bytes 4718596
  899.0 46.1 %collective-permute-start.29 = (bf16[288,1536]{1,0:T(8,128)(2,1)S(1)}, bf16[288,1536]{1,0:T(8,128)(2,1)S(1)}, u32[]{:S(2)}, u32[]{:S(2)}) collective-permute-start(bf16[288,1536]{1,0:T(8,128)(2,1)S(1)} %fusion.66), channel_id=1, source_target_pairs={{0,16},{16,0},{1,17},{17,1},{2,18},{18,2},{3,19},{19,3},{4,20},{20... | collective-permute-start | bytes 2654216 | tf_op jit(solution)/shard_map/ppermute | solution.py:34
  932.4 15.5 %collective-permute-start.31 = (bf16[288,1536]{1,0:T(8,128)(2,1)S(1)}, bf16[288,1536]{1,0:T(8,128)(2,1)S(1)}, u32[]{:S(2)}, u32[]{:S(2)}) collective-permute-start(bf16[288,1536]{1,0:T(8,128)(2,1)S(1)} %fusion.67), channel_id=1, source_target_pairs={{0,8},{8,0},{1,9},{9,1},{2,10},{10,2},{3,11},{11,3},{4,12},{12,4},... | collective-permute-start | bytes 2654216 | tf_op jit(solution)/shard_map/ppermute | solution.py:34
  950.8 2.5 collective-permute-start.32
  953.8 47.2 %copy-start.108 = (f32[2]{0:T(128)S(1)}, f32[2]{0:T(128)}, u32[]{:S(2)}) copy-start(f32[2]{0:T(128)} %refs_1_.7) | copy-start | bytes 28
  953.8 47.8 %copy-start.98 = (f32[1536]{0:T(1024)S(1)}, f32[1536]{0:T(1024)}, u32[]{:S(2)}) copy-start(f32[1536]{0:T(1024)} %get-tuple-element.51) | copy-start | bytes 18436
  953.8 47.8 %copy-start.113 = (f32[1536]{0:T(1024)S(1)}, f32[1536]{0:T(1024)}, u32[]{:S(2)}) copy-start(f32[1536]{0:T(1024)} %get-tuple-element.53) | copy-start | bytes 18436
  953.8 87.4 %copy-start.110 = (f32[2,384]{1,0:T(2,128)S(1)}, f32[2,384]{1,0:T(2,128)}, u32[]{:S(2)}) copy-start(f32[2,384]{1,0:T(2,128)} %param.22) | copy-start | bytes 9220
  953.8 87.4 %copy-start.114 = (f32[2,2,384]{2,1,0:T(2,128)S(1)}, f32[2,2,384]{2,1,0:T(2,128)}, u32[]{:S(2)}) copy-start(f32[2,2,384]{2,1,0:T(2,128)} %param.27) | copy-start | bytes 18436
  953.8 89.8 %copy-start.104 = (f32[512]{0:T(512)S(1)}, f32[512]{0:T(512)}, u32[]{:S(2)}) copy-start(f32[512]{0:T(512)} %copy-done.103) | copy-start | bytes 6148
  953.9 89.8 %copy-start.17 = (bf16[1,512,1536]{2,1,0:T(8,128)(2,1)S(1)}, bf16[1,512,1536]{2,1,0:T(8,128)(2,1)}, u32[]{:S(2)}) copy-start(bf16[1,512,1536]{2,1,0:T(8,128)(2,1)} %param.15) | copy-start | bytes 4718596
  955.2 93.5 %all-gather.8.cloned.1.call-start = ((), (), s32[]{:S(2)}) async-start(), calls=%async_computation.8 | async-start | bytes 1327104 | tf_op jit(solution)/shard_map/all_gather | solution.py:420
  955.8 102.5 %all-gather.6.cloned.1.call-start = ((), (), s32[]{:S(2)}) async-start(), calls=%async_computation.6 | async-start | bytes 1548288 | tf_op jit(solution)/shard_map/all_gather | solution.py:420
  956.5 131.7 %all-gather.10.cloned.1.call-start = ((), (), s32[]{:S(2)}) async-start(), calls=%async_computation.10 | async-start | bytes 3981312 | tf_op jit(solution)/shard_map/all_gather | solution.py:420
  957.3 166.8 %all-gather.12.cloned.1.call-start = ((), (), s32[]{:S(2)}) async-start(), calls=%async_computation.12 | async-start | bytes 3981312 | tf_op jit(solution)/shard_map/all_gather | solution.py:420
  958.0 215.3 %all-gather.14.cloned.1.call-start = ((), (), s32[]{:S(2)}) async-start(), calls=%async_computation.14 | async-start | bytes 3981312 | tf_op jit(solution)/shard_map/all_gather | solution.py:420
  (137 other events, 747.9 us)
Sparse Core Ops, SparseCore 0:
  777.0 28.0 reduce-scatter.7
  838.8 29.7 reduce-scatter.5
  871.6 37.2 reduce-scatter.9
  911.7 37.4 reduce-scatter.11
  955.3 44.8 reduce-scatter.13
  1002.0 23.2 all-gather.7
  1027.1 25.1 all-gather.5
  1054.2 33.9 all-gather.9
  1090.1 33.9 all-gather.11
  1125.9 33.9 all-gather.13

commit v2 on v1

--- a/solution.py
+++ b/solution.py
@@ -16,12 +16,13 @@
 adam_eps = 1e-08
 beta_first = 0.9
 beta_second = 0.95
-head_group = 4
 BF = jnp.bfloat16
 F32 = jnp.float32
 MESH_ID = pl.DeviceIdType.MESH
 VMEM_BYTES = 56 * 1024 * 1024
 ANY = pl.BlockSpec(memory_space=pl.ANY)
+VM = pl.BlockSpec(memory_space=pltpu.VMEM)
+LOG2E = 1.4426950408889634
 
 
 def passed_along(block, axis, distance):
@@ -56,10 +57,6 @@
 
 def root_norm(values, gain):
     return values * lax.rsqrt(jnp.mean(values * values, axis=-1, keepdims=True) + norm_eps) * gain
-
-
-def gated_unit(gate_part, up_part):
-    return jax.nn.gelu(gate_part, approximate=True) * up_part
 
 
 def adamw_step(weight, moments, grad, step_value, optimizer_rates):
@@ -295,70 +292,470 @@
     )(*own)
 
 
-def adam_kernel(total, parts, scal_ref, rates_ref, *refs):
-    grads = refs[:parts]
-    w_ref, m_ref, g_out, w_out, m_out = refs[parts:]
-    step_value = scal_ref[0].astype(F32)
+def nt(a, b):
+    return lax.dot_general(a, b, (((1,), (1,)), ((), ())), preferred_element_type=F32)
+
+def nn(a, b):
+    return lax.dot_general(a, b, (((1,), (0,)), ((), ())), preferred_element_type=F32)
+
+def fill_bias(bias, q_ids, k_ids, first, rows, span):
+    key = lax.broadcasted_iota(jnp.int32, (span, rows), 0)
+    query = lax.broadcasted_iota(jnp.int32, (span, rows), 1)
+    distance = query + WINDOW - key
+    same = k_ids[pl.ds(first, span), :1] == q_ids[:1, pl.ds(first, rows)]
+    allowed = (distance >= 0) & (distance < WINDOW) & same
+    bias[...] = jnp.where(allowed, 0.0, -1e30)
+
+def fwd_kernel(heads, rows, q_ids, k_ids, q_ref, k_ref, v_ref, o_ref, l_ref, bias, vt):
+    piece = q_ref.shape[0]
+    span = WINDOW + rows
+    vt[...] = v_ref[...].T
+    factor = HEAD ** -0.5 * LOG2E
+    for block in range(piece // rows):
+        first = block * rows
+        fill_bias(bias, q_ids, k_ids, first, rows, span)
+        live = q_ids[:1, pl.ds(first, rows)] != 0
+        @pl.loop(0, heads)
+        def _(h):
+            cols = pl.ds(pl.multiple_of(h * HEAD, HEAD), HEAD)
+            q = q_ref[pl.ds(first, rows), cols]
+            s = nt(k_ref[pl.ds(first, span), :], q) * factor + bias[...]
+            top = jnp.max(s, axis=0, keepdims=True)
+            p = jnp.exp2(s - top)
+            total = jnp.sum(p, axis=0, keepdims=True)
+            o = nn(vt[:, pl.ds(first, span)], p.astype(BF))
+            o = jnp.where(live, o * (1.0 / total), 0.0)
+            o_ref[pl.ds(first, rows), cols] = o.T.astype(BF)
+            l_ref[h, :, pl.ds(first, rows)] = top + jnp.log2(total)
+
+def bwd_kernel(heads, rows, q_ids, k_ids, q_ref, k_ref, v_ref, o_ref, do_ref, l_ref, dq_ref, dk_ref, dv_ref, bias, kt):
+    piece = q_ref.shape[0]
+    span = WINDOW + rows
+    kt[...] = k_ref[...].T
+    factor = HEAD ** -0.5 * LOG2E
+    dk_ref[...] = jnp.zeros_like(dk_ref)
+    dv_ref[...] = jnp.zeros_like(dv_ref)
+    for block in range(piece // rows):
+        first = block * rows
+        fill_bias(bias, q_ids, k_ids, first, rows, span)
+        @pl.loop(0, heads, unroll=2)
+        def _(h):
+            cols = pl.ds(pl.multiple_of(h * HEAD, HEAD), HEAD)
+            q = q_ref[pl.ds(first, rows), cols]
+            do = do_ref[pl.ds(first, rows), cols]
+            o = o_ref[pl.ds(first, rows), cols]
+            delta = jnp.sum((do.astype(F32) * o.astype(F32)).T, axis=0, keepdims=True)
+            s = nt(k_ref[pl.ds(first, span), :], q) * factor + bias[...]
+            p = jnp.exp2(s - l_ref[h, :, pl.ds(first, rows)])
+            dp = nt(v_ref[pl.ds(first, span), :], do)
+            ds = (p * ((dp - delta) * HEAD ** -0.5)).astype(BF)
+            dv_ref[pl.ds(first, span), :] += nn(p.astype(BF), do)
+            dk_ref[pl.ds(first, span), :] += nn(ds, q)
+            dq_ref[pl.ds(first, rows), cols] = nn(kt[:, pl.ds(first, span)], ds).T
+
+
+def attend(q_ids, k_ids, q, k, v, heads, rows):
+    def body(*refs):
+        fwd_kernel(heads, rows, *refs)
+
+    return pl.pallas_call(
+        body,
+        out_shape=(
+            jax.ShapeDtypeStruct(q.shape, BF),
+            jax.ShapeDtypeStruct((heads, 1, q.shape[0]), F32),
+        ),
+        in_specs=[VM] * 5,
+        out_specs=(VM, VM),
+        scratch_shapes=[
+            pltpu.VMEM((WINDOW + rows, rows), F32),
+            pltpu.VMEM((HEAD, k.shape[0]), BF),
+        ],
+        compiler_params=pltpu.CompilerParams(vmem_limit_bytes=VMEM_BYTES),
+        cost_estimate=pl.CostEstimate(
+            flops=4 * q.size * k.shape[0], bytes_accessed=4 * q.size, transcendentals=q.size * 12
+        ),
+    )(q_ids, k_ids, q, k, v)
+
+
+def attend_back(q_ids, k_ids, q, k, v, o, do, l, heads, rows):
+    def body(*refs):
+        bwd_kernel(heads, rows, *refs)
+
+    return pl.pallas_call(
+        body,
+        out_shape=(
+            jax.ShapeDtypeStruct(q.shape, F32),
+            jax.ShapeDtypeStruct(k.shape, F32),
+            jax.ShapeDtypeStruct(k.shape, F32),
+        ),
+        in_specs=[VM] * 8,
+        out_specs=(VM, VM, VM),
+        scratch_shapes=[
+            pltpu.VMEM((WINDOW + rows, rows), F32),
+            pltpu.VMEM((HEAD, k.shape[0]), BF),
+        ],
+        compiler_params=pltpu.CompilerParams(vmem_limit_bytes=VMEM_BYTES),
+        cost_estimate=pl.CostEstimate(
+            flops=10 * q.size * k.shape[0], bytes_accessed=12 * q.size, transcendentals=q.size * 12
+        ),
+    )(q_ids, k_ids, q, k, v, o, do, l)
+
+
+def mlp_kernel(where, two_ref, df_ref, gate_ref, up_ref, down_ref, two_t, hid_t, grads, out, back):
+    step = pl.program_id(0)
+    tile = gate_ref.shape[1]
+    half = down_ref.shape[2]
+    rows = 256
+
+    @pl.when(step == 0)
+    def _():
+        out[...] = jnp.zeros_like(out)
+        back[...] = jnp.zeros_like(back)
+
+    part = two_t.shape[0]
+    two_t[...] = two_ref[:, pl.ds(pl.multiple_of(step * part, part), part)].T
+
+    @pl.loop(0, two_ref.shape[0] // rows)
+    def _(i):
+        at = pl.ds(pl.multiple_of(i * rows, rows), rows)
+        two = two_ref[at, :]
+        gate = nn(two, gate_ref[...])
+        up = nn(two, up_ref[...])
+        grad = nt(df_ref[at, :half], down_ref[0]) + nt(df_ref[at, half:], down_ref[1])
+        slope = 0.7978845608028654
+        bent = jnp.tanh(slope * (gate + 0.044715 * (gate * gate * gate)))
+        upper = 0.5 * (1.0 + bent)
+        act = gate * upper
+        act_slope = upper + 0.5 * gate * (1.0 - bent * bent) * (
+            slope * (1.0 + 3 * 0.044715 * (gate * gate))
+        )
+        hid = (act * up).astype(BF)
+        grad_gate = (grad * up * act_slope).astype(BF)
+        grad_up = (grad * act).astype(BF)
+        hid_t[:, at] = hid.T
+        grads[0, at, :] = grad_gate
+        grads[1, at, :] = grad_up
+        out[at, :half] += nn(hid, down_ref[0])
+        out[at, half:] += nn(hid, down_ref[1])
+        back[at, :] += nt(grad_gate, gate_ref[...]) + nt(grad_up, up_ref[...])
+
+
+def mlp_call(core, two, df, gate_full, down_full):
+    T, D = two.shape
+    half_ff = gate_full.shape[1] // 2
+    tile = 384
+    tiles = half_ff // tile
+    half = down_full.shape[2]
+    part = D // tiles
+
+    def body(where, *refs):
+        mlp_kernel(where, *refs)
+
+    whole = pl.BlockSpec((T, D), lambda i, w: (0, 0))
+    return pl.pallas_call(
+        body,
+        grid_spec=pltpu.PrefetchScalarGridSpec(
+            num_scalar_prefetch=1,
+            grid=(tiles,),
+            in_specs=[
+                whole,
+                whole,
+                pl.BlockSpec((D, tile), lambda i, w: (0, i)),
+                pl.BlockSpec((D, tile), lambda i, w: (0, tiles + i)),
+                pl.BlockSpec((2, tile, half), lambda i, w: (0, w[0] * tiles + i, 0)),
+            ],
+            out_specs=[
+                pl.BlockSpec((part, T), lambda i, w: (i, 0)),
+                pl.BlockSpec((tile, T), lambda i, w: (i, 0)),
+                pl.BlockSpec((2, T, tile), lambda i, w: (0, 0, i)),
+                whole,
+                whole,
+            ],
+        ),
+        out_shape=[
+            jax.ShapeDtypeStruct((D, T), BF),
+            jax.ShapeDtypeStruct((half_ff, T), BF),
+            jax.ShapeDtypeStruct((2, T, half_ff), BF),
+            jax.ShapeDtypeStruct((T, D), F32),
+            jax.ShapeDtypeStruct((T, D), F32),
+        ],
+        compiler_params=pltpu.CompilerParams(
+            dimension_semantics=("arbitrary",), vmem_limit_bytes=VMEM_BYTES
+        ),
+        cost_estimate=pl.CostEstimate(
+            flops=12 * T * D * half_ff, bytes_accessed=40 * 2**20, transcendentals=T * half_ff
+        ),
+    )(core, two, df, gate_full, gate_full, down_full)
+
+
+def reduce_kernel(sides, parts, S, two, hid_own, hid_other, grads, df, out, *scratch):
+    left, right, s1, g1, s2, g2, fz, gz, mine, *sems = scratch
+    lds, rds, s1s, s1r, s2s, s2r, zs, zr, ls, xs, xr, ys, yr, cs, cr = sems
+    groups, _, _, r, T = left.shape
+    n = right.shape[2]
+    wide = sides * parts
+    nc = wide + groups - 1
+    y, x, c, z = (lax.axis_index(a) for a in ("y", "x", "c", "z"))
+    k = y * 2 + x
+    kx = y * 2 + 1 - x
+    ky = (1 - y) * 2 + x
+    kxy = 3 - k
+    to_x = {"x": 1 - x}
+    to_y = {"y": 1 - y}
+    to_c = {"c": 1 - c}
+    loads = {}
+
+    def fetch(key, src, dst, sem):
+        copy = pltpu.make_async_copy(src, dst, sem)
+        copy.start()
+        loads.setdefault(key, []).append(copy)
+
+    def fetch_left(g):
+        for p in range(8):
+            h, kk = p // 4, p % 4
+            if g == 0:
+                fetch(("l", 0), two.at[:, kk, h], left.at[0, p], lds.at[0, p, 0])
+            else:
+                for i, (src, cc) in enumerate(((hid_own, c), (hid_other, 1 - c))):
+                    dst = left.at[g, p, pl.ds(cc * (S // 2), S // 2)]
+                    fetch(("l", g), src.at[:, g - 1, kk, h], dst, lds.at[g, p, i])
+
+    def slot_of(t):
+        return t % 4 if t < wide else 4
+
+    def fetch_right(t):
+        if t < wide:
+            src = grads.at[t // parts, :, pl.ds((t % parts) * n, n)]
+            fetch(("r", t), src, right.at[t % 4], rds.at[t])
+        elif t == wide:
+            fetch(("r", t), df, right.at[4], rds.at[t])
+
+    def landed(key):
+        for copy in loads.pop(key, []):
+            copy.wait()
+
+    fetch_right(0)
+    fetch_left(0)
+    fetch_right(1)
+    barrier = pltpu.get_barrier_semaphore()
+    peers = [to_x, to_y, to_c] + [{"z": lax.rem(z + e, S)} for e in range(1, S)]
+    for target in peers:
+        pl.semaphore_signal(barrier, inc=1, device_id=target, device_id_type=MESH_ID)
+    pl.semaphore_wait(barrier, len(peers))
+    for g in range(1, groups):
+        fetch_left(g)
+
+    def remote(src, dst, s, r_, target):
+        return pltpu.make_async_remote_copy(
+            src_ref=src, dst_ref=dst, send_sem=s, recv_sem=r_, device_id=target, device_id_type=MESH_ID
+        )
+
+    def product(t, p):
+        g = max(0, t - wide + 1)
+        return nn(left[g, p].reshape(S * r, T), right[slot_of(t)])
+
+    pending = {}
+
+    def launch(key, copy):
+        copy.start()
+        pending.setdefault(key, []).append(copy)
+
+    def drain(key):
+        for copy in pending.pop(key, []):
+            copy.wait_send()
+
+    def first(t):
+        slot = t % 2
+        landed(("l", max(0, t - wide + 1)))
+        landed(("r", t))
+        drain(("s1", t - 2))
+
+        for i in range(2):
+            for j, p, target in ((i, i * 2 + 1 - x, to_x), (2 + i, 4 + (1 - y) * 2 + i, to_y)):
+                s1[slot, j] = product(t, p).astype(BF)
+                launch(("s1", t), remote(s1.at[slot, j], g1.at[t, j], s1s.at[t, j], s1r.at[t, j], target))
+
+    def got1(t, j):
+        remote(g1.at[t, j], g1.at[t, j], s1s.at[t, j], s1r.at[t, j], to_x).wait_recv()
+
+    def second(t):
+        slot = t % 2
+        drain(("s2", t - 2))
+        for j in range(4):
+            got1(t, j)
+        for h, p, j, target in ((0, (1 - y) * 2 + x, 1 - y, to_y), (1, 4 + y * 2 + 1 - x, 3 - x, to_x)):
+            s2[slot, h] = (product(t, p) + g1[t, j].astype(F32)).astype(BF)
+            launch(("s2", t), remote(s2.at[slot, h], g2.at[t, h], s2s.at[t, h], s2r.at[t, h], target))
+
+    def third(t):
+        slot = t % 2
+        drain(("z", t - 2))
+        for h, p, j in ((0, k, y), (1, 4 + k, 2 + x)):
+            remote(g2.at[t, h], g2.at[t, h], s2s.at[t, h], s2r.at[t, h], to_x).wait_recv()
+            total = (product(t, p) + g1[t, j].astype(F32) + g2[t, h].astype(F32)).astype(BF)
+            for zz in range(S):
+                fz[slot, zz, h] = total[zz * r : (zz + 1) * r]
+        for e in range(1, S):
+            zz = lax.rem(z + e, S)
+            launch(("z", t), remote(fz.at[slot, zz], gz.at[t, S - e - 1], zs.at[t, e - 1], zr.at[t, S - e - 1], {"z": zz}))
+
+    def fourth(t):
+        slot = t % 2
+        drain(("ag", t - 2))
+        for copy in pending.pop(("l", t - 2), []):
+            copy.wait()
+        for e in range(S - 1):
+            remote(gz.at[t, e], gz.at[t, e], zs.at[t, e], zr.at[t, e], to_x).wait_recv()
+        for h in range(2):
+            total = fz[slot, z, h].astype(F32)
+            for e in range(S - 1):
+                total = total + gz[t, e, h].astype(F32)
+            mine[slot, h] = total.astype(BF)
+        copy = pltpu.make_async_copy(mine.at[slot], out.at[t, k, c], ls.at[t])
+        copy.start()
+        pending[("l", t)] = [copy]
+        for h, s, r_, target in ((0, xs, xr, to_x), (1, ys, yr, to_y)):
+            launch(("ag", t), remote(mine.at[slot, h], out.at[t, k, c, h], s.at[t, 0], r_.at[t, 0], target))
+        for h, s, r_, target in ((0, ys, yr, to_y), (1, xs, xr, to_x)):
+            launch(("ag", t), remote(mine.at[slot, h], out.at[t, k, c, h], s.at[t, 1], r_.at[t, 1], target))
+
+    def land(t, kk, h, s, r_, j, target):
+        p = out.at[t, kk, c, h]
+        remote(p, p, s.at[t, j], r_.at[t, j], target).wait_recv()
+        return p
+
+    def fifth(t):
+        p = land(t, kx, 0, xs, xr, 0, to_x)
+        launch("end", remote(p, p, ys.at[t, 2], yr.at[t, 2], to_y))
+        p = land(t, ky, 1, ys, yr, 0, to_y)
+        launch("end", remote(p, p, xs.at[t, 2], xr.at[t, 2], to_x))
+
+    def sixth(t):
+        land(t, kx, 1, xs, xr, 1, to_x)
+        land(t, ky, 0, ys, yr, 1, to_y)
+        land(t, kxy, 1, xs, xr, 2, to_x)
+        land(t, kxy, 0, ys, yr, 2, to_y)
+        for copy in pending.pop(("l", t), []):
+            copy.wait()
+        p = out.at[t, :, c]
+        launch("end", remote(p, p, cs.at[t], cr.at[t], to_c))
+
+    stages = (first, second, third, fourth, fifth, sixth)
+    for t in range(nc + len(stages) - 1):
+        for lag, stage in enumerate(stages):
+            if 0 <= t - lag < nc:
+                stage(t - lag)
+        fetch_right(t + 2)
+    for t in range(nc):
+        p = out.at[t, :, 1 - c]
+        remote(p, p, cs.at[t], cr.at[t], to_c).wait_recv()
+    for key in list(pending):
+        drain(key) if key[0] != "l" else [copy.wait() for copy in pending.pop(key)]
+
+
+def reduced(two_t, hid_own, hid_other, grads, df, S, cid):
+    D, T = two_t.shape
+    sides, _, half_ff = grads.shape
+    n = df.shape[1]
+    r = D // (S * 8)
+    parts = half_ff // n
+    groups = 1 + 2 * half_ff // (S * 8 * r)
+    nc = sides * parts + groups - 1
+    m = S * r
+    dma = pltpu.SemaphoreType.DMA
+    hid_shape = (S // 2, groups - 1, 4, 2, r, T)
+
+    def body(*refs):
+        reduce_kernel(sides, parts, S, *refs)
+
+    return pl.pallas_call(
+        body,
+        out_shape=jax.ShapeDtypeStruct((nc, 4, 2, 2, r, n), BF),
+        in_specs=[ANY] * 5,
+        out_specs=ANY,
+        scratch_shapes=[
+            pltpu.VMEM((groups, 8, S, r, T), BF),
+            pltpu.VMEM((5, T, n), BF),
+            pltpu.VMEM((2, 4, m, n), BF),
+            pltpu.VMEM((nc, 4, m, n), BF),
+            pltpu.VMEM((2, 2, m, n), BF),
+            pltpu.VMEM((nc, 2, m, n), BF),
+            pltpu.VMEM((2, S, 2, r, n), BF),
+            pltpu.VMEM((nc, S - 1, 2, r, n), BF),
+            pltpu.VMEM((2, 2, r, n), BF),
+            dma((groups, 8, 2)),
+            dma((nc,)),
+            dma((nc, 4)),
+            dma((nc, 4)),
+            dma((nc, 2)),
+            dma((nc, 2)),
+            dma((nc, S)),
+            dma((nc, S)),
+            dma((nc,)),
+            dma((nc, 3)),
+            dma((nc, 3)),
+            dma((nc, 3)),
+            dma((nc, 3)),
+            dma((nc,)),
+            dma((nc,)),
+        ],
+        compiler_params=pltpu.CompilerParams(
+            collective_id=cid, has_side_effects=True, vmem_limit_bytes=VMEM_BYTES
+        ),
+        cost_estimate=pl.CostEstimate(
+            flops=4 * T * D * 3 * half_ff, bytes_accessed=400 * 2**20, transcendentals=0
+        ),
+    )(
+        two_t.reshape(S, 4, 2, r, T),
+        hid_own.reshape(hid_shape),
+        hid_other.reshape(hid_shape),
+        grads,
+        df,
+    )
+
+
+def adam_kernel(total, count_ref, rates_ref, g_ref, w_ref, m_ref, g_out, w_out, m_out):
+    step_value = count_ref[0].astype(F32)
     log_first = jnp.log(jnp.full((8, 128), beta_first, F32))
     log_second = jnp.log(jnp.full((8, 128), beta_second, F32))
     fix_first = (1.0 - jnp.exp(step_value * log_first))[:1, :1]
     fix_second = (1.0 - jnp.exp(step_value * log_second))[:1, :1]
-
-    def update(g_ref):
-        grad = g_ref[0, 0].astype(F32) / total
-        w = w_ref[...]
-        first = beta_first * m_ref[0] + (1.0 - beta_first) * grad
-        second = beta_second * m_ref[1] + (1.0 - beta_second) * grad * grad
-        step = first / fix_first / (jnp.sqrt(second / fix_second) + adam_eps) + rates_ref[1] * w
-        g_out[...] = grad
-        w_out[...] = w - rates_ref[0] * step
-        m_out[0] = first
-        m_out[1] = second
-
-    if parts == 1:
-        update(grads[0])
-    else:
-        for j in range(parts):
-
-            @pl.when(pl.program_id(0) == j)
-            def _(j=j):
-                update(grads[j])
-
-
-def adam_call(weight, moments, grads, count, rates, total, tile_rows, tile_cols, sides):
-    parts = len(grads)
-    K, _, rows, _ = grads[0].shape
-    tiles = rows // tile_rows
-
-    def g_spec(j):
-        def index(jj, kk, cc, ss, tt, *_):
-            on = jj == j
-            return (
-                jnp.where(on, kk, 0),
-                jnp.where(on, cc, 0),
-                jnp.where(on, tt, 0),
-                jnp.where(on, ss, 0),
-            )
-
-        return pl.BlockSpec((1, 1, tile_rows, tile_cols), index)
-
-    def place(jj, kk, cc, ss, tt, *_):
-        return (kk * tiles + tt, (ss * 2 + cc) * parts + jj)
-
-    def place3(jj, kk, cc, ss, tt, *_):
-        return (0,) + place(jj, kk, cc, ss, tt)
-
-    w_spec = pl.BlockSpec((tile_rows, tile_cols), place)
-    m_spec = pl.BlockSpec((2, tile_rows, tile_cols), place3)
+    grad = g_ref[0, 0, 0].reshape(w_ref.shape).astype(F32) / total
+    w = w_ref[...]
+    first = beta_first * m_ref[0] + (1.0 - beta_first) * grad
+    second = beta_second * m_ref[1] + (1.0 - beta_second) * grad * grad
+    step = first / fix_first / (jnp.sqrt(second / fix_second) + adam_eps) + rates_ref[1] * w
+    g_out[...] = grad
+    w_out[...] = w - rates_ref[0] * step
+    m_out[0] = first
+    m_out[1] = second
+
+
+def adam_call(weight, moments, grads, count, rates, total, base, sides, tiles, down):
+    _, _, _, _, r, n = grads.shape
+
+    def g_place(kk, cc, ss, tt):
+        return (base + ss * tiles + tt, kk, cc, 0, 0, 0)
+
+    def place(kk, cc, ss, tt):
+        if down:
+            return (tt * 4 + kk, cc)
+        return (kk, (ss * 2 + cc) * tiles + tt)
+
+    def m_place(*at):
+        return (0,) + place(*at)
+
+    w_spec = pl.BlockSpec((2 * r, n), place)
+    m_spec = pl.BlockSpec((2, 2 * r, n), m_place)
     smem = pl.BlockSpec(memory_space=pltpu.SMEM)
 
     def body(*refs):
-        adam_kernel(total, parts, *refs)
+        adam_kernel(total, *refs)
 
     return pl.pallas_call(
         body,
-        grid=(parts, K, 2, sides, tiles),
-        in_specs=[smem, smem] + [g_spec(j) for j in range(parts)] + [w_spec, m_spec],
+        grid=(4, 2, sides, tiles),
+        in_specs=[smem, smem, pl.BlockSpec((1, 1, 1, 2, r, n), g_place), w_spec, m_spec],
         out_specs=[w_spec, w_spec, m_spec],
         out_shape=[
             jax.ShapeDtypeStruct(weight.shape, F32),
@@ -366,12 +763,12 @@
             jax.ShapeDtypeStruct(moments.shape, F32),
         ],
         compiler_params=pltpu.CompilerParams(
-            dimension_semantics=("arbitrary",) * 5, vmem_limit_bytes=VMEM_BYTES
+            dimension_semantics=("arbitrary",) * 4, vmem_limit_bytes=VMEM_BYTES
         ),
         cost_estimate=pl.CostEstimate(
             flops=20 * weight.size, bytes_accessed=30 * weight.size, transcendentals=weight.size
         ),
-    )(count, rates, *grads, weight, moments)
+    )(count, rates, grads, weight, moments)
 
 
 def dot(a, b):
@@ -441,14 +838,15 @@
 ):
     seq_place = lax.axis_index("z")
     core = lax.axis_index("c")
+    first_core = core == 0
     D = block_in.shape[-1]
     half_ff = FF // 2
-    quarter_ff = FF // 4
     rows_d = input_proj.shape[0]
     rows_f = down_weight.shape[0]
     fast = Y == 2 and rows_d % 128 == 0
     in_half = input_proj.shape[1] // 2
     d_half = D // 2
+    r = rows_d // 8
 
     in_low = input_proj.astype(BF)
     out_low = output_proj.astype(BF)
@@ -458,21 +856,24 @@
         n = w.shape[1] // 2
         return jnp.stack([w[:, :n], w[:, n:]])
 
-    def gate_part(j):
-        cols = []
-        for side in range(2):
-            first = side * FF + core * half_ff + j * quarter_ff
-            cols.append(lax.dynamic_slice_in_dim(gate_up, first, quarter_ff, 1))
-        return jnp.concatenate(cols, axis=1).astype(BF)
+    gate_low = jnp.concatenate(
+        [
+            lax.dynamic_slice_in_dim(gate_up, side * FF + core * half_ff, half_ff, 1)
+            for side in range(2)
+        ],
+        axis=1,
+    ).astype(BF)
 
     if fast:
-        r = rows_d // 8
-        rf = rows_f // 8
-        own_in = halves(in_low).reshape(2, 4, 2, r, in_half)
-        own_out = halves(out_low).reshape(2, 4, 2, r, d_half)
-        own_down = halves(down_low).reshape(2, 4, 2, rf, d_half)
         in_full, out_full = gathered(
-            [own_in, own_out], [True, True], [(0, 0, r), (1, 0, r)], S, 0
+            [
+                halves(in_low).reshape(2, 4, 2, r, in_half),
+                halves(out_low).reshape(2, 4, 2, r, d_half),
+            ],
+            [True, True],
+            [(0, 0, r), (1, 0, r)],
+            S,
+            0,
         )
         in_full = in_full.reshape(2, D, in_half)
         out_full = out_full.reshape(2, D, d_half)
@@ -480,7 +881,7 @@
         in_full = halves(lax.all_gather(in_low, "z", axis=0, tiled=True))
         out_full = halves(lax.all_gather(out_low, "z", axis=0, tiled=True))
         down_full = halves(lax.all_gather(down_low, "z", axis=0, tiled=True))
-        gate_full = [lax.all_gather(gate_part(j), "z", axis=0, tiled=True) for j in range(2)]
+        gate_full = lax.all_gather(gate_low, "z", axis=0, tiled=True)
     gains_full = lax.all_gather(norm_gains.astype(BF), "z", axis=1, tiled=True)
 
     gains_wide = gains_full.astype(F32)
@@ -490,9 +891,11 @@
     positions = seq_place * piece_len + jnp.arange(piece_len, dtype=jnp.int32)
     normed = root_norm(tokens, gains_wide[0]).astype(BF)
     mixed_proj = jnp.concatenate([dot(normed, in_full[0]), dot(normed, in_full[1])], axis=1)
-    queries = rotate(
-        mixed_proj[:, :width_q].reshape(piece_len, HEADS, HEAD), positions, 1.0
-    ).astype(BF)
+    queries = (
+        rotate(mixed_proj[:, :width_q].reshape(piece_len, HEADS, HEAD), positions, 1.0)
+        .astype(BF)
+        .reshape(piece_len, width_q)
+    )
     own_keys = rotate(mixed_proj[:, width_q : width_q + HEAD], positions, 1.0)
     own_pair = jnp.concatenate([own_keys, mixed_proj[:, width_q + HEAD :]], axis=1).astype(BF)
     reach_count = (WINDOW + piece_len - 2) // piece_len
@@ -507,169 +910,106 @@
     padded_ids = jnp.concatenate([jnp.full((key_span,), -1, jnp.int32), segments])
     query_ids = lax.dynamic_slice_in_dim(segments, seq_place * piece_len, piece_len)
     key_ids = lax.dynamic_slice_in_dim(padded_ids, seq_place * piece_len, key_span + piece_len)
-    distance = jnp.arange(piece_len)[:, None] + key_span - jnp.arange(key_span + piece_len)[None, :]
-    allowed = (distance >= 0) & (distance < WINDOW) & (query_ids[:, None] == key_ids[None, :])
     live_rows = query_ids != 0
-    score_scale = HEAD ** (-0.5)
-
-    def masked_scores(query_part):
-        scores = (
-            jnp.einsum("thd,kd->htk", query_part, key_rows, preferred_element_type=F32)
-            * score_scale
-        )
-        return jnp.where(allowed[None], scores, -1e30)
-
-    group_outputs = []
-    group_totals = []
-    for first_head in range(0, HEADS, head_group):
-        scores = masked_scores(queries[:, first_head : first_head + head_group])
-        log_totals = jax.nn.logsumexp(scores, axis=-1)
-        weights = jnp.exp(scores - log_totals[..., None]).astype(BF)
-        group_outputs.append(
-            jnp.einsum("htk,kd->thd", weights, values, preferred_element_type=F32)
-        )
-        group_totals.append(log_totals)
-    attended = jnp.concatenate(group_outputs, axis=1)
-    attended = jnp.where(live_rows[:, None, None], attended, 0.0)
-    flat_heads = attended.reshape(piece_len, width_q).astype(BF)
+    query_row = query_ids[None, :]
+    key_column = key_ids[:, None]
+
+    flat_heads, log_totals = attend(
+        query_row, key_column, queries, key_rows, values, HEADS, piece_len
+    )
     middle = tokens + jnp.concatenate(
         [dot(flat_heads, out_full[0]), dot(flat_heads, out_full[1])], axis=1
     )
     normed_two = root_norm(middle, gains_wide[1]).astype(BF)
 
     if fast:
-        gate_own = [gate_part(j).reshape(4, 2, r, 2 * quarter_ff) for j in range(2)]
-        down_full, gate_a, gate_b = gathered(
-            [own_down] + gate_own,
-            [True, False, False],
-            [(0, i * 48, 48) for i in range(rf // 48)]
-            + [(1 + j, i * 16, 16) for j in range(2) for i in range(r // 16)],
+        down_full, gate_full = gathered(
+            [
+                halves(down_low).reshape(2, 4, 2, rows_f // 8, d_half),
+                gate_low.reshape(4, 2, r, 2 * half_ff),
+            ],
+            [True, False],
+            [(0, i * 48, 48) for i in range(rows_f // 8 // 48)]
+            + [(1, i * 16, 16) for i in range(r // 16)],
             S,
             1,
         )
         down_full = down_full.reshape(2, FF, d_half)
-        gate_full = [g.reshape(D, 2 * quarter_ff) for g in (gate_a, gate_b)]
-    down_mine = lax.dynamic_slice_in_dim(down_full, core * half_ff, half_ff, 1)
+        gate_full = gate_full.reshape(D, 2 * half_ff)
 
     upstream = cotangent[0].astype(F32)
 
+    def ordered(mine, other):
+        return jnp.concatenate(
+            [jnp.where(first_core, mine, other), jnp.where(first_core, other, mine)], axis=0
+        )
+
     def pair(v):
-        return jnp.concatenate([v, swapped(v, "c")], axis=0)
-
-    low_both = pair(cotangent[0])
+        return ordered(v, swapped(v, "c"))
+
+    def half_pair(v):
+        n = v.shape[1] // 2
+        keep = lax.dynamic_slice_in_dim(v, core * n, n, 1)
+        give = lax.dynamic_slice_in_dim(v, (1 - core) * n, n, 1)
+        return ordered(keep, swapped(give, "c"))
+
+    def core_sum(v):
+        keep = lax.dynamic_slice_in_dim(v, core * piece_len, piece_len, 0)
+        give = lax.dynamic_slice_in_dim(v, (1 - core) * piece_len, piece_len, 0)
+        return keep + swapped(give.astype(BF), "c").astype(F32)
+
+    df_both = pair(cotangent[0])
     normed_both = pair(normed)
+    flat_both = pair(flat_heads)
     two_both = pair(normed_two)
-    flat_both = pair(flat_heads)
-
-    hidden = []
-    grad_gated = []
-    grad_two = 0.0
-    out_sum = 0.0
-    for j in range(2):
-        gated = dot(two_both, gate_full[j])
-        down_j = lax.slice_in_dim(down_mine, j * quarter_ff, (j + 1) * quarter_ff, axis=1)
-        grad_hidden = dot_t(low_both[:, :d_half], down_j[0]) + dot_t(
-            low_both[:, d_half:], down_j[1]
-        )
-        gate, up = gated[:, :quarter_ff], gated[:, quarter_ff:]
-        unit, unit_pull = jax.vjp(gated_unit, gate, up)
-        grad_gate, grad_up = unit_pull(grad_hidden)
-        hidden.append(unit.astype(BF))
-        grad_gated.append(jnp.concatenate([grad_gate, grad_up], axis=1).astype(BF))
-        grad_two = grad_two + dot_t(grad_gated[j], gate_full[j])
-        out_sum = out_sum + jnp.concatenate([dot(hidden[j], down_j[i]) for i in range(2)], axis=1)
-
-    def core_sum(v):
-        return v[:piece_len] + swapped(v[piece_len:].astype(BF), "c").astype(F32)
-
-    hidden = jnp.concatenate(hidden, axis=1)
-
-    def summed(left, right, zb):
-        if fast:
-            return handed_out(plane_sum(left, right, zb))
-        whole = dot_rows(left.T, right).astype(BF)
-        whole = whole.reshape(S, left.shape[1] // S, right.shape[1])
-        mine = lax.psum_scatter(whole, "z", scatter_dimension=0, tiled=False)
-        mine = lax.psum(mine, ("y", "x"))
-        return lax.all_gather(mine, "c", axis=0)[None]
-
-    def summed_down():
-        if fast:
-            share = plane_sum(hidden, low_both, S // 2)
-            keep = lax.dynamic_slice_in_dim(share, core * d_half, d_half, 3)
-            give = lax.dynamic_slice_in_dim(share, (1 - core) * d_half, d_half, 3)
-            got = swapped(give, "c")
-            first = jnp.where(core == 0, keep, got)
-            second = jnp.where(core == 0, got, keep)
-            return handed_out(jnp.concatenate([first, second], axis=0))
-        whole = dot_rows(hidden.T, low_both).astype(BF)
-        mine = lax.psum(whole, ("y", "x"))
-        mine = lax.all_gather(mine, "c", axis=0, tiled=True)
-        mine = lax.dynamic_slice_in_dim(mine, core * d_half, d_half, 1)
-        mine = lax.psum_scatter(mine, "z", scatter_dimension=0, tiled=True)
-        return lax.all_gather(mine, "c", axis=0)[None]
-
-    gate_sums = [summed(two_both, grad_gated[j], S) for j in range(2)]
-    down_sum = summed_down()
+
+    two_t, hid_t, grad_gated, out_sum, two_sum = mlp_call(
+        core.reshape(1).astype(jnp.int32), two_both, df_both, gate_full, down_full
+    )
 
     output = middle + core_sum(out_sum)
     block_out = output.astype(BF)[None]
-    grad_normed_two = core_sum(grad_two)
+    grad_normed_two = core_sum(two_sum)
     _, norm_pull_two = jax.vjp(root_norm, middle, gains_wide[1])
     grad_middle_norm, grad_gain_two = norm_pull_two(grad_normed_two)
     grad_middle = upstream + grad_middle_norm
     grad_branch = grad_middle.astype(BF)
 
-    def half_pair(v):
-        n = v.shape[1] // 2
-        keep = lax.dynamic_slice_in_dim(v, core * n, n, 1)
-        give = lax.dynamic_slice_in_dim(v, (1 - core) * n, n, 1)
-        return jnp.concatenate([keep, swapped(give, "c")], axis=0)
-
-    out_total = summed(flat_both, half_pair(grad_branch), S)
     grad_flat = dot_t(grad_branch[:, :d_half], out_full[0]) + dot_t(
         grad_branch[:, d_half:], out_full[1]
     )
-    grad_attended = (
-        jnp.where(live_rows[:, None], grad_flat, 0.0).astype(BF).reshape(piece_len, HEADS, HEAD)
-    )
-    grad_queries = []
-    grad_key_sum = jnp.zeros((key_span + piece_len, HEAD), F32)
-    grad_value_sum = jnp.zeros((key_span + piece_len, HEAD), F32)
-    for group_index, first_head in enumerate(range(0, HEADS, head_group)):
-        query_part = queries[:, first_head : first_head + head_group]
-        scores = masked_scores(query_part)
-        probabilities = jnp.exp(scores - group_totals[group_index][..., None])
-        weights = probabilities.astype(BF)
-        grad_part = grad_attended[:, first_head : first_head + head_group]
-        grad_probs = jnp.einsum("thd,kd->htk", grad_part, values, preferred_element_type=F32)
-        grad_scores = probabilities * (
-            grad_probs - jnp.sum(probabilities * grad_probs, axis=-1, keepdims=True)
-        )
-        grad_raw = (grad_scores * score_scale).astype(BF)
-        grad_queries.append(
-            jnp.einsum("htk,kd->thd", grad_raw, key_rows, preferred_element_type=F32)
-        )
-        grad_key_sum = grad_key_sum + jnp.einsum(
-            "htk,thd->kd", grad_raw, query_part, preferred_element_type=F32
-        )
-        grad_value_sum = grad_value_sum + jnp.einsum(
-            "htk,thd->kd", weights, grad_part, preferred_element_type=F32
-        )
-    grad_pairs = jnp.concatenate([grad_key_sum, grad_value_sum], axis=1)
+    grad_attended = jnp.where(live_rows[:, None], grad_flat, 0.0).astype(BF)
+
+    if fast:
+        df_half = lax.dynamic_slice_in_dim(df_both, core * d_half, d_half, 1)
+        mlp_sums = reduced(two_t, hid_t, swapped(hid_t, "c"), grad_gated, df_half, S, 2)
+
+    grad_query_all, grad_keys, grad_values = attend_back(
+        query_row,
+        key_column,
+        queries,
+        key_rows,
+        values,
+        flat_heads,
+        grad_attended,
+        log_totals,
+        HEADS,
+        piece_len // 2,
+    )
+    grad_pairs = jnp.concatenate([grad_keys, grad_values], axis=1)
     own_grad = grad_pairs[key_span:]
     for back_step in range(1, reach_count + 1):
         sent_rows = grad_pairs[
             key_span - back_step * piece_len : key_span - (back_step - 1) * piece_len
         ]
         own_grad = own_grad + passed_along(sent_rows, "z", -back_step)
-    grad_query_all = jnp.concatenate(grad_queries, axis=1)
-    grad_query_raw = rotate(grad_query_all, positions, -1.0).reshape(piece_len, width_q)
+    grad_query_raw = rotate(
+        grad_query_all.reshape(piece_len, HEADS, HEAD), positions, -1.0
+    ).reshape(piece_len, width_q)
     grad_key_raw = rotate(own_grad[:, :HEAD], positions, -1.0)
     grad_mixed = jnp.concatenate([grad_query_raw, grad_key_raw, own_grad[:, HEAD:]], axis=1).astype(
         BF
     )
-    in_total = summed(normed_both, half_pair(grad_mixed), S)
     grad_normed = dot_t(grad_mixed[:, :in_half], in_full[0]) + dot_t(
         grad_mixed[:, in_half:], in_full[1]
     )
@@ -681,19 +1021,56 @@
 
     token_total = piece_len * S * Y * 4 * block_in.shape[0]
     step_value = update_count[0].astype(F32)
-    count = update_count
     rates = optimizer_rates
-
-    def adam(weight, moments, grads, sides):
-        rows, cols = grads[0].shape[2:]
-        return adam_call(
-            weight, moments, grads, count, rates, float(token_total), rows, cols // sides, sides
+    grad_half = half_pair(grad_branch)
+    mixed_half = half_pair(grad_mixed)
+
+    if fast:
+
+        def adam(weight, moments, grads, base, sides, tiles, down=False):
+            return adam_call(
+                weight, moments, grads, update_count, rates, float(token_total), base, sides, tiles, down
+            )
+
+        def summed(left, right):
+            return handed_out(plane_sum(left, right, S)).reshape(1, 4, 2, 2, r, right.shape[1])
+
+        tiles = half_ff // d_half
+        out_grad, out_new, out_mom = adam(
+            output_proj, output_moments, summed(flat_both, grad_half), 0, 1, 1
         )
-
-    in_grad, in_new, in_mom = adam(input_proj, input_moments, [in_total], 1)
-    out_grad, out_new, out_mom = adam(output_proj, output_moments, [out_total], 1)
-    gate_grad, gate_new, gate_mom = adam(gate_up, gate_moments, gate_sums, 2)
-    down_grad, down_new, down_mom = adam(down_weight, down_moments, [down_sum], 1)
+        in_grad, in_new, in_mom = adam(
+            input_proj, input_moments, summed(normed_both, mixed_half), 0, 1, 1
+        )
+        gate_grad, gate_new, gate_mom = adam(gate_up, gate_moments, mlp_sums, 0, 2, tiles)
+        down_grad, down_new, down_mom = adam(
+            down_weight, down_moments, mlp_sums, 2 * tiles, 1, tiles, True
+        )
+    else:
+
+        def adam(weight, moments, grad):
+            grad = grad.astype(F32) / token_total
+            change, new = adamw_step(weight, moments, grad, step_value, rates)
+            return grad, weight - change, new
+
+        def summed(left, right):
+            whole = dot_rows(left.T, right).astype(BF)
+            mine = lax.psum_scatter(whole, "z", scatter_dimension=0, tiled=True)
+            return lax.psum(mine, ("y", "x"))
+
+        gate_half = [summed(two_both, grad_gated[side]) for side in range(2)]
+        gate_sum = jnp.concatenate(
+            [lax.all_gather(g, "c", axis=1, tiled=True) for g in gate_half], axis=1
+        )
+        down_part = lax.psum(dot_rows(hid_t, df_both).astype(BF), ("y", "x"))
+        down_part = lax.all_gather(down_part, "c", axis=0, tiled=True)
+        down_sum = lax.psum_scatter(down_part, "z", scatter_dimension=0, tiled=True)
+        out_total = lax.all_gather(summed(flat_both, grad_half), "c", axis=1, tiled=True)
+        in_total = lax.all_gather(summed(normed_both, mixed_half), "c", axis=1, tiled=True)
+        out_grad, out_new, out_mom = adam(output_proj, output_moments, out_total)
+        in_grad, in_new, in_mom = adam(input_proj, input_moments, in_total)
+        gate_grad, gate_new, gate_mom = adam(gate_up, gate_moments, gate_sum)
+        down_grad, down_new, down_mom = adam(down_weight, down_moments, down_sum)
     gain_grad = gains_mine / token_total
     gains_step, gain_moments_new = adamw_step(norm_gains, gain_moments, gain_grad, step_value, rates)
     return (

time: 1210 us -> 979 us (0.81)
  Pallas kernels: 284 us -> 657 us
  matrix products: 385 us -> 42.3 us
  waiting for transfers between devices: 231 us -> 53.2 us
  local copies, waits for them, and re-layouts: 111 us -> 65.3 us
  other arithmetic: 90.7 us -> 67.5 us
    pallas_call x4 -> x8, Pallas kernels: 89.5 us -> 462 us  [the longest x1 236 us: reduced(): pl.pallas_call(body, out_shape=jax.ShapeDtypeStruct((nc, 4, 2, 2, r, n),...]
    dot_general x18 -> x0, matrix products: 186 us -> none  [the longest x3 58.7 us: on_device(): jnp.einsum('htk,kd->thd', grad_raw, key_rows, preferred_element_type=F32)]
    ppermute x29 -> x17, waiting for transfers between devices: 129 us -> 28.5 us  [swapped(): return lax.ppermute(block, axis, [(0, 1), (1, 0)])]
    dot_general x30 -> x12, matrix products: 82.4 us -> 21.9 us  [dot_rows(): lax.dot_general(a, b, (((1,), (0,)), ((), ())), preferred_element_type=F32)]
    dot_general x10 -> x4, matrix products: 68.5 us -> 10.6 us  [dot_t(): lax.dot_general(a, b, (((1,), (1,)), ((), ())), preferred_element_type=F32)]
    all_gather x5 -> x2, waiting for transfers between devices: 55.3 us -> 0.01 us  [handed_out(): return lax.all_gather(mine, ('y', 'x', 'c'), axis=0).reshape(4, 2, 2 * r, N)]
    reduce_scatter x5 -> x2, waiting for transfers between devices: 42.2 us -> 0.02 us  [handed_out(): lax.psum_scatter(share.reshape(S, 2 * r, N), 'z', scatter_dimension=0, ti...]
    dot_general x10 -> x4, matrix products: 48 us -> 9.87 us  [dot(): return jnp.dot(a, b, preferred_element_type=F32)]
  transfers between devices with their start and end apart: 43 -> 25, of which waited for: 16 -> 9; matrix products, arithmetic and copies ran while one was open for 45% -> 14% of each run, Pallas kernels for 18% -> 59%
where the time goes in v2:
time: 979 us; the launch traced here: 970 us
  Pallas kernels  657 us (67%)
  other arithmetic  67.5 us (7%)
  local copies, waits for them, and re-layouts  65.3 us (7%)
  waiting for transfers between devices  53.2 us (5%)
  blocking collectives  49.3 us (5%)
  matrix products  42.3 us (4%)
  starting transfers between devices  19.3 us (2%)
  between operations  15.9 us (2%)
    pallas_call x1, Pallas kernels, reduced(): pl.pallas_call(body, out_shape=jax.ShapeDtypeStruct((nc, 4, 2, 2, r, n),...  236 us
    pallas_call x2, Pallas kernels, gathered(): pl.pallas_call(body, out_shape=tuple(outs), in_specs=[pl.BlockSpec(memory...  195 us
    pallas_call x4, Pallas kernels, adam_call(): pl.pallas_call(body, grid=(4, 2, sides, tiles), in_specs=[smem, smem, pl....  102 us
    pallas_call x1, Pallas kernels, mlp_call(): pl.pallas_call(body, grid_spec=pltpu.PrefetchScalarGridSpec(num_scalar_pr...  76.4 us
    psum x1, blocking collectives, on_device(): lax.psum(jnp.stack([grad_gain_one, grad_gain_two]), ('y', 'x', 'c', 'z'))  37.4 us
    ppermute x17, waiting for transfers between devices, swapped(): return lax.ppermute(block, axis, [(0, 1), (1, 0)])  28.5 us
    pallas_call x1, Pallas kernels, attend_back(): pl.pallas_call(body, out_shape=(jax.ShapeDtypeStruct(q.shape, F32), jax.S...  26.9 us
    ppermute x4, waiting for transfers between devices, passed_along(): return lax.ppermute(block, axis, route)  24 us
  transfers between devices with their start and end apart: 25, of which 9 were waited for; matrix products, arithmetic and copies ran while one was open for 14% of the time, Pallas kernels for 59%

profile of v2, /device:TPU:0, one launch (start us, length us, event | category | flops | bytes accessed | tf_op | source)
XLA Modules:
  0.0 969.5 jit_solution(10279966127225393520)
XLA Ops:
  7.3 1.9 convert_element_type.201
  12.3 47.4 %shard_map.278 = (bf16[2,4,4,2,48,896]{5,4,3,2,1,0:T(8,128)(2,1)}, bf16[2,4,4,2,48,768]{5,4,3,2,1,0:T(8,128)(2,1)}) custom-call(bf16[2,4,2,48,896]{4,3,2,1,0:T(8,128)(2,1)} %pad_maximum_fusion.10.refs_0_, bf16[2,4,2,48,768]{4,3,2,1,0:T(8,128)(2,1)} %pad_maximum_fusion.11.refs_1_), custom_call_target="tpu_custom_call" | custom-call | tf_op jit(solution)/shard_map/pallas_call | solution.py:273
  59.7 5.7 fusion.82
  65.4 11.9 %all_gather.9 = bf16[2,1536]{1,0:T(2,128)(2,1)S(1)} all-gather(bf16[2,384]{1,0:T(2,128)(2,1)S(1)} %convert_element_type.196), channel_id=1, replica_groups=mesh['y'=2,'x'=2,'c'=2,'z'=4] {'z'}, dimensions={1}, use_global_device_ids=true | all-gather | bytes 7680 | tf_op jit(solution)/shard_map/all_gather | solution.py:885
  78.3 3.7 fusion.53
  82.1 1.9 fusion.65
  84.8 3.5 collective-permute-start
  88.2 3.4 collective-permute-start.1
  91.8 1.8 fusion.55
  93.7 2.1 pad_maximum_fusion.3
  95.8 2.4 copy.66
  105.1 3.8 convert_element_type.206
  112.5 20.6 %shard_map.279 = (bf16[512,1536]{1,0:T(8,128)(2,1)}, f32[12,1,512]{2,1,0:T(1,128)}) custom-call(s32[1,512]{1,0:T(1,128)} %get-tuple-element.79.refs_0_, s32[1536,1]{1,0:T(8,128)} %broadcast_in_dim.29.refs_1_, bf16[512,1536]{1,0:T(8,128)(2,1)} %copy.71.refs_2_, bf16[1536,128]{1,0:T(8,128)(2,1)} %get-tuple-element.139.refs_3_, ...), custom_call_target="tpu_custom_call" | custom-call | flops 4831838208 | bytes 3145728 | tf_op jit(solution)/shard_map/pallas_call | solution.py:361
  133.0 2.9 fusion.94
  139.8 2.0 fusion.84
  141.8 4.1 pad_maximum_fusion.1.refs_0_
  146.0 3.4 dynamic-slice_convert_fusion.1
  149.4 2.1 pad_maximum_fusion.2.refs_1_
  151.5 147.4 %shard_map.280 = (bf16[2,4,4,2,144,768]{5,4,3,2,1,0:T(8,128)(2,1)}, bf16[4,4,2,48,4608]{4,3,2,1,0:T(8,128)(2,1)}) custom-call(bf16[2,4,2,144,768]{4,3,2,1,0:T(8,128)(2,1)} %pad_maximum_fusion.1.refs_0_, bf16[4,2,48,4608]{3,2,1,0:T(8,128)(2,1)} %pad_maximum_fusion.2.refs_1_), custom_call_target="tpu_custom_call" | custom-call | tf_op jit(solution)/shard_map/pallas_call | solution.py:273
  299.0 3.0 broadcast_select_fusion.5
  301.9 2.0 pad_maximum_fusion.refs_1_
  304.5 1.9 pad_maximum_fusion.4.refs_0_
  306.4 76.4 %shard_map.281 = (bf16[1536,1024]{1,0:T(8,128)(2,1)}, bf16[2304,1024]{1,0:T(8,128)(2,1)}, bf16[2,1024,2304]{2,1,0:T(8,128)(2,1)}, f32[1024,1536]{1,0:T(8,128)}, f32[1024,1536]{1,0:T(8,128)}) custom-call(s32[1]{0:T(128)} %bitcast.13.where, bf16[1024,1536]{1,0:T(8,128)(2,1)} %pad_maximum_fusion.4.refs_0_, bf16[1024,1536]{1,0:T(8,128)(2,1)} %pad_maximum_fusion.refs_1_, ...), custom_call_target="tpu_custom_call" | custom-call | flops 43486543872 | bytes 41943040 | tf_op jit(solution)/shard_map/pallas_call | solution.py:455
  382.8 3.2 dynamic-slice_convert_fusion.2
  386.5 3.3 dynamic-slice_convert_fusion.3
  390.2 1.9 maximum_bitcast_fusion.1
  392.0 4.6 copy.81
  399.3 4.1 multiply_reduce_fusion
  403.4 5.9 fusion.79
  411.6 2.6 fusion.17.refs_6_
  414.2 26.9 %shard_map.282 = (f32[512,1536]{1,0:T(8,128)}, f32[1536,128]{1,0:T(8,128)}, f32[1536,128]{1,0:T(8,128)}) custom-call(s32[1,512]{1,0:T(1,128)} %get-tuple-element.79.refs_0_, s32[1536,1]{1,0:T(8,128)} %broadcast_in_dim.29.refs_1_, bf16[512,1536]{1,0:T(8,128)(2,1)} %copy.71.refs_2_, bf16[1536,128]{1,0:T(8,128)(2,1)} %get-tuple-element.139.refs_3_, ...), custom_call_target="tpu_custom_call" | custom-call | flops 12079595520 | bytes 9437184 | tf_op jit(solution)/shard_map/pallas_call | solution.py:384
  450.1 2.4 copy.74
  452.5 2.1 constant_dynamic-slice_fusion.9
  455.0 9.7 collective-permute-done.6
  464.6 14.3 %collective-permute-done.7 = f32[512,256]{1,0:T(8,128)} collective-permute-done((f32[512,256]{1,0:T(8,128)}, f32[512,256]{1,0:T(8,128)}, u32[]{:S(2)}, u32[]{:S(2)}) %collective-permute-start.7) | collective-permute-done | bytes 524320 | tf_op jit(solution)/shard_map/ppermute | solution.py:31
  480.4 1.9 fusion.69
  490.0 1.8 fusion.35
  493.2 4.7 fusion.9
  506.2 10.9 %collective-permute-done.16 = bf16[384,768]{1,0:T(8,128)(2,1)} collective-permute-done((bf16[384,768]{1,0:T(8,128)(2,1)}, bf16[384,768]{1,0:T(8,128)(2,1)}, u32[]{:S(2)}, u32[]{:S(2)}) %collective-permute-start.16) | collective-permute-done | bytes 589856 | tf_op jit(solution)/shard_map/ppermute | solution.py:35
  517.1 1.9 fusion.30
  521.4 2.2 fusion.31
  524.1 2.7 broadcast_select_fusion.9
  527.6 2.2 fusion.32
  529.8 2.1 broadcast_select_fusion.3
  531.9 1.9 maximum_bitcast_fusion
  533.7 3.4 copy.79
  539.1 1.9 convolution_convert_fusion.1
  543.5 1.9 convolution_convert_fusion
  549.2 8.1 collective-permute-done.10
  557.3 1.8 fusion.27
  560.6 2.5 collective-permute-done.12
  563.2 1.8 fusion.29
  565.0 3.7 collective-permute-done.11
  568.7 1.8 fusion.26
  572.3 1.8 fusion.28
  577.2 2.5 fusion.21.refs_4_
  579.8 37.4 %psum.7 = f32[2,1536]{1,0:T(2,128)S(1)} all-reduce(f32[2,1536]{1,0:T(2,128)S(1)} %pad_maximum_fusion.15), channel_id=1, replica_groups=mesh['y'=2,'x'=2,'c'=2,'z'=4] {'y','x','c','z'}, use_global_device_ids=true, to_apply=%region_8.9 | all-reduce | flops 3072 | bytes 24576 | tf_op jit(solution)/shard_map/psum | solution.py:1019
  617.3 1.9 add_multiply_fusion
  619.8 4.8 fusion.19
  624.7 236.2 %shard_map.285.refs_2_ = bf16[9,4,2,2,48,768]{5,4,3,2,1,0:T(8,128)(2,1)} custom-call(bf16[4,4,2,48,1024]{4,3,2,1,0:T(8,128)(2,1)} %bitcast.224, bf16[2,3,4,2,48,1024]{5,4,3,2,1,0:T(8,128)(2,1)} %bitcast.223, bf16[2,3,4,2,48,1024]{5,4,3,2,1,0:T(8,128)(2,1)} %bitcast.71.refs_2_, bf16[2,1024,2304]{2,1,0:T(8,128)(2,1)} %get-tuple-element.58.refs_3_, ...), custom_call_target="tpu_custom_call" | custom-call | flops 43486543872 | bytes 419430400 | tf_op jit(solution)/shard_map/pallas_call | solution.py:671
  860.8 27.5 %shard_map.287 = (f32[1152,1536]{1,0:T(8,128)}, f32[1152,1536]{1,0:T(8,128)}, f32[2,1152,1536]{2,1,0:T(8,128)}) custom-call(s32[1]{0:T(128)S(6)} %copy.84.refs_0_, f32[2]{0:T(128)} %refs_1_.7, bf16[9,4,2,2,48,768]{5,4,3,2,1,0:T(8,128)(2,1)} %shard_map.285.refs_2_, f32[1152,1536]{1,0:T(8,128)} %refs_3_.7, f32[2,1152,1536]{2,1,0:T(8,128)} %refs_4_.7), custom_call_target="tpu_custom_call" | custom-call | flops 35389440 | bytes 53084160 | tf_op jit(solution)/shard_map/pallas_call | solution.py:755
  888.4 54.4 %shard_map.286 = (f32[384,9216]{1,0:T(8,128)}, f32[384,9216]{1,0:T(8,128)}, f32[2,384,9216]{2,1,0:T(8,128)}) custom-call(s32[1]{0:T(128)S(6)} %copy.84.refs_0_, f32[2]{0:T(128)} %refs_1_.7, bf16[9,4,2,2,48,768]{5,4,3,2,1,0:T(8,128)(2,1)} %shard_map.285.refs_2_, f32[384,9216]{1,0:T(8,128)} %refs_3_.6, f32[2,384,9216]{2,1,0:T(8,128)} %refs_4_.6), custom_call_target="tpu_custom_call" | custom-call | flops 70778880 | bytes 106168320 | tf_op jit(solution)/shard_map/pallas_call | solution.py:755
  942.7 9.6 shard_map.284
  952.3 10.5 %shard_map.283 = (f32[384,1792]{1,0:T(8,128)}, f32[384,1792]{1,0:T(8,128)}, f32[2,384,1792]{2,1,0:T(8,128)}) custom-call(s32[1]{0:T(128)S(6)} %copy.84.refs_0_, f32[2]{0:T(128)} %refs_1_.7, bf16[1,4,2,2,48,896]{5,4,3,2,1,0:T(8,128)(2,1)} %bitcast.196, f32[384,1792]{1,0:T(8,128)} %refs_3_.4, f32[2,384,1792]{2,1,0:T(8,128)} %refs_4_.4), custom_call_target="tpu_custom_call" | custom-call | flops 13762560 | bytes 20643840 | tf_op jit(solution)/shard_map/pallas_call | solution.py:755
  (254 shorter events, 71.8 us)
Async XLA Ops:
  7.2 568.0 %reduce-scatter.5.cloned.1.call-start = ((), (), s32[]{:S(2)}) async-start(), calls=%async_computation.4 | async-start | bytes 737280 | tf_op jit(solution)/shard_map/reduce_scatter | solution.py:816
  7.2 74.8 %copy-start.62 = (f32[64]{0:T(128)}, f32[64]{0:T(128)S(1)}, u32[]{:S(2)}) copy-start(f32[64]{0:T(128)S(1)} %multiply_power_fusion) | copy-start | bytes 772
  59.7 5.7 copy-start.57
  59.7 17.6 %copy-start.1 = (bf16[1,512,1536]{2,1,0:T(8,128)(2,1)S(1)}, bf16[1,512,1536]{2,1,0:T(8,128)(2,1)}, u32[]{:S(2)}) copy-start(bf16[1,512,1536]{2,1,0:T(8,128)(2,1)} %param.15) | copy-start | bytes 4718596
  77.7 14.1 %copy-start.59 = (f32[512]{0:T(512)}, f32[512]{0:T(512)S(1)}, u32[]{:S(2)}) copy-start(f32[512]{0:T(512)S(1)} %fusion.72) | copy-start | bytes 6148
  78.3 3.8 copy-start.51
  78.3 13.6 %copy-start.15 = (bf16[1,4,4,2,48,896]{5,4,3,2,1,0:T(8,128)(2,1)S(1)}, bf16[1,4,4,2,48,896]{5,4,3,2,1,0:T(8,128)(2,1)}, u32[]{:S(2)}) copy-start(bf16[1,4,4,2,48,896]{5,4,3,2,1,0:T(8,128)(2,1)} %get-tuple-element.86) | copy-start | bytes 8257540
  82.1 9.8 %copy-start.29 = (bf16[512,128]{1,0:T(8,128)(2,1)}, bf16[512,128]{1,0:T(8,128)(2,1)S(1)}, u32[]{:S(2)}) copy-start(bf16[512,128]{1,0:T(8,128)(2,1)S(1)} %slice.272) | copy-start | bytes 393220
  83.9 7.9 copy-start.25
  83.9 7.9 copy-start.27
  84.8 24.5 %collective-permute-start = (bf16[512,256]{1,0:T(8,128)(2,1)}, bf16[512,256]{1,0:T(8,128)(2,1)}, u32[]{:S(2)}, u32[]{:S(2)}) collective-permute-start(bf16[512,256]{1,0:T(8,128)(2,1)} %pad_maximum_fusion.14), channel_id=1, source_target_pairs={{0,2},{1,3},{4,6},{5,7},{8,10},{9,11},{12,14},{13,15},{16,18},{17,... | collective-permute-start | bytes 786440 | tf_op jit(solution)/shard_map/ppermute | solution.py:31
  88.2 21.0 %collective-permute-start.1 = (bf16[512,256]{1,0:T(8,128)(2,1)}, bf16[512,256]{1,0:T(8,128)(2,1)}, u32[]{:S(2)}, u32[]{:S(2)}) collective-permute-start(bf16[512,256]{1,0:T(8,128)(2,1)} %pad_maximum_fusion.14), channel_id=1, source_target_pairs={{0,1},{1,2},{2,3},{4,5},{5,6},{6,7},{8,9},{9,10},{10,11},{12,13},{... | collective-permute-start | bytes 786440 | tf_op jit(solution)/shard_map/ppermute | solution.py:31
  91.7 207.2 %collective-permute-start.3 = (bf16[512,1536]{1,0:T(8,128)(2,1)}, bf16[512,1536]{1,0:T(8,128)(2,1)}, u32[]{:S(2)}, u32[]{:S(2)}) collective-permute-start(bf16[512,1536]{1,0:T(8,128)(2,1)} %bitcast.14), channel_id=1, source_target_pairs={{0,4},{4,0},{1,5},{5,1},{2,6},{6,2},{3,7},{7,3},{8,12},{12,8},{9,1... | collective-permute-start | bytes 4718600 | tf_op jit(solution)/shard_map/ppermute | solution.py:35
  103.9 5.0 slice-start.2
  105.1 3.8 slice-start.3
  109.2 23.8 %copy-start.19 = (bf16[1,4,4,2,48,768]{5,4,3,2,1,0:T(8,128)(2,1)}, bf16[1,4,4,2,48,768]{5,4,3,2,1,0:T(8,128)(2,1)S(1)}, u32[]{:S(2)}) copy-start(bf16[1,4,4,2,48,768]{5,4,3,2,1,0:T(8,128)(2,1)S(1)} %get-tuple-element.88) | copy-start | bytes 7077892
  109.3 26.7 %copy-start.17 = (bf16[1,4,4,2,48,768]{5,4,3,2,1,0:T(8,128)(2,1)}, bf16[1,4,4,2,48,768]{5,4,3,2,1,0:T(8,128)(2,1)S(1)}, u32[]{:S(2)}) copy-start(bf16[1,4,4,2,48,768]{5,4,3,2,1,0:T(8,128)(2,1)S(1)} %get-tuple-element.89) | copy-start | bytes 7077892
  133.0 2.9 copy-start.21
  139.4 159.6 %collective-permute-start.2 = (bf16[512,1536]{1,0:T(8,128)(2,1)}, bf16[512,1536]{1,0:T(8,128)(2,1)}, u32[]{:S(2)}, u32[]{:S(2)}) collective-permute-start(bf16[512,1536]{1,0:T(8,128)(2,1)} %multiply_convert_fusion), channel_id=1, source_target_pairs={{0,4},{4,0},{1,5},{5,1},{2,6},{6,2},{3,7},{7,3},{8,12},{12,8},{9,1... | collective-permute-start | bytes 4718600 | tf_op jit(solution)/shard_map/ppermute | solution.py:35
  298.9 91.1 %collective-permute-start.14 = (bf16[512,1536]{1,0:T(8,128)(2,1)}, bf16[512,1536]{1,0:T(8,128)(2,1)S(1)}, u32[]{:S(2)}, u32[]{:S(2)}) collective-permute-start(bf16[512,1536]{1,0:T(8,128)(2,1)} %get-tuple-element.44.refs_5_), channel_id=1, source_target_pairs={{0,4},{4,0},{1,5},{5,1},{2,6},{6,2},{3,7},{7,3},{8,12},{12,8},{9,1... | collective-permute-start | bytes 4718600 | tf_op jit(solution)/shard_map/ppermute | solution.py:35
  386.1 3.9 copy-start.22
  386.1 13.3 %collective-permute-start.5 = (bf16[512,1536]{1,0:T(8,128)(2,1)}, bf16[512,1536]{1,0:T(8,128)(2,1)}, u32[]{:S(2)}, u32[]{:S(2)}) collective-permute-start(bf16[512,1536]{1,0:T(8,128)(2,1)} %dynamic-slice_convert_fusion.2), channel_id=1, source_target_pairs={{0,4},{4,0},{1,5},{5,1},{2,6},{6,2},{3,7},{7,3},{8,12},{12,8},{9,1... | collective-permute-start | bytes 4718600 | tf_op jit(solution)/shard_map/ppermute | solution.py:35
  389.8 13.6 %collective-permute-start.4 = (bf16[512,1536]{1,0:T(8,128)(2,1)}, bf16[512,1536]{1,0:T(8,128)(2,1)}, u32[]{:S(2)}, u32[]{:S(2)}) collective-permute-start(bf16[512,1536]{1,0:T(8,128)(2,1)} %dynamic-slice_convert_fusion.3), channel_id=1, source_target_pairs={{0,4},{4,0},{1,5},{5,1},{2,6},{6,2},{3,7},{7,3},{8,12},{12,8},{9,1... | collective-permute-start | bytes 4718600 | tf_op jit(solution)/shard_map/ppermute | solution.py:35
  396.7 6.8 slice-start
  399.3 4.1 slice-start.1
  403.4 5.9 copy-start.20
  441.1 6.3 copy-start
  444.7 19.9 %collective-permute-start.6 = (f32[512,256]{1,0:T(8,128)}, f32[512,256]{1,0:T(8,128)}, u32[]{:S(2)}, u32[]{:S(2)}) collective-permute-start(f32[512,256]{1,0:T(8,128)} %get-tuple-element.132), channel_id=1, source_target_pairs={{1,0},{2,1},{3,2},{5,4},{6,5},{7,6},{9,8},{10,9},{11,10},{13,12},{... | collective-permute-start | bytes 1572872 | tf_op jit(solution)/shard_map/ppermute | solution.py:31
  446.0 32.9 %collective-permute-start.7 = (f32[512,256]{1,0:T(8,128)}, f32[512,256]{1,0:T(8,128)}, u32[]{:S(2)}, u32[]{:S(2)}) collective-permute-start(f32[512,256]{1,0:T(8,128)} %get-tuple-element.133), channel_id=1, source_target_pairs={{2,0},{3,1},{6,4},{7,5},{10,8},{11,9},{14,12},{15,13},{18,16},{19,... | collective-permute-start | bytes 1572872 | tf_op jit(solution)/shard_map/ppermute | solution.py:31
  452.5 27.9 %copy-start.52 = (f32[512]{0:T(512)S(1)}, f32[512]{0:T(512)}, u32[]{:S(2)}) copy-start(f32[512]{0:T(512)} %copy-done.51) | copy-start | bytes 6148
  452.5 27.9 %copy-start.63 = (f32[64]{0:T(128)S(1)}, f32[64]{0:T(128)}, u32[]{:S(2)}) copy-start(f32[64]{0:T(128)} %copy-done.62) | copy-start | bytes 772
  454.6 32.2 %copy-start.24 = (f32[512,64]{0,1:T(8,128)S(1)}, f32[512,64]{0,1:T(8,128)}, u32[]{:S(2)}) copy-start(f32[512,64]{0,1:T(8,128)} %copy-done.23) | copy-start | bytes 393220
  454.6 43.4 %collective-permute-start.15 = (bf16[512,768]{1,0:T(8,128)(2,1)}, bf16[512,768]{1,0:T(8,128)(2,1)}, u32[]{:S(2)}, u32[]{:S(2)}) collective-permute-start(bf16[512,768]{1,0:T(8,128)(2,1)} %constant_dynamic-slice_fusion.9), channel_id=1, source_target_pairs={{0,4},{4,0},{1,5},{5,1},{2,6},{6,2},{3,7},{7,3},{8,12},{12,8},{9,1... | collective-permute-start | bytes 2359304 | tf_op jit(solution)/shard_map/ppermute | solution.py:35
  493.2 4.8 copy-start.10
  498.0 31.8 %collective-permute-start.8 = (bf16[512,1536]{1,0:T(8,128)(2,1)}, bf16[512,1536]{1,0:T(8,128)(2,1)}, u32[]{:S(2)}, u32[]{:S(2)}) collective-permute-start(bf16[512,1536]{1,0:T(8,128)(2,1)} %get-tuple-element.119), channel_id=1, source_target_pairs={{0,4},{4,0},{1,5},{5,1},{2,6},{6,2},{3,7},{7,3},{8,12},{12,8},{9,1... | collective-permute-start | bytes 4718600 | tf_op jit(solution)/shard_map/ppermute | solution.py:35
  499.5 4.2 copy-start.35
  499.5 4.2 copy-start.38
  499.5 4.2 copy-start.43
  499.6 4.2 copy-start.44
  501.2 15.9 %collective-permute-start.16 = (bf16[384,768]{1,0:T(8,128)(2,1)}, bf16[384,768]{1,0:T(8,128)(2,1)}, u32[]{:S(2)}, u32[]{:S(2)}) collective-permute-start(bf16[384,768]{1,0:T(8,128)(2,1)} %convolution_convert_fusion.3), channel_id=1, source_target_pairs={{0,8},{8,0},{1,9},{9,1},{2,10},{10,2},{3,11},{11,3},{4,12},{12,4},... | collective-permute-start | bytes 1769480 | tf_op jit(solution)/shard_map/ppermute | solution.py:35
  503.7 20.4 %collective-permute-start.9 = (bf16[512,896]{0,1:T(8,128)(2,1)}, bf16[512,896]{0,1:T(8,128)(2,1)}, u32[]{:S(2)}, u32[]{:S(2)}) collective-permute-start(bf16[512,896]{0,1:T(8,128)(2,1)} %constant_dynamic-slice_fusion.17), channel_id=1, source_target_pairs={{0,4},{4,0},{1,5},{5,1},{2,6},{6,2},{3,7},{7,3},{8,12},{12,8},{9,1... | collective-permute-start | bytes 2752520 | tf_op jit(solution)/shard_map/ppermute | solution.py:35
  505.4 16.0 %collective-permute-start.18 = (bf16[384,768]{1,0:T(8,128)(2,1)}, bf16[384,768]{1,0:T(8,128)(2,1)}, u32[]{:S(2)}, u32[]{:S(2)}) collective-permute-start(bf16[384,768]{1,0:T(8,128)(2,1)} %convolution_convert_fusion.2), channel_id=1, source_target_pairs={{0,16},{16,0},{1,17},{17,1},{2,18},{18,2},{3,19},{19,3},{4,20},{20... | collective-permute-start | bytes 1769480 | tf_op jit(solution)/shard_map/ppermute | solution.py:35
  505.9 118.7 %collective-permute-start.20 = (bf16[2304,1024]{1,0:T(8,128)(2,1)}, bf16[2304,1024]{1,0:T(8,128)(2,1)}, u32[]{:S(2)}, u32[]{:S(2)}) collective-permute-start(bf16[2304,1024]{1,0:T(8,128)(2,1)} %get-tuple-element.57), channel_id=1, source_target_pairs={{0,4},{4,0},{1,5},{5,1},{2,6},{6,2},{3,7},{7,3},{8,12},{12,8},{9,1... | collective-permute-start | bytes 14155784 | tf_op jit(solution)/shard_map/ppermute | solution.py:35
  506.1 15.3 %copy-start.36 = (bf16[512,768]{1,0:T(8,128)(2,1)S(1)}, bf16[512,768]{1,0:T(8,128)(2,1)}, u32[]{:S(2)}) copy-start(bf16[512,768]{1,0:T(8,128)(2,1)} %copy-done.35) | copy-start | bytes 2359300
  506.1 15.3 %copy-start.39 = (bf16[512,768]{1,0:T(8,128)(2,1)S(1)}, bf16[512,768]{1,0:T(8,128)(2,1)}, u32[]{:S(2)}) copy-start(bf16[512,768]{1,0:T(8,128)(2,1)} %copy-done.38) | copy-start | bytes 2359300
  506.1 15.3 %copy-start.42 = (bf16[1,1,1,4,48,1024]{5,4,0,2,1,3:T(8,128)(2,1)S(1)}, bf16[1,1,1,4,48,1024]{5,4,0,2,1,3:T(8,128)(2,1)}, u32[]{:S(2)}) copy-start(bf16[1,1,1,4,48,1024]{5,4,0,2,1,3:T(8,128)(2,1)} %get-tuple-element.123) | copy-start | bytes 1179652
  519.0 8.6 collective-permute-start.17
  523.6 22.4 %collective-permute-start.19 = (bf16[192,768]{1,0:T(8,128)(2,1)}, bf16[192,768]{1,0:T(8,128)(2,1)}, u32[]{:S(2)}, u32[]{:S(2)}) collective-permute-start(bf16[192,768]{1,0:T(8,128)(2,1)} %fusion.31), channel_id=1, source_target_pairs={{0,8},{8,0},{1,9},{9,1},{2,10},{10,2},{3,11},{11,3},{4,12},{12,4},... | collective-permute-start | bytes 884744 | tf_op jit(solution)/shard_map/ppermute | solution.py:35
  541.0 16.3 %collective-permute-start.10 = (bf16[384,896]{1,0:T(8,128)(2,1)}, bf16[384,896]{1,0:T(8,128)(2,1)}, u32[]{:S(2)}, u32[]{:S(2)}) collective-permute-start(bf16[384,896]{1,0:T(8,128)(2,1)} %convolution_convert_fusion.1), channel_id=1, source_target_pairs={{0,8},{8,0},{1,9},{9,1},{2,10},{10,2},{3,11},{11,3},{4,12},{12,4},... | collective-permute-start | bytes 2064392 | tf_op jit(solution)/shard_map/ppermute | solution.py:35
  545.4 17.8 %collective-permute-start.12 = (bf16[384,896]{1,0:T(8,128)(2,1)}, bf16[384,896]{1,0:T(8,128)(2,1)}, u32[]{:S(2)}, u32[]{:S(2)}) collective-permute-start(bf16[384,896]{1,0:T(8,128)(2,1)} %convolution_convert_fusion), channel_id=1, source_target_pairs={{0,16},{16,0},{1,17},{17,1},{2,18},{18,2},{3,19},{19,3},{4,20},{20... | collective-permute-start | bytes 2064392 | tf_op jit(solution)/shard_map/ppermute | solution.py:35
  547.5 9.8 %copy-start.32 = (bf16[512,896]{0,1:T(8,128)(2,1)S(1)}, bf16[512,896]{0,1:T(8,128)(2,1)}, u32[]{:S(2)}) copy-start(bf16[512,896]{0,1:T(8,128)(2,1)} %get-tuple-element.113) | copy-start | bytes 2752516
  547.6 9.8 %copy-start.34 = (bf16[512,896]{0,1:T(8,128)(2,1)S(1)}, bf16[512,896]{0,1:T(8,128)(2,1)}, u32[]{:S(2)}) copy-start(bf16[512,896]{0,1:T(8,128)(2,1)} %get-tuple-element.114) | copy-start | bytes 2752516
  548.5 76.1 %reduce-scatter.3.cloned.1.call-start = ((), (), s32[]{:S(2)}) async-start(), calls=%async_computation.2 | async-start | bytes 860160 | tf_op jit(solution)/shard_map/reduce_scatter | solution.py:816
  549.2 14.0 %copy-start.46 = (bf16[1,1,1,4,48,1024]{5,4,0,2,1,3:T(8,128)(2,1)S(1)}, bf16[1,1,1,4,48,1024]{5,4,0,2,1,3:T(8,128)(2,1)}, u32[]{:S(2)}) copy-start(bf16[1,1,1,4,48,1024]{5,4,0,2,1,3:T(8,128)(2,1)} %get-tuple-element.129) | copy-start | bytes 1179652
  559.1 9.6 collective-permute-start.11
  564.9 7.3 collective-permute-start.13
  568.7 3.6 copy-start.45
  574.1 3.1 copy-start.6
  575.1 367.7 %all-gather.5.cloned.1.call-start = ((), (), s32[]{:S(2)}) async-start(), calls=%async_computation.5 | async-start | bytes 1327104 | tf_op jit(solution)/shard_map/all_gather | solution.py:817
  575.8 376.5 %all-gather.3.cloned.1.call-start = ((), (), s32[]{:S(2)}) async-start(), calls=%async_computation.3 | async-start | bytes 1548288 | tf_op jit(solution)/shard_map/all_gather | solution.py:817
  577.2 40.1 %copy-start.58 = (f32[2,384]{1,0:T(2,128)S(1)}, f32[2,384]{1,0:T(2,128)}, u32[]{:S(2)}) copy-start(f32[2,384]{1,0:T(2,128)} %param.22) | copy-start | bytes 9220
  577.2 40.1 %copy-start.61 = (f32[2,2,384]{2,1,0:T(2,128)S(1)}, f32[2,2,384]{2,1,0:T(2,128)}, u32[]{:S(2)}) copy-start(f32[2,2,384]{2,1,0:T(2,128)} %param.27) | copy-start | bytes 18436
  577.2 42.6 %copy-start.55 = (f32[512]{0:T(512)S(1)}, f32[512]{0:T(512)}, u32[]{:S(2)}) copy-start(f32[512]{0:T(512)} %copy-done.54) | copy-start | bytes 6148
  577.2 42.6 %copy-start.4 = (bf16[1,512,1536]{2,1,0:T(8,128)(2,1)S(1)}, bf16[1,512,1536]{2,1,0:T(8,128)(2,1)}, u32[]{:S(2)}) copy-start(bf16[1,512,1536]{2,1,0:T(8,128)(2,1)} %param.15) | copy-start | bytes 4718596
  (29 other events, 53.7 us)
Sparse Core Ops, SparseCore 0:
  548.6 19.2 reduce-scatter.4
  575.2 19.7 reduce-scatter.2
  597.0 23.1 all-gather.4
  624.8 31.1 all-gather.2

commit v3 on v2

--- a/solution.py
+++ b/solution.py
@@ -19,7 +19,7 @@
 BF = jnp.bfloat16
 F32 = jnp.float32
 MESH_ID = pl.DeviceIdType.MESH
-VMEM_BYTES = 56 * 1024 * 1024
+VMEM_BYTES = 60 * 1024 * 1024
 ANY = pl.BlockSpec(memory_space=pl.ANY)
 VM = pl.BlockSpec(memory_space=pltpu.VMEM)
 LOG2E = 1.4426950408889634
@@ -71,13 +71,11 @@
     return (optimizer_rates[0] * update, jnp.stack([first_moment, second]))
 
 
-def gather_kernel(shared, chunks, S, refs):
+def gather_kernel(shared, chunks, S, own, full, sems, small_own, small_full, work):
     n = len(shared)
     nc = len(chunks)
     F = S - 1
-    own = refs[:n]
-    full = refs[n : 2 * n]
-    loc, zs, zr, xs, xr, ys, yr, cs, cr = refs[2 * n :]
+    loc, zs, zr, xs, xr, ys, yr, cs, cr, ss, sr = sems
     y, x, c, z = (lax.axis_index(a) for a in ("y", "x", "c", "z"))
     k = y * 2 + x
     kx = y * 2 + 1 - x
@@ -98,18 +96,10 @@
         sign = jnp.where(near, (j % 2) * 2 - 1, jnp.where(high > low, 1, -1))
         blocks.append((z + sign * dist, sign))
     barrier = pltpu.get_barrier_semaphore()
-    for target in (to_x, to_y, to_c):
+    others = [lax.rem(z + e, S) for e in range(1, S)]
+    for target in [to_x, to_y, to_c] + [{"z": zz} for zz in others]:
         pl.semaphore_signal(barrier, inc=1, device_id=target, device_id_type=MESH_ID)
-
-    @pl.when(z + 1 < S)
-    def _():
-        pl.semaphore_signal(barrier, inc=1, device_id={"z": above}, device_id_type=MESH_ID)
-
-    @pl.when(z > 0)
-    def _():
-        pl.semaphore_signal(barrier, inc=1, device_id={"z": below}, device_id_type=MESH_ID)
-
-    pl.semaphore_wait(barrier, 3 + jnp.minimum(low, 1) + jnp.minimum(high, 1))
+    pl.semaphore_wait(barrier, 3 + F)
 
     def own_half(i):
         return own[i].at[c] if shared[i] else own[i]
@@ -117,11 +107,15 @@
     def full_half(i):
         return full[i].at[c] if shared[i] else full[i]
 
+    def box(q):
+        _, r0, rn, c0, cn = chunks[q]
+        return pl.ds(r0, rn), pl.ds(c0, cn)
+
     def part(ref, q, zz, kk, h=None):
-        _, r0, rn = chunks[q]
+        rr, cc = box(q)
         if h is None:
-            return ref.at[zz, kk, :, pl.ds(r0, rn)]
-        return ref.at[zz, kk, h, pl.ds(r0, rn)]
+            return ref.at[zz, kk, :, rr, cc]
+        return ref.at[zz, kk, h, rr, cc]
 
     def remote(src, dst, s, r, target):
         return pltpu.make_async_remote_copy(
@@ -135,20 +129,26 @@
 
     tail = []
     local = []
+    arriving = {i: [] for i in range(n)}
+    arriving[None] = []
+    finished = [0] * n
     for i in range(n):
         if shared[i]:
             for half in range(2):
-                local.append(
-                    pltpu.make_async_copy(
-                        own[i].at[half], full[i].at[half, z], loc.at[len(local)]
-                    )
+                copy = pltpu.make_async_copy(
+                    own[i].at[half], full[i].at[half, z], loc.at[len(local)]
                 )
+                local.append(copy)
+                arriving[i].append(copy.wait)
         else:
-            local.append(pltpu.make_async_copy(own[i], full[i].at[z], loc.at[len(local)]))
+            copy = pltpu.make_async_copy(own[i], full[i].at[z], loc.at[len(local)])
+            local.append(copy)
+            arriving[i].append(copy.wait)
 
     def z_first(q):
-        i, r0, rn = chunks[q]
-        src = own_half(i).at[k, :, pl.ds(r0, rn)]
+        i = chunks[q][0]
+        rr, cc = box(q)
+        src = own_half(i).at[k, :, rr, cc]
         dst = part(full_half(i), q, z, k)
         for ok, target, slot in ((z + 1 < S, above, F), (z > 0, below, F + 1)):
 
@@ -214,9 +214,11 @@
         tail.append(copy.wait_send)
 
     def last(q, j):
-        i, r0, rn = chunks[q]
+        i = chunks[q][0]
+        rr, cc = box(q)
         zz, _ = blocks[j]
         held = full_half(i)
+        finished[i] += 1
         for kk, h, s, r, slot, target in (
             (kx, 1, xs, xr, 1, to_x),
             (ky, 0, ys, yr, 1, to_y),
@@ -226,20 +228,36 @@
             p = part(held, q, zz, kk, h)
             remote(p, p, s.at[q, j, slot], r.at[q, j, slot], target).wait_recv()
         if shared[i]:
-            p = held.at[zz, :, :, pl.ds(r0, rn)]
+            p = held.at[zz, :, :, rr, cc]
             copy = remote(p, p, cs.at[q, j], cr.at[q, j], to_c)
             copy.start()
             tail.append(copy.wait_send)
-            other = full[i].at[1 - c].at[zz, :, :, pl.ds(r0, rn)]
+            other = full[i].at[1 - c].at[zz, :, :, rr, cc]
 
             def finish():
                 remote(other, other, cs.at[q, j], cr.at[q, j], to_c).wait_recv()
 
-            tail.append(finish)
+            arriving[i].append(finish)
+
+    def ready(i):
+        if i is not None:
+            assert finished[i] == F * sum(chunk[0] == i for chunk in chunks)
+        for wait in arriving.pop(i, []):
+            wait()
 
     z_first(0)
     for copy in local:
         copy.start()
+    if small_own is not None:
+        place = pltpu.make_async_copy(small_own, small_full.at[z], ss.at[0])
+        place.start()
+        arriving[None].append(place.wait)
+        for e, zz in enumerate(others, 1):
+            copy = remote(small_own, small_full.at[z], ss.at[e], sr.at[S - e], {"z": zz})
+            copy.start()
+            tail.append(copy.wait_send)
+            came = small_full.at[zz]
+            arriving[None].append(remote(came, came, ss.at[e], sr.at[e], {"z": zz}).wait_recv)
     for t in range(1, nc + F + 3):
         if t < nc:
             z_first(t)
@@ -252,44 +270,29 @@
         for j in range(F):
             if 0 <= t - 3 - j < nc:
                 last(t - 3 - j, j)
-    for copy in local:
-        copy.wait()
+        work(t, ready)
+    for i in list(arriving):
+        ready(i)
     for wait in tail:
         wait()
 
 
-def gathered(own, shared, chunks, S, cid):
-    n = len(own)
-    nc = len(chunks)
+def gather_sems(n, nc, S):
+    dma = pltpu.SemaphoreType.DMA
     F = S - 1
-    outs = []
-    for o, s in zip(own, shared):
-        outs.append(jax.ShapeDtypeStruct((2, S) + o.shape[1:] if s else (S,) + o.shape, o.dtype))
-    dma = pltpu.SemaphoreType.DMA
-
-    def body(*refs):
-        gather_kernel(shared, chunks, S, refs)
-
-    return pl.pallas_call(
-        body,
-        out_shape=tuple(outs),
-        in_specs=[pl.BlockSpec(memory_space=pltpu.VMEM)] * n,
-        out_specs=tuple([ANY] * n),
-        scratch_shapes=[
-            dma((2 * n,)),
-            dma((nc, F + 2)),
-            dma((nc, S)),
-            dma((nc, F, 3)),
-            dma((nc, F, 3)),
-            dma((nc, F, 3)),
-            dma((nc, F, 3)),
-            dma((nc, F)),
-            dma((nc, F)),
-        ],
-        compiler_params=pltpu.CompilerParams(
-            collective_id=cid, has_side_effects=True, vmem_limit_bytes=VMEM_BYTES
-        ),
-    )(*own)
+    return [
+        dma((2 * n,)),
+        dma((nc, F + 2)),
+        dma((nc, S)),
+        dma((nc, F, 3)),
+        dma((nc, F, 3)),
+        dma((nc, F, 3)),
+        dma((nc, F, 3)),
+        dma((nc, F)),
+        dma((nc, F)),
+        dma((S,)),
+        dma((S,)),
+    ]
 
 
 def nt(a, b):
@@ -306,52 +309,263 @@
     allowed = (distance >= 0) & (distance < WINDOW) & same
     bias[...] = jnp.where(allowed, 0.0, -1e30)
 
+def fwd_step(h, first, rows, q_ids, q_ref, k_ref, o_ref, l_ref, bias, vt):
+    span = WINDOW + rows
+    factor = HEAD**-0.5 * LOG2E
+    cols = pl.ds(h * HEAD, HEAD)
+    q = q_ref[pl.ds(first, rows), cols]
+    s = nt(k_ref[pl.ds(first, span), :], q) * factor + bias[...]
+    top = jnp.max(s, axis=0, keepdims=True)
+    p = jnp.exp2(s - top)
+    total = jnp.sum(p, axis=0, keepdims=True)
+    o = nn(vt[:, pl.ds(first, span)], p.astype(BF))
+    live = q_ids[:1, pl.ds(first, rows)] != 0
+    o = jnp.where(live, o * (1.0 / total), 0.0)
+    o_ref[pl.ds(first, rows), cols] = o.T.astype(BF)
+    l_ref[h, :, pl.ds(first, rows)] = top + jnp.log2(total)
+
+
 def fwd_kernel(heads, rows, q_ids, k_ids, q_ref, k_ref, v_ref, o_ref, l_ref, bias, vt):
-    piece = q_ref.shape[0]
+    vt[...] = v_ref[...].T
+    for first in range(0, q_ref.shape[0], rows):
+        fill_bias(bias, q_ids, k_ids, first, rows, WINDOW + rows)
+        for h in range(heads):
+            fwd_step(h, first, rows, q_ids, q_ref, k_ref, o_ref, l_ref, bias, vt)
+
+
+def norm_rows(source, gain, target):
+    rows = 64
+
+    @pl.loop(0, target.shape[0] // rows)
+    def _(i):
+        at = pl.ds(pl.multiple_of(i * rows, rows), rows)
+        u = source[at, :].astype(F32)
+        scale = lax.rsqrt(jnp.mean(u * u, axis=1, keepdims=True) + norm_eps)
+        target[at, :] = (u * scale * gain).astype(target.dtype)
+
+
+def turned(u, cos_ref, sin_ref):
+    return u * cos_ref[...] + pltpu.roll(u, HEAD // 2, 1) * sin_ref[...]
+
+
+def remote_copy(src, dst, send, receive, target):
+    return pltpu.make_async_remote_copy(
+        src_ref=src,
+        dst_ref=dst,
+        send_sem=send,
+        recv_sem=receive,
+        device_id=target,
+        device_id_type=MESH_ID,
+    )
+
+
+def started(src, dst, sem):
+    copy = pltpu.make_async_copy(src, dst, sem)
+    copy.start()
+    return copy
+
+
+def forward_kernel(heads, chunks, S, *refs):
+    own = refs[:4]
+    small_own, x_ref, cos_ref, sin_ref, q_ids, k_ids = refs[4:10]
+    full = refs[10:14]
+    small_full, h1_ref, q_ref, k_out, v_out, o_ref, l_ref, mid_ref, h2_ref, h2_other = refs[14:24]
+    w_in, w_out, gains, mix, kv, bias, vt, lds, hs, hr, h2_sems = refs[24:35]
+    sems = refs[35:]
+    z = lax.axis_index("z")
+    c = lax.axis_index("c")
+    piece = x_ref.shape[0]
+    reach = kv.shape[0] // piece - 1
+    half = w_in.shape[-1]
+    D = x_ref.shape[1]
+    own_rows = pl.ds(reach * piece, piece)
+    kv[...] = jnp.zeros_like(kv)
+    sent = []
+    loads = {}
+
+    def gain_row(i):
+        return jnp.concatenate([gains[zz, i : i + 1, :] for zz in range(S)], axis=1).astype(F32)
+
+    def start_norm(ready):
+        ready(None)
+        started(small_full, gains, lds.at[0]).wait()
+        norm_rows(x_ref, gain_row(0), h1_ref)
+
+    def start_project(ready):
+        ready(0)
+        for i in range(2):
+            loads[i] = started(full[0].at[i], w_in.at[i], lds.at[1 + i])
+
+    def project(i):
+        loads.pop(i).wait()
+        mix[...] = nn(h1_ref[...], w_in[i].reshape(D, half))
+        for j in range(half // HEAD):
+            h = i * (half // HEAD) + j
+            u = mix[:, j * HEAD : (j + 1) * HEAD]
+            if h < heads:
+                q_ref[:, h * HEAD : (h + 1) * HEAD] = turned(u, cos_ref, sin_ref).astype(BF)
+            elif h == heads:
+                kv[own_rows, :HEAD] = turned(u, cos_ref, sin_ref).astype(BF)
+            else:
+                kv[own_rows, HEAD:] = u.astype(BF)
+
+    def halo(d, starting):
+        there = kv.at[pl.ds((reach - d) * piece, piece)]
+        target = {"z": jnp.minimum(z + d, S - 1)}
+        copy = remote_copy(kv.at[own_rows], there, hs.at[d - 1], hr.at[d - 1], target)
+
+        @pl.when(z + d < S)
+        def _():
+            if starting:
+                copy.start()
+            else:
+                copy.wait_send()
+
+        if not starting:
+
+            @pl.when(z >= d)
+            def _():
+                remote_copy(there, there, hs.at[d - 1], hr.at[d - 1], target).wait_recv()
+
+    def start_attention():
+        for d in range(1, reach + 1):
+            halo(d, False)
+        k_out[...] = kv[:, :HEAD]
+        v_out[...] = kv[:, HEAD:]
+        vt[...] = kv[:, HEAD:].T
+        fill_bias(bias, q_ids, k_ids, 0, piece, WINDOW + piece)
+
+    def attention(first, count):
+        for h in range(first, first + count):
+            fwd_step(h, 0, piece, q_ids, q_ref, k_out, o_ref, l_ref, bias, vt)
+
+    def start_output(ready):
+        ready(1)
+        for i in range(2):
+            loads[i] = started(full[1].at[i], w_out.at[i], lds.at[3 + i])
+
+    def output():
+        n = w_out.shape[-1]
+        for i in range(2):
+            loads.pop(i).wait()
+            at = slice(i * n, (i + 1) * n)
+            mid_ref[:, at] = x_ref[:, at].astype(F32) + nn(o_ref[...], w_out[i].reshape(D, n))
+
+    def finish():
+        norm_rows(mid_ref, gain_row(1), h2_ref)
+        copy = remote_copy(h2_ref, h2_other, h2_sems.at[0], h2_sems.at[1], {"c": 1 - c})
+        copy.start()
+        sent.append(copy.wait)
+
+    third = heads // 3
+    plan = {
+        2: lambda ready: start_norm(ready),
+        5: lambda ready: start_project(ready),
+        6: lambda ready: (project(0), project(1), [halo(d, True) for d in range(1, reach + 1)]),
+        7: lambda ready: (start_attention(), attention(0, third), start_output(ready)),
+        8: lambda ready: attention(third, third),
+        9: lambda ready: attention(2 * third, third),
+        10: lambda ready: output(),
+        11: lambda ready: finish(),
+    }
+
+    def work(t, ready):
+        if t in plan:
+            plan[t](ready)
+
+    gather_kernel(
+        [True, True, True, False], chunks, S, own, full, sems, small_own, small_full, work
+    )
+    for wait in sent:
+        wait()
+
+
+def forward(own, small, x, cos, sin, q_ids, k_ids, heads, S, cid):
+    piece, D = x.shape
+    keys = k_ids.shape[0]
+    r, gate_cols = own[3].shape[2:]
+    rf = own[2].shape[3]
+    half_in, half_out = own[0].shape[-1], own[1].shape[-1]
+    chunks = [(0, 0, r, 0, half_in), (1, 0, r, 0, half_out)]
+    chunks += [(2, i, 48, 0, half_out) for i in range(0, rf, 48)]
+    chunks += [
+        (3, i, 16, j, gate_cols // 2) for j in (0, gate_cols // 2) for i in range(0, r, 16)
+    ]
+
+    def body(*refs):
+        forward_kernel(heads, chunks, S, *refs)
+
+    def shape(*dims, dtype=BF):
+        return jax.ShapeDtypeStruct(dims, dtype)
+
+    outs = [shape(2, S, *o.shape[1:]) for o in own[:3]] + [shape(S, *own[3].shape)]
+    outs += [
+        shape(S, *small.shape),
+        shape(piece, D),
+        shape(piece, heads * HEAD),
+        shape(keys, HEAD),
+        shape(keys, HEAD),
+        shape(piece, heads * HEAD),
+        shape(heads, 1, piece, dtype=F32),
+        shape(piece, D, dtype=F32),
+        shape(piece, D),
+        shape(piece, D),
+    ]
+    dma = pltpu.SemaphoreType.DMA
+    return pl.pallas_call(
+        body,
+        out_shape=tuple(outs),
+        in_specs=[VM] * 10,
+        out_specs=tuple([ANY] * 5 + [VM] * 8 + [ANY]),
+        scratch_shapes=[
+            pltpu.VMEM((2, S) + own[0].shape[1:], BF),
+            pltpu.VMEM((2, S) + own[1].shape[1:], BF),
+            pltpu.VMEM((S,) + small.shape, BF),
+            pltpu.VMEM((piece, half_in), F32),
+            pltpu.VMEM((keys, 2 * HEAD), BF),
+            pltpu.VMEM((keys, piece), F32),
+            pltpu.VMEM((HEAD, keys), BF),
+            dma((5,)),
+            dma((2,)),
+            dma((2,)),
+            dma((2,)),
+        ]
+        + gather_sems(4, len(chunks), S),
+        compiler_params=pltpu.CompilerParams(
+            collective_id=cid, has_side_effects=True, vmem_limit_bytes=VMEM_BYTES
+        ),
+    )(*own, small, x, cos, sin, q_ids, k_ids)
+
+
+def back_step(h, first, rows, refs, bias, kt):
+    q_ref, k_ref, v_ref, o_ref, do_ref, l_ref, dq_ref, dk_ref, dv_ref = refs
     span = WINDOW + rows
-    vt[...] = v_ref[...].T
-    factor = HEAD ** -0.5 * LOG2E
-    for block in range(piece // rows):
-        first = block * rows
-        fill_bias(bias, q_ids, k_ids, first, rows, span)
-        live = q_ids[:1, pl.ds(first, rows)] != 0
-        @pl.loop(0, heads)
-        def _(h):
-            cols = pl.ds(pl.multiple_of(h * HEAD, HEAD), HEAD)
-            q = q_ref[pl.ds(first, rows), cols]
-            s = nt(k_ref[pl.ds(first, span), :], q) * factor + bias[...]
-            top = jnp.max(s, axis=0, keepdims=True)
-            p = jnp.exp2(s - top)
-            total = jnp.sum(p, axis=0, keepdims=True)
-            o = nn(vt[:, pl.ds(first, span)], p.astype(BF))
-            o = jnp.where(live, o * (1.0 / total), 0.0)
-            o_ref[pl.ds(first, rows), cols] = o.T.astype(BF)
-            l_ref[h, :, pl.ds(first, rows)] = top + jnp.log2(total)
-
-def bwd_kernel(heads, rows, q_ids, k_ids, q_ref, k_ref, v_ref, o_ref, do_ref, l_ref, dq_ref, dk_ref, dv_ref, bias, kt):
-    piece = q_ref.shape[0]
-    span = WINDOW + rows
+    factor = HEAD**-0.5 * LOG2E
+    cols = pl.ds(h * HEAD, HEAD)
+    q = q_ref[pl.ds(first, rows), cols]
+    do = do_ref[pl.ds(first, rows), cols]
+    o = o_ref[pl.ds(first, rows), cols]
+    delta = jnp.sum((do.astype(F32) * o.astype(F32)).T, axis=0, keepdims=True)
+    s = nt(k_ref[pl.ds(first, span), :], q) * factor + bias[...]
+    p = jnp.exp2(s - l_ref[h, :, pl.ds(first, rows)])
+    dp = nt(v_ref[pl.ds(first, span), :], do)
+    ds = (p * ((dp - delta) * HEAD**-0.5)).astype(BF)
+    dv_ref[pl.ds(first, span), :] += nn(p.astype(BF), do)
+    dk_ref[pl.ds(first, span), :] += nn(ds, q)
+    dq_ref[pl.ds(first, rows), cols] = nn(kt[:, pl.ds(first, span)], ds).T
+
+
+def bwd_kernel(heads, rows, q_ids, k_ids, *refs):
+    *arrays, bias, kt = refs
+    q_ref, k_ref = arrays[:2]
+    dk_ref, dv_ref = arrays[-2:]
     kt[...] = k_ref[...].T
-    factor = HEAD ** -0.5 * LOG2E
     dk_ref[...] = jnp.zeros_like(dk_ref)
     dv_ref[...] = jnp.zeros_like(dv_ref)
-    for block in range(piece // rows):
-        first = block * rows
-        fill_bias(bias, q_ids, k_ids, first, rows, span)
-        @pl.loop(0, heads, unroll=2)
-        def _(h):
-            cols = pl.ds(pl.multiple_of(h * HEAD, HEAD), HEAD)
-            q = q_ref[pl.ds(first, rows), cols]
-            do = do_ref[pl.ds(first, rows), cols]
-            o = o_ref[pl.ds(first, rows), cols]
-            delta = jnp.sum((do.astype(F32) * o.astype(F32)).T, axis=0, keepdims=True)
-            s = nt(k_ref[pl.ds(first, span), :], q) * factor + bias[...]
-            p = jnp.exp2(s - l_ref[h, :, pl.ds(first, rows)])
-            dp = nt(v_ref[pl.ds(first, span), :], do)
-            ds = (p * ((dp - delta) * HEAD ** -0.5)).astype(BF)
-            dv_ref[pl.ds(first, span), :] += nn(p.astype(BF), do)
-            dk_ref[pl.ds(first, span), :] += nn(ds, q)
-            dq_ref[pl.ds(first, rows), cols] = nn(kt[:, pl.ds(first, span)], ds).T
+    for first in range(0, q_ref.shape[0], rows):
+        fill_bias(bias, q_ids, k_ids, first, rows, WINDOW + rows)
+        for h in range(heads):
+            back_step(h, first, rows, arrays, bias, kt)
 
 
 def attend(q_ids, k_ids, q, k, v, heads, rows):
@@ -401,27 +615,35 @@
     )(q_ids, k_ids, q, k, v, o, do, l)
 
 
-def mlp_kernel(where, two_ref, df_ref, gate_ref, up_ref, down_ref, two_t, hid_t, grads, out, back):
+def mlp_kernel(
+    where, two_own, two_other, df_own, df_other, gate_ref, up_ref, down_ref, *results
+):
+    two_t, hid_t, grads, out, back = results
     step = pl.program_id(0)
-    tile = gate_ref.shape[1]
+    rows, D = two_own.shape
     half = down_ref.shape[2]
-    rows = 256
+    part = two_t.shape[0]
+    core = where[0]
+    places = [
+        pl.ds(pl.multiple_of(core * rows, rows), rows),
+        pl.ds(pl.multiple_of((1 - core) * rows, rows), rows),
+    ]
 
     @pl.when(step == 0)
     def _():
         out[...] = jnp.zeros_like(out)
         back[...] = jnp.zeros_like(back)
 
-    part = two_t.shape[0]
-    two_t[...] = two_ref[:, pl.ds(pl.multiple_of(step * part, part), part)].T
-
-    @pl.loop(0, two_ref.shape[0] // rows)
-    def _(i):
-        at = pl.ds(pl.multiple_of(i * rows, rows), rows)
-        two = two_ref[at, :]
-        gate = nn(two, gate_ref[...])
-        up = nn(two, up_ref[...])
-        grad = nt(df_ref[at, :half], down_ref[0]) + nt(df_ref[at, half:], down_ref[1])
+    @pl.when(step < D // part)
+    def _():
+        cols = pl.ds(pl.multiple_of(step * part, part), part)
+        for two_ref, at in zip((two_own, two_other), places):
+            two_t[:, at] = two_ref[:, cols].T
+
+    for two_ref, df_ref, at in zip((two_own, two_other), (df_own, df_other), places):
+        gate = nn(two_ref[...], gate_ref[...])
+        up = nn(two_ref[...], up_ref[...])
+        grad = nt(df_ref[:, :half], down_ref[0]) + nt(df_ref[:, half:], down_ref[1])
         slope = 0.7978845608028654
         bent = jnp.tanh(slope * (gate + 0.044715 * (gate * gate * gate)))
         upper = 0.5 * (1.0 + bent)
@@ -441,35 +663,38 @@
 
 
 def mlp_call(core, two, df, gate_full, down_full):
-    T, D = two.shape
+    T, D = 2 * two[0].shape[0], two[0].shape[1]
     half_ff = gate_full.shape[1] // 2
-    tile = 384
+    tile = 256
     tiles = half_ff // tile
     half = down_full.shape[2]
-    part = D // tiles
-
-    def body(where, *refs):
-        mlp_kernel(where, *refs)
-
-    whole = pl.BlockSpec((T, D), lambda i, w: (0, 0))
+    last = D // tile - 1
+
+    def body(*refs):
+        mlp_kernel(*refs)
+
+    once = pl.Buffered(1)
+    piece = pl.BlockSpec((T // 2, D), lambda i, w: (0, 0), pipeline_mode=once)
     return pl.pallas_call(
         body,
         grid_spec=pltpu.PrefetchScalarGridSpec(
             num_scalar_prefetch=1,
             grid=(tiles,),
             in_specs=[
-                whole,
-                whole,
+                piece,
+                piece,
+                piece,
+                piece,
                 pl.BlockSpec((D, tile), lambda i, w: (0, i)),
                 pl.BlockSpec((D, tile), lambda i, w: (0, tiles + i)),
                 pl.BlockSpec((2, tile, half), lambda i, w: (0, w[0] * tiles + i, 0)),
             ],
             out_specs=[
-                pl.BlockSpec((part, T), lambda i, w: (i, 0)),
+                pl.BlockSpec((tile, T), lambda i, w: (jnp.minimum(i, last), 0)),
                 pl.BlockSpec((tile, T), lambda i, w: (i, 0)),
                 pl.BlockSpec((2, T, tile), lambda i, w: (0, 0, i)),
-                whole,
-                whole,
+                pl.BlockSpec((T, D), lambda i, w: (0, 0)),
+                pl.BlockSpec((T, D), lambda i, w: (0, 0)),
             ],
         ),
         out_shape=[
@@ -485,16 +710,22 @@
         cost_estimate=pl.CostEstimate(
             flops=12 * T * D * half_ff, bytes_accessed=40 * 2**20, transcendentals=T * half_ff
         ),
-    )(core, two, df, gate_full, gate_full, down_full)
-
-
-def reduce_kernel(sides, parts, S, two, hid_own, hid_other, grads, df, out, *scratch):
-    left, right, s1, g1, s2, g2, fz, gz, mine, *sems = scratch
-    lds, rds, s1s, s1r, s2s, s2r, zs, zr, ls, xs, xr, ys, yr, cs, cr = sems
+    )(core, *two, *df, gate_full, gate_full, down_full)
+
+
+def reduce_kernel(heads, sides, parts, S, two, hid_own, hid_other, flat, grads, df, da, *more):
+    q_ids, k_ids, *given = more[:8]
+    out, *found = more[8:12]
+    left, right, tail_right, s1, g1, s2, g2, fz, gz, mine, bias, kt, *sems = more[12:]
+    arrays = given + found
+    rows = given[0].shape[0] // 2
+    ts, lds, rds, s1s, s1r, s2s, s2r, zs, zr, ls, xs, xr, ys, yr, cs, cr = sems
     groups, _, _, r, T = left.shape
     n = right.shape[2]
     wide = sides * parts
-    nc = wide + groups - 1
+    last = wide + groups - 1
+    nc = last + 1
+    slots = g1.shape[0]
     y, x, c, z = (lax.axis_index(a) for a in ("y", "x", "c", "z"))
     k = y * 2 + x
     kx = y * 2 + 1 - x
@@ -515,6 +746,8 @@
             h, kk = p // 4, p % 4
             if g == 0:
                 fetch(("l", 0), two.at[:, kk, h], left.at[0, p], lds.at[0, p, 0])
+            elif g == groups:
+                fetch(("l", g), flat.at[:, kk, h], left.at[0, p], lds.at[g, p, 0])
             else:
                 for i, (src, cc) in enumerate(((hid_own, c), (hid_other, 1 - c))):
                     dst = left.at[g, p, pl.ds(cc * (S // 2), S // 2)]
@@ -533,6 +766,9 @@
     def landed(key):
         for copy in loads.pop(key, []):
             copy.wait()
+
+    def group_of(t):
+        return max(0, t - wide + 1)
 
     fetch_right(0)
     fetch_left(0)
@@ -551,8 +787,20 @@
         )
 
     def product(t, p):
-        g = max(0, t - wide + 1)
-        return nn(left[g, p].reshape(S * r, T), right[slot_of(t)])
+        if t == last:
+            return nn(left[0, p].reshape(S * r, T), tail_right[...])
+        return nn(left[group_of(t), p].reshape(S * r, T), right[slot_of(t)])
+
+    half_rows = da.shape[0]
+    place = pl.ds(pl.multiple_of(c * half_rows, half_rows), half_rows)
+    other_place = pl.ds(pl.multiple_of((1 - c) * half_rows, half_rows), half_rows)
+    keep = pl.ds(pl.multiple_of(c * n, n), n)
+    give = pl.ds(pl.multiple_of((1 - c) * n, n), n)
+    fetch(("r", last), da.at[:, keep], tail_right.at[place], ts.at[0])
+    given_copy = remote(da.at[:, give], tail_right.at[place], ts.at[1], ts.at[2], to_c)
+    given_copy.start()
+    other = tail_right.at[other_place]
+    other_copy = remote(other, other, ts.at[1], ts.at[2], to_c)
 
     pending = {}
 
@@ -566,17 +814,20 @@
 
     def first(t):
         slot = t % 2
-        landed(("l", max(0, t - wide + 1)))
+        landed(("l", group_of(t)))
         landed(("r", t))
+        if t == last:
+            other_copy.wait_recv()
+            given_copy.wait_send()
         drain(("s1", t - 2))
 
         for i in range(2):
             for j, p, target in ((i, i * 2 + 1 - x, to_x), (2 + i, 4 + (1 - y) * 2 + i, to_y)):
                 s1[slot, j] = product(t, p).astype(BF)
-                launch(("s1", t), remote(s1.at[slot, j], g1.at[t, j], s1s.at[t, j], s1r.at[t, j], target))
+                launch(("s1", t), remote(s1.at[slot, j], g1.at[t % slots, j], s1s.at[t, j], s1r.at[t, j], target))
 
     def got1(t, j):
-        remote(g1.at[t, j], g1.at[t, j], s1s.at[t, j], s1r.at[t, j], to_x).wait_recv()
+        remote(g1.at[t % slots, j], g1.at[t % slots, j], s1s.at[t, j], s1r.at[t, j], to_x).wait_recv()
 
     def second(t):
         slot = t % 2
@@ -584,15 +835,15 @@
         for j in range(4):
             got1(t, j)
         for h, p, j, target in ((0, (1 - y) * 2 + x, 1 - y, to_y), (1, 4 + y * 2 + 1 - x, 3 - x, to_x)):
-            s2[slot, h] = (product(t, p) + g1[t, j].astype(F32)).astype(BF)
-            launch(("s2", t), remote(s2.at[slot, h], g2.at[t, h], s2s.at[t, h], s2r.at[t, h], target))
+            s2[slot, h] = (product(t, p) + g1[t % slots, j].astype(F32)).astype(BF)
+            launch(("s2", t), remote(s2.at[slot, h], g2.at[t % slots, h], s2s.at[t, h], s2r.at[t, h], target))
 
     def third(t):
         slot = t % 2
         drain(("z", t - 2))
         for h, p, j in ((0, k, y), (1, 4 + k, 2 + x)):
-            remote(g2.at[t, h], g2.at[t, h], s2s.at[t, h], s2r.at[t, h], to_x).wait_recv()
-            total = (product(t, p) + g1[t, j].astype(F32) + g2[t, h].astype(F32)).astype(BF)
+            remote(g2.at[t % slots, h], g2.at[t % slots, h], s2s.at[t, h], s2r.at[t, h], to_x).wait_recv()
+            total = (product(t, p) + g1[t % slots, j].astype(F32) + g2[t % slots, h].astype(F32)).astype(BF)
             for zz in range(S):
                 fz[slot, zz, h] = total[zz * r : (zz + 1) * r]
         for e in range(1, S):
@@ -640,12 +891,28 @@
         p = out.at[t, :, c]
         launch("end", remote(p, p, cs.at[t], cr.at[t], to_c))
 
+    steps = [(block, h) for block in range(2) for h in range(heads)]
+
+    def attention(t):
+        if t == 0:
+            kt[...] = given[1][...].T
+            found[1][...] = jnp.zeros_like(found[1])
+            found[2][...] = jnp.zeros_like(found[2])
+        for block, h in steps[2 * t : 2 * t + 2]:
+            if h == 0:
+                fill_bias(bias, q_ids, k_ids, block * rows, rows, WINDOW + rows)
+            back_step(h, block * rows, rows, arrays, bias, kt)
+
     stages = (first, second, third, fourth, fifth, sixth)
     for t in range(nc + len(stages) - 1):
         for lag, stage in enumerate(stages):
             if 0 <= t - lag < nc:
                 stage(t - lag)
+            if lag == 0:
+                attention(t)
         fetch_right(t + 2)
+        if t == wide + 2:
+            fetch_left(groups)
     for t in range(nc):
         p = out.at[t, :, 1 - c]
         remote(p, p, cs.at[t], cr.at[t], to_c).wait_recv()
@@ -653,37 +920,48 @@
         drain(key) if key[0] != "l" else [copy.wait() for copy in pending.pop(key)]
 
 
-def reduced(two_t, hid_own, hid_other, grads, df, S, cid):
+def reduced(two_t, hid_own, hid_other, flat_t, grads, df, da, attention, heads, S, cid):
     D, T = two_t.shape
     sides, _, half_ff = grads.shape
     n = df.shape[1]
     r = D // (S * 8)
     parts = half_ff // n
     groups = 1 + 2 * half_ff // (S * 8 * r)
-    nc = sides * parts + groups - 1
+    nc = sides * parts + groups
+    slots = min(nc, 6)
     m = S * r
+    queries, keys = attention[2:4]
     dma = pltpu.SemaphoreType.DMA
     hid_shape = (S // 2, groups - 1, 4, 2, r, T)
 
     def body(*refs):
-        reduce_kernel(sides, parts, S, *refs)
+        reduce_kernel(heads, sides, parts, S, *refs)
 
     return pl.pallas_call(
         body,
-        out_shape=jax.ShapeDtypeStruct((nc, 4, 2, 2, r, n), BF),
-        in_specs=[ANY] * 5,
-        out_specs=ANY,
+        out_shape=(
+            jax.ShapeDtypeStruct((nc, 4, 2, 2, r, n), BF),
+            jax.ShapeDtypeStruct(queries.shape, F32),
+            jax.ShapeDtypeStruct(keys.shape, F32),
+            jax.ShapeDtypeStruct(keys.shape, F32),
+        ),
+        in_specs=[ANY] * 7 + [VM] * 8,
+        out_specs=(ANY, VM, VM, VM),
         scratch_shapes=[
             pltpu.VMEM((groups, 8, S, r, T), BF),
             pltpu.VMEM((5, T, n), BF),
+            pltpu.VMEM((T, n), BF),
             pltpu.VMEM((2, 4, m, n), BF),
-            pltpu.VMEM((nc, 4, m, n), BF),
+            pltpu.VMEM((slots, 4, m, n), BF),
             pltpu.VMEM((2, 2, m, n), BF),
-            pltpu.VMEM((nc, 2, m, n), BF),
+            pltpu.VMEM((slots, 2, m, n), BF),
             pltpu.VMEM((2, S, 2, r, n), BF),
             pltpu.VMEM((nc, S - 1, 2, r, n), BF),
             pltpu.VMEM((2, 2, r, n), BF),
-            dma((groups, 8, 2)),
+            pltpu.VMEM((WINDOW + queries.shape[0] // 2, queries.shape[0] // 2), F32),
+            pltpu.VMEM((HEAD, keys.shape[0]), BF),
+            dma((3,)),
+            dma((groups + 1, 8, 2)),
             dma((nc,)),
             dma((nc, 4)),
             dma((nc, 4)),
@@ -709,66 +987,95 @@
         two_t.reshape(S, 4, 2, r, T),
         hid_own.reshape(hid_shape),
         hid_other.reshape(hid_shape),
+        flat_t.reshape(S, 4, 2, r, T),
         grads,
         df,
+        da,
+        *attention,
     )
 
 
-def adam_kernel(total, count_ref, rates_ref, g_ref, w_ref, m_ref, g_out, w_out, m_out):
+def adam_kernel(total, tiles, gains, count_ref, rates_ref, g_ref, w_ref, m_ref, g_out, w_out, m_out, *more):
     step_value = count_ref[0].astype(F32)
     log_first = jnp.log(jnp.full((8, 128), beta_first, F32))
     log_second = jnp.log(jnp.full((8, 128), beta_second, F32))
-    fix_first = (1.0 - jnp.exp(step_value * log_first))[:1, :1]
-    fix_second = (1.0 - jnp.exp(step_value * log_second))[:1, :1]
-    grad = g_ref[0, 0, 0].reshape(w_ref.shape).astype(F32) / total
-    w = w_ref[...]
-    first = beta_first * m_ref[0] + (1.0 - beta_first) * grad
-    second = beta_second * m_ref[1] + (1.0 - beta_second) * grad * grad
-    step = first / fix_first / (jnp.sqrt(second / fix_second) + adam_eps) + rates_ref[1] * w
-    g_out[...] = grad
-    w_out[...] = w - rates_ref[0] * step
-    m_out[0] = first
-    m_out[1] = second
-
-
-def adam_call(weight, moments, grads, count, rates, total, base, sides, tiles, down):
+    unfix_first = (1.0 / (1.0 - jnp.exp(step_value * log_first)))[:1, :1]
+    unfix_second = (1.0 / (1.0 - jnp.exp(step_value * log_second)))[:1, :1]
+    rate, decay = rates_ref[0], rates_ref[1]
+    rows = w_ref.shape[0]
+    n = w_ref.shape[1] // tiles
+
+    @pl.when((pl.program_id(1) == 0) & (pl.program_id(2) == 0))
+    def _():
+        more[0][...] = jnp.zeros_like(more[0])
+
+    for i in range(tiles):
+        at = pl.ds(i * n, n)
+        grad = g_ref[i, 0, 0].reshape(rows, n).astype(F32) * (1.0 / total)
+        w = w_ref[:, at]
+        first = beta_first * m_ref[0, :, at] + (1.0 - beta_first) * grad
+        second = beta_second * m_ref[1, :, at] + (1.0 - beta_second) * grad * grad
+        step = first * unfix_first / (jnp.sqrt(second * unfix_second) + adam_eps) + decay * w
+        g_out[:, at] = grad
+        w_out[:, at] = w - rate * step
+        m_out[0, :, at] = first
+        m_out[1, :, at] = second
+        if gains:
+            both = w.astype(BF).astype(F32) * grad
+            for j in range(0, n, 128):
+                more[0][...] += both[:, j : j + 128]
+
+
+def adam_call(
+    weight, moments, grads, count, rates, total, base, sides, tiles, down=False, gains=False, cores=(0, 1), held=None
+):
     _, _, _, _, r, n = grads.shape
+    wide = 1 if down else tiles
 
     def g_place(kk, cc, ss, tt):
-        return (base + ss * tiles + tt, kk, cc, 0, 0, 0)
+        return (base // wide + ss + tt, kk, cores[0] + cc, 0, 0, 0)
 
     def place(kk, cc, ss, tt):
-        if down:
-            return (tt * 4 + kk, cc)
-        return (kk, (ss * 2 + cc) * tiles + tt)
+        return (tt * 4 + kk, ss * 2 + cores[0] + cc)
 
     def m_place(*at):
         return (0,) + place(*at)
 
-    w_spec = pl.BlockSpec((2 * r, n), place)
-    m_spec = pl.BlockSpec((2, 2 * r, n), m_place)
+    w_spec = pl.BlockSpec((2 * r, wide * n), place)
+    m_spec = pl.BlockSpec((2, 2 * r, wide * n), m_place)
     smem = pl.BlockSpec(memory_space=pltpu.SMEM)
+    like = jax.ShapeDtypeStruct(weight.shape, F32)
+    out_specs = [w_spec, w_spec, m_spec]
+    out_shape = [like, like, jax.ShapeDtypeStruct(moments.shape, F32)]
+    if gains:
+        out_specs.append(pl.BlockSpec((2 * r, 128), lambda kk, cc, ss, tt: (kk, 0)))
+        out_shape.append(jax.ShapeDtypeStruct((weight.shape[0], 128), F32))
+    else:
+        out_specs.append(pl.BlockSpec((8, 128), lambda *at: (0, 0)))
+        out_shape.append(jax.ShapeDtypeStruct((8, 128), F32))
+    before = [] if held is None else list(held[:3])
 
     def body(*refs):
-        adam_kernel(total, *refs)
+        five, results = refs[:5], refs[5 + len(before) :]
+        adam_kernel(total, wide, gains, *five, *results)
 
     return pl.pallas_call(
         body,
-        grid=(4, 2, sides, tiles),
-        in_specs=[smem, smem, pl.BlockSpec((1, 1, 1, 2, r, n), g_place), w_spec, m_spec],
-        out_specs=[w_spec, w_spec, m_spec],
-        out_shape=[
-            jax.ShapeDtypeStruct(weight.shape, F32),
-            jax.ShapeDtypeStruct(weight.shape, F32),
-            jax.ShapeDtypeStruct(moments.shape, F32),
-        ],
+        grid=(4, len(cores), sides, tiles // wide),
+        in_specs=[smem, smem, pl.BlockSpec((wide, 1, 1, 2, r, n), g_place), w_spec, m_spec]
+        + [ANY] * len(before),
+        out_specs=out_specs,
+        out_shape=out_shape,
+        input_output_aliases={5 + i: i for i in range(len(before))},
         compiler_params=pltpu.CompilerParams(
             dimension_semantics=("arbitrary",) * 4, vmem_limit_bytes=VMEM_BYTES
         ),
         cost_estimate=pl.CostEstimate(
-            flops=20 * weight.size, bytes_accessed=30 * weight.size, transcendentals=weight.size
+            flops=10 * len(cores) * weight.size,
+            bytes_accessed=15 * len(cores) * weight.size,
+            transcendentals=weight.size,
         ),
-    )(count, rates, grads, weight, moments)
+    )(count, rates, grads, weight, moments, *before)
 
 
 def dot(a, b):
@@ -783,38 +1090,47 @@
     return lax.dot_general(a, b, (((1,), (1,)), ((), ())), preferred_element_type=F32)
 
 
-def plane_sum(left, right, zb):
+def arranged(left, S):
+    T, D = left.shape
+    r = D // (S * 8)
+    return left.T.reshape(S, 2, 2, 2, r, T).transpose(3, 1, 2, 0, 4, 5)
+
+
+def plane_sum(rows, right, between, S):
     y = lax.axis_index("y")
     x = lax.axis_index("x")
-    T, M = left.shape
+    r, T = rows.shape[4:]
     N = right.shape[1]
-    r = M // (zb * 8)
-    rows = left.T.reshape(zb, 2, 2, 2, r, T).transpose(3, 1, 2, 0, 4, 5)
 
     def pick(h, yy, xx):
         block = lax.dynamic_index_in_dim(rows[h], yy, 0, keepdims=False)
-        return lax.dynamic_index_in_dim(block, xx, 0, keepdims=False).reshape(zb * r, T)
-
-    sent0 = jnp.concatenate([pick(0, 0, 1 - x), pick(0, 1, 1 - x)], axis=0)
-    sent1 = jnp.concatenate([pick(1, 1 - y, 0), pick(1, 1 - y, 1)], axis=0)
-    got0 = swapped(dot_rows(sent0, right).astype(BF), "x").reshape(2, zb * r, N)
-    got1 = swapped(dot_rows(sent1, right).astype(BF), "y").reshape(2, zb * r, N)
+        return lax.dynamic_index_in_dim(block, xx, 0, keepdims=False).reshape(S * r, T)
+
+    first0 = jnp.concatenate([pick(0, 0, 1 - x), pick(0, 1, 1 - x)], axis=0)
+    first1 = jnp.concatenate([pick(1, 1 - y, 0), pick(1, 1 - y, 1)], axis=0)
+    sent = (dot_rows(first0, right).astype(BF), dot_rows(first1, right).astype(BF))
+    sent = between(0, sent)
+    got0 = swapped(sent[0], "x")
+    got1 = swapped(sent[1], "y")
+    got0, got1 = between(1, (got0, got1))
+    got0 = got0.reshape(2, S * r, N)
+    got1 = got1.reshape(2, S * r, N)
 
     def at(got, i):
         return lax.dynamic_index_in_dim(got, i, 0, keepdims=False).astype(F32)
 
-    next0 = swapped((dot_rows(pick(0, 1 - y, x), right) + at(got0, 1 - y)).astype(BF), "y")
-    next1 = swapped((dot_rows(pick(1, y, 1 - x), right) + at(got1, 1 - x)).astype(BF), "x")
+    sent = (
+        (dot_rows(pick(0, 1 - y, x), right) + at(got0, 1 - y)).astype(BF),
+        (dot_rows(pick(1, y, 1 - x), right) + at(got1, 1 - x)).astype(BF),
+    )
+    sent = between(2, sent)
+    next0 = swapped(sent[0], "y")
+    next1 = swapped(sent[1], "x")
+    next0, next1 = between(3, (next0, next1))
     last0 = dot_rows(pick(0, y, x), right) + at(got0, y) + next0.astype(F32)
     last1 = dot_rows(pick(1, y, x), right) + at(got1, x) + next1.astype(F32)
-    both = [v.astype(BF).reshape(zb, 1, r, N) for v in (last0, last1)]
-    return jnp.concatenate(both, axis=1)
-
-
-def handed_out(share):
-    S, _, r, N = share.shape
-    mine = lax.psum_scatter(share.reshape(S, 2 * r, N), "z", scatter_dimension=0, tiled=False)
-    return lax.all_gather(mine, ("y", "x", "c"), axis=0).reshape(4, 2, 2 * r, N)
+    both = [v.astype(BF).reshape(S, 1, r, N) for v in (last0, last1)]
+    return jnp.concatenate(both, axis=1).reshape(S, 2 * r, N)
 
 
 def on_device(
@@ -864,49 +1180,14 @@
         axis=1,
     ).astype(BF)
 
-    if fast:
-        in_full, out_full = gathered(
-            [
-                halves(in_low).reshape(2, 4, 2, r, in_half),
-                halves(out_low).reshape(2, 4, 2, r, d_half),
-            ],
-            [True, True],
-            [(0, 0, r), (1, 0, r)],
-            S,
-            0,
-        )
-        in_full = in_full.reshape(2, D, in_half)
-        out_full = out_full.reshape(2, D, d_half)
-    else:
-        in_full = halves(lax.all_gather(in_low, "z", axis=0, tiled=True))
-        out_full = halves(lax.all_gather(out_low, "z", axis=0, tiled=True))
-        down_full = halves(lax.all_gather(down_low, "z", axis=0, tiled=True))
-        gate_full = lax.all_gather(gate_low, "z", axis=0, tiled=True)
-    gains_full = lax.all_gather(norm_gains.astype(BF), "z", axis=1, tiled=True)
-
-    gains_wide = gains_full.astype(F32)
+    gains_low = norm_gains.astype(BF)
     tokens = block_in[0].astype(F32)
     piece_len = tokens.shape[0]
     width_q = HEADS * HEAD
     positions = seq_place * piece_len + jnp.arange(piece_len, dtype=jnp.int32)
-    normed = root_norm(tokens, gains_wide[0]).astype(BF)
-    mixed_proj = jnp.concatenate([dot(normed, in_full[0]), dot(normed, in_full[1])], axis=1)
-    queries = (
-        rotate(mixed_proj[:, :width_q].reshape(piece_len, HEADS, HEAD), positions, 1.0)
-        .astype(BF)
-        .reshape(piece_len, width_q)
-    )
-    own_keys = rotate(mixed_proj[:, width_q : width_q + HEAD], positions, 1.0)
-    own_pair = jnp.concatenate([own_keys, mixed_proj[:, width_q + HEAD :]], axis=1).astype(BF)
     reach_count = (WINDOW + piece_len - 2) // piece_len
-    earlier = []
-    for back_step in range(reach_count, 0, -1):
-        earlier.append(passed_along(own_pair, "z", back_step))
-    key_pairs = jnp.concatenate(earlier + [own_pair], axis=0)
-    key_rows = key_pairs[:, :HEAD]
-    values = key_pairs[:, HEAD:]
+    key_span = reach_count * piece_len
     segments = segment_ids[0]
-    key_span = reach_count * piece_len
     padded_ids = jnp.concatenate([jnp.full((key_span,), -1, jnp.int32), segments])
     query_ids = lax.dynamic_slice_in_dim(segments, seq_place * piece_len, piece_len)
     key_ids = lax.dynamic_slice_in_dim(padded_ids, seq_place * piece_len, key_span + piece_len)
@@ -914,28 +1195,79 @@
     query_row = query_ids[None, :]
     key_column = key_ids[:, None]
 
-    flat_heads, log_totals = attend(
-        query_row, key_column, queries, key_rows, values, HEADS, piece_len
-    )
-    middle = tokens + jnp.concatenate(
-        [dot(flat_heads, out_full[0]), dot(flat_heads, out_full[1])], axis=1
-    )
-    normed_two = root_norm(middle, gains_wide[1]).astype(BF)
-
     if fast:
-        down_full, gate_full = gathered(
+        frequency = 10000.0 ** (-2.0 * jnp.arange(HEAD // 2).astype(F32) / HEAD)
+        angles = positions.astype(F32)[:, None] * jnp.concatenate([frequency, frequency])[None, :]
+        side = jnp.where(jnp.arange(HEAD) < HEAD // 2, -1.0, 1.0)
+        cos_table, sin_table = jnp.cos(angles), jnp.sin(angles) * side
+        (
+            in_full,
+            out_full,
+            down_full,
+            gate_full,
+            gains_full,
+            normed,
+            queries,
+            key_rows,
+            values,
+            flat_heads,
+            log_totals,
+            middle,
+            normed_two,
+            two_other,
+        ) = forward(
             [
+                halves(in_low).reshape(2, 4, 2, r, in_half),
+                halves(out_low).reshape(2, 4, 2, r, d_half),
                 halves(down_low).reshape(2, 4, 2, rows_f // 8, d_half),
                 gate_low.reshape(4, 2, r, 2 * half_ff),
             ],
-            [True, False],
-            [(0, i * 48, 48) for i in range(rows_f // 8 // 48)]
-            + [(1, i * 16, 16) for i in range(r // 16)],
+            jnp.concatenate([gains_low] * 8, axis=0),
+            block_in[0],
+            cos_table,
+            sin_table,
+            query_row,
+            key_column,
+            HEADS,
             S,
-            1,
+            0,
         )
+        in_full = in_full.reshape(2, D, in_half)
+        out_full = out_full.reshape(2, D, d_half)
+        gains_full = gains_full[:, :2].transpose(1, 0, 2).reshape(2, D)
         down_full = down_full.reshape(2, FF, d_half)
         gate_full = gate_full.reshape(D, 2 * half_ff)
+        gains_wide = gains_full.astype(F32)
+    else:
+        in_full = halves(lax.all_gather(in_low, "z", axis=0, tiled=True))
+        out_full = halves(lax.all_gather(out_low, "z", axis=0, tiled=True))
+        down_full = halves(lax.all_gather(down_low, "z", axis=0, tiled=True))
+        gate_full = lax.all_gather(gate_low, "z", axis=0, tiled=True)
+        gains_full = lax.all_gather(gains_low, "z", axis=1, tiled=True)
+        gains_wide = gains_full.astype(F32)
+        normed = root_norm(tokens, gains_wide[0]).astype(BF)
+        mixed_proj = jnp.concatenate([dot(normed, in_full[0]), dot(normed, in_full[1])], axis=1)
+        queries = (
+            rotate(mixed_proj[:, :width_q].reshape(piece_len, HEADS, HEAD), positions, 1.0)
+            .astype(BF)
+            .reshape(piece_len, width_q)
+        )
+        own_keys = rotate(mixed_proj[:, width_q : width_q + HEAD], positions, 1.0)
+        own_pair = jnp.concatenate([own_keys, mixed_proj[:, width_q + HEAD :]], axis=1).astype(BF)
+        earlier = []
+        for back_step in range(reach_count, 0, -1):
+            earlier.append(passed_along(own_pair, "z", back_step))
+        key_pairs = jnp.concatenate(earlier + [own_pair], axis=0)
+        key_rows = key_pairs[:, :HEAD]
+        values = key_pairs[:, HEAD:]
+        flat_heads, log_totals = attend(
+            query_row, key_column, queries, key_rows, values, HEADS, piece_len
+        )
+        middle = tokens + jnp.concatenate(
+            [dot(flat_heads, out_full[0]), dot(flat_heads, out_full[1])], axis=1
+        )
+        normed_two = root_norm(middle, gains_wide[1]).astype(BF)
+        two_other = swapped(normed_two, "c")
 
     upstream = cotangent[0].astype(F32)
 
@@ -958,13 +1290,17 @@
         give = lax.dynamic_slice_in_dim(v, (1 - core) * piece_len, piece_len, 0)
         return keep + swapped(give.astype(BF), "c").astype(F32)
 
-    df_both = pair(cotangent[0])
+    df_other = swapped(cotangent[0], "c")
+    df_both = ordered(cotangent[0], df_other)
     normed_both = pair(normed)
     flat_both = pair(flat_heads)
-    two_both = pair(normed_two)
 
     two_t, hid_t, grad_gated, out_sum, two_sum = mlp_call(
-        core.reshape(1).astype(jnp.int32), two_both, df_both, gate_full, down_full
+        core.reshape(1).astype(jnp.int32),
+        (normed_two, two_other),
+        (cotangent[0], df_other),
+        gate_full,
+        down_full,
     )
 
     output = middle + core_sum(out_sum)
@@ -980,11 +1316,7 @@
     )
     grad_attended = jnp.where(live_rows[:, None], grad_flat, 0.0).astype(BF)
 
-    if fast:
-        df_half = lax.dynamic_slice_in_dim(df_both, core * d_half, d_half, 1)
-        mlp_sums = reduced(two_t, hid_t, swapped(hid_t, "c"), grad_gated, df_half, S, 2)
-
-    grad_query_all, grad_keys, grad_values = attend_back(
+    attention = (
         query_row,
         key_column,
         queries,
@@ -993,16 +1325,59 @@
         flat_heads,
         grad_attended,
         log_totals,
-        HEADS,
-        piece_len // 2,
     )
+    if fast:
+        df_half = lax.dynamic_slice_in_dim(df_both, core * d_half, d_half, 1)
+        mlp_sums, grad_query_all, grad_keys, grad_values = reduced(
+            two_t,
+            hid_t,
+            swapped(hid_t, "c"),
+            flat_both.T,
+            grad_gated,
+            df_half,
+            grad_branch,
+            attention,
+            HEADS,
+            S,
+            2,
+        )
+    else:
+        grad_query_all, grad_keys, grad_values = attend_back(*attention, HEADS, piece_len // 2)
     grad_pairs = jnp.concatenate([grad_keys, grad_values], axis=1)
     own_grad = grad_pairs[key_span:]
-    for back_step in range(1, reach_count + 1):
-        sent_rows = grad_pairs[
-            key_span - back_step * piece_len : key_span - (back_step - 1) * piece_len
-        ]
-        own_grad = own_grad + passed_along(sent_rows, "z", -back_step)
+    grad_pairs = grad_pairs.astype(BF)
+    sent_rows = [
+        grad_pairs[key_span - back_step * piece_len : key_span - (back_step - 1) * piece_len]
+        for back_step in range(1, reach_count + 1)
+    ]
+    token_total = piece_len * S * Y * 4 * block_in.shape[0]
+    rates = optimizer_rates
+    done = {}
+
+    def update(name, *arguments):
+        wait, weight, moments, grads, *rest = arguments
+        count, wait = lax.optimization_barrier((update_count, wait))
+        done[name] = adam_call(
+            weight, moments, grads, count, rates, float(token_total), *rest, held=done.get(name)
+        )
+        return wait
+
+    def behind(name, arrays):
+        arrays, token = lax.optimization_barrier((arrays, done[name][3]))
+        done[name] = tuple(done[name][:3]) + (token,)
+        return arrays
+
+    tiles = half_ff // d_half
+    chunk_out = 3 * tiles
+    if fast:
+        sent_rows = update(
+            "out", sent_rows, output_proj, output_moments, mlp_sums, chunk_out, 1, 1
+        )
+    got_rows = [passed_along(rows, "z", -i - 1) for i, rows in enumerate(sent_rows)]
+    if fast:
+        got_rows = behind("out", got_rows)
+    for rows in got_rows:
+        own_grad = own_grad + rows.astype(F32)
     grad_query_raw = rotate(
         grad_query_all.reshape(piece_len, HEADS, HEAD), positions, -1.0
     ).reshape(piece_len, width_q)
@@ -1016,36 +1391,43 @@
     _, norm_pull_one = jax.vjp(root_norm, tokens, gains_wide[0])
     grad_tokens_norm, grad_gain_one = norm_pull_one(grad_normed)
     block_in_grad = (grad_middle + grad_tokens_norm).astype(BF)[None]
-    gains_sum = lax.psum(jnp.stack([grad_gain_one, grad_gain_two]), ("y", "x", "c", "z"))
-    gains_mine = lax.dynamic_slice_in_dim(gains_sum, seq_place * rows_d, rows_d, 1)
-
-    token_total = piece_len * S * Y * 4 * block_in.shape[0]
     step_value = update_count[0].astype(F32)
-    rates = optimizer_rates
-    grad_half = half_pair(grad_branch)
     mixed_half = half_pair(grad_mixed)
 
     if fast:
-
-        def adam(weight, moments, grads, base, sides, tiles, down=False):
-            return adam_call(
-                weight, moments, grads, update_count, rates, float(token_total), base, sides, tiles, down
+        gains_two = []
+
+        def gate_update(wait, which):
+            wait = update(
+                "gate", wait, gate_up, gate_moments, mlp_sums, 0, 2, tiles, False, True, (which,)
             )
-
-        def summed(left, right):
-            return handed_out(plane_sum(left, right, S)).reshape(1, 4, 2, 2, r, right.shape[1])
-
-        tiles = half_ff // d_half
-        out_grad, out_new, out_mom = adam(
-            output_proj, output_moments, summed(flat_both, grad_half), 0, 1, 1
+            gains_two.append(done["gate"][3])
+            return wait
+
+        def between(i, arrays):
+            if i == 0:
+                return gate_update(arrays, 0)
+            if i == 1:
+                return behind("gate", arrays)
+            return arrays
+
+        share = plane_sum(arranged(normed_both, S), mixed_half, between, S)
+        share = update(
+            "down", share, down_weight, down_moments, mlp_sums, 2 * tiles, 1, tiles, True
         )
-        in_grad, in_new, in_mom = adam(
-            input_proj, input_moments, summed(normed_both, mixed_half), 0, 1, 1
-        )
-        gate_grad, gate_new, gate_mom = adam(gate_up, gate_moments, mlp_sums, 0, 2, tiles)
-        down_grad, down_new, down_mom = adam(
-            down_weight, down_moments, mlp_sums, 2 * tiles, 1, tiles, True
-        )
+        mine = lax.psum_scatter(share, "z", scatter_dimension=0, tiled=False)
+        mine = behind("down", mine)
+        mine = gate_update(mine, 1)
+        in_sum = lax.all_gather(mine, ("y", "x", "c"), axis=0)
+        in_sum = behind("gate", in_sum).reshape(1, 4, 2, 2, r, in_half)
+        update("in", in_sum, input_proj, input_moments, in_sum, 0, 1, 1, False, True)
+        in_grad, in_new, in_mom, gain_one = done["in"]
+        out_grad, out_new, out_mom, _ = done["out"]
+        gate_grad, gate_new, gate_mom, _ = done["gate"]
+        down_grad, down_new, down_mom, _ = done["down"]
+        gain_grad = jnp.stack(
+            [jnp.sum(v, axis=1) for v in (gain_one, gains_two[0] + gains_two[1])]
+        ) / gains_low.astype(F32)
     else:
 
         def adam(weight, moments, grad):
@@ -1058,6 +1440,8 @@
             mine = lax.psum_scatter(whole, "z", scatter_dimension=0, tiled=True)
             return lax.psum(mine, ("y", "x"))
 
+        two_both = ordered(normed_two, two_other)
+        grad_half = half_pair(grad_branch)
         gate_half = [summed(two_both, grad_gated[side]) for side in range(2)]
         gate_sum = jnp.concatenate(
             [lax.all_gather(g, "c", axis=1, tiled=True) for g in gate_half], axis=1
@@ -1071,7 +1455,8 @@
         in_grad, in_new, in_mom = adam(input_proj, input_moments, in_total)
         gate_grad, gate_new, gate_mom = adam(gate_up, gate_moments, gate_sum)
         down_grad, down_new, down_mom = adam(down_weight, down_moments, down_sum)
-    gain_grad = gains_mine / token_total
+        gains_sum = lax.psum(jnp.stack([grad_gain_one, grad_gain_two]), ("y", "x", "c", "z"))
+        gain_grad = lax.dynamic_slice_in_dim(gains_sum, seq_place * rows_d, rows_d, 1) / token_total
     gains_step, gain_moments_new = adamw_step(norm_gains, gain_moments, gain_grad, step_value, rates)
     return (
         block_out,

time: 979 us -> 795 us (0.81)
  Pallas kernels: 657 us -> 604 us
  blocking collectives: 49.3 us -> 0 us
  matrix products: 42.3 us -> 18.9 us
  other arithmetic: 67.5 us -> 50 us
  waiting for transfers between devices: 53.2 us -> 40.1 us
  local copies, waits for them, and re-layouts: 65.3 us -> 52.7 us
  starting transfers between devices: 19.3 us -> 8.52 us
    psum x1 -> x0, blocking collectives: 37.4 us -> none  [on_device(): lax.psum(jnp.stack([grad_gain_one, grad_gain_two]), ('y', 'x', 'c', 'z'))]
    pallas_call x9 -> x7, Pallas kernels: 580 us -> 543 us  [the longest x1 261 us: reduced(): pl.pallas_call(body, out_shape=(jax.ShapeDtypeStruct((nc, 4, 2, 2, r, n),...]
    ppermute x17 -> x11, waiting for transfers between devices: 28.5 us -> 8.01 us  [swapped(): return lax.ppermute(block, axis, [(0, 1), (1, 0)])]
    reduce_scatter x2 -> x1, waiting for transfers between devices: 0.02 us -> 19.9 us  [on_device(): mine = lax.psum_scatter(share, 'z', scatter_dimension=0, tiled=False)]
    pallas_call x1, Pallas kernels: 76.4 us -> 60.2 us  [mlp_call(): pl.pallas_call(body, grid_spec=pltpu.PrefetchScalarGridSpec(num_scalar_pr...]
    dot_general x12 -> x6, matrix products: 21.9 us -> 8.98 us  [dot_rows(): lax.dot_general(a, b, (((1,), (0,)), ((), ())), preferred_element_type=F32)]
    all_gather x1 -> x0, blocking collectives: 11.9 us -> none  [on_device(): gains_full = lax.all_gather(norm_gains.astype(BF), 'z', axis=1, tiled=True)]
    ppermute x4 -> x2, waiting for transfers between devices: 24 us -> 12.2 us  [passed_along(): return lax.ppermute(block, axis, route)]
  transfers between devices with their start and end apart: 25 -> 15, of which waited for: 9 -> 5; matrix products, arithmetic and copies ran while one was open for 14% -> 12% of each run, Pallas kernels for 59% -> 42%
where the time goes in v3:
time: 795 us; the launch traced here: 790 us
  Pallas kernels  604 us (76%)
  local copies, waits for them, and re-layouts  52.7 us (7%)
  other arithmetic  50 us (6%)
  waiting for transfers between devices  40.1 us (5%)
  matrix products  18.9 us (2%)
  between operations  15.6 us (2%)
  starting transfers between devices  8.52 us (1%)
    pallas_call x1, Pallas kernels, reduced(): pl.pallas_call(body, out_shape=(jax.ShapeDtypeStruct((nc, 4, 2, 2, r, n),...  261 us
    pallas_call x1, Pallas kernels, forward(): pl.pallas_call(body, out_shape=tuple(outs), in_specs=[VM] * 10, out_specs...  189 us
    pallas_call x5, Pallas kernels, adam_call(): pl.pallas_call(body, grid=(4, len(cores), sides, tiles // wide), in_specs...  93.3 us
    pallas_call x1, Pallas kernels, mlp_call(): pl.pallas_call(body, grid_spec=pltpu.PrefetchScalarGridSpec(num_scalar_pr...  60.2 us
    reduce_scatter x1, waiting for transfers between devices, on_device(): mine = lax.psum_scatter(share, 'z', scatter_dimension=0, tiled=False)  19.9 us
  transfers between devices with their start and end apart: 15, of which 5 were waited for; matrix products, arithmetic and copies ran while one was open for 12% of the time, Pallas kernels for 42%

profile of v3, /device:TPU:0, one launch (start us, length us, event | category | flops | bytes accessed | tf_op | source)
XLA Modules:
  0.0 789.7 jit_solution(17535994560431960856)
XLA Ops:
  7.8 2.1 convert_element_type.138
  9.9 1.2 fusion.46
  11.2 1.1 fusion.47
  12.3 1.2 slice-done.1
  14.8 2.4 pad_maximum_fusion.6.refs_1_
  17.1 2.1 pad_maximum_fusion.refs_2_
  20.0 3.5 dynamic-slice_convert_fusion.1
  23.5 1.8 fusion.30
  25.3 1.8 compare_reduce_fusion
  27.1 1.2 concatenate.56.refs_4_
  28.4 1.1 broadcast_in_dim.58.refs_9_.refs_8_
  29.5 2.5 pad_maximum_fusion.5.refs_0_
  32.0 2.1 pad_maximum_fusion.1.refs_3_
  34.1 189.1 %shard_map.278 = (bf16[2,4,4,2,48,896]{5,4,3,2,1,0:T(8,128)(2,1)}, bf16[2,4,4,2,48,768]{5,4,3,2,1,0:T(8,128)(2,1)}, bf16[2,4,4,2,144,768]{5,4,3,2,1,0:T(8,128)(2...) custom-call(bf16[2,4,2,48,896]{4,3,2,1,0:T(8,128)(2,1)} %pad_maximum, ...), custom_call_target="tpu_custom_call" | custom-call | tf_op jit(solution)/shard_map/pallas_call | solution.py:515
  225.2 4.9 fusion.42
  230.1 60.2 %shard_map.279 = (bf16[1536,1024]{1,0:T(8,128)(2,1)}, bf16[2304,1024]{1,0:T(8,128)(2,1)}, bf16[2,1024,2304]{2,1,0:T(8,128)(2,1)}, f32[1024,1536]{1,0:T(8,128)}, f32[1024,1536]{1,0:T(8,128)}) custom-call(s32[1]{0:T(128)} %bitcast.10.refs_0_, bf16[512,1536]{1,0:T(8,128)(2,1)} %get-tuple-element.75.refs_1_, bf16[512,1536]{1,0:T(8,128)(2,1)} %get-tuple-element.76.refs_2_, ...), custom_call_target="tpu_custom_call" | custom-call | flops 43486543872 | bytes 41943040 | tf_op jit(solution)/shard_map/pallas_call | solution.py:678
  290.3 3.3 dynamic-slice_convert_fusion.2
  293.7 3.2 dynamic-slice_convert_fusion.3
  297.5 3.4 broadcast_select_fusion.2
  301.3 2.9 copy.49
  304.1 2.8 fusion.9.refs_5_
  306.9 1.8 broadcast_select_fusion.1
  309.3 3.4 multiply_reduce_fusion.1
  312.8 5.9 fusion.39
  318.7 1.4 fusion.21
  320.9 2.6 fusion.7.refs_13_
  323.5 261.0 %shard_map.280 = (bf16[10,4,2,2,48,768]{5,4,3,2,1,0:T(8,128)(2,1)}, f32[512,1536]{1,0:T(8,128)}, f32[1536,128]{1,0:T(8,128)}, f32[1536,128]{1,0:T(8,128)}) custom-call(bf16[4,4,2,48,1024]{4,3,2,1,0:T(8,128)(2,1)} %bitcast.148, bf16[2,3,4,2,48,1024]{5,4,3,2,1,0:T(8,128)(2,1)} %bitcast.17.refs_1_, bf16[2,3,4,2,48,1024]{5,4,3,2,1,0:T(8,128)(2,1)} %bitcast.18.refs_2_, ...), custom_call_target="tpu_custom_call" | custom-call | flops 43486543872 | bytes 419430400 | tf_op jit(solution)/shard_map/pallas_call | solution.py:940
  584.5 1.2 constant_dynamic-update-slice_fusion.1
  585.7 1.2 constant_dynamic-update-slice_fusion
  586.9 1.1 copy-done.10
  588.9 1.3 collective-permute-start.5
  590.2 1.3 collective-permute-start.6
  591.5 1.9 maximum_bitcast_fusion.1
  593.4 3.6 copy.58
  596.9 3.5 copy.51
  600.5 12.2 %collective-permute-done.6 = bf16[512,256]{1,0:T(8,128)(2,1)} collective-permute-done((bf16[512,256]{1,0:T(8,128)(2,1)S(1)}, bf16[512,256]{1,0:T(8,128)(2,1)}, u32[]{:S(2)}, u32[]{:S(2)}) %collective-permute-start.6) | collective-permute-done | bytes 262176 | tf_op jit(solution)/shard_map/ppermute | solution.py:31
  612.7 1.3 fusion.29
  614.0 1.9 subtract_convert_fusion.1
  616.6 1.1 copy.54
  618.4 1.0 copy.57
  619.4 1.0 copy.56
  620.4 1.0 copy.55
  621.4 2.4 subtract_convert_fusion
  625.3 1.5 fusion.44
  628.0 1.9 convolution_convert_fusion.1
  629.9 1.9 convolution_convert_fusion
  631.8 2.0 collective-permute-start.9
  634.4 22.0 %shard_map.281 = (f32[384,9216]{1,0:T(8,128)}, f32[384,9216]{1,0:T(8,128)}, f32[2,384,9216]{2,1,0:T(8,128)}, f32[384,128]{1,0:T(8,128)}) custom-call(s32[1]{0:T(128)S(6)} %copy.65.refs_0_, f32[2]{0:T(128)} %refs_1_.9, bf16[10,4,2,2,48,768]{5,4,3,2,1,0:T(8,128)(2,1)} %get-tuple-element.103.refs_2_, f32[384,9216]{1,0:T(8,128)} %refs_3_.6, f32[2,384,9216]{2,1,0:T(8,128)} %refs_4_.6), custom_call_target="tpu_custom_call" | custom-call | flops 35389440 | bytes 53084160 | tf_op jit(solution)/shard_map/pallas_call | solution.py:1062
  656.5 1.9 fusion.16
  658.4 2.0 collective-permute-start.12
  661.4 6.8 collective-permute-done.12
  668.2 1.8 fusion.15
  672.4 19.9 %reduce-scatter.2.cloned.1.call-done = bf16[1,96,896]{2,1,0:T(8,128)(2,1)} async-done(((bf16[4,96,896]{2,1,0:T(8,128)(2,1)}), bf16[1,96,896]{2,1,0:T(8,128)(2,1)}) %reduce-scatter.2.cloned.1.call-update) | async-done | bytes 172048 | tf_op jit(solution)/shard_map/reduce_scatter | solution.py:1418
  692.3 5.6 fusion.41
  698.6 22.3 %shard_map.282 = (f32[384,9216]{1,0:T(8,128)}, f32[384,9216]{1,0:T(8,128)}, f32[2,384,9216]{2,1,0:T(8,128)}, f32[384,128]{1,0:T(8,128)}) custom-call(s32[1]{0:T(128)S(6)} %copy.65.refs_0_, f32[2]{0:T(128)} %refs_1_.9, bf16[10,4,2,2,48,768]{5,4,3,2,1,0:T(8,128)(2,1)} %get-tuple-element.103.refs_2_, ...), custom_call_target="tpu_custom_call", output_to_operand_aliasing={{0}: (5, {}), {1}: (6, {}), {2}: (7, {})} | custom-call | flops 35389440 | bytes 53084160 | tf_op jit(solution)/shard_map/pallas_call | solution.py:1062
  721.0 1.1 add_reduce_fusion
  722.0 9.6 %shard_map.284 = (f32[384,1536]{1,0:T(8,128)}, f32[384,1536]{1,0:T(8,128)}, f32[2,384,1536]{2,1,0:T(8,128)}, f32[8,128]{1,0:T(8,128)}) custom-call(s32[1]{0:T(128)S(6)} %copy.65.refs_0_, f32[2]{0:T(128)} %refs_1_.9, bf16[10,4,2,2,48,768]{5,4,3,2,1,0:T(8,128)(2,1)} %get-tuple-element.103.refs_2_, f32[384,1536]{1,0:T(8,128)} %refs_3_.8, f32[2,384,1536]{2,1,0:T(8,128)} %refs_4_.8), custom_call_target="tpu_custom_call" | custom-call | flops 11796480 | bytes 17694720 | tf_op jit(solution)/shard_map/pallas_call | solution.py:1062
  731.6 28.0 %shard_map.285 = (f32[1152,1536]{1,0:T(8,128)}, f32[1152,1536]{1,0:T(8,128)}, f32[2,1152,1536]{2,1,0:T(8,128)}, f32[8,128]{1,0:T(8,128)}) custom-call(s32[1]{0:T(128)S(6)} %copy.65.refs_0_, f32[2]{0:T(128)} %refs_1_.9, bf16[10,4,2,2,48,768]{5,4,3,2,1,0:T(8,128)(2,1)} %get-tuple-element.103.refs_2_, f32[1152,1536]{1,0:T(8,128)} %refs_3_.9, ...), custom_call_target="tpu_custom_call" | custom-call | flops 35389440 | bytes 53084160 | tf_op jit(solution)/shard_map/pallas_call | solution.py:1062
  759.7 3.8 fusion.18
  763.5 2.2 fusion.3
  765.7 1.9 fusion.10
  767.6 11.4 %shard_map.283 = (f32[384,1792]{1,0:T(8,128)}, f32[384,1792]{1,0:T(8,128)}, f32[2,384,1792]{2,1,0:T(8,128)}, f32[384,128]{1,0:T(8,128)}) custom-call(s32[1]{0:T(128)S(6)} %copy.65.refs_0_, f32[2]{0:T(128)} %refs_1_.9, bf16[1,4,2,2,48,896]{5,4,3,2,1,0:T(8,128)(2,1)} %bitcast.130, f32[384,1792]{1,0:T(8,128)} %refs_3_.7, f32[2,384,1792]{2,1,0:T(8,128)} %refs_4_.7), custom_call_target="tpu_custom_call" | custom-call | flops 13762560 | bytes 20643840 | tf_op jit(solution)/shard_map/pallas_call | solution.py:1062
  778.9 1.1 reduce_sum.66
  780.1 2.0 fusion.38
  (130 shorter events, 16.8 us)
Async XLA Ops:
  7.2 685.1 %reduce-scatter.2.cloned.1.call-start = ((), (), s32[]{:S(2)}) async-start(), calls=%async_computation.1 | async-start | bytes 860160 | tf_op jit(solution)/shard_map/reduce_scatter | solution.py:1418
  7.2 222.9 %collective-permute-start = (bf16[512,1536]{1,0:T(8,128)(2,1)}, bf16[512,1536]{1,0:T(8,128)(2,1)}, u32[]{:S(2)}, u32[]{:S(2)}) collective-permute-start(bf16[512,1536]{1,0:T(8,128)(2,1)} %bitcast.115), channel_id=1, source_target_pairs={{0,4},{4,0},{1,5},{5,1},{2,6},{6,2},{3,7},{7,3},{8,12},{12,8},{9,1... | collective-permute-start | bytes 4718600 | tf_op jit(solution)/shard_map/ppermute | solution.py:35
  7.8 6.4 copy-start.25
  7.8 3.3 copy-start.2
  7.8 4.5 slice-start
  9.8 3.6 slice-start.1
  20.0 3.5 copy-start.28
  20.0 3.5 copy-start.29
  20.0 7.1 copy-start.19
  223.3 77.6 %collective-permute-start.4 = (bf16[512,1536]{1,0:T(8,128)(2,1)}, bf16[512,1536]{1,0:T(8,128)(2,1)S(1)}, u32[]{:S(2)}, u32[]{:S(2)}) collective-permute-start(bf16[512,1536]{1,0:T(8,128)(2,1)} %get-tuple-element.84.refs_12_), channel_id=1, source_target_pairs={{0,4},{4,0},{1,5},{5,1},{2,6},{6,2},{3,7},{7,3},{8,12},{12,8},{9,1... | collective-permute-start | bytes 4718600 | tf_op jit(solution)/shard_map/ppermute | solution.py:35
  223.3 83.6 %collective-permute-start.7 = (bf16[512,1536]{1,0:T(8,128)(2,1)}, bf16[512,1536]{1,0:T(8,128)(2,1)}, u32[]{:S(2)}, u32[]{:S(2)}) collective-permute-start(bf16[512,1536]{1,0:T(8,128)(2,1)} %get-tuple-element.99), channel_id=1, source_target_pairs={{0,4},{4,0},{1,5},{5,1},{2,6},{6,2},{3,7},{7,3},{8,12},{12,8},{9,1... | collective-permute-start | bytes 4718600 | tf_op jit(solution)/shard_map/ppermute | solution.py:35
  290.3 7.1 copy-start.5
  293.7 15.0 %collective-permute-start.2 = (bf16[512,1536]{1,0:T(8,128)(2,1)}, bf16[512,1536]{1,0:T(8,128)(2,1)}, u32[]{:S(2)}, u32[]{:S(2)}) collective-permute-start(bf16[512,1536]{1,0:T(8,128)(2,1)} %dynamic-slice_convert_fusion.2), channel_id=1, source_target_pairs={{0,4},{4,0},{1,5},{5,1},{2,6},{6,2},{3,7},{7,3},{8,12},{12,8},{9,1... | collective-permute-start | bytes 4718600 | tf_op jit(solution)/shard_map/ppermute | solution.py:35
  296.9 15.7 %collective-permute-start.1 = (bf16[512,1536]{1,0:T(8,128)(2,1)}, bf16[512,1536]{1,0:T(8,128)(2,1)}, u32[]{:S(2)}, u32[]{:S(2)}) collective-permute-start(bf16[512,1536]{1,0:T(8,128)(2,1)} %dynamic-slice_convert_fusion.3), channel_id=1, source_target_pairs={{0,4},{4,0},{1,5},{5,1},{2,6},{6,2},{3,7},{7,3},{8,12},{12,8},{9,1... | collective-permute-start | bytes 4718600 | tf_op jit(solution)/shard_map/ppermute | solution.py:35
  297.4 3.5 copy-start.16
  297.4 26.1 %collective-permute-start.3 = (bf16[2304,1024]{1,0:T(8,128)(2,1)}, bf16[2304,1024]{1,0:T(8,128)(2,1)}, u32[]{:S(2)}, u32[]{:S(2)}) collective-permute-start(bf16[2304,1024]{1,0:T(8,128)(2,1)} %get-tuple-element.83), channel_id=1, source_target_pairs={{0,4},{4,0},{1,5},{5,1},{2,6},{6,2},{3,7},{7,3},{8,12},{12,8},{9,1... | collective-permute-start | bytes 14155784 | tf_op jit(solution)/shard_map/ppermute | solution.py:35
  304.1 2.8 copy-start.17
  304.1 8.6 %slice-start.2 = ((s8[6291456]{0:T(1024)(128)(4,1)}), s8[4194304]{0:T(1024)(128)(4,1)S(1)}, s32[]{:S(2)}) async-start(s8[6291456]{0:T(1024)(128)(4,1)} %bitcast.109), calls=%async_computation.5 | async-start | bytes 8388608
  306.9 2.4 copy-start
  306.9 5.8 slice-start.3
  309.3 3.5 copy-start.6
  312.7 5.9 copy-start.14
  318.6 1.5 copy-start.15
  318.6 2.2 copy-start.13
  318.7 2.2 copy-start.27
  586.9 1.1 copy-start.10
  588.9 11.6 %collective-permute-start.5 = (bf16[512,256]{1,0:T(8,128)(2,1)}, bf16[512,256]{1,0:T(8,128)(2,1)}, u32[]{:S(2)}, u32[]{:S(2)}) collective-permute-start(bf16[512,256]{1,0:T(8,128)(2,1)} %get-tuple-element.95), channel_id=1, source_target_pairs={{1,0},{2,1},{3,2},{5,4},{6,5},{7,6},{9,8},{10,9},{11,10},{13,12},{... | collective-permute-start | bytes 786440 | tf_op jit(solution)/shard_map/ppermute | solution.py:31
  590.2 22.5 %collective-permute-start.6 = (bf16[512,256]{1,0:T(8,128)(2,1)S(1)}, bf16[512,256]{1,0:T(8,128)(2,1)}, u32[]{:S(2)}, u32[]{:S(2)}) collective-permute-start(bf16[512,256]{1,0:T(8,128)(2,1)S(1)} %get-tuple-element.96), channel_id=1, source_target_pairs={{2,0},{3,1},{6,4},{7,5},{10,8},{11,9},{14,12},{15,13},{18,16},{19,... | collective-permute-start | bytes 786440 | tf_op jit(solution)/shard_map/ppermute | solution.py:31
  596.9 17.0 %copy-start.26 = (f32[64]{0:T(128)S(1)}, f32[64]{0:T(128)}, u32[]{:S(2)}) copy-start(f32[64]{0:T(128)} %copy-done.25) | copy-start | bytes 772
  623.9 1.1 copy-start.7
  624.1 3.5 copy-start.3
  625.1 2.5 collective-permute-start.8
  631.8 24.7 %collective-permute-start.9 = (bf16[384,896]{1,0:T(8,128)(2,1)}, bf16[384,896]{1,0:T(8,128)(2,1)S(1)}, u32[]{:S(2)}, u32[]{:S(2)}) collective-permute-start(bf16[384,896]{1,0:T(8,128)(2,1)} %convolution_convert_fusion.1), channel_id=1, source_target_pairs={{0,8},{8,0},{1,9},{9,1},{2,10},{10,2},{3,11},{11,3},{4,12},{12,4},... | collective-permute-start | bytes 2064392 | tf_op jit(solution)/shard_map/ppermute | solution.py:35
  633.7 22.8 %collective-permute-start.10 = (bf16[384,896]{1,0:T(8,128)(2,1)}, bf16[384,896]{1,0:T(8,128)(2,1)}, u32[]{:S(2)}, u32[]{:S(2)}) collective-permute-start(bf16[384,896]{1,0:T(8,128)(2,1)} %convolution_convert_fusion), channel_id=1, source_target_pairs={{0,16},{16,0},{1,17},{17,1},{2,18},{18,2},{3,19},{19,3},{4,20},{20... | collective-permute-start | bytes 2064392 | tf_op jit(solution)/shard_map/ppermute | solution.py:35
  656.5 3.9 copy-start.11
  658.4 9.8 %collective-permute-start.12 = (bf16[192,896]{1,0:T(8,128)(2,1)S(1)}, bf16[192,896]{1,0:T(8,128)(2,1)S(1)}, u32[]{:S(2)}, u32[]{:S(2)}) collective-permute-start(bf16[192,896]{1,0:T(8,128)(2,1)S(1)} %fusion.16), channel_id=1, source_target_pairs={{0,8},{8,0},{1,9},{9,1},{2,10},{10,2},{3,11},{11,3},{4,12},{12,4},... | collective-permute-start | bytes 1032200 | tf_op jit(solution)/shard_map/ppermute | solution.py:35
  661.2 9.3 %collective-permute-start.11 = (bf16[192,896]{1,0:T(8,128)(2,1)S(1)}, bf16[192,896]{1,0:T(8,128)(2,1)S(1)}, u32[]{:S(2)}, u32[]{:S(2)}) collective-permute-start(bf16[192,896]{1,0:T(8,128)(2,1)S(1)} %fusion.14), channel_id=1, source_target_pairs={{0,16},{16,0},{1,17},{17,1},{2,18},{18,2},{3,19},{19,3},{4,20},{20... | collective-permute-start | bytes 1032200 | tf_op jit(solution)/shard_map/ppermute | solution.py:35
  672.3 95.2 %all-gather.3.cloned.1.call-start = ((), (), s32[]{:S(2)}) async-start(), calls=%async_computation.2 | async-start | bytes 1548288 | tf_op jit(solution)/shard_map/all_gather | solution.py:1421
  692.3 5.6 copy-start.22
  692.3 5.7 copy-start.21
  698.6 22.3 %copy-start.18 = (f32[384,128]{1,0:T(8,128)S(1)}, f32[384,128]{1,0:T(8,128)}, u32[]{:S(2)}) copy-start(f32[384,128]{1,0:T(8,128)} %get-tuple-element.104) | copy-start | bytes 589828
  731.6 28.0 %copy-start.8 = (bf16[512,12,128]{0,2,1:T(8,128)(2,1)S(1)}, bf16[512,12,128]{0,2,1:T(8,128)(2,1)}, u32[]{:S(2)}) copy-start(bf16[512,12,128]{0,2,1:T(8,128)(2,1)} %copy-done.7) | copy-start | bytes 4718596
  759.6 3.8 copy-start.4
  759.6 3.8 copy-start.9
  759.7 3.8 copy-start.12
  763.5 2.2 copy-start.1
  767.6 12.5 %copy-start.20 = (f32[2,384]{1,0:T(2,128)S(1)}, f32[2,384]{1,0:T(2,128)}, u32[]{:S(2)}) copy-start(f32[2,384]{1,0:T(2,128)} %param.22) | copy-start | bytes 9220
  767.6 12.5 %copy-start.23 = (f32[2,2,384]{2,1,0:T(2,128)S(1)}, f32[2,2,384]{2,1,0:T(2,128)}, u32[]{:S(2)}) copy-start(f32[2,2,384]{2,1,0:T(2,128)} %param.27) | copy-start | bytes 18436
  780.0 2.6 copy-start.24
Sparse Core Ops, SparseCore 0:
  672.5 19.7 reduce-scatter.1
  694.3 23.6 all-gather.2

commit v4 on v3

--- a/solution.py
+++ b/solution.py
@@ -20,6 +20,7 @@
 F32 = jnp.float32
 MESH_ID = pl.DeviceIdType.MESH
 VMEM_BYTES = 60 * 1024 * 1024
+BACKWARD_VMEM = 127 * 512 * 1024
 ANY = pl.BlockSpec(memory_space=pl.ANY)
 VM = pl.BlockSpec(memory_space=pltpu.VMEM)
 LOG2E = 1.4426950408889634
@@ -370,8 +371,9 @@
     small_own, x_ref, cos_ref, sin_ref, q_ids, k_ids = refs[4:10]
     full = refs[10:14]
     small_full, h1_ref, q_ref, k_out, v_out, o_ref, l_ref, mid_ref, h2_ref, h2_other = refs[14:24]
-    w_in, w_out, gains, mix, kv, bias, vt, lds, hs, hr, h2_sems = refs[24:35]
-    sems = refs[35:]
+    h1_t, h1_t_other, o_t, o_t_other = refs[24:28]
+    w_in, w_out, gains, mix, kv, bias, vt, lds, hs, hr, h2_sems = refs[28:39]
+    sems = refs[39:]
     z = lax.axis_index("z")
     c = lax.axis_index("c")
     piece = x_ref.shape[0]
@@ -453,9 +455,17 @@
 
     def finish():
         norm_rows(mid_ref, gain_row(1), h2_ref)
-        copy = remote_copy(h2_ref, h2_other, h2_sems.at[0], h2_sems.at[1], {"c": 1 - c})
+        to_partner(h2_ref, h2_other, 0)
+
+    def to_partner(src, dst, i):
+        copy = remote_copy(src, dst, h2_sems.at[2 * i], h2_sems.at[2 * i + 1], {"c": 1 - c})
         copy.start()
         sent.append(copy.wait)
+
+    def transpose(src, dst, there, i):
+        for j in range(0, D, HEAD):
+            dst[j : j + HEAD, :] = src[:, j : j + HEAD].T
+        to_partner(dst, there, i)
 
     third = heads // 3
     plan = {
@@ -466,7 +476,8 @@
         8: lambda ready: attention(third, third),
         9: lambda ready: attention(2 * third, third),
         10: lambda ready: output(),
-        11: lambda ready: finish(),
+        11: lambda ready: (finish(), transpose(h1_ref, h1_t, h1_t_other, 1)),
+        12: lambda ready: transpose(o_ref, o_t, o_t_other, 2),
     }
 
     def work(t, ready):
@@ -510,13 +521,17 @@
         shape(piece, D, dtype=F32),
         shape(piece, D),
         shape(piece, D),
+        shape(D, piece),
+        shape(D, piece),
+        shape(D, piece),
+        shape(D, piece),
     ]
     dma = pltpu.SemaphoreType.DMA
     return pl.pallas_call(
         body,
         out_shape=tuple(outs),
         in_specs=[VM] * 10,
-        out_specs=tuple([ANY] * 5 + [VM] * 8 + [ANY]),
+        out_specs=tuple([ANY] * 5 + [VM] * 8 + [ANY] + [VM, ANY] * 2),
         scratch_shapes=[
             pltpu.VMEM((2, S) + own[0].shape[1:], BF),
             pltpu.VMEM((2, S) + own[1].shape[1:], BF),
@@ -528,7 +543,7 @@
             dma((5,)),
             dma((2,)),
             dma((2,)),
-            dma((2,)),
+            dma((6,)),
         ]
         + gather_sems(4, len(chunks), S),
         compiler_params=pltpu.CompilerParams(
@@ -537,7 +552,7 @@
     )(*own, small, x, cos, sin, q_ids, k_ids)
 
 
-def back_step(h, first, rows, refs, bias, kt):
+def back_step(h, first, rows, refs, bias, kt, finish):
     q_ref, k_ref, v_ref, o_ref, do_ref, l_ref, dq_ref, dk_ref, dv_ref = refs
     span = WINDOW + rows
     factor = HEAD**-0.5 * LOG2E
@@ -552,7 +567,8 @@
     ds = (p * ((dp - delta) * HEAD**-0.5)).astype(BF)
     dv_ref[pl.ds(first, span), :] += nn(p.astype(BF), do)
     dk_ref[pl.ds(first, span), :] += nn(ds, q)
-    dq_ref[pl.ds(first, rows), cols] = nn(kt[:, pl.ds(first, span)], ds).T
+    dq = nn(kt[:, pl.ds(first, span)], ds).T
+    dq_ref[pl.ds(first, rows), cols] = finish(dq, first).astype(dq_ref.dtype)
 
 
 def bwd_kernel(heads, rows, q_ids, k_ids, *refs):
@@ -565,7 +581,7 @@
     for first in range(0, q_ref.shape[0], rows):
         fill_bias(bias, q_ids, k_ids, first, rows, WINDOW + rows)
         for h in range(heads):
-            back_step(h, first, rows, arrays, bias, kt)
+            back_step(h, first, rows, arrays, bias, kt, lambda dq, first: dq)
 
 
 def attend(q_ids, k_ids, q, k, v, heads, rows):
@@ -618,7 +634,7 @@
 def mlp_kernel(
     where, two_own, two_other, df_own, df_other, gate_ref, up_ref, down_ref, *results
 ):
-    two_t, hid_t, grads, out, back = results
+    two_t, hid_t, grads, out_low, back_low, out, back = results
     step = pl.program_id(0)
     rows, D = two_own.shape
     half = down_ref.shape[2]
@@ -660,6 +676,11 @@
         out[at, :half] += nn(hid, down_ref[0])
         out[at, half:] += nn(hid, down_ref[1])
         back[at, :] += nt(grad_gate, gate_ref[...]) + nt(grad_up, up_ref[...])
+
+    @pl.when(step == pl.num_programs(0) - 1)
+    def _():
+        out_low[...] = out[...].astype(BF)
+        back_low[...] = back[...].astype(BF)
 
 
 def mlp_call(core, two, df, gate_full, down_full):
@@ -696,13 +717,14 @@
                 pl.BlockSpec((T, D), lambda i, w: (0, 0)),
                 pl.BlockSpec((T, D), lambda i, w: (0, 0)),
             ],
+            scratch_shapes=[pltpu.VMEM((T, D), F32), pltpu.VMEM((T, D), F32)],
         ),
         out_shape=[
             jax.ShapeDtypeStruct((D, T), BF),
             jax.ShapeDtypeStruct((half_ff, T), BF),
             jax.ShapeDtypeStruct((2, T, half_ff), BF),
-            jax.ShapeDtypeStruct((T, D), F32),
-            jax.ShapeDtypeStruct((T, D), F32),
+            jax.ShapeDtypeStruct((T, D), BF),
+            jax.ShapeDtypeStruct((T, D), BF),
         ],
         compiler_params=pltpu.CompilerParams(
             dimension_semantics=("arbitrary",), vmem_limit_bytes=VMEM_BYTES
@@ -713,18 +735,33 @@
     )(core, *two, *df, gate_full, gate_full, down_full)
 
 
-def reduce_kernel(heads, sides, parts, S, two, hid_own, hid_other, flat, grads, df, da, *more):
-    q_ids, k_ids, *given = more[:8]
-    out, *found = more[8:12]
-    left, right, tail_right, s1, g1, s2, g2, fz, gz, mine, bias, kt, *sems = more[12:]
-    arrays = given + found
-    rows = given[0].shape[0] // 2
-    ts, lds, rds, s1s, s1r, s2s, s2r, zs, zr, ls, xs, xr, ys, yr, cs, cr = sems
-    groups, _, _, r, T = left.shape
+def split_widths(total, most):
+    first = -(-total // 256) * 128
+    assert first <= most
+    return (first, total - first)
+
+
+def backward_kernel(heads, sides, parts, S, *refs):
+    two, hid, *flats = refs[:6]
+    flat_own, flat_other, norm_own, norm_other = flats[2], flats[3], flats[0], flats[1]
+    grads, dy_own, dy_other, back, middle, w_out, gains_ref = refs[6:13]
+    q_ids, k_ids, q_ref, k_ref, v_ref, o_ref, l_ref, cos_ref, sin_ref = refs[13:22]
+    out, hid_land, dx_out, mixed = refs[22:26]
+    left, right, out_right, mix_right, s1, g1, s2, g2, fz, gz, mine, da, do, got, tails, landed_tails, gains = refs[26:43]
+    x1, dk, dv, bias, kt = refs[43:48]
+    lds, rds, fs, cs_in, hs, hr, s1s, s1r, s2s, s2r, zs, zr, ls, xs, xr, ys, yr, cs, cr = refs[48:]
+    _, _, _, r, T = left.shape
     n = right.shape[2]
+    piece, D = da.shape
+    reach = tails.shape[0]
     wide = sides * parts
-    last = wide + groups - 1
-    nc = last + 1
+    rows_groups = hid.shape[1]
+    chunk_out = wide + rows_groups
+    mix_half = mix_right.shape[1]
+    widths = [n] * (chunk_out + 1) + list(split_widths(mix_half, n))
+    nc = len(widths)
+    left_slots = left.shape[0]
+    right_slots = right.shape[0]
     slots = g1.shape[0]
     y, x, c, z = (lax.axis_index(a) for a in ("y", "x", "c", "z"))
     k = y * 2 + x
@@ -734,235 +771,385 @@
     to_x = {"x": 1 - x}
     to_y = {"y": 1 - y}
     to_c = {"c": 1 - c}
+    place = pl.ds(pl.multiple_of(c * piece, piece), piece)
+    other_place = pl.ds(pl.multiple_of((1 - c) * piece, piece), piece)
     loads = {}
+    pending = {}
 
     def fetch(key, src, dst, sem):
-        copy = pltpu.make_async_copy(src, dst, sem)
+        loads.setdefault(key, []).append(started(src, dst, sem))
+
+    def landed(key):
+        for copy in loads.pop(key, []):
+            copy.wait()
+
+    def launch(key, copy):
         copy.start()
-        loads.setdefault(key, []).append(copy)
+        pending.setdefault(key, []).append(copy)
+
+    def drain(key):
+        for copy in pending.pop(key, []):
+            copy.wait_send()
+
+    groups = 3 + rows_groups
+
+    def group_of(t):
+        if t < wide:
+            return 0
+        return min(t - wide + 1, groups - 1)
 
     def fetch_left(g):
+        slot = g % left_slots
         for p in range(8):
             h, kk = p // 4, p % 4
             if g == 0:
-                fetch(("l", 0), two.at[:, kk, h], left.at[0, p], lds.at[0, p, 0])
-            elif g == groups:
-                fetch(("l", g), flat.at[:, kk, h], left.at[0, p], lds.at[g, p, 0])
+                fetch(("l", g), two.at[:, kk, h], left.at[slot, p], lds.at[g, p, 0])
+                continue
+            if g <= rows_groups:
+                if g == 1 and p == 0:
+                    landed_hid.wait_recv()
+                half = left.shape[2] // 2
+                pairs = [
+                    (hid.at[:, g - 1, kk, h], left.at[slot, p, pl.ds(c * half, half)]),
+                    (hid_land.at[:, g - 1, kk, h], left.at[slot, p, pl.ds((1 - c) * half, half)]),
+                ]
             else:
-                for i, (src, cc) in enumerate(((hid_own, c), (hid_other, 1 - c))):
-                    dst = left.at[g, p, pl.ds(cc * (S // 2), S // 2)]
-                    fetch(("l", g), src.at[:, g - 1, kk, h], dst, lds.at[g, p, i])
-
-    def slot_of(t):
-        return t % 4 if t < wide else 4
+                own, other = (flat_own, flat_other) if g == groups - 2 else (norm_own, norm_other)
+                pairs = [
+                    (own.at[:, kk, h], left.at[slot, p, :, :, place]),
+                    (other.at[:, kk, h], left.at[slot, p, :, :, other_place]),
+                ]
+            for i, (src, dst) in enumerate(pairs):
+                fetch(("l", g), src, dst, lds.at[g, p, i])
 
     def fetch_right(t):
+        slot = t % right_slots
         if t < wide:
             src = grads.at[t // parts, :, pl.ds((t % parts) * n, n)]
-            fetch(("r", t), src, right.at[t % 4], rds.at[t])
+            fetch(("r", t), src, right.at[slot], rds.at[t, 0])
         elif t == wide:
-            fetch(("r", t), df, right.at[4], rds.at[t])
-
-    def landed(key):
-        for copy in loads.pop(key, []):
-            copy.wait()
-
-    def group_of(t):
-        return max(0, t - wide + 1)
+            keep = pl.ds(pl.multiple_of(c * n, n), n)
+            fetch(("r", t), dy_own.at[:, keep], right.at[slot, place], rds.at[t, 0])
+            fetch(("r", t), dy_other.at[:, keep], right.at[slot, other_place], rds.at[t, 1])
 
     fetch_right(0)
     fetch_left(0)
     fetch_right(1)
+    landed_tails[...] = jnp.zeros_like(landed_tails)
     barrier = pltpu.get_barrier_semaphore()
     peers = [to_x, to_y, to_c] + [{"z": lax.rem(z + e, S)} for e in range(1, S)]
     for target in peers:
         pl.semaphore_signal(barrier, inc=1, device_id=target, device_id_type=MESH_ID)
     pl.semaphore_wait(barrier, len(peers))
-    for g in range(1, groups):
-        fetch_left(g)
-
-    def remote(src, dst, s, r_, target):
-        return pltpu.make_async_remote_copy(
-            src_ref=src, dst_ref=dst, send_sem=s, recv_sem=r_, device_id=target, device_id_type=MESH_ID
-        )
+    launch("end", remote_copy(back.at[other_place], got, cs_in.at[0], cs_in.at[1], to_c))
+    launch("end", remote_copy(hid, hid_land, cs_in.at[2], cs_in.at[3], to_c))
+    landed_hid = remote_copy(hid, hid_land, cs_in.at[2], cs_in.at[3], to_c)
+    landed_back = remote_copy(got, got, cs_in.at[0], cs_in.at[1], to_c)
 
     def product(t, p):
-        if t == last:
-            return nn(left[0, p].reshape(S * r, T), tail_right[...])
-        return nn(left[group_of(t), p].reshape(S * r, T), right[slot_of(t)])
-
-    half_rows = da.shape[0]
-    place = pl.ds(pl.multiple_of(c * half_rows, half_rows), half_rows)
-    other_place = pl.ds(pl.multiple_of((1 - c) * half_rows, half_rows), half_rows)
-    keep = pl.ds(pl.multiple_of(c * n, n), n)
-    give = pl.ds(pl.multiple_of((1 - c) * n, n), n)
-    fetch(("r", last), da.at[:, keep], tail_right.at[place], ts.at[0])
-    given_copy = remote(da.at[:, give], tail_right.at[place], ts.at[1], ts.at[2], to_c)
-    given_copy.start()
-    other = tail_right.at[other_place]
-    other_copy = remote(other, other, ts.at[1], ts.at[2], to_c)
-
-    pending = {}
-
-    def launch(key, copy):
-        copy.start()
-        pending.setdefault(key, []).append(copy)
-
-    def drain(key):
-        for copy in pending.pop(key, []):
-            copy.wait_send()
+        lhs = left[group_of(t) % left_slots, p].reshape(S * r, T)
+        if t <= chunk_out - 1:
+            return nn(lhs, right[min(t, wide) % right_slots])
+        if t == chunk_out:
+            return nn(lhs, out_right[...])
+        first = sum(widths[chunk_out + 1 : t])
+        return nn(lhs, mix_right[:, first : first + widths[t]])
+
+    def cut(ref, t):
+        return ref if widths[t] == n else ref.at[:, pl.ds(0, widths[t])]
 
     def first(t):
         slot = t % 2
         landed(("l", group_of(t)))
         landed(("r", t))
-        if t == last:
-            other_copy.wait_recv()
-            given_copy.wait_send()
         drain(("s1", t - 2))
-
         for i in range(2):
             for j, p, target in ((i, i * 2 + 1 - x, to_x), (2 + i, 4 + (1 - y) * 2 + i, to_y)):
-                s1[slot, j] = product(t, p).astype(BF)
-                launch(("s1", t), remote(s1.at[slot, j], g1.at[t % slots, j], s1s.at[t, j], s1r.at[t, j], target))
-
-    def got1(t, j):
-        remote(g1.at[t % slots, j], g1.at[t % slots, j], s1s.at[t, j], s1r.at[t, j], to_x).wait_recv()
+                src, dst = cut(s1.at[slot, j], t), cut(g1.at[t % slots, j], t)
+                src[...] = product(t, p).astype(BF)
+                launch(("s1", t), remote_copy(src, dst, s1s.at[t, j], s1r.at[t, j], target))
 
     def second(t):
         slot = t % 2
         drain(("s2", t - 2))
         for j in range(4):
-            got1(t, j)
+            dst = cut(g1.at[t % slots, j], t)
+            remote_copy(dst, dst, s1s.at[t, j], s1r.at[t, j], to_x).wait_recv()
         for h, p, j, target in ((0, (1 - y) * 2 + x, 1 - y, to_y), (1, 4 + y * 2 + 1 - x, 3 - x, to_x)):
-            s2[slot, h] = (product(t, p) + g1[t % slots, j].astype(F32)).astype(BF)
-            launch(("s2", t), remote(s2.at[slot, h], g2.at[t % slots, h], s2s.at[t, h], s2r.at[t, h], target))
+            src, dst = cut(s2.at[slot, h], t), cut(g2.at[t % slots, h], t)
+            came = cut(g1.at[t % slots, j], t)
+            src[...] = (product(t, p) + came[...].astype(F32)).astype(BF)
+            launch(("s2", t), remote_copy(src, dst, s2s.at[t, h], s2r.at[t, h], target))
 
     def third(t):
         slot = t % 2
+        w = widths[t]
         drain(("z", t - 2))
         for h, p, j in ((0, k, y), (1, 4 + k, 2 + x)):
-            remote(g2.at[t % slots, h], g2.at[t % slots, h], s2s.at[t, h], s2r.at[t, h], to_x).wait_recv()
-            total = (product(t, p) + g1[t % slots, j].astype(F32) + g2[t % slots, h].astype(F32)).astype(BF)
+            dst = cut(g2.at[t % slots, h], t)
+            remote_copy(dst, dst, s2s.at[t, h], s2r.at[t, h], to_x).wait_recv()
+            came = cut(g1.at[t % slots, j], t)
+            total = (product(t, p) + came[...].astype(F32) + dst[...].astype(F32)).astype(BF)
             for zz in range(S):
-                fz[slot, zz, h] = total[zz * r : (zz + 1) * r]
+                fz[slot, zz, h, :, :w] = total[zz * r : (zz + 1) * r]
         for e in range(1, S):
-            zz = lax.rem(z + e, S)
-            launch(("z", t), remote(fz.at[slot, zz], gz.at[t, S - e - 1], zs.at[t, e - 1], zr.at[t, S - e - 1], {"z": zz}))
+            src = fz.at[slot, lax.rem(z + e, S), :, :, pl.ds(0, w)]
+            dst = gz.at[t, S - e - 1, :, :, pl.ds(0, w)]
+            target = {"z": lax.rem(z + e, S)}
+            launch(("z", t), remote_copy(src, dst, zs.at[t, e - 1], zr.at[t, S - e - 1], target))
 
     def fourth(t):
         slot = t % 2
+        w = widths[t]
         drain(("ag", t - 2))
-        for copy in pending.pop(("l", t - 2), []):
-            copy.wait()
+        landed(("o", t - 2))
         for e in range(S - 1):
-            remote(gz.at[t, e], gz.at[t, e], zs.at[t, e], zr.at[t, e], to_x).wait_recv()
+            dst = gz.at[t, e, :, :, pl.ds(0, w)]
+            remote_copy(dst, dst, zs.at[t, e], zr.at[t, e], to_x).wait_recv()
         for h in range(2):
-            total = fz[slot, z, h].astype(F32)
+            total = fz[slot, z, h, :, :w].astype(F32)
             for e in range(S - 1):
-                total = total + gz[t, e, h].astype(F32)
-            mine[slot, h] = total.astype(BF)
-        copy = pltpu.make_async_copy(mine.at[slot], out.at[t, k, c], ls.at[t])
-        copy.start()
-        pending[("l", t)] = [copy]
-        for h, s, r_, target in ((0, xs, xr, to_x), (1, ys, yr, to_y)):
-            launch(("ag", t), remote(mine.at[slot, h], out.at[t, k, c, h], s.at[t, 0], r_.at[t, 0], target))
-        for h, s, r_, target in ((0, ys, yr, to_y), (1, xs, xr, to_x)):
-            launch(("ag", t), remote(mine.at[slot, h], out.at[t, k, c, h], s.at[t, 1], r_.at[t, 1], target))
+                total = total + gz[t, e, h, :, :w].astype(F32)
+            mine[slot, h, :, :w] = total.astype(BF)
+        cols = pl.ds(0, w)
+        fetch(("o", t), mine.at[slot, :, :, cols], out.at[t, k, c, :, :, cols], ls.at[t])
+        for i, hs_ in enumerate(((0, 1), (1, 0))):
+            for h, s, r_, target in ((hs_[0], xs, xr, to_x), (hs_[1], ys, yr, to_y)):
+                src, dst = mine.at[slot, h, :, cols], out.at[t, k, c, h, :, cols]
+                launch(("ag", t), remote_copy(src, dst, s.at[t, i], r_.at[t, i], target))
 
     def land(t, kk, h, s, r_, j, target):
-        p = out.at[t, kk, c, h]
-        remote(p, p, s.at[t, j], r_.at[t, j], target).wait_recv()
+        p = out.at[t, kk, c, h, :, pl.ds(0, widths[t])]
+        remote_copy(p, p, s.at[t, j], r_.at[t, j], target).wait_recv()
         return p
 
     def fifth(t):
         p = land(t, kx, 0, xs, xr, 0, to_x)
-        launch("end", remote(p, p, ys.at[t, 2], yr.at[t, 2], to_y))
+        launch("end", remote_copy(p, p, ys.at[t, 2], yr.at[t, 2], to_y))
         p = land(t, ky, 1, ys, yr, 0, to_y)
-        launch("end", remote(p, p, xs.at[t, 2], xr.at[t, 2], to_x))
+        launch("end", remote_copy(p, p, xs.at[t, 2], xr.at[t, 2], to_x))
 
     def sixth(t):
         land(t, kx, 1, xs, xr, 1, to_x)
         land(t, ky, 0, ys, yr, 1, to_y)
         land(t, kxy, 1, xs, xr, 2, to_x)
         land(t, kxy, 0, ys, yr, 2, to_y)
-        for copy in pending.pop(("l", t), []):
-            copy.wait()
-        p = out.at[t, :, c]
-        launch("end", remote(p, p, cs.at[t], cr.at[t], to_c))
-
+        landed(("o", t))
+        p = out.at[t, :, c, :, :, pl.ds(0, widths[t])]
+        launch("end", remote_copy(p, p, cs.at[t], cr.at[t], to_c))
+
+
+    def norm_back():
+        for key in ("near", "x1", "dy", "gains"):
+            landed(key)
+        landed_back.wait_recv()
+        gain = jnp.concatenate([gains[zz, 1:2, :] for zz in range(S)], axis=1).astype(F32)
+        step = 64
+
+        @pl.loop(0, piece // step)
+        def _(i):
+            at = pl.ds(pl.multiple_of(i * step, step), step)
+            u = x1[at, :]
+            scale = lax.rsqrt(jnp.mean(u * u, axis=1, keepdims=True) + norm_eps)
+            hat = u * scale
+            e = (do[at, :].astype(F32) + got[at, :].astype(F32)) * gain
+            inner = jnp.mean(e * hat, axis=1, keepdims=True)
+            dx = mixed[at, :D].astype(F32) + scale * (e - hat * inner)
+            x1[at, :] = dx
+            da[at, :] = dx.astype(BF)
+
+        fetch("dx", x1, dx_out, fs.at[4])
+        launch("end", remote_copy(give_of(da, n), out_right.at[place], cs_in.at[4], cs_in.at[5], to_c))
+        out_right[place, :] = keep_of(da, n)[...]
+        for i in range(2):
+            fetch("w", w_out.at[i, pl.ds(T, piece)], got.at[:, pl.ds(i * n, n)], fs.at[7 + i])
+
+    def give_of(ref, width):
+        return ref.at[:, pl.ds(pl.multiple_of((1 - c) * width, width), width)]
+
+    def keep_of(ref, width):
+        return ref.at[:, pl.ds(pl.multiple_of(c * width, width), width)]
+
+    def heads_back():
+        landed("w")
+        live = k_ids[pl.ds(reach * piece, piece), :1] != 0
+        for j in range(0, D, piece):
+            if j < T:
+                low, high = right[2, j : j + piece, :], right[3, j : j + piece, :]
+            else:
+                low, high = got[:, :n], got[:, n:]
+            part = nt(da[:, :n], low) + nt(da[:, n:], high)
+            do[:, j : j + piece] = jnp.where(live, part, 0.0).astype(BF)
+
+    half_rows = piece // 2
     steps = [(block, h) for block in range(2) for h in range(heads)]
 
-    def attention(t):
+    def turn_back(dq, first):
+        at = pl.ds(first, half_rows)
+        return dq * cos_ref[at, :] - pltpu.roll(dq, HEAD // 2, 1) * sin_ref[at, :]
+
+    def attention(first_step, count):
+        arrays = (q_ref, k_ref, v_ref, o_ref, do, l_ref, mixed, dk, dv)
+        if first_step == 0:
+            kt[...] = k_ref[...].T
+            dk[...] = jnp.zeros_like(dk)
+            dv[...] = jnp.zeros_like(dv)
+        for block, h in steps[first_step : first_step + count]:
+            if h == 0:
+                fill_bias(bias, q_ids, k_ids, block * half_rows, half_rows, WINDOW + half_rows)
+            back_step(h, block * half_rows, half_rows, arrays, bias, kt, turn_back)
+
+    def tail(d):
+        target = {"z": jnp.maximum(z - d, 0)}
+        return remote_copy(tails.at[d - 1], landed_tails.at[d - 1], hs.at[d - 1], hr.at[d - 1], target)
+
+    def send_tails():
+        for d in range(1, reach + 1):
+            at = pl.ds((reach - d) * piece, piece)
+            tails[d - 1, :, :HEAD] = dk[at, :].astype(BF)
+            tails[d - 1, :, HEAD:] = dv[at, :].astype(BF)
+
+            @pl.when(z >= d)
+            def _(d=d):
+                tail(d).start()
+
+    def mix_back():
+        for d in range(1, reach + 1):
+
+            @pl.when(z >= d)
+            def _(d=d):
+                tail(d).wait_send()
+
+            @pl.when(z + d < S)
+            def _(d=d):
+                tail(d).wait_recv()
+
+        at = pl.ds(reach * piece, piece)
+        keys, values = dk[at, :], dv[at, :]
+        for d in range(1, reach + 1):
+            keys = keys + landed_tails[d - 1, :, :HEAD].astype(F32)
+            values = values + landed_tails[d - 1, :, HEAD:].astype(F32)
+        keys = keys * cos_ref[...] - pltpu.roll(keys, HEAD // 2, 1) * sin_ref[...]
+        width = heads * HEAD
+        mixed[:, width : width + HEAD] = keys.astype(BF)
+        mixed[:, width + HEAD :] = values.astype(BF)
+        launch("end", remote_copy(give_of(mixed, mix_half), mix_right.at[place], cs_in.at[6], cs_in.at[7], to_c))
+        mix_right[place, :] = keep_of(mixed, mix_half)[...]
+
+    def came(ref, i):
+        ref = ref.at[other_place]
+        remote_copy(ref, ref, cs_in.at[i], cs_in.at[i + 1], to_c).wait_recv()
+
+    stages = (first, second, third, fourth, fifth, sixth)
+
+    fetch("near", back.at[place], do, fs.at[0])
+    fetch("x1", middle, x1, fs.at[1])
+    fetch("dy", dy_own, mixed.at[:, pl.ds(0, D)], fs.at[2])
+    fetch("gains", gains_ref, gains, fs.at[3])
+    for i in range(2):
+        fetch("w", w_out.at[i, pl.ds(0, T)], right.at[2 + i], fs.at[5 + i])
+    each = 5
+
+    def work(t):
         if t == 0:
-            kt[...] = given[1][...].T
-            found[1][...] = jnp.zeros_like(found[1])
-            found[2][...] = jnp.zeros_like(found[2])
-        for block, h in steps[2 * t : 2 * t + 2]:
-            if h == 0:
-                fill_bias(bias, q_ids, k_ids, block * rows, rows, WINDOW + rows)
-            back_step(h, block * rows, rows, arrays, bias, kt)
-
-    stages = (first, second, third, fourth, fifth, sixth)
+            norm_back()
+        if t == 1:
+            heads_back()
+        if t >= 2 and (t - 2) * each < len(steps):
+            attention((t - 2) * each, each)
+        if t == 7:
+            send_tails()
+        if t == 8:
+            mix_back()
+
     for t in range(nc + len(stages) - 1):
         for lag, stage in enumerate(stages):
+            if lag == 0 and t == chunk_out:
+                came(out_right, 4)
+            if lag == 0 and t == chunk_out + 1:
+                came(mix_right, 6)
             if 0 <= t - lag < nc:
                 stage(t - lag)
             if lag == 0:
-                attention(t)
-        fetch_right(t + 2)
-        if t == wide + 2:
-            fetch_left(groups)
+                work(t)
+        if t == 1:
+            fetch_right(2)
+        if t >= 1:
+            fetch_right(t + 2)
+        for g in range(1, groups):
+            if t == wide + g - (3 if g < left_slots else 2):
+                fetch_left(g)
     for t in range(nc):
-        p = out.at[t, :, 1 - c]
-        remote(p, p, cs.at[t], cr.at[t], to_c).wait_recv()
+        p = out.at[t, :, 1 - c, :, :, pl.ds(0, widths[t])]
+        remote_copy(p, p, cs.at[t], cr.at[t], to_c).wait_recv()
     for key in list(pending):
-        drain(key) if key[0] != "l" else [copy.wait() for copy in pending.pop(key)]
-
-
-def reduced(two_t, hid_own, hid_other, flat_t, grads, df, da, attention, heads, S, cid):
+        drain(key)
+    for key in list(loads):
+        landed(key)
+
+
+def backward(two_t, hid_t, transposed, grads, dy, back, middle, w_out, gains, attention, tables, heads, S, cid):
     D, T = two_t.shape
     sides, _, half_ff = grads.shape
-    n = df.shape[1]
+    piece = middle.shape[0]
+    n = w_out.shape[2]
     r = D // (S * 8)
     parts = half_ff // n
-    groups = 1 + 2 * half_ff // (S * 8 * r)
-    nc = sides * parts + groups
-    slots = min(nc, 6)
+    rows_groups = 2 * half_ff // (S * 8 * r)
+    mixed = attention[2].shape[1] + 2 * HEAD
+    nc = sides * parts + rows_groups + 3
     m = S * r
-    queries, keys = attention[2:4]
+    slots = 5
+    keys = attention[3].shape[0]
+    reach = keys // piece - 1
     dma = pltpu.SemaphoreType.DMA
-    hid_shape = (S // 2, groups - 1, 4, 2, r, T)
+    hid_shape = (S // 2, rows_groups, 4, 2, r, T)
 
     def body(*refs):
-        reduce_kernel(heads, sides, parts, S, *refs)
-
-    return pl.pallas_call(
+        backward_kernel(heads, sides, parts, S, *refs)
+
+    def vmem(*shape):
+        return pltpu.VMEM(shape, BF)
+
+    results = pl.pallas_call(
         body,
         out_shape=(
             jax.ShapeDtypeStruct((nc, 4, 2, 2, r, n), BF),
-            jax.ShapeDtypeStruct(queries.shape, F32),
-            jax.ShapeDtypeStruct(keys.shape, F32),
-            jax.ShapeDtypeStruct(keys.shape, F32),
+            jax.ShapeDtypeStruct(hid_shape, BF),
+            jax.ShapeDtypeStruct((piece, D), F32),
+            jax.ShapeDtypeStruct((piece, mixed), BF),
         ),
-        in_specs=[ANY] * 7 + [VM] * 8,
-        out_specs=(ANY, VM, VM, VM),
+        in_specs=[ANY] * 13 + [VM] * 9,
+        out_specs=(ANY, ANY, ANY, VM),
         scratch_shapes=[
-            pltpu.VMEM((groups, 8, S, r, T), BF),
-            pltpu.VMEM((5, T, n), BF),
-            pltpu.VMEM((T, n), BF),
-            pltpu.VMEM((2, 4, m, n), BF),
-            pltpu.VMEM((slots, 4, m, n), BF),
-            pltpu.VMEM((2, 2, m, n), BF),
-            pltpu.VMEM((slots, 2, m, n), BF),
-            pltpu.VMEM((2, S, 2, r, n), BF),
-            pltpu.VMEM((nc, S - 1, 2, r, n), BF),
-            pltpu.VMEM((2, 2, r, n), BF),
-            pltpu.VMEM((WINDOW + queries.shape[0] // 2, queries.shape[0] // 2), F32),
-            pltpu.VMEM((HEAD, keys.shape[0]), BF),
-            dma((3,)),
-            dma((groups + 1, 8, 2)),
-            dma((nc,)),
+            vmem(3, 8, S, r, T),
+            vmem(4, T, n),
+            vmem(T, n),
+            vmem(T, mixed // 2),
+            vmem(2, 4, m, n),
+            vmem(slots, 4, m, n),
+            vmem(2, 2, m, n),
+            vmem(slots, 2, m, n),
+            vmem(2, S, 2, r, n),
+            vmem(nc, S - 1, 2, r, n),
+            vmem(2, 2, r, n),
+            vmem(piece, D),
+            vmem(piece, D),
+            vmem(piece, D),
+            vmem(reach, piece, 2 * HEAD),
+            vmem(reach, piece, 2 * HEAD),
+            vmem(*gains.shape),
+            pltpu.VMEM((piece, D), F32),
+            pltpu.VMEM((keys, HEAD), F32),
+            pltpu.VMEM((keys, HEAD), F32),
+            pltpu.VMEM((WINDOW + piece // 2, piece // 2), F32),
+            pltpu.VMEM((HEAD, keys), BF),
+            dma((rows_groups + 3, 8, 2)),
+            dma((nc, 2)),
+            dma((9,)),
+            dma((8,)),
+            dma((reach,)),
+            dma((reach,)),
             dma((nc, 4)),
             dma((nc, 4)),
             dma((nc, 2)),
@@ -978,24 +1165,25 @@
             dma((nc,)),
         ],
         compiler_params=pltpu.CompilerParams(
-            collective_id=cid, has_side_effects=True, vmem_limit_bytes=VMEM_BYTES
-        ),
-        cost_estimate=pl.CostEstimate(
-            flops=4 * T * D * 3 * half_ff, bytes_accessed=400 * 2**20, transcendentals=0
+            collective_id=cid, has_side_effects=True, vmem_limit_bytes=BACKWARD_VMEM
         ),
     )(
         two_t.reshape(S, 4, 2, r, T),
-        hid_own.reshape(hid_shape),
-        hid_other.reshape(hid_shape),
-        flat_t.reshape(S, 4, 2, r, T),
+        hid_t.reshape(hid_shape),
+        *[v.reshape(S, 4, 2, r, piece) for v in transposed],
         grads,
-        df,
-        da,
+        *dy,
+        back,
+        middle,
+        w_out,
+        gains,
         *attention,
+        *tables,
     )
-
-
-def adam_kernel(total, tiles, gains, count_ref, rates_ref, g_ref, w_ref, m_ref, g_out, w_out, m_out, *more):
+    return results[0], results[2], results[3]
+
+
+def adam_kernel(total, widths, gains, count_ref, rates_ref, g_ref, w_ref, m_ref, g_out, w_out, m_out, *more):
     step_value = count_ref[0].astype(F32)
     log_first = jnp.log(jnp.full((8, 128), beta_first, F32))
     log_second = jnp.log(jnp.full((8, 128), beta_second, F32))
@@ -1003,15 +1191,16 @@
     unfix_second = (1.0 / (1.0 - jnp.exp(step_value * log_second)))[:1, :1]
     rate, decay = rates_ref[0], rates_ref[1]
     rows = w_ref.shape[0]
-    n = w_ref.shape[1] // tiles
-
-    @pl.when((pl.program_id(1) == 0) & (pl.program_id(2) == 0))
-    def _():
-        more[0][...] = jnp.zeros_like(more[0])
-
-    for i in range(tiles):
-        at = pl.ds(i * n, n)
-        grad = g_ref[i, 0, 0].reshape(rows, n).astype(F32) * (1.0 / total)
+
+    if gains:
+
+        @pl.when((pl.program_id(1) == 0) & (pl.program_id(2) == 0))
+        def _():
+            more[0][...] = jnp.zeros_like(more[0])
+
+    for i, n in enumerate(widths):
+        at = pl.ds(sum(widths[:i]), n)
+        grad = g_ref[i, :, 0, :, :, :n].reshape(rows, n).astype(F32) * (1.0 / total)
         w = w_ref[:, at]
         first = beta_first * m_ref[0, :, at] + (1.0 - beta_first) * grad
         second = beta_second * m_ref[1, :, at] + (1.0 - beta_second) * grad * grad
@@ -1027,55 +1216,49 @@
 
 
 def adam_call(
-    weight, moments, grads, count, rates, total, base, sides, tiles, down=False, gains=False, cores=(0, 1), held=None
+    weight, moments, grads, count, rates, total, base, widths, sides=1, tiles=1, gains=False, chips=4
 ):
     _, _, _, _, r, n = grads.shape
-    wide = 1 if down else tiles
+    wide = len(widths)
 
     def g_place(kk, cc, ss, tt):
-        return (base // wide + ss + tt, kk, cores[0] + cc, 0, 0, 0)
+        return (base // wide + ss + tt, kk, cc, 0, 0, 0)
 
     def place(kk, cc, ss, tt):
-        return (tt * 4 + kk, ss * 2 + cores[0] + cc)
+        return (tt * (4 // chips) + kk, ss * 2 + cc)
 
     def m_place(*at):
         return (0,) + place(*at)
 
-    w_spec = pl.BlockSpec((2 * r, wide * n), place)
-    m_spec = pl.BlockSpec((2, 2 * r, wide * n), m_place)
+    rows = chips * 2 * r
+    w_spec = pl.BlockSpec((rows, sum(widths)), place)
+    m_spec = pl.BlockSpec((2, rows, sum(widths)), m_place)
     smem = pl.BlockSpec(memory_space=pltpu.SMEM)
     like = jax.ShapeDtypeStruct(weight.shape, F32)
     out_specs = [w_spec, w_spec, m_spec]
     out_shape = [like, like, jax.ShapeDtypeStruct(moments.shape, F32)]
     if gains:
-        out_specs.append(pl.BlockSpec((2 * r, 128), lambda kk, cc, ss, tt: (kk, 0)))
+        out_specs.append(pl.BlockSpec((rows, 128), lambda kk, cc, ss, tt: (kk, 0)))
         out_shape.append(jax.ShapeDtypeStruct((weight.shape[0], 128), F32))
-    else:
-        out_specs.append(pl.BlockSpec((8, 128), lambda *at: (0, 0)))
-        out_shape.append(jax.ShapeDtypeStruct((8, 128), F32))
-    before = [] if held is None else list(held[:3])
 
     def body(*refs):
-        five, results = refs[:5], refs[5 + len(before) :]
-        adam_kernel(total, wide, gains, *five, *results)
+        adam_kernel(total, widths, gains, *refs)
 
     return pl.pallas_call(
         body,
-        grid=(4, len(cores), sides, tiles // wide),
-        in_specs=[smem, smem, pl.BlockSpec((wide, 1, 1, 2, r, n), g_place), w_spec, m_spec]
-        + [ANY] * len(before),
+        grid=(4 // chips, 2, sides, tiles),
+        in_specs=[smem, smem, pl.BlockSpec((wide, chips, 1, 2, r, n), g_place), w_spec, m_spec],
         out_specs=out_specs,
         out_shape=out_shape,
-        input_output_aliases={5 + i: i for i in range(len(before))},
         compiler_params=pltpu.CompilerParams(
             dimension_semantics=("arbitrary",) * 4, vmem_limit_bytes=VMEM_BYTES
         ),
         cost_estimate=pl.CostEstimate(
-            flops=10 * len(cores) * weight.size,
-            bytes_accessed=15 * len(cores) * weight.size,
+            flops=20 * weight.size,
+            bytes_accessed=30 * weight.size,
             transcendentals=weight.size,
         ),
-    )(count, rates, grads, weight, moments, *before)
+    )(count, rates, grads, weight, moments)
 
 
 def dot(a, b):
@@ -1088,49 +1271,6 @@
 
 def dot_t(a, b):
     return lax.dot_general(a, b, (((1,), (1,)), ((), ())), preferred_element_type=F32)
-
-
-def arranged(left, S):
-    T, D = left.shape
-    r = D // (S * 8)
-    return left.T.reshape(S, 2, 2, 2, r, T).transpose(3, 1, 2, 0, 4, 5)
-
-
-def plane_sum(rows, right, between, S):
-    y = lax.axis_index("y")
-    x = lax.axis_index("x")
-    r, T = rows.shape[4:]
-    N = right.shape[1]
-
-    def pick(h, yy, xx):
-        block = lax.dynamic_index_in_dim(rows[h], yy, 0, keepdims=False)
-        return lax.dynamic_index_in_dim(block, xx, 0, keepdims=False).reshape(S * r, T)
-
-    first0 = jnp.concatenate([pick(0, 0, 1 - x), pick(0, 1, 1 - x)], axis=0)
-    first1 = jnp.concatenate([pick(1, 1 - y, 0), pick(1, 1 - y, 1)], axis=0)
-    sent = (dot_rows(first0, right).astype(BF), dot_rows(first1, right).astype(BF))
-    sent = between(0, sent)
-    got0 = swapped(sent[0], "x")
-    got1 = swapped(sent[1], "y")
-    got0, got1 = between(1, (got0, got1))
-    got0 = got0.reshape(2, S * r, N)
-    got1 = got1.reshape(2, S * r, N)
-
-    def at(got, i):
-        return lax.dynamic_index_in_dim(got, i, 0, keepdims=False).astype(F32)
-
-    sent = (
-        (dot_rows(pick(0, 1 - y, x), right) + at(got0, 1 - y)).astype(BF),
-        (dot_rows(pick(1, y, 1 - x), right) + at(got1, 1 - x)).astype(BF),
-    )
-    sent = between(2, sent)
-    next0 = swapped(sent[0], "y")
-    next1 = swapped(sent[1], "x")
-    next0, next1 = between(3, (next0, next1))
-    last0 = dot_rows(pick(0, y, x), right) + at(got0, y) + next0.astype(F32)
-    last1 = dot_rows(pick(1, y, x), right) + at(got1, x) + next1.astype(F32)
-    both = [v.astype(BF).reshape(S, 1, r, N) for v in (last0, last1)]
-    return jnp.concatenate(both, axis=1).reshape(S, 2 * r, N)
 
 
 def on_device(
@@ -1215,6 +1355,7 @@
             middle,
             normed_two,
             two_other,
+            *transposed,
         ) = forward(
             [
                 halves(in_low).reshape(2, 4, 2, r, in_half),
@@ -1234,6 +1375,7 @@
         )
         in_full = in_full.reshape(2, D, in_half)
         out_full = out_full.reshape(2, D, d_half)
+        gains_small = gains_full
         gains_full = gains_full[:, :2].transpose(1, 0, 2).reshape(2, D)
         down_full = down_full.reshape(2, FF, d_half)
         gate_full = gate_full.reshape(D, 2 * half_ff)
@@ -1288,13 +1430,9 @@
     def core_sum(v):
         keep = lax.dynamic_slice_in_dim(v, core * piece_len, piece_len, 0)
         give = lax.dynamic_slice_in_dim(v, (1 - core) * piece_len, piece_len, 0)
-        return keep + swapped(give.astype(BF), "c").astype(F32)
+        return keep.astype(F32) + swapped(give, "c").astype(F32)
 
     df_other = swapped(cotangent[0], "c")
-    df_both = ordered(cotangent[0], df_other)
-    normed_both = pair(normed)
-    flat_both = pair(flat_heads)
-
     two_t, hid_t, grad_gated, out_sum, two_sum = mlp_call(
         core.reshape(1).astype(jnp.int32),
         (normed_two, two_other),
@@ -1302,131 +1440,93 @@
         gate_full,
         down_full,
     )
-
     output = middle + core_sum(out_sum)
     block_out = output.astype(BF)[None]
-    grad_normed_two = core_sum(two_sum)
-    _, norm_pull_two = jax.vjp(root_norm, middle, gains_wide[1])
-    grad_middle_norm, grad_gain_two = norm_pull_two(grad_normed_two)
-    grad_middle = upstream + grad_middle_norm
-    grad_branch = grad_middle.astype(BF)
-
-    grad_flat = dot_t(grad_branch[:, :d_half], out_full[0]) + dot_t(
-        grad_branch[:, d_half:], out_full[1]
-    )
-    grad_attended = jnp.where(live_rows[:, None], grad_flat, 0.0).astype(BF)
-
-    attention = (
-        query_row,
-        key_column,
-        queries,
-        key_rows,
-        values,
-        flat_heads,
-        grad_attended,
-        log_totals,
-    )
+    token_total = piece_len * S * Y * 4 * block_in.shape[0]
+    step_value = update_count[0].astype(F32)
+    rates = optimizer_rates
+
     if fast:
-        df_half = lax.dynamic_slice_in_dim(df_both, core * d_half, d_half, 1)
-        mlp_sums, grad_query_all, grad_keys, grad_values = reduced(
+        sums, grad_middle, grad_mixed = backward(
             two_t,
             hid_t,
-            swapped(hid_t, "c"),
-            flat_both.T,
+            transposed,
             grad_gated,
-            df_half,
-            grad_branch,
-            attention,
+            (cotangent[0], df_other),
+            two_sum,
+            middle,
+            out_full,
+            gains_small,
+            (query_row, key_column, queries, key_rows, values, flat_heads, log_totals),
+            (cos_table, sin_table),
             HEADS,
             S,
             2,
         )
     else:
-        grad_query_all, grad_keys, grad_values = attend_back(*attention, HEADS, piece_len // 2)
-    grad_pairs = jnp.concatenate([grad_keys, grad_values], axis=1)
-    own_grad = grad_pairs[key_span:]
-    grad_pairs = grad_pairs.astype(BF)
-    sent_rows = [
-        grad_pairs[key_span - back_step * piece_len : key_span - (back_step - 1) * piece_len]
-        for back_step in range(1, reach_count + 1)
-    ]
-    token_total = piece_len * S * Y * 4 * block_in.shape[0]
-    rates = optimizer_rates
-    done = {}
-
-    def update(name, *arguments):
-        wait, weight, moments, grads, *rest = arguments
-        count, wait = lax.optimization_barrier((update_count, wait))
-        done[name] = adam_call(
-            weight, moments, grads, count, rates, float(token_total), *rest, held=done.get(name)
+        grad_normed_two = core_sum(two_sum)
+        _, norm_pull_two = jax.vjp(root_norm, middle, gains_wide[1])
+        grad_middle_norm, grad_gain_two = norm_pull_two(grad_normed_two)
+        grad_middle = upstream + grad_middle_norm
+        grad_branch = grad_middle.astype(BF)
+        grad_flat = dot_t(grad_branch[:, :d_half], out_full[0]) + dot_t(
+            grad_branch[:, d_half:], out_full[1]
         )
-        return wait
-
-    def behind(name, arrays):
-        arrays, token = lax.optimization_barrier((arrays, done[name][3]))
-        done[name] = tuple(done[name][:3]) + (token,)
-        return arrays
-
-    tiles = half_ff // d_half
-    chunk_out = 3 * tiles
-    if fast:
-        sent_rows = update(
-            "out", sent_rows, output_proj, output_moments, mlp_sums, chunk_out, 1, 1
+        grad_attended = jnp.where(live_rows[:, None], grad_flat, 0.0).astype(BF)
+        grad_query_all, grad_keys, grad_values = attend_back(
+            query_row,
+            key_column,
+            queries,
+            key_rows,
+            values,
+            flat_heads,
+            grad_attended,
+            log_totals,
+            HEADS,
+            piece_len // 2,
         )
-    got_rows = [passed_along(rows, "z", -i - 1) for i, rows in enumerate(sent_rows)]
-    if fast:
-        got_rows = behind("out", got_rows)
-    for rows in got_rows:
-        own_grad = own_grad + rows.astype(F32)
-    grad_query_raw = rotate(
-        grad_query_all.reshape(piece_len, HEADS, HEAD), positions, -1.0
-    ).reshape(piece_len, width_q)
-    grad_key_raw = rotate(own_grad[:, :HEAD], positions, -1.0)
-    grad_mixed = jnp.concatenate([grad_query_raw, grad_key_raw, own_grad[:, HEAD:]], axis=1).astype(
-        BF
-    )
+        grad_pairs = jnp.concatenate([grad_keys, grad_values], axis=1)
+        own_grad = grad_pairs[key_span:]
+        for back_step in range(1, reach_count + 1):
+            sent_rows = grad_pairs[
+                key_span - back_step * piece_len : key_span - (back_step - 1) * piece_len
+            ]
+            own_grad = own_grad + passed_along(sent_rows, "z", -back_step)
+        grad_query_raw = rotate(
+            grad_query_all.reshape(piece_len, HEADS, HEAD), positions, -1.0
+        ).reshape(piece_len, width_q)
+        grad_key_raw = rotate(own_grad[:, :HEAD], positions, -1.0)
+        grad_mixed = jnp.concatenate(
+            [grad_query_raw, grad_key_raw, own_grad[:, HEAD:]], axis=1
+        ).astype(BF)
     grad_normed = dot_t(grad_mixed[:, :in_half], in_full[0]) + dot_t(
         grad_mixed[:, in_half:], in_full[1]
     )
     _, norm_pull_one = jax.vjp(root_norm, tokens, gains_wide[0])
     grad_tokens_norm, grad_gain_one = norm_pull_one(grad_normed)
     block_in_grad = (grad_middle + grad_tokens_norm).astype(BF)[None]
-    step_value = update_count[0].astype(F32)
-    mixed_half = half_pair(grad_mixed)
 
     if fast:
-        gains_two = []
-
-        def gate_update(wait, which):
-            wait = update(
-                "gate", wait, gate_up, gate_moments, mlp_sums, 0, 2, tiles, False, True, (which,)
+
+        def adam(weight, moments, *rest, **more):
+            return adam_call(
+                weight, moments, sums, update_count, rates, float(token_total), *rest, **more
             )
-            gains_two.append(done["gate"][3])
-            return wait
-
-        def between(i, arrays):
-            if i == 0:
-                return gate_update(arrays, 0)
-            if i == 1:
-                return behind("gate", arrays)
-            return arrays
-
-        share = plane_sum(arranged(normed_both, S), mixed_half, between, S)
-        share = update(
-            "down", share, down_weight, down_moments, mlp_sums, 2 * tiles, 1, tiles, True
+
+        tiles = half_ff // d_half
+        same = (d_half,) * tiles
+        gate_grad, gate_new, gate_mom, gain_two = adam(
+            gate_up, gate_moments, 0, same, sides=2, gains=True, chips=2
         )
-        mine = lax.psum_scatter(share, "z", scatter_dimension=0, tiled=False)
-        mine = behind("down", mine)
-        mine = gate_update(mine, 1)
-        in_sum = lax.all_gather(mine, ("y", "x", "c"), axis=0)
-        in_sum = behind("gate", in_sum).reshape(1, 4, 2, 2, r, in_half)
-        update("in", in_sum, input_proj, input_moments, in_sum, 0, 1, 1, False, True)
-        in_grad, in_new, in_mom, gain_one = done["in"]
-        out_grad, out_new, out_mom, _ = done["out"]
-        gate_grad, gate_new, gate_mom, _ = done["gate"]
-        down_grad, down_new, down_mom, _ = done["down"]
+        down_grad, down_new, down_mom = adam(
+            down_weight, down_moments, 2 * tiles, (d_half,), tiles=tiles
+        )
+        out_grad, out_new, out_mom = adam(output_proj, output_moments, 3 * tiles, (d_half,))
+        in_grad, in_new, in_mom, gain_one = adam(
+            input_proj, input_moments, 3 * tiles + 1, split_widths(in_half, d_half), gains=True
+        )
         gain_grad = jnp.stack(
-            [jnp.sum(v, axis=1) for v in (gain_one, gains_two[0] + gains_two[1])]
+            [jnp.sum(v, axis=1) for v in (gain_one, gain_two)]
         ) / gains_low.astype(F32)
     else:
 
@@ -1442,6 +1542,10 @@
 
         two_both = ordered(normed_two, two_other)
         grad_half = half_pair(grad_branch)
+        mixed_half = half_pair(grad_mixed)
+        normed_both = pair(normed)
+        flat_both = pair(flat_heads)
+        df_both = pair(cotangent[0])
         gate_half = [summed(two_both, grad_gated[side]) for side in range(2)]
         gate_sum = jnp.concatenate(
             [lax.all_gather(g, "c", axis=1, tiled=True) for g in gate_half], axis=1

time: 795 us -> 669 us (0.84)
  waiting for transfers between devices: 40.1 us -> 0.01 us
  local copies, waits for them, and re-layouts: 52.7 us -> 23 us
  other arithmetic: 50 us -> 23.5 us
  matrix products: 18.9 us -> 5.29 us
  between operations: 15.6 us -> 2.04 us
  starting transfers between devices: 8.52 us -> 0.52 us
    reduce_scatter x1 -> x0, waiting for transfers between devices: 19.9 us -> none  [on_device(): mine = lax.psum_scatter(share, 'z', scatter_dimension=0, tiled=False)]
    ppermute x2 -> x0, waiting for transfers between devices: 12.2 us -> none  [passed_along(): return lax.ppermute(block, axis, route)]
    slice x7 -> x1, local copies, waits for them, and re-layouts: 15 us -> 5.56 us  [on_device(): in_full[0]]
    dot_general x6 -> x0, matrix products: 8.98 us -> none  [dot_rows(): lax.dot_general(a, b, (((1,), (0,)), ((), ())), preferred_element_type=F32)]
    ppermute x11 -> x2, waiting for transfers between devices: 8.01 us -> 0.01 us  [swapped(): return lax.ppermute(block, axis, [(0, 1), (1, 0)])]
    pallas_call x6 -> x5, Pallas kernels: 354 us -> 361 us  [the longest x1 284 us: backward(): pl.pallas_call(body, out_shape=(jax.ShapeDtypeStruct((nc, 4, 2, 2, r, n),...]
  transfers between devices with their start and end apart: 15 -> 2, of which waited for: 5 -> 0; matrix products, arithmetic and copies ran while one was open for 12% -> 6% of each run, Pallas kernels for 42% -> 83%
where the time goes in v4:
time: 669 us; the launch traced here: 665 us
  Pallas kernels  610 us (91%)
  other arithmetic  23.5 us (4%)
  local copies, waits for them, and re-layouts  23 us (3%)
    pallas_call x1, Pallas kernels, backward(): pl.pallas_call(body, out_shape=(jax.ShapeDtypeStruct((nc, 4, 2, 2, r, n),...  284 us
    pallas_call x1, Pallas kernels, forward(): pl.pallas_call(body, out_shape=tuple(outs), in_specs=[VM] * 10, out_specs...  191 us
    pallas_call x4, Pallas kernels, adam_call(): pl.pallas_call(body, grid=(4 // chips, 2, sides, tiles), in_specs=[smem,...  77.6 us
    pallas_call x1, Pallas kernels, mlp_call(): pl.pallas_call(body, grid_spec=pltpu.PrefetchScalarGridSpec(num_scalar_pr...  58.5 us
  transfers between devices with their start and end apart: 2, of which 0 were waited for; matrix products, arithmetic and copies ran while one was open for 6% of the time, Pallas kernels for 83%

profile of v4, /device:TPU:0, one launch (start us, length us, event | category | flops | bytes accessed | tf_op | source)
XLA Modules:
  0.0 664.9 jit_solution(1935973324329148625)
XLA Ops:
  0.7 0.0 copy-start.2
  0.7 0.5 collective-permute-start
  1.2 0.6 compare_select_fusion
  1.8 1.8 convert_element_type.54
  3.6 0.0 copy-start
  3.6 1.1 fusion.19
  4.7 0.0 copy-done.2
  4.7 0.1 convert_element_type.53
  4.8 1.2 fusion.18
  6.0 1.5 copy-done
  7.5 0.4 convert_element_type.55
  8.0 0.2 fusion.17
  8.2 0.8 pad_dynamic-slice_fusion
  9.0 2.4 pad_maximum_fusion.3.refs_1_
  11.3 2.5 pad_maximum_fusion.2.refs_0_
  13.9 0.0 copy-start.12
  13.9 2.1 pad_maximum_fusion.refs_2_
  16.0 0.0 copy-done.12
  16.0 1.8 fusion.10
  17.8 3.4 dynamic-slice_convert_fusion.1
  21.2 1.3 constant_dynamic-slice_fusion.1.refs_8_.refs_13_
  23.2 0.0 copy-done.8
  23.2 1.2 concatenate.24.refs_4_
  24.5 1.1 broadcast_in_dim.32.refs_9_.refs_14_
  25.6 2.1 pad_maximum_fusion.1.refs_3_
  27.7 190.8 %shard_map.278 = (bf16[2,4,4,2,48,896]{5,4,3,2,1,0:T(8,128)(2,1)}, bf16[2,4,4,2,48,768]{5,4,3,2,1,0:T(8,128)(2,1)}, bf16[2,4,4,2,144,768]{5,4,3,2,1,0:T(8,128)(2...) custom-call(bf16[2,4,2,48,896]{4,3,2,1,0:T(8,128)(2,1)} %pad_maximum, ...), custom_call_target="tpu_custom_call" | custom-call | tf_op jit(solution)/shard_map/pallas_call | solution.py:530
  218.5 0.7 slice_bitcast_fusion
  219.3 0.0 copy-done.9
  219.3 0.6 fusion.20
  219.9 5.6 fusion.16
  225.5 0.0 collective-permute-done.refs_4_.refs_8_
  225.5 58.5 %shard_map.279 = (bf16[1536,1024]{1,0:T(8,128)(2,1)}, bf16[2304,1024]{1,0:T(8,128)(2,1)}, bf16[2,1024,2304]{2,1,0:T(8,128)(2,1)}, bf16[1024,1536]{1,0:T(8,128)(2,1)}, bf16[1024,1536]{1,0:T(8,128)(2,1)}) custom-call(s32[1]{0:T(128)} %bitcast.10.refs_0_, bf16[512,1536]{1,0:T(8,128)(2,1)} %get-tuple-element.57.refs_1_, ...), custom_call_target="tpu_custom_call" | custom-call | flops 43486543872 | bytes 41943040 | tf_op jit(solution)/shard_map/pallas_call | solution.py:699
  284.0 2.7 constant_dynamic-slice_fusion
  286.7 0.0 collective-permute-start.1
  286.7 283.5 %shard_map.280 = (bf16[12,4,2,2,48,768]{5,4,3,2,1,0:T(8,128)(2,1)}, bf16[2,3,4,2,48,1024]{5,4,3,2,1,0:T(8,128)(2,1)}, f32[512,1536]{1,0:T(8,128)}, bf16[512,1792]{1,0:T(8,128)(2,1)}) custom-call(bf16[4,4,2,48,1024]{4,3,2,1,0:T(8,128)(2,1)} %bitcast.61, bf16[2,3,4,2,48,1024]{5,4,3,2,1,0:T(8,128)(2,1)} %bitcast.60, bf16[4,4,2,48,512]{4,3,2,1,0:T(8,128)(2,1)} %bitcast.71, ...), custom_call_target="tpu_custom_call" | custom-call | tf_op jit(solution)/shard_map/pallas_call | solution.py:1114
  570.2 7.1 %shard_map.282 = (f32[384,1536]{1,0:T(8,128)}, f32[384,1536]{1,0:T(8,128)}, f32[2,384,1536]{2,1,0:T(8,128)}) custom-call(s32[1]{0:T(128)S(6)} %copy.34.refs_0_, f32[2]{0:T(128)} %refs_1_.7, bf16[12,4,2,2,48,768]{5,4,3,2,1,0:T(8,128)(2,1)} %get-tuple-element.80.refs_2_, f32[384,1536]{1,0:T(8,128)} %refs_3_.5, f32[2,384,1536]{2,1,0:T(8,128)} %refs_4_.5), custom_call_target="tpu_custom_call" | custom-call | flops 11796480 | bytes 17694720 | tf_op jit(solution)/shard_map/pallas_call | solution.py:1247
  577.4 9.3 %shard_map.281 = (f32[384,1792]{1,0:T(8,128)}, f32[384,1792]{1,0:T(8,128)}, f32[2,384,1792]{2,1,0:T(8,128)}, f32[384,128]{1,0:T(8,128)}) custom-call(s32[1]{0:T(128)S(6)} %copy.34.refs_0_, f32[2]{0:T(128)} %refs_1_.7, bf16[12,4,2,2,48,768]{5,4,3,2,1,0:T(8,128)(2,1)} %get-tuple-element.80.refs_2_, f32[384,1792]{1,0:T(8,128)} %refs_3_.4, f32[2,384,1792]{2,1,0:T(8,128)} %refs_4_.4), custom_call_target="tpu_custom_call" | custom-call | flops 13762560 | bytes 20643840 | tf_op jit(solution)/shard_map/pallas_call | solution.py:1247
  586.7 1.1 reduce_sum.42
  587.8 19.7 %shard_map.284 = (f32[1152,1536]{1,0:T(8,128)}, f32[1152,1536]{1,0:T(8,128)}, f32[2,1152,1536]{2,1,0:T(8,128)}) custom-call(s32[1]{0:T(128)S(6)} %copy.34.refs_0_, f32[2]{0:T(128)} %refs_1_.7, bf16[12,4,2,2,48,768]{5,4,3,2,1,0:T(8,128)(2,1)} %get-tuple-element.80.refs_2_, f32[1152,1536]{1,0:T(8,128)} %refs_3_.7, f32[2,1152,1536]{2,1,0:T(8,128)} %refs_4_.7), custom_call_target="tpu_custom_call" | custom-call | flops 35389440 | bytes 53084160 | tf_op jit(solution)/shard_map/pallas_call | solution.py:1247
  607.5 41.4 %shard_map.283 = (f32[384,9216]{1,0:T(8,128)}, f32[384,9216]{1,0:T(8,128)}, f32[2,384,9216]{2,1,0:T(8,128)}, f32[384,128]{1,0:T(8,128)}) custom-call(s32[1]{0:T(128)S(6)} %copy.34.refs_0_, f32[2]{0:T(128)} %refs_1_.7, bf16[12,4,2,2,48,768]{5,4,3,2,1,0:T(8,128)(2,1)} %get-tuple-element.80.refs_2_, f32[384,9216]{1,0:T(8,128)} %refs_3_.6, f32[2,384,9216]{2,1,0:T(8,128)} %refs_4_.6), custom_call_target="tpu_custom_call" | custom-call | flops 70778880 | bytes 106168320 | tf_op jit(solution)/shard_map/pallas_call | solution.py:1247
  648.9 1.1 reduce_sum.43
  650.0 0.0 copy-done.7
  650.0 0.0 copy-start.10
  650.0 0.0 copy-start.3
  650.0 0.0 copy-start.6
  650.0 0.0 copy-start.13
  650.0 3.2 fusion.7
  653.2 0.0 copy-done.10
  653.2 0.0 copy-start.11
  653.2 1.9 fusion.15
  655.1 0.6 pad_maximum_fusion.4
  655.7 0.0 copy-done.3
  655.7 0.0 copy-done.6
  655.7 0.0 copy-done.13
  655.7 2.1 fusion.1
  657.8 0.0 copy-done.11
  657.8 0.0 copy-done.4
  657.9 0.0 copy-start.1
  657.9 0.0 copy-start.5
  657.9 1.9 fusion.6
  659.8 0.0 collective-permute-done.1
  659.8 0.4 copy-done.1
  660.2 1.1 copy-done.5
  661.3 3.2 fusion.5
  (13 shorter events, 0.1 us)
Async XLA Ops:
  0.7 4.0 copy-start.2
  0.7 224.8 %collective-permute-start = (bf16[512,1536]{1,0:T(8,128)(2,1)}, bf16[512,1536]{1,0:T(8,128)(2,1)}, u32[]{:S(2)}, u32[]{:S(2)}) collective-permute-start(bf16[512,1536]{1,0:T(8,128)(2,1)} %bitcast.68), channel_id=1, source_target_pairs={{0,4},{4,0},{1,5},{5,1},{2,6},{6,2},{3,7},{7,3},{8,12},{12,8},{9,1... | collective-permute-start | bytes 4718600 | tf_op jit(solution)/shard_map/ppermute | solution.py:36
  3.6 3.9 copy-start
  13.9 2.1 copy-start.12
  17.8 5.4 copy-start.8
  27.7 191.6 %copy-start.9 = (f32[2]{0:T(128)S(1)}, f32[2]{0:T(128)}, u32[]{:S(2)}) copy-start(f32[2]{0:T(128)} %refs_1_.7) | copy-start | bytes 28
  286.7 373.1 %collective-permute-start.1 = (bf16[512,1536]{1,0:T(8,128)(2,1)}, bf16[512,1536]{1,0:T(8,128)(2,1)}, u32[]{:S(2)}, u32[]{:S(2)}) collective-permute-start(bf16[512,1536]{1,0:T(8,128)(2,1)} %constant_dynamic-slice_fusion), channel_id=1, source_target_pairs={{0,4},{4,0},{1,5},{5,1},{2,6},{6,2},{3,7},{7,3},{8,12},{12,8},{9,1... | collective-permute-start | bytes 4718600 | tf_op jit(solution)/shard_map/ppermute | solution.py:36
  607.5 42.5 %copy-start.7 = (bf16[1,4,4,2,48,896]{5,4,3,2,1,0:T(8,128)(2,1)S(1)}, bf16[1,4,4,2,48,896]{5,4,3,2,1,0:T(8,128)(2,1)}, u32[]{:S(2)}) copy-start(bf16[1,4,4,2,48,896]{5,4,3,2,1,0:T(8,128)(2,1)} %get-tuple-element.102) | copy-start | bytes 8257540
  650.0 3.2 copy-start.10
  650.0 5.7 copy-start.3
  650.0 5.7 copy-start.6
  650.0 5.7 copy-start.13
  653.2 4.6 copy-start.11
  655.7 2.2 copy-start.4
  657.9 2.3 copy-start.1
  657.9 3.4 copy-start.5

commit v5 on v4

--- a/solution.py
+++ b/solution.py
@@ -72,9 +72,14 @@
     return (optimizer_rates[0] * update, jnp.stack([first_moment, second]))
 
 
-def gather_kernel(shared, chunks, S, own, full, sems, small_own, small_full, work):
+def gather_kernel(shared, groups, S, own, full, sems, small_own, small_full, prepare, work):
     n = len(shared)
-    nc = len(chunks)
+    chunks = [chunk for group in groups for chunk in group]
+    members = []
+    for group in groups:
+        first = members[-1][-1] + 1 if members else 0
+        members.append(range(first, first + len(group)))
+    ng = len(groups)
     F = S - 1
     loc, zs, zr, xs, xr, ys, yr, cs, cr, ss, sr = sems
     y, x, c, z = (lax.axis_index(a) for a in ("y", "x", "c", "z"))
@@ -102,21 +107,30 @@
         pl.semaphore_signal(barrier, inc=1, device_id=target, device_id_type=MESH_ID)
     pl.semaphore_wait(barrier, 3 + F)
 
-    def own_half(i):
-        return own[i].at[c] if shared[i] else own[i]
-
-    def full_half(i):
-        return full[i].at[c] if shared[i] else full[i]
-
-    def box(q):
-        _, r0, rn, c0, cn = chunks[q]
+    def box(q, half):
+        i, r0, rn, c0, cn, _ = chunks[q]
+        if shared[i]:
+            columns = full[i].shape[-1] // 2
+            c0 = pl.multiple_of(half * columns + c0, 128)
         return pl.ds(r0, rn), pl.ds(c0, cn)
 
-    def part(ref, q, zz, kk, h=None):
-        rr, cc = box(q)
+    def part(q, zz, kk, h=None, half=c):
+        rr, cc = box(q, half)
+        held = full[chunks[q][0]]
         if h is None:
-            return ref.at[zz, kk, :, rr, cc]
-        return ref.at[zz, kk, h, rr, cc]
+            return held.at[zz, kk, :, rr, cc]
+        return held.at[zz, kk, h, rr, cc]
+
+    def carried(q):
+        route = chunks[q][5]
+        if route == "xy":
+            return (k,)
+        return (x, 2 + x) if route == "x" else (2 * y, 2 * y + 1)
+
+    def exchanged(q):
+        if chunks[q][5] == "x":
+            return xs, xr, to_x, (1 - x, 3 - x)
+        return ys, yr, to_y, (2 - 2 * y, 3 - 2 * y)
 
     def remote(src, dst, s, r, target):
         return pltpu.make_async_remote_copy(
@@ -129,111 +143,124 @@
         )
 
     tail = []
-    local = []
     arriving = {i: [] for i in range(n)}
     arriving[None] = []
     finished = [0] * n
-    for i in range(n):
+
+    def begin(g):
+        i, r0, rn, c0 = groups[g][0][:4]
+        prepare(g)
+        rows = pl.ds(r0, rn)
         if shared[i]:
-            for half in range(2):
-                copy = pltpu.make_async_copy(
-                    own[i].at[half], full[i].at[half, z], loc.at[len(local)]
-                )
-                local.append(copy)
-                arriving[i].append(copy.wait)
+            src, dst = own[i].at[:, :, rows], full[i].at[z, :, :, rows]
         else:
-            copy = pltpu.make_async_copy(own[i], full[i].at[z], loc.at[len(local)])
-            local.append(copy)
-            arriving[i].append(copy.wait)
+            cc = pl.ds(c0, sum(chunk[4] for chunk in groups[g]))
+            src, dst = own[i].at[:, :, rows, cc], full[i].at[z, :, :, rows, cc]
+        for q in members[g]:
+            z_first(q)
+        copy = pltpu.make_async_copy(src, dst, loc.at[g])
+        copy.start()
+        arriving[i].append(copy.wait)
 
     def z_first(q):
         i = chunks[q][0]
-        rr, cc = box(q)
-        src = own_half(i).at[k, :, rr, cc]
-        dst = part(full_half(i), q, z, k)
-        for ok, target, slot in ((z + 1 < S, above, F), (z > 0, below, F + 1)):
-
-            def make(target=target, slot=slot):
-                return remote(src, dst, zs.at[q, slot], zr.at[q, z], {"z": target})
+        rr, cc = box(q, c)
+        for m, kk in enumerate(carried(q)):
+            for ok, target, slot in ((z + 1 < S, above, F), (z > 0, below, F + 1)):
+
+                def make(target=target, slot=slot, m=m, kk=kk):
+                    return remote(
+                        own[i].at[kk, :, rr, cc],
+                        part(q, z, kk),
+                        zs.at[q, slot, m],
+                        zr.at[q, z, m],
+                        {"z": target},
+                    )
+
+                @pl.when(ok)
+                def _(make=make):
+                    make().start()
+
+                def finish(ok=ok, make=make):
+                    @pl.when(ok)
+                    def _():
+                        make().wait_send()
+
+                tail.append(finish)
+
+    def send(p, s, r, q, j, slot, target):
+        copy = remote(p, p, s.at[q, j, slot], r.at[q, j, slot], target)
+        copy.start()
+        tail.append(copy.wait_send)
+
+    def z_next(q, j):
+        zz, sign = blocks[j]
+        onward = z - sign
+        ok = (onward >= 0) & (onward < S)
+        target = jnp.clip(onward, 0, S - 1)
+        for m, kk in enumerate(carried(q)):
+            piece = part(q, zz, kk)
+            remote(piece, piece, zs.at[q, j, m], zr.at[q, zz, m], {"z": above}).wait_recv()
+
+            def make(piece=piece, m=m):
+                return remote(piece, piece, zs.at[q, j, m], zr.at[q, zz, m], {"z": target})
 
             @pl.when(ok)
             def _(make=make):
                 make().start()
 
-            def finish(ok=ok, make=make):
+            def finish(make=make):
                 @pl.when(ok)
                 def _():
                     make().wait_send()
 
             tail.append(finish)
-
-    def z_next(q, j):
-        zz, sign = blocks[j]
-        held = full_half(chunks[q][0])
-        piece = part(held, q, zz, k)
-        remote(piece, piece, zs.at[q, j], zr.at[q, zz], {"z": above}).wait_recv()
-        onward = z - sign
-        ok = (onward >= 0) & (onward < S)
-        target = jnp.clip(onward, 0, S - 1)
-
-        def make():
-            return remote(piece, piece, zs.at[q, j], zr.at[q, zz], {"z": target})
-
-        @pl.when(ok)
-        def _():
-            make().start()
-
-        def finish():
-            @pl.when(ok)
-            def _():
-                make().wait_send()
-
-        tail.append(finish)
-        for h, s, r, target in ((0, xs, xr, to_x), (1, ys, yr, to_y)):
-            p = part(held, q, zz, k, h)
-            copy = remote(p, p, s.at[q, j, 0], r.at[q, j, 0], target)
-            copy.start()
-            tail.append(copy.wait_send)
-        for h, s, r, target in ((0, ys, yr, to_y), (1, xs, xr, to_x)):
-            p = part(held, q, zz, k, h)
-            copy = remote(p, p, s.at[q, j, 1], r.at[q, j, 1], target)
-            copy.start()
-            tail.append(copy.wait_send)
+            if chunks[q][5] != "xy":
+                s, r, neighbour, _ = exchanged(q)
+                send(piece, s, r, q, j, m, neighbour)
+        if chunks[q][5] == "xy":
+            send(part(q, zz, k, 0), xs, xr, q, j, 0, to_x)
+            send(part(q, zz, k, 1), ys, yr, q, j, 0, to_y)
+            send(part(q, zz, k, 0), ys, yr, q, j, 1, to_y)
+            send(part(q, zz, k, 1), xs, xr, q, j, 1, to_x)
 
     def xy_next(q, j):
+        if chunks[q][5] != "xy":
+            return
         zz, _ = blocks[j]
-        held = full_half(chunks[q][0])
-        p = part(held, q, zz, kx, 0)
+        p = part(q, zz, kx, 0)
         remote(p, p, xs.at[q, j, 0], xr.at[q, j, 0], to_x).wait_recv()
-        copy = remote(p, p, ys.at[q, j, 2], yr.at[q, j, 2], to_y)
-        copy.start()
-        tail.append(copy.wait_send)
-        p = part(held, q, zz, ky, 1)
+        send(p, ys, yr, q, j, 2, to_y)
+        p = part(q, zz, ky, 1)
         remote(p, p, ys.at[q, j, 0], yr.at[q, j, 0], to_y).wait_recv()
-        copy = remote(p, p, xs.at[q, j, 2], xr.at[q, j, 2], to_x)
-        copy.start()
-        tail.append(copy.wait_send)
+        send(p, xs, xr, q, j, 2, to_x)
 
     def last(q, j):
         i = chunks[q][0]
-        rr, cc = box(q)
         zz, _ = blocks[j]
-        held = full_half(i)
         finished[i] += 1
-        for kk, h, s, r, slot, target in (
-            (kx, 1, xs, xr, 1, to_x),
-            (ky, 0, ys, yr, 1, to_y),
-            (kxy, 1, xs, xr, 2, to_x),
-            (kxy, 0, ys, yr, 2, to_y),
-        ):
-            p = part(held, q, zz, kk, h)
-            remote(p, p, s.at[q, j, slot], r.at[q, j, slot], target).wait_recv()
+        if chunks[q][5] == "xy":
+            for kk, h, s, r, slot, target in (
+                (kx, 1, xs, xr, 1, to_x),
+                (ky, 0, ys, yr, 1, to_y),
+                (kxy, 1, xs, xr, 2, to_x),
+                (kxy, 0, ys, yr, 2, to_y),
+            ):
+                p = part(q, zz, kk, h)
+                remote(p, p, s.at[q, j, slot], r.at[q, j, slot], target).wait_recv()
+        else:
+            s, r, neighbour, theirs = exchanged(q)
+            for m, kk in enumerate(theirs):
+                p = part(q, zz, kk)
+                remote(p, p, s.at[q, j, m], r.at[q, j, m], neighbour).wait_recv()
         if shared[i]:
-            p = held.at[zz, :, :, rr, cc]
+            rr, cc = box(q, c)
+            p = full[i].at[zz, :, :, rr, cc]
             copy = remote(p, p, cs.at[q, j], cr.at[q, j], to_c)
             copy.start()
             tail.append(copy.wait_send)
-            other = full[i].at[1 - c].at[zz, :, :, rr, cc]
+            rr, cc = box(q, 1 - c)
+            other = full[i].at[zz, :, :, rr, cc]
 
             def finish():
                 remote(other, other, cs.at[q, j], cr.at[q, j], to_c).wait_recv()
@@ -246,9 +273,7 @@
         for wait in arriving.pop(i, []):
             wait()
 
-    z_first(0)
-    for copy in local:
-        copy.start()
+    begin(0)
     if small_own is not None:
         place = pltpu.make_async_copy(small_own, small_full.at[z], ss.at[0])
         place.start()
@@ -259,18 +284,14 @@
             tail.append(copy.wait_send)
             came = small_full.at[zz]
             arriving[None].append(remote(came, came, ss.at[e], sr.at[e], {"z": zz}).wait_recv)
-    for t in range(1, nc + F + 3):
-        if t < nc:
-            z_first(t)
-        for j in range(F):
-            if 0 <= t - 1 - j < nc:
-                z_next(t - 1 - j, j)
-        for j in range(F):
-            if 0 <= t - 2 - j < nc:
-                xy_next(t - 2 - j, j)
-        for j in range(F):
-            if 0 <= t - 3 - j < nc:
-                last(t - 3 - j, j)
+    for t in range(1, ng + F + 3):
+        if t < ng:
+            begin(t)
+        for lag, stage in ((1, z_next), (2, xy_next), (3, last)):
+            for j in reversed(range(F)):
+                if 0 <= t - lag - j < ng:
+                    for q in members[t - lag - j]:
+                        stage(q, j)
         work(t, ready)
     for i in list(arriving):
         ready(i)
@@ -278,13 +299,13 @@
         wait()
 
 
-def gather_sems(n, nc, S):
+def gather_sems(ng, nc, S):
     dma = pltpu.SemaphoreType.DMA
     F = S - 1
     return [
-        dma((2 * n,)),
-        dma((nc, F + 2)),
-        dma((nc, S)),
+        dma((ng,)),
+        dma((nc, F + 2, 2)),
+        dma((nc, S, 2)),
         dma((nc, F, 3)),
         dma((nc, F, 3)),
         dma((nc, F, 3)),
@@ -366,20 +387,24 @@
     return copy
 
 
-def forward_kernel(heads, chunks, S, *refs):
-    own = refs[:4]
+def forward_kernel(heads, groups, S, *refs):
+    masters = refs[:4]
     small_own, x_ref, cos_ref, sin_ref, q_ids, k_ids = refs[4:10]
     full = refs[10:14]
     small_full, h1_ref, q_ref, k_out, v_out, o_ref, l_ref, mid_ref, h2_ref, h2_other = refs[14:24]
     h1_t, h1_t_other, o_t, o_t_other = refs[24:28]
     w_in, w_out, gains, mix, kv, bias, vt, lds, hs, hr, h2_sems = refs[28:39]
-    sems = refs[39:]
+    own = refs[39:43]
+    stages = refs[43:47]
+    stage_sems = refs[47]
+    sems = refs[48:]
     z = lax.axis_index("z")
     c = lax.axis_index("c")
     piece = x_ref.shape[0]
     reach = kv.shape[0] // piece - 1
-    half = w_in.shape[-1]
+    half = w_in.shape[-1] // 2
     D = x_ref.shape[1]
+    half_ff = own[3].shape[-1] // 2
     own_rows = pl.ds(reach * piece, piece)
     kv[...] = jnp.zeros_like(kv)
     sent = []
@@ -393,14 +418,49 @@
         started(small_full, gains, lds.at[0]).wait()
         norm_rows(x_ref, gain_row(0), h1_ref)
 
+
+    def of_weight(g):
+        return sum(group[0][0] == groups[g][0][0] for group in groups[:g])
+
+    def stage(g):
+        i, r0, rn, c0 = groups[g][0][:4]
+        slot = of_weight(g) % stages[i].shape[0]
+        cols = pl.ds(0, masters[i].shape[-1])
+        if i == 3:
+            first = c0 // half_ff * 2 * half_ff + c * half_ff
+            cols = pl.ds(pl.multiple_of(first, 128), half_ff)
+        src = masters[i].at[:, :, pl.ds(r0, rn), cols]
+        loads["stage", g] = started(src, stages[i].at[slot], stage_sems.at[g])
+
+    for g in range(len(groups)):
+        if of_weight(g) < stages[groups[g][0][0]].shape[0]:
+            stage(g)
+
+    def prepare(g):
+        i, r0, rn, c0 = groups[g][0][:4]
+        slot = of_weight(g) % stages[i].shape[0]
+        loads.pop(("stage", g)).wait()
+        cols = pl.ds(c0, half_ff) if i == 3 else pl.ds(0, own[i].shape[-1])
+
+        @pl.loop(0, 8)
+        def _(p):
+            kk, h = p // 2, p % 2
+            own[i][kk, h, pl.ds(r0, rn), cols] = stages[i][slot, kk, h].astype(BF)
+
+        later = g + stages[i].shape[0]
+        if later < len(groups) and groups[later][0][0] == i:
+            stage(later)
+
     def start_project(ready):
         ready(0)
         for i in range(2):
-            loads[i] = started(full[0].at[i], w_in.at[i], lds.at[1 + i])
+            at = pl.ds(i * half, half)
+            loads[i] = started(full[0].at[:, :, :, :, at], w_in.at[:, :, :, :, at], lds.at[1 + i])
 
     def project(i):
         loads.pop(i).wait()
-        mix[...] = nn(h1_ref[...], w_in[i].reshape(D, half))
+        weight = w_in[:, :, :, :, i * half : (i + 1) * half].reshape(D, half)
+        mix[...] = nn(h1_ref[...], weight)
         for j in range(half // HEAD):
             h = i * (half // HEAD) + j
             u = mix[:, j * HEAD : (j + 1) * HEAD]
@@ -444,14 +504,16 @@
     def start_output(ready):
         ready(1)
         for i in range(2):
-            loads[i] = started(full[1].at[i], w_out.at[i], lds.at[3 + i])
+            at = pl.ds(i * (D // 2), D // 2)
+            loads[i] = started(full[1].at[:, :, :, :, at], w_out.at[:, :, :, :, at], lds.at[3 + i])
 
     def output():
-        n = w_out.shape[-1]
+        n = D // 2
         for i in range(2):
             loads.pop(i).wait()
             at = slice(i * n, (i + 1) * n)
-            mid_ref[:, at] = x_ref[:, at].astype(F32) + nn(o_ref[...], w_out[i].reshape(D, n))
+            weight = w_out[:, :, :, :, at].reshape(D, n)
+            mid_ref[:, at] = x_ref[:, at].astype(F32) + nn(o_ref[...], weight)
 
     def finish():
         norm_rows(mid_ref, gain_row(1), h2_ref)
@@ -485,31 +547,35 @@
             plan[t](ready)
 
     gather_kernel(
-        [True, True, True, False], chunks, S, own, full, sems, small_own, small_full, work
+        [True, True, True, False], groups, S, own, full, sems, small_own, small_full, prepare, work
     )
     for wait in sent:
         wait()
 
 
-def forward(own, small, x, cos, sin, q_ids, k_ids, heads, S, cid):
+def forward(masters, small, x, cos, sin, q_ids, k_ids, heads, S, cid):
     piece, D = x.shape
     keys = k_ids.shape[0]
-    r, gate_cols = own[3].shape[2:]
-    rf = own[2].shape[3]
-    half_in, half_out = own[0].shape[-1], own[1].shape[-1]
-    chunks = [(0, 0, r, 0, half_in), (1, 0, r, 0, half_out)]
-    chunks += [(2, i, 48, 0, half_out) for i in range(0, rf, 48)]
-    chunks += [
-        (3, i, 16, j, gate_cols // 2) for j in (0, gate_cols // 2) for i in range(0, r, 16)
-    ]
+    r = masters[0].shape[2]
+    rf = masters[2].shape[2]
+    all_in, all_out, all_gate = (masters[i].shape[-1] for i in (0, 1, 3))
+    half_in, half_out, half_ff = all_in // 2, all_out // 2, all_gate // 4
+
+    def routed(i, r0, rn, c0, cn):
+        return [(i, r0, rn, c0, cn, "xy")]
+
+    groups = [routed(0, 0, r, 0, half_in), routed(1, 0, r, 0, half_out)]
+    groups += [routed(2, i, 48, 0, half_out) for i in range(0, rf, 48)]
+    groups += [routed(3, i, 16, j * half_ff, half_ff) for j in range(2) for i in range(0, r, 16)]
 
     def body(*refs):
-        forward_kernel(heads, chunks, S, *refs)
+        forward_kernel(heads, groups, S, *refs)
 
     def shape(*dims, dtype=BF):
         return jax.ShapeDtypeStruct(dims, dtype)
 
-    outs = [shape(2, S, *o.shape[1:]) for o in own[:3]] + [shape(S, *own[3].shape)]
+    own = [(4, 2) + masters[i].shape[2:] for i in range(3)] + [(4, 2, r, 2 * half_ff)]
+    outs = [shape(S, *o) for o in own]
     outs += [
         shape(S, *small.shape),
         shape(piece, D),
@@ -530,11 +596,11 @@
     return pl.pallas_call(
         body,
         out_shape=tuple(outs),
-        in_specs=[VM] * 10,
+        in_specs=[ANY] * 4 + [VM] * 6,
         out_specs=tuple([ANY] * 5 + [VM] * 8 + [ANY] + [VM, ANY] * 2),
         scratch_shapes=[
-            pltpu.VMEM((2, S) + own[0].shape[1:], BF),
-            pltpu.VMEM((2, S) + own[1].shape[1:], BF),
+            pltpu.VMEM((S,) + own[0], BF),
+            pltpu.VMEM((S,) + own[1], BF),
             pltpu.VMEM((S,) + small.shape, BF),
             pltpu.VMEM((piece, half_in), F32),
             pltpu.VMEM((keys, 2 * HEAD), BF),
@@ -545,11 +611,19 @@
             dma((2,)),
             dma((6,)),
         ]
-        + gather_sems(4, len(chunks), S),
+        + [pltpu.VMEM(o, BF) for o in own]
+        + [
+            pltpu.VMEM((1, 4, 2, r, all_in), F32),
+            pltpu.VMEM((1, 4, 2, r, all_out), F32),
+            pltpu.VMEM((2, 4, 2, 48, all_out), F32),
+            pltpu.VMEM((2, 4, 2, 16, half_ff), F32),
+            dma((len(groups),)),
+        ]
+        + gather_sems(len(groups), sum(map(len, groups)), S),
         compiler_params=pltpu.CompilerParams(
             collective_id=cid, has_side_effects=True, vmem_limit_bytes=VMEM_BYTES
         ),
-    )(*own, small, x, cos, sin, q_ids, k_ids)
+    )(*masters, small, x, cos, sin, q_ids, k_ids)
 
 
 def back_step(h, first, rows, refs, bias, kt, finish):
@@ -637,13 +711,9 @@
     two_t, hid_t, grads, out_low, back_low, out, back = results
     step = pl.program_id(0)
     rows, D = two_own.shape
-    half = down_ref.shape[2]
     part = two_t.shape[0]
     core = where[0]
-    places = [
-        pl.ds(pl.multiple_of(core * rows, rows), rows),
-        pl.ds(pl.multiple_of((1 - core) * rows, rows), rows),
-    ]
+    block = 512
 
     @pl.when(step == 0)
     def _():
@@ -653,13 +723,17 @@
     @pl.when(step < D // part)
     def _():
         cols = pl.ds(pl.multiple_of(step * part, part), part)
-        for two_ref, at in zip((two_own, two_other), places):
+        for two_ref, owner in ((two_own, core), (two_other, 1 - core)):
+            at = pl.ds(pl.multiple_of(owner * rows, rows), rows)
             two_t[:, at] = two_ref[:, cols].T
 
-    for two_ref, df_ref, at in zip((two_own, two_other), (df_own, df_other), places):
-        gate = nn(two_ref[...], gate_ref[...])
-        up = nn(two_ref[...], up_ref[...])
-        grad = nt(df_ref[:, :half], down_ref[0]) + nt(df_ref[:, half:], down_ref[1])
+    def tokens(two_ref, df_ref, owner, first):
+        here = pl.ds(first, block)
+        at = pl.ds(pl.multiple_of(owner * rows + first, block), block)
+        two = two_ref[here, :]
+        gate = nn(two, gate_ref[...])
+        up = nn(two, up_ref[...])
+        grad = nt(df_ref[here, :], down_ref[...])
         slope = 0.7978845608028654
         bent = jnp.tanh(slope * (gate + 0.044715 * (gate * gate * gate)))
         upper = 0.5 * (1.0 + bent)
@@ -673,9 +747,12 @@
         hid_t[:, at] = hid.T
         grads[0, at, :] = grad_gate
         grads[1, at, :] = grad_up
-        out[at, :half] += nn(hid, down_ref[0])
-        out[at, half:] += nn(hid, down_ref[1])
+        out[at, :] += nn(hid, down_ref[...])
         back[at, :] += nt(grad_gate, gate_ref[...]) + nt(grad_up, up_ref[...])
+
+    for two_ref, df_ref, owner in ((two_own, df_own, core), (two_other, df_other, 1 - core)):
+        for first in range(0, rows, block):
+            tokens(two_ref, df_ref, owner, first)
 
     @pl.when(step == pl.num_programs(0) - 1)
     def _():
@@ -688,8 +765,8 @@
     half_ff = gate_full.shape[1] // 2
     tile = 256
     tiles = half_ff // tile
-    half = down_full.shape[2]
-    last = D // tile - 1
+    part = max(D // tiles // 128 * 128, 256)
+    last = D // part - 1
 
     def body(*refs):
         mlp_kernel(*refs)
@@ -708,14 +785,14 @@
                 piece,
                 pl.BlockSpec((D, tile), lambda i, w: (0, i)),
                 pl.BlockSpec((D, tile), lambda i, w: (0, tiles + i)),
-                pl.BlockSpec((2, tile, half), lambda i, w: (0, w[0] * tiles + i, 0)),
+                pl.BlockSpec((tile, D), lambda i, w: (w[0] * tiles + i, 0)),
             ],
             out_specs=[
-                pl.BlockSpec((tile, T), lambda i, w: (jnp.minimum(i, last), 0)),
+                pl.BlockSpec((part, T), lambda i, w: (jnp.minimum(i, last), 0)),
                 pl.BlockSpec((tile, T), lambda i, w: (i, 0)),
                 pl.BlockSpec((2, T, tile), lambda i, w: (0, 0, i)),
-                pl.BlockSpec((T, D), lambda i, w: (0, 0)),
-                pl.BlockSpec((T, D), lambda i, w: (0, 0)),
+                pl.BlockSpec((T, D), lambda i, w: (0, 0), pipeline_mode=once),
+                pl.BlockSpec((T, D), lambda i, w: (0, 0), pipeline_mode=once),
             ],
             scratch_shapes=[pltpu.VMEM((T, D), F32), pltpu.VMEM((T, D), F32)],
         ),
@@ -727,7 +804,7 @@
             jax.ShapeDtypeStruct((T, D), BF),
         ],
         compiler_params=pltpu.CompilerParams(
-            dimension_semantics=("arbitrary",), vmem_limit_bytes=VMEM_BYTES
+            dimension_semantics=("arbitrary",), vmem_limit_bytes=BACKWARD_VMEM
         ),
         cost_estimate=pl.CostEstimate(
             flops=12 * T * D * half_ff, bytes_accessed=40 * 2**20, transcendentals=T * half_ff
@@ -744,12 +821,12 @@
 def backward_kernel(heads, sides, parts, S, *refs):
     two, hid, *flats = refs[:6]
     flat_own, flat_other, norm_own, norm_other = flats[2], flats[3], flats[0], flats[1]
-    grads, dy_own, dy_other, back, middle, w_out, gains_ref = refs[6:13]
-    q_ids, k_ids, q_ref, k_ref, v_ref, o_ref, l_ref, cos_ref, sin_ref = refs[13:22]
-    out, hid_land, dx_out, mixed = refs[22:26]
-    left, right, out_right, mix_right, s1, g1, s2, g2, fz, gz, mine, da, do, got, tails, landed_tails, gains = refs[26:43]
-    x1, dk, dv, bias, kt = refs[43:48]
-    lds, rds, fs, cs_in, hs, hr, s1s, s1r, s2s, s2r, zs, zr, ls, xs, xr, ys, yr, cs, cr = refs[48:]
+    grads, dy_own, dy_other, back, middle, w_out, gains_ref, x_ref, w_in = refs[6:15]
+    q_ids, k_ids, q_ref, k_ref, v_ref, o_ref, l_ref, cos_ref, sin_ref = refs[15:24]
+    out, hid_land, x_grad = refs[24:27]
+    left, right, out_right, mix_right, s1, g1, s2, g2, fz, gz, mine, da, do, got = refs[27:41]
+    tails, landed_tails, gains, x1, dk, dv, bias, kt, mixed, w_rows = refs[41:51]
+    lds, rds, fs, cs_in, hs, hr, s1s, s1r, s2s, s2r, zs, zr, ls, xs, xr, ys, yr, cs, cr = refs[51:]
     _, _, _, r, T = left.shape
     n = right.shape[2]
     piece, D = da.shape
@@ -958,11 +1035,10 @@
             x1[at, :] = dx
             da[at, :] = dx.astype(BF)
 
-        fetch("dx", x1, dx_out, fs.at[4])
-        launch("end", remote_copy(give_of(da, n), out_right.at[place], cs_in.at[4], cs_in.at[5], to_c))
+        launch("da", remote_copy(give_of(da, n), out_right.at[place], cs_in.at[4], cs_in.at[5], to_c))
         out_right[place, :] = keep_of(da, n)[...]
         for i in range(2):
-            fetch("w", w_out.at[i, pl.ds(T, piece)], got.at[:, pl.ds(i * n, n)], fs.at[7 + i])
+            fetch("w", w_out.at[pl.ds(T, piece), pl.ds(i * n, n)], got.at[:, pl.ds(i * n, n)], fs.at[7 + i])
 
     def give_of(ref, width):
         return ref.at[:, pl.ds(pl.multiple_of((1 - c) * width, width), width)]
@@ -1036,6 +1112,40 @@
         launch("end", remote_copy(give_of(mixed, mix_half), mix_right.at[place], cs_in.at[6], cs_in.at[7], to_c))
         mix_right[place, :] = keep_of(mixed, mix_half)[...]
 
+    step_rows = w_rows.shape[1]
+
+    def fetch_rows(j):
+        if j * step_rows < D:
+            fetch(("q", j), w_in.at[pl.ds(j * step_rows, step_rows)], w_rows.at[j % 2], fs.at[9 + j % 2])
+
+    def start_input():
+        drain("da")
+        fetch_rows(0)
+        fetch_rows(1)
+        fetch("x0", x_ref, got, fs.at[4])
+
+    def project_back(j):
+        landed(("q", j))
+        da[:, j * step_rows : (j + 1) * step_rows] = nt(mixed[...], w_rows[j % 2]).astype(BF)
+        fetch_rows(j + 2)
+
+    def input_back():
+        landed("x0")
+        gain = jnp.concatenate([gains[zz, 0:1, :] for zz in range(S)], axis=1).astype(F32)
+        step = 64
+
+        @pl.loop(0, piece // step)
+        def _(i):
+            at = pl.ds(pl.multiple_of(i * step, step), step)
+            u = got[at, :].astype(F32)
+            scale = lax.rsqrt(jnp.mean(u * u, axis=1, keepdims=True) + norm_eps)
+            hat = u * scale
+            e = da[at, :].astype(F32) * gain
+            inner = jnp.mean(e * hat, axis=1, keepdims=True)
+            do[at, :] = (x1[at, :] + scale * (e - hat * inner)).astype(BF)
+
+        fetch("x_grad", do, x_grad, fs.at[0])
+
     def came(ref, i):
         ref = ref.at[other_place]
         remote_copy(ref, ref, cs_in.at[i], cs_in.at[i + 1], to_c).wait_recv()
@@ -1047,7 +1157,7 @@
     fetch("dy", dy_own, mixed.at[:, pl.ds(0, D)], fs.at[2])
     fetch("gains", gains_ref, gains, fs.at[3])
     for i in range(2):
-        fetch("w", w_out.at[i, pl.ds(0, T)], right.at[2 + i], fs.at[5 + i])
+        fetch("w", w_out.at[pl.ds(0, T), pl.ds(i * n, n)], right.at[2 + i], fs.at[5 + i])
     each = 5
 
     def work(t):
@@ -1061,6 +1171,11 @@
             send_tails()
         if t == 8:
             mix_back()
+            start_input()
+        if t >= 9 and (t - 9) * step_rows < D:
+            project_back(t - 9)
+        if t == 15:
+            input_back()
 
     for t in range(nc + len(stages) - 1):
         for lag, stage in enumerate(stages):
@@ -1088,11 +1203,13 @@
         landed(key)
 
 
-def backward(two_t, hid_t, transposed, grads, dy, back, middle, w_out, gains, attention, tables, heads, S, cid):
+def backward(
+    two_t, hid_t, transposed, grads, dy, back, middle, w_out, gains, x, w_in, attention, tables, heads, S, cid
+):
     D, T = two_t.shape
     sides, _, half_ff = grads.shape
     piece = middle.shape[0]
-    n = w_out.shape[2]
+    n = D // 2
     r = D // (S * 8)
     parts = half_ff // n
     rows_groups = 2 * half_ff // (S * 8 * r)
@@ -1116,11 +1233,10 @@
         out_shape=(
             jax.ShapeDtypeStruct((nc, 4, 2, 2, r, n), BF),
             jax.ShapeDtypeStruct(hid_shape, BF),
-            jax.ShapeDtypeStruct((piece, D), F32),
-            jax.ShapeDtypeStruct((piece, mixed), BF),
+            jax.ShapeDtypeStruct((piece, D), BF),
         ),
-        in_specs=[ANY] * 13 + [VM] * 9,
-        out_specs=(ANY, ANY, ANY, VM),
+        in_specs=[ANY] * 15 + [VM] * 9,
+        out_specs=(ANY, ANY, ANY),
         scratch_shapes=[
             vmem(3, 8, S, r, T),
             vmem(4, T, n),
@@ -1144,9 +1260,11 @@
             pltpu.VMEM((keys, HEAD), F32),
             pltpu.VMEM((WINDOW + piece // 2, piece // 2), F32),
             pltpu.VMEM((HEAD, keys), BF),
+            vmem(piece, mixed),
+            vmem(2, 256, mixed),
             dma((rows_groups + 3, 8, 2)),
             dma((nc, 2)),
-            dma((9,)),
+            dma((11,)),
             dma((8,)),
             dma((reach,)),
             dma((reach,)),
@@ -1177,10 +1295,12 @@
         middle,
         w_out,
         gains,
+        x,
+        w_in,
         *attention,
         *tables,
     )
-    return results[0], results[2], results[3]
+    return results[0], results[2]
 
 
 def adam_kernel(total, widths, gains, count_ref, rates_ref, g_ref, w_ref, m_ref, g_out, w_out, m_out, *more):
@@ -1304,22 +1424,6 @@
     d_half = D // 2
     r = rows_d // 8
 
-    in_low = input_proj.astype(BF)
-    out_low = output_proj.astype(BF)
-    down_low = down_weight.astype(BF)
-
-    def halves(w):
-        n = w.shape[1] // 2
-        return jnp.stack([w[:, :n], w[:, n:]])
-
-    gate_low = jnp.concatenate(
-        [
-            lax.dynamic_slice_in_dim(gate_up, side * FF + core * half_ff, half_ff, 1)
-            for side in range(2)
-        ],
-        axis=1,
-    ).astype(BF)
-
     gains_low = norm_gains.astype(BF)
     tokens = block_in[0].astype(F32)
     piece_len = tokens.shape[0]
@@ -1358,10 +1462,8 @@
             *transposed,
         ) = forward(
             [
-                halves(in_low).reshape(2, 4, 2, r, in_half),
-                halves(out_low).reshape(2, 4, 2, r, d_half),
-                halves(down_low).reshape(2, 4, 2, rows_f // 8, d_half),
-                gate_low.reshape(4, 2, r, 2 * half_ff),
+                w.reshape(4, 2, w.shape[0] // 8, w.shape[1])
+                for w in (input_proj, output_proj, down_weight, gate_up)
             ],
             jnp.concatenate([gains_low] * 8, axis=0),
             block_in[0],
@@ -1373,22 +1475,29 @@
             S,
             0,
         )
-        in_full = in_full.reshape(2, D, in_half)
-        out_full = out_full.reshape(2, D, d_half)
+        in_full = in_full.reshape(D, 2 * in_half)
+        out_full = out_full.reshape(D, D)
         gains_small = gains_full
         gains_full = gains_full[:, :2].transpose(1, 0, 2).reshape(2, D)
-        down_full = down_full.reshape(2, FF, d_half)
+        down_full = down_full.reshape(FF, D)
         gate_full = gate_full.reshape(D, 2 * half_ff)
         gains_wide = gains_full.astype(F32)
     else:
-        in_full = halves(lax.all_gather(in_low, "z", axis=0, tiled=True))
-        out_full = halves(lax.all_gather(out_low, "z", axis=0, tiled=True))
-        down_full = halves(lax.all_gather(down_low, "z", axis=0, tiled=True))
-        gate_full = lax.all_gather(gate_low, "z", axis=0, tiled=True)
+        gate_low = jnp.concatenate(
+            [
+                lax.dynamic_slice_in_dim(gate_up, side * FF + core * half_ff, half_ff, 1)
+                for side in range(2)
+            ],
+            axis=1,
+        )
+        in_full, out_full, down_full, gate_full = (
+            lax.all_gather(w.astype(BF), "z", axis=0, tiled=True)
+            for w in (input_proj, output_proj, down_weight, gate_low)
+        )
         gains_full = lax.all_gather(gains_low, "z", axis=1, tiled=True)
         gains_wide = gains_full.astype(F32)
         normed = root_norm(tokens, gains_wide[0]).astype(BF)
-        mixed_proj = jnp.concatenate([dot(normed, in_full[0]), dot(normed, in_full[1])], axis=1)
+        mixed_proj = dot(normed, in_full)
         queries = (
             rotate(mixed_proj[:, :width_q].reshape(piece_len, HEADS, HEAD), positions, 1.0)
             .astype(BF)
@@ -1405,9 +1514,7 @@
         flat_heads, log_totals = attend(
             query_row, key_column, queries, key_rows, values, HEADS, piece_len
         )
-        middle = tokens + jnp.concatenate(
-            [dot(flat_heads, out_full[0]), dot(flat_heads, out_full[1])], axis=1
-        )
+        middle = tokens + dot(flat_heads, out_full)
         normed_two = root_norm(middle, gains_wide[1]).astype(BF)
         two_other = swapped(normed_two, "c")
 
@@ -1447,7 +1554,7 @@
     rates = optimizer_rates
 
     if fast:
-        sums, grad_middle, grad_mixed = backward(
+        sums, block_in_grad = backward(
             two_t,
             hid_t,
             transposed,
@@ -1457,6 +1564,8 @@
             middle,
             out_full,
             gains_small,
+            block_in[0],
+            in_full,
             (query_row, key_column, queries, key_rows, values, flat_heads, log_totals),
             (cos_table, sin_table),
             HEADS,
@@ -1469,9 +1578,7 @@
         grad_middle_norm, grad_gain_two = norm_pull_two(grad_normed_two)
         grad_middle = upstream + grad_middle_norm
         grad_branch = grad_middle.astype(BF)
-        grad_flat = dot_t(grad_branch[:, :d_half], out_full[0]) + dot_t(
-            grad_branch[:, d_half:], out_full[1]
-        )
+        grad_flat = dot_t(grad_branch, out_full)
         grad_attended = jnp.where(live_rows[:, None], grad_flat, 0.0).astype(BF)
         grad_query_all, grad_keys, grad_values = attend_back(
             query_row,
@@ -1499,12 +1606,10 @@
         grad_mixed = jnp.concatenate(
             [grad_query_raw, grad_key_raw, own_grad[:, HEAD:]], axis=1
         ).astype(BF)
-    grad_normed = dot_t(grad_mixed[:, :in_half], in_full[0]) + dot_t(
-        grad_mixed[:, in_half:], in_full[1]
-    )
-    _, norm_pull_one = jax.vjp(root_norm, tokens, gains_wide[0])
-    grad_tokens_norm, grad_gain_one = norm_pull_one(grad_normed)
-    block_in_grad = (grad_middle + grad_tokens_norm).astype(BF)[None]
+        grad_normed = dot_t(grad_mixed, in_full)
+        _, norm_pull_one = jax.vjp(root_norm, tokens, gains_wide[0])
+        grad_tokens_norm, grad_gain_one = norm_pull_one(grad_normed)
+        block_in_grad = (grad_middle + grad_tokens_norm).astype(BF)
 
     if fast:
 
@@ -1564,7 +1669,7 @@
     gains_step, gain_moments_new = adamw_step(norm_gains, gain_moments, gain_grad, step_value, rates)
     return (
         block_out,
-        block_in_grad,
+        block_in_grad[None],
         in_grad,
         out_grad,
         gate_grad,

time: 669 us -> 643 us (0.961)
  local copies, waits for them, and re-layouts: 23 us -> 8.92 us
  other arithmetic: 23.5 us -> 11 us
    slice x4 -> x0, local copies, waits for them, and re-layouts: 8.06 us -> none  [the longest x1 5.56 us: on_device(): in_full[0]]
    another operation x3 -> x0, other arithmetic: 6.98 us -> none  [halves(): return jnp.stack([w[:, :n], w[:, n:]])]
  transfers between devices with their start and end apart: 2 -> 2, of which waited for: 0 -> 0; matrix products, arithmetic and copies ran while one was open for 6% -> 2% of each run, Pallas kernels for 83% -> 87%
where the time goes in v5:
time: 643 us; the launch traced here: 634 us
  Pallas kernels  612 us (95%)
  other arithmetic  11 us (2%)
  local copies, waits for them, and re-layouts  8.92 us (1%)
    pallas_call x1, Pallas kernels, backward(): pl.pallas_call(body, out_shape=(jax.ShapeDtypeStruct((nc, 4, 2, 2, r, n),...  284 us
    pallas_call x1, Pallas kernels, forward(): pl.pallas_call(body, out_shape=tuple(outs), in_specs=[ANY] * 4 + [VM] * 6...  192 us
    pallas_call x4, Pallas kernels, adam_call(): pl.pallas_call(body, grid=(4 // chips, 2, sides, tiles), in_specs=[smem,...  77.3 us
    pallas_call x1, Pallas kernels, mlp_call(): pl.pallas_call(body, grid_spec=pltpu.PrefetchScalarGridSpec(num_scalar_pr...  59 us
  transfers between devices with their start and end apart: 2, of which 0 were waited for; matrix products, arithmetic and copies ran while one was open for 2% of the time, Pallas kernels for 87%

profile of v5, /device:TPU:0, one launch (start us, length us, event | category | flops | bytes accessed | tf_op | source)
XLA Modules:
  0.0 634.4 jit_solution(4738151928116346502)
XLA Ops:
  0.7 0.5 collective-permute-start
  1.2 0.7 convert_element_type.31
  1.9 1.2 concatenate.9.refs_4_
  3.1 0.8 pad_dynamic-slice_fusion
  3.9 1.1 broadcast_in_dim.27.refs_9_.refs_16_
  5.0 0.1 compare_select_fusion
  5.1 1.3 constant_dynamic-slice_fusion.1.refs_8_.refs_15_
  6.4 1.8 fusion.1
  8.2 191.9 %shard_map.278 = (bf16[4,4,2,48,1792]{4,3,2,1,0:T(8,128)(2,1)}, bf16[4,4,2,48,1536]{4,3,2,1,0:T(8,128)(2,1)}, bf16[4,4,2,144,1536]{4,3,2,1,0:T(8,128)(2,1)}, bf1...) custom-call(f32[4,2,48,1792]{3,2,1,0:T(8,128)} %bitcast.43, ...), custom_call_target="tpu_custom_call" | custom-call | tf_op jit(solution)/shard_map/pallas_call | solution.py:596
  200.1 0.0 collective-permute-done.refs_4_.refs_8_
  200.1 59.0 %shard_map.279 = (bf16[1536,1024]{1,0:T(8,128)(2,1)}, bf16[2304,1024]{1,0:T(8,128)(2,1)}, bf16[2,1024,2304]{2,1,0:T(8,128)(2,1)}, bf16[1024,1536]{1,0:T(8,128)(2,1)}, bf16[1024,1536]{1,0:T(8,128)(2,1)}) custom-call(s32[1]{0:T(128)} %bitcast.6.refs_0_, bf16[512,1536]{1,0:T(8,128)(2,1)} %get-tuple-element.56.refs_1_, ...), custom_call_target="tpu_custom_call" | custom-call | flops 43486543872 | bytes 41943040 | tf_op jit(solution)/shard_map/pallas_call | solution.py:776
  259.1 0.0 copy-start.3
  259.1 2.7 constant_dynamic-slice_fusion
  261.8 0.0 collective-permute-start.1
  262.5 0.0 copy-done.3
  262.5 0.7 fusion.5
  263.2 283.8 %shard_map.280 = (bf16[12,4,2,2,48,768]{5,4,3,2,1,0:T(8,128)(2,1)}, bf16[2,3,4,2,48,1024]{5,4,3,2,1,0:T(8,128)(2,1)}, bf16[512,1536]{1,0:T(8,128)(2,1)}) custom-call(bf16[4,4,2,48,1024]{4,3,2,1,0:T(8,128)(2,1)} %bitcast.50, bf16[2,3,4,2,48,1024]{5,4,3,2,1,0:T(8,128)(2,1)} %bitcast.49, bf16[4,4,2,48,512]{4,3,2,1,0:T(8,128)(2,1)} %bitcast.55, ...), custom_call_target="tpu_custom_call" | custom-call | tf_op jit(solution)/shard_map/pallas_call | solution.py:1231
  547.0 9.1 %shard_map.281 = (f32[384,1792]{1,0:T(8,128)}, f32[384,1792]{1,0:T(8,128)}, f32[2,384,1792]{2,1,0:T(8,128)}, f32[384,128]{1,0:T(8,128)}) custom-call(s32[1]{0:T(128)S(6)} %copy.35.refs_0_, f32[2]{0:T(128)} %refs_1_.7, bf16[12,4,2,2,48,768]{5,4,3,2,1,0:T(8,128)(2,1)} %get-tuple-element.78.refs_2_, f32[384,1792]{1,0:T(8,128)} %refs_3_.4, f32[2,384,1792]{2,1,0:T(8,128)} %refs_4_.4), custom_call_target="tpu_custom_call" | custom-call | flops 13762560 | bytes 20643840 | tf_op jit(solution)/shard_map/pallas_call | solution.py:1367
  556.1 1.1 reduce_sum.18
  557.2 41.3 %shard_map.283 = (f32[384,9216]{1,0:T(8,128)}, f32[384,9216]{1,0:T(8,128)}, f32[2,384,9216]{2,1,0:T(8,128)}, f32[384,128]{1,0:T(8,128)}) custom-call(s32[1]{0:T(128)S(6)} %copy.35.refs_0_, f32[2]{0:T(128)} %refs_1_.7, bf16[12,4,2,2,48,768]{5,4,3,2,1,0:T(8,128)(2,1)} %get-tuple-element.78.refs_2_, f32[384,9216]{1,0:T(8,128)} %refs_3_.6, f32[2,384,9216]{2,1,0:T(8,128)} %refs_4_.6), custom_call_target="tpu_custom_call" | custom-call | flops 70778880 | bytes 106168320 | tf_op jit(solution)/shard_map/pallas_call | solution.py:1367
  598.4 1.1 reduce_sum.19
  599.5 7.1 %shard_map.282 = (f32[384,1536]{1,0:T(8,128)}, f32[384,1536]{1,0:T(8,128)}, f32[2,384,1536]{2,1,0:T(8,128)}) custom-call(s32[1]{0:T(128)S(6)} %copy.35.refs_0_, f32[2]{0:T(128)} %refs_1_.7, bf16[12,4,2,2,48,768]{5,4,3,2,1,0:T(8,128)(2,1)} %get-tuple-element.78.refs_2_, f32[384,1536]{1,0:T(8,128)} %refs_3_.5, f32[2,384,1536]{2,1,0:T(8,128)} %refs_4_.5), custom_call_target="tpu_custom_call" | custom-call | flops 11796480 | bytes 17694720 | tf_op jit(solution)/shard_map/pallas_call | solution.py:1367
  606.6 0.0 copy-start.2
  606.6 0.0 copy-start.4
  606.6 0.0 copy-start
  606.7 19.9 %shard_map.284 = (f32[1152,1536]{1,0:T(8,128)}, f32[1152,1536]{1,0:T(8,128)}, f32[2,1152,1536]{2,1,0:T(8,128)}) custom-call(s32[1]{0:T(128)S(6)} %copy.35.refs_0_, f32[2]{0:T(128)} %refs_1_.7, bf16[12,4,2,2,48,768]{5,4,3,2,1,0:T(8,128)(2,1)} %get-tuple-element.78.refs_2_, f32[1152,1536]{1,0:T(8,128)} %refs_3_.7, f32[2,1152,1536]{2,1,0:T(8,128)} %refs_4_.7), custom_call_target="tpu_custom_call" | custom-call | flops 35389440 | bytes 53084160 | tf_op jit(solution)/shard_map/pallas_call | solution.py:1367
  626.5 0.0 copy-done.2
  626.5 0.0 copy-done.4
  626.5 0.0 copy-start.5
  626.5 1.9 fusion.4
  628.5 0.6 pad_maximum_fusion
  629.1 0.0 copy-start.1
  629.1 0.0 collective-permute-done.1
  629.1 0.0 copy-done
  629.1 3.8 fusion
  632.9 0.0 copy-done.5
  632.9 0.0 copy-done.1
  632.9 1.1 copy.36
  (5 shorter events, 0.0 us)
Async XLA Ops:
  0.7 199.4 %collective-permute-start = (bf16[512,1536]{1,0:T(8,128)(2,1)}, bf16[512,1536]{1,0:T(8,128)(2,1)}, u32[]{:S(2)}, u32[]{:S(2)}) collective-permute-start(bf16[512,1536]{1,0:T(8,128)(2,1)} %bitcast.52), channel_id=1, source_target_pairs={{0,4},{4,0},{1,5},{5,1},{2,6},{6,2},{3,7},{7,3},{8,12},{12,8},{9,1... | collective-permute-start | bytes 4718600 | tf_op jit(solution)/shard_map/ppermute | solution.py:36
  259.1 3.4 copy-start.3
  261.8 367.3 %collective-permute-start.1 = (bf16[512,1536]{1,0:T(8,128)(2,1)}, bf16[512,1536]{1,0:T(8,128)(2,1)}, u32[]{:S(2)}, u32[]{:S(2)}) collective-permute-start(bf16[512,1536]{1,0:T(8,128)(2,1)} %constant_dynamic-slice_fusion), channel_id=1, source_target_pairs={{0,4},{4,0},{1,5},{5,1},{2,6},{6,2},{3,7},{7,3},{8,12},{12,8},{9,1... | collective-permute-start | bytes 4718600 | tf_op jit(solution)/shard_map/ppermute | solution.py:36
  606.6 19.9 %copy-start.2 = (f32[2,384]{1,0:T(2,128)S(1)}, f32[2,384]{1,0:T(2,128)}, u32[]{:S(2)}) copy-start(f32[2,384]{1,0:T(2,128)} %param.22) | copy-start | bytes 9220
  606.6 19.9 %copy-start.4 = (f32[2,2,384]{2,1,0:T(2,128)S(1)}, f32[2,2,384]{2,1,0:T(2,128)}, u32[]{:S(2)}) copy-start(f32[2,2,384]{2,1,0:T(2,128)} %param.27) | copy-start | bytes 18436
  606.6 22.4 %copy-start = (f32[512,1536]{1,0:T(8,128)S(1)}, f32[512,1536]{1,0:T(8,128)}, u32[]{:S(2)}) copy-start(f32[512,1536]{1,0:T(8,128)} %get-tuple-element.55.refs_10_) | copy-start | bytes 9437188
  626.5 6.3 copy-start.5
  629.1 3.8 copy-start.1

commit v6 on v5

--- a/solution.py
+++ b/solution.py
@@ -708,7 +708,7 @@
 def mlp_kernel(
     where, two_own, two_other, df_own, df_other, gate_ref, up_ref, down_ref, *results
 ):
-    two_t, hid_t, grads, out_low, back_low, out, back = results
+    two_t, hid_t, grads, back_low, back = results
     step = pl.program_id(0)
     rows, D = two_own.shape
     part = two_t.shape[0]
@@ -717,7 +717,6 @@
 
     @pl.when(step == 0)
     def _():
-        out[...] = jnp.zeros_like(out)
         back[...] = jnp.zeros_like(back)
 
     @pl.when(step < D // part)
@@ -747,7 +746,6 @@
         hid_t[:, at] = hid.T
         grads[0, at, :] = grad_gate
         grads[1, at, :] = grad_up
-        out[at, :] += nn(hid, down_ref[...])
         back[at, :] += nt(grad_gate, gate_ref[...]) + nt(grad_up, up_ref[...])
 
     for two_ref, df_ref, owner in ((two_own, df_own, core), (two_other, df_other, 1 - core)):
@@ -756,7 +754,6 @@
 
     @pl.when(step == pl.num_programs(0) - 1)
     def _():
-        out_low[...] = out[...].astype(BF)
         back_low[...] = back[...].astype(BF)
 
 
@@ -792,22 +789,20 @@
                 pl.BlockSpec((tile, T), lambda i, w: (i, 0)),
                 pl.BlockSpec((2, T, tile), lambda i, w: (0, 0, i)),
                 pl.BlockSpec((T, D), lambda i, w: (0, 0), pipeline_mode=once),
-                pl.BlockSpec((T, D), lambda i, w: (0, 0), pipeline_mode=once),
             ],
-            scratch_shapes=[pltpu.VMEM((T, D), F32), pltpu.VMEM((T, D), F32)],
+            scratch_shapes=[pltpu.VMEM((T, D), F32)],
         ),
         out_shape=[
             jax.ShapeDtypeStruct((D, T), BF),
             jax.ShapeDtypeStruct((half_ff, T), BF),
             jax.ShapeDtypeStruct((2, T, half_ff), BF),
             jax.ShapeDtypeStruct((T, D), BF),
-            jax.ShapeDtypeStruct((T, D), BF),
         ],
         compiler_params=pltpu.CompilerParams(
             dimension_semantics=("arbitrary",), vmem_limit_bytes=BACKWARD_VMEM
         ),
         cost_estimate=pl.CostEstimate(
-            flops=12 * T * D * half_ff, bytes_accessed=40 * 2**20, transcendentals=T * half_ff
+            flops=10 * T * D * half_ff, bytes_accessed=40 * 2**20, transcendentals=T * half_ff
         ),
     )(core, *two, *df, gate_full, gate_full, down_full)
 
@@ -821,12 +816,12 @@
 def backward_kernel(heads, sides, parts, S, *refs):
     two, hid, *flats = refs[:6]
     flat_own, flat_other, norm_own, norm_other = flats[2], flats[3], flats[0], flats[1]
-    grads, dy_own, dy_other, back, middle, w_out, gains_ref, x_ref, w_in = refs[6:15]
-    q_ids, k_ids, q_ref, k_ref, v_ref, o_ref, l_ref, cos_ref, sin_ref = refs[15:24]
-    out, hid_land, x_grad = refs[24:27]
-    left, right, out_right, mix_right, s1, g1, s2, g2, fz, gz, mine, da, do, got = refs[27:41]
-    tails, landed_tails, gains, x1, dk, dv, bias, kt, mixed, w_rows = refs[41:51]
-    lds, rds, fs, cs_in, hs, hr, s1s, s1r, s2s, s2r, zs, zr, ls, xs, xr, ys, yr, cs, cr = refs[51:]
+    grads, dy_own, dy_other, back, middle, w_out, gains_ref, x_ref, w_in, w_down = refs[6:16]
+    q_ids, k_ids, q_ref, k_ref, v_ref, o_ref, l_ref, cos_ref, sin_ref = refs[16:25]
+    out, hid_land, x_grad, y_out, dx_land = refs[25:30]
+    left, right, out_right, mix_right, s1, g1, s2, g2, fz, gz, mine, da, do, got = refs[30:44]
+    tails, landed_tails, gains, x1, dk, dv, bias, kt, mixed, w_rows, w_tiles = refs[44:55]
+    lds, rds, fs, cs_in, hs, hr, s1s, s1r, s2s, s2r, zs, zr, ls, xs, xr, ys, yr, cs, cr = refs[55:]
     _, _, _, r, T = left.shape
     n = right.shape[2]
     piece, D = da.shape
@@ -1035,6 +1030,7 @@
             x1[at, :] = dx
             da[at, :] = dx.astype(BF)
 
+        fetch("dx", x1, dx_land, fs.at[11])
         launch("da", remote_copy(give_of(da, n), out_right.at[place], cs_in.at[4], cs_in.at[5], to_c))
         out_right[place, :] = keep_of(da, n)[...]
         for i in range(2):
@@ -1131,6 +1127,7 @@
 
     def input_back():
         landed("x0")
+        landed("dx")
         gain = jnp.concatenate([gains[zz, 0:1, :] for zz in range(S)], axis=1).astype(F32)
         step = 64
 
@@ -1145,6 +1142,46 @@
             do[at, :] = (x1[at, :] + scale * (e - hat * inner)).astype(BF)
 
         fetch("x_grad", do, x_grad, fs.at[0])
+
+    spread = {6: ((1, 0, 3),), 7: ((1, 3, 6), (2, 0, 3)), 8: ((1, 6, 8), (2, 3, 6), (3, 0, 3))}
+    spread.update({9: ((2, 6, 8), (3, 3, 6)), 10: ((3, 6, 8),)})
+    out_steps = [(g, p) for t in sorted(spread) for g, a, b in spread[t] for p in range(a, b)]
+    out_count = {t: sum(b - a for _, a, b in spread[t]) for t in spread}
+    assert rows_groups == 3 and wide == 6
+
+    def fetch_tile(i):
+        if i < len(out_steps):
+            g, p = out_steps[i]
+            fetch(("d", i), w_down.at[:, g - 1, p % 4, p // 4], w_tiles.at[i % 2], fs.at[12 + i % 2])
+
+    def output_step(i):
+        g, p = out_steps[i]
+        landed(("d", i))
+        fetch_tile(i + 1)
+        lhs = left[g % left_slots, p, :, :, place].reshape(S * r, piece)
+        for j in range(0, D, piece):
+            rhs = w_tiles[i % 2, :, :, j : j + piece].reshape(S * r, piece)
+            x1[:, j : j + piece] += lax.dot_general(
+                lhs, rhs, (((0,), (0,)), ((), ())), preferred_element_type=F32
+            )
+
+    def output_work(t):
+        if t == 2:
+            landed("dx")
+            fetch("x1", middle, x1, fs.at[1])
+        if t == 5:
+            landed("x1")
+            fetch_tile(0)
+        if t in out_count:
+            done = sum(out_count[u] for u in out_count if u < t)
+            for i in range(done, done + out_count[t]):
+                output_step(i)
+        if t == 11:
+            do[...] = x1[...].astype(BF)
+            fetch("y", do, y_out, fs.at[2])
+        if t == 13:
+            landed("y")
+            fetch("dx", dx_land, x1, fs.at[11])
 
     def came(ref, i):
         ref = ref.at[other_place]
@@ -1174,6 +1211,7 @@
             start_input()
         if t >= 9 and (t - 9) * step_rows < D:
             project_back(t - 9)
+        output_work(t)
         if t == 15:
             input_back()
 
@@ -1204,7 +1242,7 @@
 
 
 def backward(
-    two_t, hid_t, transposed, grads, dy, back, middle, w_out, gains, x, w_in, attention, tables, heads, S, cid
+    two_t, hid_t, transposed, grads, dy, back, middle, w_out, gains, x, w_in, w_down, attention, tables, heads, S, cid
 ):
     D, T = two_t.shape
     sides, _, half_ff = grads.shape
@@ -1234,9 +1272,11 @@
             jax.ShapeDtypeStruct((nc, 4, 2, 2, r, n), BF),
             jax.ShapeDtypeStruct(hid_shape, BF),
             jax.ShapeDtypeStruct((piece, D), BF),
+            jax.ShapeDtypeStruct((piece, D), BF),
+            jax.ShapeDtypeStruct((piece, D), F32),
         ),
-        in_specs=[ANY] * 15 + [VM] * 9,
-        out_specs=(ANY, ANY, ANY),
+        in_specs=[ANY] * 16 + [VM] * 9,
+        out_specs=(ANY,) * 5,
         scratch_shapes=[
             vmem(3, 8, S, r, T),
             vmem(4, T, n),
@@ -1262,9 +1302,10 @@
             pltpu.VMEM((HEAD, keys), BF),
             vmem(piece, mixed),
             vmem(2, 256, mixed),
+            vmem(2, S, r, D),
             dma((rows_groups + 3, 8, 2)),
             dma((nc, 2)),
-            dma((11,)),
+            dma((14,)),
             dma((8,)),
             dma((reach,)),
             dma((reach,)),
@@ -1297,10 +1338,11 @@
         gains,
         x,
         w_in,
+        w_down.reshape(S, rows_groups, 4, 2, r, D),
         *attention,
         *tables,
     )
-    return results[0], results[2]
+    return results[0], results[2], results[3]
 
 
 def adam_kernel(total, widths, gains, count_ref, rates_ref, g_ref, w_ref, m_ref, g_out, w_out, m_out, *more):
@@ -1540,21 +1582,19 @@
         return keep.astype(F32) + swapped(give, "c").astype(F32)
 
     df_other = swapped(cotangent[0], "c")
-    two_t, hid_t, grad_gated, out_sum, two_sum = mlp_call(
+    two_t, hid_t, grad_gated, two_sum = mlp_call(
         core.reshape(1).astype(jnp.int32),
         (normed_two, two_other),
         (cotangent[0], df_other),
         gate_full,
         down_full,
     )
-    output = middle + core_sum(out_sum)
-    block_out = output.astype(BF)[None]
     token_total = piece_len * S * Y * 4 * block_in.shape[0]
     step_value = update_count[0].astype(F32)
     rates = optimizer_rates
 
     if fast:
-        sums, block_in_grad = backward(
+        sums, block_in_grad, block_out = backward(
             two_t,
             hid_t,
             transposed,
@@ -1566,6 +1606,7 @@
             gains_small,
             block_in[0],
             in_full,
+            down_full,
             (query_row, key_column, queries, key_rows, values, flat_heads, log_totals),
             (cos_table, sin_table),
             HEADS,
@@ -1573,6 +1614,8 @@
             2,
         )
     else:
+        down_mine = lax.dynamic_slice_in_dim(down_full, core * half_ff, half_ff, 0)
+        block_out = (middle + core_sum(dot(hid_t.T, down_mine).astype(BF))).astype(BF)
         grad_normed_two = core_sum(two_sum)
         _, norm_pull_two = jax.vjp(root_norm, middle, gains_wide[1])
         grad_middle_norm, grad_gain_two = norm_pull_two(grad_normed_two)
@@ -1668,7 +1711,7 @@
         gain_grad = lax.dynamic_slice_in_dim(gains_sum, seq_place * rows_d, rows_d, 1) / token_total
     gains_step, gain_moments_new = adamw_step(norm_gains, gain_moments, gain_grad, step_value, rates)
     return (
-        block_out,
+        block_out[None],
         block_in_grad[None],
         in_grad,
         out_grad,

time: 643 us -> 633 us (0.984)
  transfers between devices with their start and end apart: 2 -> 1, of which waited for: 0 -> 0; matrix products, arithmetic and copies ran while one was open for 2% -> 1% of each run, Pallas kernels for 87% -> 31%
where the time goes in v6:
time: 633 us; the launch traced here: 624 us
  Pallas kernels  607 us (96%)
  local copies, waits for them, and re-layouts  7.35 us (1%)
  other arithmetic  7.29 us (1%)
    pallas_call x1, Pallas kernels, backward(): pl.pallas_call(body, out_shape=(jax.ShapeDtypeStruct((nc, 4, 2, 2, r, n),...  282 us
    pallas_call x1, Pallas kernels, forward(): pl.pallas_call(body, out_shape=tuple(outs), in_specs=[ANY] * 4 + [VM] * 6...  192 us
    pallas_call x4, Pallas kernels, adam_call(): pl.pallas_call(body, grid=(4 // chips, 2, sides, tiles), in_specs=[smem,...  77.5 us
    pallas_call x1, Pallas kernels, mlp_call(): pl.pallas_call(body, grid_spec=pltpu.PrefetchScalarGridSpec(num_scalar_pr...  56 us
  transfers between devices with their start and end apart: 1, of which 0 were waited for; matrix products, arithmetic and copies ran while one was open for 1% of the time, Pallas kernels for 31%

profile of v6, /device:TPU:0, one launch (start us, length us, event | category | flops | bytes accessed | tf_op | source)
XLA Modules:
  0.0 624.0 jit_solution(16601142656074752211)
XLA Ops:
  0.7 0.5 collective-permute-start
  1.2 0.8 pad_dynamic-slice_fusion
  1.9 1.1 broadcast_in_dim.27.refs_9_.refs_17_
  3.1 0.7 convert_element_type.22
  3.8 1.2 concatenate.9.refs_4_
  5.8 0.1 compare_select_fusion
  5.8 1.3 constant_dynamic-slice_fusion.refs_8_.refs_16_
  7.1 1.8 fusion
  8.9 0.0 copy-start.3
  8.9 191.9 %shard_map.278 = (bf16[4,4,2,48,1792]{4,3,2,1,0:T(8,128)(2,1)}, bf16[4,4,2,48,1536]{4,3,2,1,0:T(8,128)(2,1)}, bf16[4,4,2,144,1536]{4,3,2,1,0:T(8,128)(2,1)}, bf1...) custom-call(f32[4,2,48,1792]{3,2,1,0:T(8,128)} %bitcast.45, ...), custom_call_target="tpu_custom_call" | custom-call | tf_op jit(solution)/shard_map/pallas_call | solution.py:596
  200.9 0.0 copy-done.3
  200.9 0.6 fusion.4
  201.5 0.0 collective-permute-done.refs_4_.refs_8_
  201.5 56.0 %shard_map.279 = (bf16[1536,1024]{1,0:T(8,128)(2,1)}, bf16[2304,1024]{1,0:T(8,128)(2,1)}, bf16[2,1024,2304]{2,1,0:T(8,128)(2,1)}, bf16[1024,1536]{1,0:T(8,128)(2,1)}) custom-call(s32[1]{0:T(128)} %bitcast.refs_0_, bf16[512,1536]{1,0:T(8,128)(2,1)} %get-tuple-element.55.refs_1_, bf16[512,1536]{1,0:T(8,128)(2,1)} %get-tuple-element.56.refs_2_, ...), custom_call_target="tpu_custom_call" | custom-call | flops 36238786560 | bytes 41943040 | tf_op jit(solution)/shard_map/pallas_call | solution.py:773
  257.4 281.8 %shard_map.280 = (bf16[12,4,2,2,48,768]{5,4,3,2,1,0:T(8,128)(2,1)}, bf16[2,3,4,2,48,1024]{5,4,3,2,1,0:T(8,128)(2,1)}, bf16[512,1536]{1,0:T(8,128)(2,1)}, bf16[512,1536]{1,0:T(8,128)(2,1)}, f32[512,1536]{1,0:T(8,128)}) custom-call(bf16[4,4,2,48,1024]{4,3,2,1,0:T(8,128)(2,1)} %bitcast.52, bf16[2,3,4,2,48,1024]{5,4,3,2,1,0:T(8,128)(2,1)} %bitcast.51, ...), custom_call_target="tpu_custom_call" | custom-call | tf_op jit(solution)/shard_map/pallas_call | solution.py:1269
  539.2 41.4 %shard_map.283 = (f32[384,9216]{1,0:T(8,128)}, f32[384,9216]{1,0:T(8,128)}, f32[2,384,9216]{2,1,0:T(8,128)}, f32[384,128]{1,0:T(8,128)}) custom-call(s32[1]{0:T(128)S(6)} %copy.36.refs_0_, f32[2]{0:T(128)} %refs_1_.7, bf16[12,4,2,2,48,768]{5,4,3,2,1,0:T(8,128)(2,1)} %get-tuple-element.78.refs_2_, f32[384,9216]{1,0:T(8,128)} %refs_3_.6, f32[2,384,9216]{2,1,0:T(8,128)} %refs_4_.6), custom_call_target="tpu_custom_call" | custom-call | flops 70778880 | bytes 106168320 | tf_op jit(solution)/shard_map/pallas_call | solution.py:1409
  580.7 1.1 reduce_sum.19
  581.7 9.1 %shard_map.281 = (f32[384,1792]{1,0:T(8,128)}, f32[384,1792]{1,0:T(8,128)}, f32[2,384,1792]{2,1,0:T(8,128)}, f32[384,128]{1,0:T(8,128)}) custom-call(s32[1]{0:T(128)S(6)} %copy.36.refs_0_, f32[2]{0:T(128)} %refs_1_.7, bf16[12,4,2,2,48,768]{5,4,3,2,1,0:T(8,128)(2,1)} %get-tuple-element.78.refs_2_, f32[384,1792]{1,0:T(8,128)} %refs_3_.4, f32[2,384,1792]{2,1,0:T(8,128)} %refs_4_.4), custom_call_target="tpu_custom_call" | custom-call | flops 13762560 | bytes 20643840 | tf_op jit(solution)/shard_map/pallas_call | solution.py:1409
  590.9 1.1 reduce_sum.18
  591.9 19.7 %shard_map.284 = (f32[1152,1536]{1,0:T(8,128)}, f32[1152,1536]{1,0:T(8,128)}, f32[2,1152,1536]{2,1,0:T(8,128)}) custom-call(s32[1]{0:T(128)S(6)} %copy.36.refs_0_, f32[2]{0:T(128)} %refs_1_.7, bf16[12,4,2,2,48,768]{5,4,3,2,1,0:T(8,128)(2,1)} %get-tuple-element.78.refs_2_, f32[1152,1536]{1,0:T(8,128)} %refs_3_.7, f32[2,1152,1536]{2,1,0:T(8,128)} %refs_4_.7), custom_call_target="tpu_custom_call" | custom-call | flops 35389440 | bytes 53084160 | tf_op jit(solution)/shard_map/pallas_call | solution.py:1409
  611.7 0.0 copy-start.2
  611.7 0.0 copy-start.4
  611.7 0.0 copy-start.1
  611.7 7.2 %shard_map.282 = (f32[384,1536]{1,0:T(8,128)}, f32[384,1536]{1,0:T(8,128)}, f32[2,384,1536]{2,1,0:T(8,128)}) custom-call(s32[1]{0:T(128)S(6)} %copy.36.refs_0_, f32[2]{0:T(128)} %refs_1_.7, bf16[12,4,2,2,48,768]{5,4,3,2,1,0:T(8,128)(2,1)} %get-tuple-element.78.refs_2_, f32[384,1536]{1,0:T(8,128)} %refs_3_.5, f32[2,384,1536]{2,1,0:T(8,128)} %refs_4_.5), custom_call_target="tpu_custom_call" | custom-call | flops 11796480 | bytes 17694720 | tf_op jit(solution)/shard_map/pallas_call | solution.py:1409
  618.9 0.0 copy-start
  618.9 0.0 copy-done.2
  618.9 0.0 copy-done.4
  618.9 0.0 copy-start.5
  619.0 2.0 fusion.3
  620.9 0.6 pad_maximum_fusion
  621.5 0.0 copy-done.1
  621.5 1.1 copy.37
  622.7 0.0 copy-done
  622.7 1.1 copy.38
  623.8 0.0 copy-done.5
  (5 shorter events, 0.0 us)
Async XLA Ops:
  0.7 200.8 %collective-permute-start = (bf16[512,1536]{1,0:T(8,128)(2,1)}, bf16[512,1536]{1,0:T(8,128)(2,1)}, u32[]{:S(2)}, u32[]{:S(2)}) collective-permute-start(bf16[512,1536]{1,0:T(8,128)(2,1)} %bitcast.55), channel_id=1, source_target_pairs={{0,4},{4,0},{1,5},{5,1},{2,6},{6,2},{3,7},{7,3},{8,12},{12,8},{9,1... | collective-permute-start | bytes 4718600 | tf_op jit(solution)/shard_map/ppermute | solution.py:36
  8.9 192.0 %copy-start.3 = (f32[2]{0:T(128)S(1)}, f32[2]{0:T(128)}, u32[]{:S(2)}) copy-start(f32[2]{0:T(128)} %refs_1_.7) | copy-start | bytes 28
  611.7 7.2 %copy-start.2 = (f32[2,384]{1,0:T(2,128)S(1)}, f32[2,384]{1,0:T(2,128)}, u32[]{:S(2)}) copy-start(f32[2,384]{1,0:T(2,128)} %param.22) | copy-start | bytes 9220
  611.7 7.2 %copy-start.4 = (f32[2,2,384]{2,1,0:T(2,128)S(1)}, f32[2,2,384]{2,1,0:T(2,128)}, u32[]{:S(2)}) copy-start(f32[2,2,384]{2,1,0:T(2,128)} %param.27) | copy-start | bytes 18436
  611.7 9.9 %copy-start.1 = (bf16[512,1536]{1,0:T(8,128)(2,1)S(1)}, bf16[512,1536]{1,0:T(8,128)(2,1)}, u32[]{:S(2)}) copy-start(bf16[512,1536]{1,0:T(8,128)(2,1)} %get-tuple-element.76) | copy-start | bytes 4718596
  618.9 3.8 copy-start
  618.9 4.9 copy-start.5

commit v7 on v6

--- a/solution.py
+++ b/solution.py
@@ -713,7 +713,7 @@
     rows, D = two_own.shape
     part = two_t.shape[0]
     core = where[0]
-    block = 512
+    block = 256
 
     @pl.when(step == 0)
     def _():
@@ -734,12 +734,11 @@
         up = nn(two, up_ref[...])
         grad = nt(df_ref[here, :], down_ref[...])
         slope = 0.7978845608028654
-        bent = jnp.tanh(slope * (gate + 0.044715 * (gate * gate * gate)))
-        upper = 0.5 * (1.0 + bent)
+        cube = slope * 0.044715
+        square = gate * gate
+        upper = 0.5 + 0.5 * jnp.tanh(gate * (slope + cube * square))
         act = gate * upper
-        act_slope = upper + 0.5 * gate * (1.0 - bent * bent) * (
-            slope * (1.0 + 3 * 0.044715 * (gate * gate))
-        )
+        act_slope = upper + act * (1.0 - upper) * (2.0 * slope + 6.0 * cube * square)
         hid = (act * up).astype(BF)
         grad_gate = (grad * up * act_slope).astype(BF)
         grad_up = (grad * act).astype(BF)
@@ -760,7 +759,7 @@
 def mlp_call(core, two, df, gate_full, down_full):
     T, D = 2 * two[0].shape[0], two[0].shape[1]
     half_ff = gate_full.shape[1] // 2
-    tile = 256
+    tile = 768
     tiles = half_ff // tile
     part = max(D // tiles // 128 * 128, 256)
     last = D // part - 1

time: 633 us -> 637 us (level)
  no operation moved by 1% of the time
where the time goes in v7:
time: 637 us; the launch traced here: 628 us
  Pallas kernels  611 us (96%)
  local copies, waits for them, and re-layouts  7.35 us (1%)
  other arithmetic  7.29 us (1%)
    pallas_call x1, Pallas kernels, backward(): pl.pallas_call(body, out_shape=(jax.ShapeDtypeStruct((nc, 4, 2, 2, r, n),...  282 us
    pallas_call x1, Pallas kernels, forward(): pl.pallas_call(body, out_shape=tuple(outs), in_specs=[ANY] * 4 + [VM] * 6...  192 us
    pallas_call x4, Pallas kernels, adam_call(): pl.pallas_call(body, grid=(4 // chips, 2, sides, tiles), in_specs=[smem,...  77.6 us
    pallas_call x1, Pallas kernels, mlp_call(): pl.pallas_call(body, grid_spec=pltpu.PrefetchScalarGridSpec(num_scalar_pr...  59.8 us
  transfers between devices with their start and end apart: 1, of which 0 were waited for; matrix products, arithmetic and copies ran while one was open for 1% of the time, Pallas kernels for 31%

profile of v7, /device:TPU:0, one launch (start us, length us, event | category | flops | bytes accessed | tf_op | source)
XLA Modules:
  0.0 628.2 jit_solution(11975125123736045643)
XLA Ops:
  0.7 0.5 collective-permute-start
  1.2 0.8 pad_dynamic-slice_fusion
  1.9 1.1 broadcast_in_dim.27.refs_9_.refs_17_
  3.1 0.7 convert_element_type.22
  3.8 1.2 concatenate.9.refs_4_
  5.8 0.1 compare_select_fusion
  5.8 1.3 constant_dynamic-slice_fusion.refs_8_.refs_16_
  7.1 1.8 fusion
  8.9 0.0 copy-start.3
  8.9 192.0 %shard_map.278 = (bf16[4,4,2,48,1792]{4,3,2,1,0:T(8,128)(2,1)}, bf16[4,4,2,48,1536]{4,3,2,1,0:T(8,128)(2,1)}, bf16[4,4,2,144,1536]{4,3,2,1,0:T(8,128)(2,1)}, bf1...) custom-call(f32[4,2,48,1792]{3,2,1,0:T(8,128)} %bitcast.45, ...), custom_call_target="tpu_custom_call" | custom-call | tf_op jit(solution)/shard_map/pallas_call | solution.py:596
  200.9 0.0 copy-done.3
  201.0 0.6 fusion.4
  201.6 0.0 collective-permute-done.refs_4_.refs_8_
  201.6 59.8 %shard_map.279 = (bf16[1536,1024]{1,0:T(8,128)(2,1)}, bf16[2304,1024]{1,0:T(8,128)(2,1)}, bf16[2,1024,2304]{2,1,0:T(8,128)(2,1)}, bf16[1024,1536]{1,0:T(8,128)(2,1)}) custom-call(s32[1]{0:T(128)} %bitcast.refs_0_, bf16[512,1536]{1,0:T(8,128)(2,1)} %get-tuple-element.55.refs_1_, bf16[512,1536]{1,0:T(8,128)(2,1)} %get-tuple-element.56.refs_2_, ...), custom_call_target="tpu_custom_call" | custom-call | flops 36238786560 | bytes 41943040 | tf_op jit(solution)/shard_map/pallas_call | solution.py:772
  261.4 281.7 %shard_map.280 = (bf16[12,4,2,2,48,768]{5,4,3,2,1,0:T(8,128)(2,1)}, bf16[2,3,4,2,48,1024]{5,4,3,2,1,0:T(8,128)(2,1)}, bf16[512,1536]{1,0:T(8,128)(2,1)}, bf16[512,1536]{1,0:T(8,128)(2,1)}, f32[512,1536]{1,0:T(8,128)}) custom-call(bf16[4,4,2,48,1024]{4,3,2,1,0:T(8,128)(2,1)} %bitcast.52, bf16[2,3,4,2,48,1024]{5,4,3,2,1,0:T(8,128)(2,1)} %bitcast.51, ...), custom_call_target="tpu_custom_call" | custom-call | tf_op jit(solution)/shard_map/pallas_call | solution.py:1268
  543.1 41.5 %shard_map.283 = (f32[384,9216]{1,0:T(8,128)}, f32[384,9216]{1,0:T(8,128)}, f32[2,384,9216]{2,1,0:T(8,128)}, f32[384,128]{1,0:T(8,128)}) custom-call(s32[1]{0:T(128)S(6)} %copy.36.refs_0_, f32[2]{0:T(128)} %refs_1_.7, bf16[12,4,2,2,48,768]{5,4,3,2,1,0:T(8,128)(2,1)} %get-tuple-element.78.refs_2_, f32[384,9216]{1,0:T(8,128)} %refs_3_.6, f32[2,384,9216]{2,1,0:T(8,128)} %refs_4_.6), custom_call_target="tpu_custom_call" | custom-call | flops 70778880 | bytes 106168320 | tf_op jit(solution)/shard_map/pallas_call | solution.py:1408
  584.6 1.1 reduce_sum.19
  585.7 9.1 %shard_map.281 = (f32[384,1792]{1,0:T(8,128)}, f32[384,1792]{1,0:T(8,128)}, f32[2,384,1792]{2,1,0:T(8,128)}, f32[384,128]{1,0:T(8,128)}) custom-call(s32[1]{0:T(128)S(6)} %copy.36.refs_0_, f32[2]{0:T(128)} %refs_1_.7, bf16[12,4,2,2,48,768]{5,4,3,2,1,0:T(8,128)(2,1)} %get-tuple-element.78.refs_2_, f32[384,1792]{1,0:T(8,128)} %refs_3_.4, f32[2,384,1792]{2,1,0:T(8,128)} %refs_4_.4), custom_call_target="tpu_custom_call" | custom-call | flops 13762560 | bytes 20643840 | tf_op jit(solution)/shard_map/pallas_call | solution.py:1408
  594.8 1.1 reduce_sum.18
  595.9 19.7 %shard_map.284 = (f32[1152,1536]{1,0:T(8,128)}, f32[1152,1536]{1,0:T(8,128)}, f32[2,1152,1536]{2,1,0:T(8,128)}) custom-call(s32[1]{0:T(128)S(6)} %copy.36.refs_0_, f32[2]{0:T(128)} %refs_1_.7, bf16[12,4,2,2,48,768]{5,4,3,2,1,0:T(8,128)(2,1)} %get-tuple-element.78.refs_2_, f32[1152,1536]{1,0:T(8,128)} %refs_3_.7, f32[2,1152,1536]{2,1,0:T(8,128)} %refs_4_.7), custom_call_target="tpu_custom_call" | custom-call | flops 35389440 | bytes 53084160 | tf_op jit(solution)/shard_map/pallas_call | solution.py:1408
  615.6 0.0 copy-start.2
  615.6 0.0 copy-start.4
  615.6 0.0 copy-start.1
  615.6 7.2 %shard_map.282 = (f32[384,1536]{1,0:T(8,128)}, f32[384,1536]{1,0:T(8,128)}, f32[2,384,1536]{2,1,0:T(8,128)}) custom-call(s32[1]{0:T(128)S(6)} %copy.36.refs_0_, f32[2]{0:T(128)} %refs_1_.7, bf16[12,4,2,2,48,768]{5,4,3,2,1,0:T(8,128)(2,1)} %get-tuple-element.78.refs_2_, f32[384,1536]{1,0:T(8,128)} %refs_3_.5, f32[2,384,1536]{2,1,0:T(8,128)} %refs_4_.5), custom_call_target="tpu_custom_call" | custom-call | flops 11796480 | bytes 17694720 | tf_op jit(solution)/shard_map/pallas_call | solution.py:1408
  622.8 0.0 copy-start
  622.8 0.0 copy-done.2
  622.9 0.0 copy-done.4
  622.9 0.0 copy-start.5
  622.9 2.0 fusion.3
  624.9 0.6 pad_maximum_fusion
  625.5 0.0 copy-done.1
  625.5 1.1 copy.37
  626.6 0.0 copy-done
  626.6 1.1 copy.38
  627.8 0.0 copy-done.5
  (5 shorter events, 0.0 us)
Async XLA Ops:
  0.7 200.9 %collective-permute-start = (bf16[512,1536]{1,0:T(8,128)(2,1)}, bf16[512,1536]{1,0:T(8,128)(2,1)}, u32[]{:S(2)}, u32[]{:S(2)}) collective-permute-start(bf16[512,1536]{1,0:T(8,128)(2,1)} %bitcast.55), channel_id=1, source_target_pairs={{0,4},{4,0},{1,5},{5,1},{2,6},{6,2},{3,7},{7,3},{8,12},{12,8},{9,1... | collective-permute-start | bytes 4718600 | tf_op jit(solution)/shard_map/ppermute | solution.py:36
  8.9 192.0 %copy-start.3 = (f32[2]{0:T(128)S(1)}, f32[2]{0:T(128)}, u32[]{:S(2)}) copy-start(f32[2]{0:T(128)} %refs_1_.7) | copy-start | bytes 28
  615.6 7.2 %copy-start.2 = (f32[2,384]{1,0:T(2,128)S(1)}, f32[2,384]{1,0:T(2,128)}, u32[]{:S(2)}) copy-start(f32[2,384]{1,0:T(2,128)} %param.22) | copy-start | bytes 9220
  615.6 7.2 %copy-start.4 = (f32[2,2,384]{2,1,0:T(2,128)S(1)}, f32[2,2,384]{2,1,0:T(2,128)}, u32[]{:S(2)}) copy-start(f32[2,2,384]{2,1,0:T(2,128)} %param.27) | copy-start | bytes 18436
  615.6 9.9 %copy-start.1 = (bf16[512,1536]{1,0:T(8,128)(2,1)S(1)}, bf16[512,1536]{1,0:T(8,128)(2,1)}, u32[]{:S(2)}) copy-start(bf16[512,1536]{1,0:T(8,128)(2,1)} %get-tuple-element.76) | copy-start | bytes 4718596
  622.8 3.8 copy-start
  622.9 4.9 copy-start.5

commit v8 on v7

--- a/solution.py
+++ b/solution.py
@@ -713,7 +713,7 @@
     rows, D = two_own.shape
     part = two_t.shape[0]
     core = where[0]
-    block = 256
+    block = 512
 
     @pl.when(step == 0)
     def _():
@@ -759,7 +759,7 @@
 def mlp_call(core, two, df, gate_full, down_full):
     T, D = 2 * two[0].shape[0], two[0].shape[1]
     half_ff = gate_full.shape[1] // 2
-    tile = 768
+    tile = 256
     tiles = half_ff // tile
     part = max(D // tiles // 128 * 128, 256)
     last = D // part - 1
@@ -1672,9 +1672,7 @@
         in_grad, in_new, in_mom, gain_one = adam(
             input_proj, input_moments, 3 * tiles + 1, split_widths(in_half, d_half), gains=True
         )
-        gain_grad = jnp.stack(
-            [jnp.sum(v, axis=1) for v in (gain_one, gain_two)]
-        ) / gains_low.astype(F32)
+        gain_grad = jnp.sum(jnp.stack([gain_one, gain_two]), axis=2) / gains_low.astype(F32)
     else:
 
         def adam(weight, moments, grad):

time: 637 us -> 631 us (level)
  no operation moved by 1% of the time
where the time goes in v8:
time: 631 us; the launch traced here: 622 us
  Pallas kernels  607 us (96%)
  local copies, waits for them, and re-layouts  7.39 us (1%)
    pallas_call x1, Pallas kernels, backward(): pl.pallas_call(body, out_shape=(jax.ShapeDtypeStruct((nc, 4, 2, 2, r, n),...  282 us
    pallas_call x1, Pallas kernels, forward(): pl.pallas_call(body, out_shape=tuple(outs), in_specs=[ANY] * 4 + [VM] * 6...  192 us
    pallas_call x4, Pallas kernels, adam_call(): pl.pallas_call(body, grid=(4 // chips, 2, sides, tiles), in_specs=[smem,...  77.5 us
    pallas_call x1, Pallas kernels, mlp_call(): pl.pallas_call(body, grid_spec=pltpu.PrefetchScalarGridSpec(num_scalar_pr...  55.4 us
  transfers between devices with their start and end apart: 1, of which 0 were waited for; matrix products, arithmetic and copies ran while one was open for 1% of the time, Pallas kernels for 31%

profile of v8, /device:TPU:0, one launch (start us, length us, event | category | flops | bytes accessed | tf_op | source)
XLA Modules:
  0.0 621.6 jit_solution(17861192974374769323)
XLA Ops:
  0.7 0.5 collective-permute-start
  1.2 0.8 pad_dynamic-slice_fusion
  1.9 1.1 broadcast_in_dim.27.refs_9_.refs_17_
  3.1 0.7 convert_element_type.22
  3.8 1.2 concatenate.9.refs_4_
  5.8 0.1 compare_select_fusion
  5.8 1.3 constant_dynamic-slice_fusion.refs_8_.refs_16_
  7.1 1.8 fusion
  8.9 0.0 copy-start.5
  8.9 191.9 %shard_map.278 = (bf16[4,4,2,48,1792]{4,3,2,1,0:T(8,128)(2,1)}, bf16[4,4,2,48,1536]{4,3,2,1,0:T(8,128)(2,1)}, bf16[4,4,2,144,1536]{4,3,2,1,0:T(8,128)(2,1)}, bf1...) custom-call(f32[4,2,48,1792]{3,2,1,0:T(8,128)} %bitcast.47, ...), custom_call_target="tpu_custom_call" | custom-call | tf_op jit(solution)/shard_map/pallas_call | solution.py:596
  200.9 0.0 copy-done.5
  200.9 0.6 fusion.4
  201.5 0.0 collective-permute-done.refs_4_.refs_8_
  201.5 55.4 %shard_map.279 = (bf16[1536,1024]{1,0:T(8,128)(2,1)}, bf16[2304,1024]{1,0:T(8,128)(2,1)}, bf16[2,1024,2304]{2,1,0:T(8,128)(2,1)}, bf16[1024,1536]{1,0:T(8,128)(2,1)}) custom-call(s32[1]{0:T(128)} %bitcast.refs_0_, bf16[512,1536]{1,0:T(8,128)(2,1)} %get-tuple-element.55.refs_1_, bf16[512,1536]{1,0:T(8,128)(2,1)} %get-tuple-element.56.refs_2_, ...), custom_call_target="tpu_custom_call" | custom-call | flops 36238786560 | bytes 41943040 | tf_op jit(solution)/shard_map/pallas_call | solution.py:772
  256.9 281.8 %shard_map.280 = (bf16[12,4,2,2,48,768]{5,4,3,2,1,0:T(8,128)(2,1)}, bf16[2,3,4,2,48,1024]{5,4,3,2,1,0:T(8,128)(2,1)}, bf16[512,1536]{1,0:T(8,128)(2,1)}, bf16[512,1536]{1,0:T(8,128)(2,1)}, f32[512,1536]{1,0:T(8,128)}) custom-call(bf16[4,4,2,48,1024]{4,3,2,1,0:T(8,128)(2,1)} %bitcast.54, bf16[2,3,4,2,48,1024]{5,4,3,2,1,0:T(8,128)(2,1)} %bitcast.53, ...), custom_call_target="tpu_custom_call" | custom-call | tf_op jit(solution)/shard_map/pallas_call | solution.py:1268
  538.7 41.4 %shard_map.283 = (f32[384,9216]{1,0:T(8,128)}, f32[384,9216]{1,0:T(8,128)}, f32[2,384,9216]{2,1,0:T(8,128)}, f32[384,128]{1,0:T(8,128)}) custom-call(s32[1]{0:T(128)S(6)} %copy.36.refs_0_, f32[2]{0:T(128)} %refs_1_.7, bf16[12,4,2,2,48,768]{5,4,3,2,1,0:T(8,128)(2,1)} %get-tuple-element.78.refs_2_, f32[384,9216]{1,0:T(8,128)} %refs_3_.6, f32[2,384,9216]{2,1,0:T(8,128)} %refs_4_.6), custom_call_target="tpu_custom_call" | custom-call | flops 70778880 | bytes 106168320 | tf_op jit(solution)/shard_map/pallas_call | solution.py:1408
  580.1 9.1 %shard_map.281 = (f32[384,1792]{1,0:T(8,128)}, f32[384,1792]{1,0:T(8,128)}, f32[2,384,1792]{2,1,0:T(8,128)}, f32[384,128]{1,0:T(8,128)}) custom-call(s32[1]{0:T(128)S(6)} %copy.36.refs_0_, f32[2]{0:T(128)} %refs_1_.7, bf16[12,4,2,2,48,768]{5,4,3,2,1,0:T(8,128)(2,1)} %get-tuple-element.78.refs_2_, f32[384,1792]{1,0:T(8,128)} %refs_3_.4, f32[2,384,1792]{2,1,0:T(8,128)} %refs_4_.4), custom_call_target="tpu_custom_call" | custom-call | flops 13762560 | bytes 20643840 | tf_op jit(solution)/shard_map/pallas_call | solution.py:1408
  589.2 19.7 %shard_map.284 = (f32[1152,1536]{1,0:T(8,128)}, f32[1152,1536]{1,0:T(8,128)}, f32[2,1152,1536]{2,1,0:T(8,128)}) custom-call(s32[1]{0:T(128)S(6)} %copy.36.refs_0_, f32[2]{0:T(128)} %refs_1_.7, bf16[12,4,2,2,48,768]{5,4,3,2,1,0:T(8,128)(2,1)} %get-tuple-element.78.refs_2_, f32[1152,1536]{1,0:T(8,128)} %refs_3_.7, f32[2,1152,1536]{2,1,0:T(8,128)} %refs_4_.7), custom_call_target="tpu_custom_call" | custom-call | flops 35389440 | bytes 53084160 | tf_op jit(solution)/shard_map/pallas_call | solution.py:1408
  608.9 0.0 copy-start.2
  608.9 0.0 copy-start.3
  608.9 0.0 copy-start.4
  608.9 0.0 copy-start.6
  609.0 0.0 copy-start.1
  609.0 7.2 %shard_map.282 = (f32[384,1536]{1,0:T(8,128)}, f32[384,1536]{1,0:T(8,128)}, f32[2,384,1536]{2,1,0:T(8,128)}) custom-call(s32[1]{0:T(128)S(6)} %copy.36.refs_0_, f32[2]{0:T(128)} %refs_1_.7, bf16[12,4,2,2,48,768]{5,4,3,2,1,0:T(8,128)(2,1)} %get-tuple-element.78.refs_2_, f32[384,1536]{1,0:T(8,128)} %refs_3_.5, f32[2,384,1536]{2,1,0:T(8,128)} %refs_4_.5), custom_call_target="tpu_custom_call" | custom-call | flops 11796480 | bytes 17694720 | tf_op jit(solution)/shard_map/pallas_call | solution.py:1408
  616.2 0.0 copy-start
  616.2 0.0 copy-done.2
  616.2 0.0 copy-done.3
  616.2 0.2 maximum_reduce_fusion
  616.4 0.0 copy-done.4
  616.4 0.0 copy-done.6
  616.5 0.0 copy-start.7
  616.5 2.1 fusion.3
  618.5 0.6 pad_maximum_fusion
  619.1 0.0 copy-done.1
  619.1 1.1 copy.37
  620.3 0.0 copy-done
  620.3 1.1 copy.38
  621.4 0.0 copy-done.7
  (3 shorter events, 0.0 us)
Async XLA Ops:
  0.7 200.9 %collective-permute-start = (bf16[512,1536]{1,0:T(8,128)(2,1)}, bf16[512,1536]{1,0:T(8,128)(2,1)}, u32[]{:S(2)}, u32[]{:S(2)}) collective-permute-start(bf16[512,1536]{1,0:T(8,128)(2,1)} %bitcast.57), channel_id=1, source_target_pairs={{0,4},{4,0},{1,5},{5,1},{2,6},{6,2},{3,7},{7,3},{8,12},{12,8},{9,1... | collective-permute-start | bytes 4718600 | tf_op jit(solution)/shard_map/ppermute | solution.py:36
  8.9 191.9 %copy-start.5 = (f32[2]{0:T(128)S(1)}, f32[2]{0:T(128)}, u32[]{:S(2)}) copy-start(f32[2]{0:T(128)} %refs_1_.7) | copy-start | bytes 28
  608.9 7.3 %copy-start.2 = (f32[384,128]{1,0:T(8,128)S(1)}, f32[384,128]{1,0:T(8,128)}, u32[]{:S(2)}) copy-start(f32[384,128]{1,0:T(8,128)} %get-tuple-element.84) | copy-start | bytes 589828
  608.9 7.3 %copy-start.3 = (f32[384,128]{1,0:T(8,128)S(1)}, f32[384,128]{1,0:T(8,128)}, u32[]{:S(2)}) copy-start(f32[384,128]{1,0:T(8,128)} %get-tuple-element.83) | copy-start | bytes 589828
  608.9 7.5 %copy-start.4 = (f32[2,384]{1,0:T(2,128)S(1)}, f32[2,384]{1,0:T(2,128)}, u32[]{:S(2)}) copy-start(f32[2,384]{1,0:T(2,128)} %param.22) | copy-start | bytes 9220
  608.9 7.5 %copy-start.6 = (f32[2,2,384]{2,1,0:T(2,128)S(1)}, f32[2,2,384]{2,1,0:T(2,128)}, u32[]{:S(2)}) copy-start(f32[2,2,384]{2,1,0:T(2,128)} %param.27) | copy-start | bytes 18436
  609.0 10.2 %copy-start.1 = (bf16[512,1536]{1,0:T(8,128)(2,1)S(1)}, bf16[512,1536]{1,0:T(8,128)(2,1)}, u32[]{:S(2)}) copy-start(bf16[512,1536]{1,0:T(8,128)(2,1)} %get-tuple-element.76) | copy-start | bytes 4718596
  616.2 4.1 copy-start
  616.5 5.0 copy-start.7
